TPU v7x, 512 devices: a whole 4x4x16 slice. The times are simulated.
512 devices in a mesh: wide: 64 (over z, y_lo, core), narrow: 8 (over x, y_hi).
Axes of the slice: x: 4, y: 4 (y_hi: 2, y_lo: 2; y = y_hi * 2 + y_lo), z: 16, core: 2. Of those that a mesh axis runs over, the one named last changes fastest.
Arguments:
- queries: bfloat16 [65536, 256], P(('wide', 'narrow')), may hold values from -16 to 16
- hot_table: bfloat16 [2048, 256], replicated, may hold values from -1.5 to 1.5
- cold_table: bfloat16 [16384, 256], P(('wide', 'narrow')), may hold values from -1.25 to 1.25
- hot_ids: int32 [2048], replicated, may hold values from 0 to 18431, as said below
- targets: int32 [65536], replicated, may hold values from 0 to 18431
Outputs:
- grad_queries: bfloat16 [65536, 256], P(('wide', 'narrow'))
- grad_hot: bfloat16 [2048, 256], replicated
- grad_cold: bfloat16 [16384, 256], P(('wide', 'narrow'))
- row_loss: float32 [65536], P(('wide', 'narrow'))
Inputs may be any that keep to these rules, and one draw needn't show every extreme that they name: `hot_ids`: 2048 distinct catalogue ids in no particular order.
All inputs are finite; a program needn't handle non-finite values.
Results may differ from a plain program's by a relative error of at most 0.006.
Values may be sent and summed in bfloat16 or wider, within the bound.
No kernel may reach another device: no remote copies, remote signals or barrier semaphores. Data moves between devices by JAX's collectives and lax.ppermute only.
A program may use at most 64 MiB of HBM per device.

v0:
```python
import jax
import jax.numpy as jnp
from jax import lax
from jax.sharding import PartitionSpec as P


def decode_targets(hot_ids, targets):
    sorter = jnp.argsort(hot_ids)
    ordered = jnp.take(hot_ids, sorter)
    below = jnp.searchsorted(ordered, targets)
    clipped = jnp.minimum(below, hot_ids.shape[0] - 1)
    is_hot = jnp.take(ordered, clipped) == targets
    hot_slot = jnp.take(sorter, clipped)
    return (is_hot, hot_slot, targets - below)


def scores(query_rows, table):
    return jnp.einsum("rh,ch->rc", query_rows, table, preferred_element_type=jnp.float32)


def body(queries, hot_table, cold_table, hot_ids, targets):
    narrow_size = lax.axis_size("narrow")
    wide_pos = lax.axis_index("wide")
    narrow_pos = lax.axis_index("narrow")
    own_rows = queries.shape[0]
    feature_width = queries.shape[1]
    grouped = lax.all_gather(queries, "narrow", axis=0, tiled=True)
    cold_block = lax.all_gather(cold_table, "wide", axis=0, tiled=True)
    group_rows = grouped.shape[0]
    group_start = wide_pos * group_rows
    shard_rows = cold_table.shape[0]
    gathered_rows = cold_block.shape[0]
    group_targets = lax.dynamic_slice_in_dim(targets, group_start, group_rows, 0)
    is_hot, hot_slot, cold_row = decode_targets(hot_ids, group_targets)
    cold_shard = cold_row // shard_rows
    inside = cold_shard % narrow_size == narrow_pos
    cold_local = cold_shard // narrow_size * shard_rows + cold_row % shard_rows
    cold_column = jnp.where(jnp.logical_or(is_hot, jnp.logical_not(inside)), -1, cold_local)
    hot_offset = narrow_pos * own_rows
    hot_rows = queries.shape[0]
    part_hot = lax.dynamic_slice_in_dim(is_hot, hot_offset, hot_rows, 0)
    part_slot = lax.dynamic_slice_in_dim(hot_slot, hot_offset, hot_rows, 0)
    hot_inside = jnp.logical_and(part_slot >= 0, part_slot < hot_table.shape[0])
    hot_column = jnp.where(jnp.logical_and(part_hot, hot_inside), part_slot, -1)
    hot_scores = scores(queries, hot_table)
    block_rows = min(group_rows, 512)
    block_count = group_rows // block_rows
    query_blocks = grouped.reshape(block_count, block_rows, feature_width)
    column_blocks = cold_column.reshape(block_count, block_rows)

    def block_top(query_rows):
        return jnp.max(scores(query_rows, cold_block), axis=1)

    row_tops = lax.map(block_top, query_blocks).reshape(group_rows)
    part_top = jnp.maximum(
        lax.dynamic_slice_in_dim(row_tops, hot_offset, hot_rows, 0), jnp.max(hot_scores, axis=1)
    )
    row_tops = lax.dynamic_update_slice_in_dim(row_tops, part_top, hot_offset, 0)
    top_all = lax.pmax(row_tops, "narrow")

    def block_sum(pieces):
        query_rows, row_top = pieces
        return jnp.sum(jnp.exp(scores(query_rows, cold_block) - row_top[:, None]), axis=1)

    row_sums = lax.map(block_sum, (query_blocks, top_all.reshape(block_count, block_rows))).reshape(
        group_rows
    )
    part_tops = lax.dynamic_slice_in_dim(top_all, hot_offset, hot_rows, 0)
    part_sum = lax.dynamic_slice_in_dim(row_sums, hot_offset, hot_rows, 0) + jnp.sum(
        jnp.exp(hot_scores - part_tops[:, None]), axis=1
    )
    row_sums = lax.dynamic_update_slice_in_dim(row_sums, part_sum, hot_offset, 0)
    sum_all = lax.psum(row_sums, "narrow")
    log_total = top_all + jnp.log(sum_all)

    def block_grads(running, pieces):
        query_rows, row_logs, columns = pieces
        logits = scores(query_rows, cold_block)
        is_target = lax.broadcasted_iota(jnp.int32, logits.shape, 1) == columns[:, None]
        weights = (jnp.exp(logits - row_logs[:, None]) - is_target.astype(jnp.float32)).astype(
            jnp.bfloat16
        )
        query_part = jnp.dot(weights, cold_block, preferred_element_type=jnp.float32)
        running = running + jnp.einsum(
            "rc,rh->ch", weights, query_rows, preferred_element_type=jnp.float32
        )
        target_part = jnp.sum(jnp.where(is_target, logits, 0.0), axis=1)
        return (running, (query_part, target_part))

    cold_grad, (query_terms, target_terms) = lax.scan(
        block_grads,
        jnp.zeros((gathered_rows, feature_width), jnp.float32),
        (query_blocks, log_total.reshape(block_count, block_rows), column_blocks),
    )
    query_terms = query_terms.reshape(group_rows, feature_width)
    target_terms = target_terms.reshape(group_rows)
    part_logs = lax.dynamic_slice_in_dim(log_total, hot_offset, hot_rows, 0)
    hot_hit = lax.broadcasted_iota(jnp.int32, hot_scores.shape, 1) == hot_column[:, None]
    hot_weights = (jnp.exp(hot_scores - part_logs[:, None]) - hot_hit.astype(jnp.float32)).astype(
        jnp.bfloat16
    )
    hot_query = jnp.dot(hot_weights, hot_table, preferred_element_type=jnp.float32)
    hot_grad_part = jnp.einsum(
        "rc,rh->ch", hot_weights, queries, preferred_element_type=jnp.float32
    )
    hot_target = jnp.sum(jnp.where(hot_hit, hot_scores, 0.0), axis=1)
    query_terms = lax.dynamic_update_slice_in_dim(
        query_terms,
        lax.dynamic_slice_in_dim(query_terms, hot_offset, hot_rows, 0) + hot_query,
        hot_offset,
        0,
    )
    target_terms = lax.dynamic_update_slice_in_dim(
        target_terms,
        lax.dynamic_slice_in_dim(target_terms, hot_offset, hot_rows, 0) + hot_target,
        hot_offset,
        0,
    )
    own_query, own_target = (
        lax.psum_scatter(query_terms, "narrow", scatter_dimension=0, tiled=True),
        lax.psum_scatter(target_terms, "narrow", scatter_dimension=0, tiled=True),
    )
    own_cold = lax.psum_scatter(cold_grad, "wide", scatter_dimension=0, tiled=True)
    grad_hot = lax.psum(hot_grad_part, ("wide", "narrow")).astype(jnp.bfloat16)
    own_logs = lax.dynamic_slice_in_dim(log_total, narrow_pos * own_rows, own_rows, 0)
    row_loss = own_logs - own_target
    return (own_query.astype(jnp.bfloat16), grad_hot, own_cold.astype(jnp.bfloat16), row_loss)


def solution(mesh):
    return jax.shard_map(
        body,
        mesh=mesh,
        in_specs=(P(("wide", "narrow"), None), P(), P(("wide", "narrow"), None), P(), P()),
        out_specs=(
            P(("wide", "narrow"), None),
            P(),
            P(("wide", "narrow"), None),
            P(("wide", "narrow")),
        ),
        check_vma=False,
    )
```

profile of v0, /device:TPU:1, one launch (start us, length us, event | category | flops | bytes accessed | tf_op | source)
XLA Modules:
  0.0 576.7 jit_solution(16438915940407316873)
XLA Ops:
  8.0 5.7 sort.17
  13.8 11.8 %gather_fusion.1 = s32[2048]{0:T(1024)S(1)} fusion(s32[2048]{0:T(1024)S(1)} %copy-done.1, s32[2048]{0:T(1024)S(1)} %fusion.15), kind=kCustom, calls=%fused_computation.3 | custom fusion | bytes 24576 | tf_op jit(solution)/shard_map/jit(_take)/gather | solution.py:9
  26.3 74.8 %while.61 = (s32[]{:T(128)}, u32[1024]{0:T(1024)S(1)}, u32[1024]{0:T(1024)S(1)}, s32[2048]{0:T(1024)S(1)}, s32[1024]{0:T(1024)S(1)}, /*index=5*/s32[]{:T(128)}, s32[]{:T(128)}, s32[]{}) while((s32[]{:T(128)}, u32[1024]{0:T(1024)S(1)}, u32[1024]{0:T(1024)S(1)}, s32[2048]{0:T(1024)S(1)}, s32[1024]{0:T(1024)S(1)}, ...), condition=%wide.region_12.13_spmd.clone, body=%wide.region_11.12_spmd.clone.sunk | while | flops 19460 | bytes 67693 | solution.py:10
  26.3 6.1 %gather_fusion = s32[1024]{0:T(1024)S(1)} fusion(s32[2048]{0:T(1024)S(1)} %get-tuple-element.475, u32[1024]{0:T(1024)S(1)} %broadcast_clamp_fusion.2), kind=kCustom, calls=%fused_computation.clone.clone.1 | custom fusion | bytes 12288 | tf_op jit(solution)/shard_map/jit(searchsorted)/jit(_searchsorted_scan_impl)/vmap(jit(_searchsorted_scan_impl))/while/body/eval_jaxpr/gather | solution.py:10
  32.5 6.2 %gather_fusion = s32[1024]{0:T(1024)S(1)} fusion(s32[2048]{0:T(1024)S(1)} %get-tuple-element.475, u32[1024]{0:T(1024)S(1)} %broadcast_clamp_fusion.2), kind=kCustom, calls=%fused_computation.clone.clone.1 | custom fusion | bytes 12288 | tf_op jit(solution)/shard_map/jit(searchsorted)/jit(_searchsorted_scan_impl)/vmap(jit(_searchsorted_scan_impl))/while/body/eval_jaxpr/gather | solution.py:10
  38.7 6.2 %gather_fusion = s32[1024]{0:T(1024)S(1)} fusion(s32[2048]{0:T(1024)S(1)} %get-tuple-element.475, u32[1024]{0:T(1024)S(1)} %broadcast_clamp_fusion.2), kind=kCustom, calls=%fused_computation.clone.clone.1 | custom fusion | bytes 12288 | tf_op jit(solution)/shard_map/jit(searchsorted)/jit(_searchsorted_scan_impl)/vmap(jit(_searchsorted_scan_impl))/while/body/eval_jaxpr/gather | solution.py:10
  45.0 6.2 %gather_fusion = s32[1024]{0:T(1024)S(1)} fusion(s32[2048]{0:T(1024)S(1)} %get-tuple-element.475, u32[1024]{0:T(1024)S(1)} %broadcast_clamp_fusion.2), kind=kCustom, calls=%fused_computation.clone.clone.1 | custom fusion | bytes 12288 | tf_op jit(solution)/shard_map/jit(searchsorted)/jit(_searchsorted_scan_impl)/vmap(jit(_searchsorted_scan_impl))/while/body/eval_jaxpr/gather | solution.py:10
  51.2 6.2 %gather_fusion = s32[1024]{0:T(1024)S(1)} fusion(s32[2048]{0:T(1024)S(1)} %get-tuple-element.475, u32[1024]{0:T(1024)S(1)} %broadcast_clamp_fusion.2), kind=kCustom, calls=%fused_computation.clone.clone.1 | custom fusion | bytes 12288 | tf_op jit(solution)/shard_map/jit(searchsorted)/jit(_searchsorted_scan_impl)/vmap(jit(_searchsorted_scan_impl))/while/body/eval_jaxpr/gather | solution.py:10
  57.4 6.2 %gather_fusion = s32[1024]{0:T(1024)S(1)} fusion(s32[2048]{0:T(1024)S(1)} %get-tuple-element.475, u32[1024]{0:T(1024)S(1)} %broadcast_clamp_fusion.2), kind=kCustom, calls=%fused_computation.clone.clone.1 | custom fusion | bytes 12288 | tf_op jit(solution)/shard_map/jit(searchsorted)/jit(_searchsorted_scan_impl)/vmap(jit(_searchsorted_scan_impl))/while/body/eval_jaxpr/gather | solution.py:10
  63.7 6.2 %gather_fusion = s32[1024]{0:T(1024)S(1)} fusion(s32[2048]{0:T(1024)S(1)} %get-tuple-element.475, u32[1024]{0:T(1024)S(1)} %broadcast_clamp_fusion.2), kind=kCustom, calls=%fused_computation.clone.clone.1 | custom fusion | bytes 12288 | tf_op jit(solution)/shard_map/jit(searchsorted)/jit(_searchsorted_scan_impl)/vmap(jit(_searchsorted_scan_impl))/while/body/eval_jaxpr/gather | solution.py:10
  69.9 6.2 %gather_fusion = s32[1024]{0:T(1024)S(1)} fusion(s32[2048]{0:T(1024)S(1)} %get-tuple-element.475, u32[1024]{0:T(1024)S(1)} %broadcast_clamp_fusion.2), kind=kCustom, calls=%fused_computation.clone.clone.1 | custom fusion | bytes 12288 | tf_op jit(solution)/shard_map/jit(searchsorted)/jit(_searchsorted_scan_impl)/vmap(jit(_searchsorted_scan_impl))/while/body/eval_jaxpr/gather | solution.py:10
  76.2 6.2 %gather_fusion = s32[1024]{0:T(1024)S(1)} fusion(s32[2048]{0:T(1024)S(1)} %get-tuple-element.475, u32[1024]{0:T(1024)S(1)} %broadcast_clamp_fusion.2), kind=kCustom, calls=%fused_computation.clone.clone.1 | custom fusion | bytes 12288 | tf_op jit(solution)/shard_map/jit(searchsorted)/jit(_searchsorted_scan_impl)/vmap(jit(_searchsorted_scan_impl))/while/body/eval_jaxpr/gather | solution.py:10
  82.4 6.2 %gather_fusion = s32[1024]{0:T(1024)S(1)} fusion(s32[2048]{0:T(1024)S(1)} %get-tuple-element.475, u32[1024]{0:T(1024)S(1)} %broadcast_clamp_fusion.2), kind=kCustom, calls=%fused_computation.clone.clone.1 | custom fusion | bytes 12288 | tf_op jit(solution)/shard_map/jit(searchsorted)/jit(_searchsorted_scan_impl)/vmap(jit(_searchsorted_scan_impl))/while/body/eval_jaxpr/gather | solution.py:10
  88.6 6.2 %gather_fusion = s32[1024]{0:T(1024)S(1)} fusion(s32[2048]{0:T(1024)S(1)} %get-tuple-element.475, u32[1024]{0:T(1024)S(1)} %broadcast_clamp_fusion.2), kind=kCustom, calls=%fused_computation.clone.clone.1 | custom fusion | bytes 12288 | tf_op jit(solution)/shard_map/jit(searchsorted)/jit(_searchsorted_scan_impl)/vmap(jit(_searchsorted_scan_impl))/while/body/eval_jaxpr/gather | solution.py:10
  94.9 6.2 %gather_fusion = s32[1024]{0:T(1024)S(1)} fusion(s32[2048]{0:T(1024)S(1)} %get-tuple-element.475, u32[1024]{0:T(1024)S(1)} %broadcast_clamp_fusion.2), kind=kCustom, calls=%fused_computation.clone.clone.1 | custom fusion | bytes 12288 | tf_op jit(solution)/shard_map/jit(searchsorted)/jit(_searchsorted_scan_impl)/vmap(jit(_searchsorted_scan_impl))/while/body/eval_jaxpr/gather | solution.py:10
  101.1 6.2 %gather_fusion.3 = s32[1024]{0:T(1024)S(1)} fusion(s32[2048]{0:T(1024)S(1)} %get-tuple-element.166, s32[1024]{0:T(1024)S(1)} %fusion.25), kind=kCustom, calls=%fused_computation.2.clone | custom fusion | bytes 12288 | tf_op jit(solution)/shard_map/jit(_take)/gather | solution.py:13
  107.3 6.2 %gather_fusion.2 = s32[1024]{0:T(1024)S(1)} fusion(s32[2048]{0:T(1024)S(1)} %get-tuple-element.513, s32[1024]{0:T(1024)S(1)} %fusion.25), kind=kCustom, calls=%fused_computation.1.clone | custom fusion | bytes 12288 | tf_op jit(solution)/shard_map/jit(_take)/gather | solution.py:12
  116.2 32.5 %all_gather.6 = bf16[1024,256]{1,0:T(8,128)(2,1)} all-gather(bf16[128,256]{1,0:T(8,128)(2,1)S(1)} %copy-done.5), channel_id=1, replica_groups=mesh['wide'=64,'narrow'=8] {'narrow'}, dimensions={0}, use_global_device_ids=true | all-gather | bytes 589824 | tf_op jit(solution)/shard_map/all_gather | solution.py:27
  150.2 4.4 while.59
  154.8 19.9 %pmax.7 = f32[1024]{0:T(1024)S(1)} all-reduce(f32[1024]{0:T(1024)S(1)} %maximum_dynamic-update-slice_fusion), channel_id=1, replica_groups=mesh['wide'=64,'narrow'=8] {'narrow'}, use_global_device_ids=true, to_apply=%region_4.5 | all-reduce | flops 1024 | bytes 8192 | tf_op jit(solution)/shard_map/pmax | solution.py:59
  174.8 4.4 while.60
  174.8 2.2 exponential_reduce_fusion.3
  181.1 15.5 %psum.14 = f32[1024]{0:T(1024)S(1)} all-reduce(f32[1024]{0:T(1024)S(1)} %add_dynamic-update-slice_fusion.1), channel_id=1, replica_groups=mesh['wide'=64,'narrow'=8] {'narrow'}, use_global_device_ids=true, to_apply=%region_9.10 | all-reduce | flops 1024 | bytes 8192 | tf_op jit(solution)/shard_map/psum | solution.py:73
  196.6 19.1 %while.62 = (s32[]{:T(128)}, f32[2048,256]{1,0:T(8,128)S(1)}, f32[2,512,256]{2,1,0:T(8,128)}, f32[2,512]{1,0:T(2,128)S(1)}, bf16[2,512,256]{2,1,0:T(8,128)(2,1)}...) while((s32[]{:T(128)}, f32[2048,256]{1,0:T(8,128)S(1)}, ...), condition=%wide.region_15.17_spmd.clone, body=%wide.region_13.16_spmd.clone.sunk | while | flops 1619000832 | bytes 24135880 | solution.py:90
  196.6 4.2 select_reduce_fusion.3
  200.9 3.5 fusion.57
  206.2 4.2 select_reduce_fusion.3
  210.5 3.5 fusion.57
  215.9 18.4 %all-reduce = f32[1024]{0:T(1024)S(1)} all-reduce(f32[1024]{0:T(1024)S(1)} %add_dynamic-update-slice_fusion), channel_id=4, replica_groups=mesh['wide'=64,'narrow'=8] {'narrow'}, use_global_device_ids=true, to_apply=%region_20.22.clone | all-reduce | flops 1024 | bytes 8192
  234.9 2.3 fusion.14
  239.8 135.8 %all-reduce.2 = bf16[2048,256]{1,0:T(8,128)(2,1)} all-reduce(f32[2048,256]{1,0:T(8,128)S(1)} %fusion.26), channel_id=1, replica_groups=mesh['wide'=64,'narrow'=8] {'wide','narrow'}, use_global_device_ids=true, to_apply=%region_17.19 | all-reduce | flops 524288 | bytes 3145728 | tf_op jit(solution)/shard_map/psum | solution.py:124
  377.2 191.6 %reduce-scatter.5.cloned.1.call-done = f32[32,256]{1,0:T(8,128)} async-done(((f32[2048,256]{1,0:T(8,128)}), f32[32,256]{1,0:T(8,128)}) %reduce-scatter.5.cloned.1.call-update) | async-done | bytes 32784 | tf_op jit(solution)/shard_map/reduce_scatter | solution.py:123
  (122 shorter events, 23.8 us)
Async XLA Ops:
  7.2 141.6 %copy-start = (bf16[2048,256]{1,0:T(8,128)(2,1)S(1)}, bf16[2048,256]{1,0:T(8,128)(2,1)}, u32[]{:S(2)}) copy-start(bf16[2048,256]{1,0:T(8,128)(2,1)} %param.16) | copy-start | bytes 3145732
  7.2 6.6 %copy-start.1 = (s32[2048]{0:T(1024)S(1)}, s32[2048]{0:T(1024)}, u32[]{:S(2)}) copy-start(s32[2048]{0:T(1024)} %param.18) | copy-start | bytes 24580
  7.2 143.0 %all-gather.2.cloned.1.call-start = ((), (), s32[]{:S(2)}) async-start(), calls=%async_computation.2 | async-start | bytes 1064960 | tf_op jit(solution)/shard_map/all_gather | solution.py:28
  7.9 367.7 %reduce-scatter.3.cloned.1.call-start = ((), (), s32[]{:S(2)}) async-start(), calls=%async_computation.3 | async-start | bytes 1179648 | tf_op jit(solution)/shard_map/reduce_scatter | solution.py:120
  107.3 8.9 %copy-start.5 = (bf16[128,256]{1,0:T(8,128)(2,1)S(1)}, bf16[128,256]{1,0:T(8,128)(2,1)}, u32[]{:S(2)}) copy-start(bf16[128,256]{1,0:T(8,128)(2,1)} %param.15) | copy-start | bytes 196612
  200.9 3.5 copy-start.3
  200.9 3.5 copy-start.4
  210.5 3.6 copy-start.3
  210.5 3.6 copy-start.4
  215.7 21.6 %copy-start.2 = (f32[2048,256]{1,0:T(8,128)}, f32[2048,256]{1,0:T(8,128)S(1)}, u32[]{:S(2)}) copy-start(f32[2048,256]{1,0:T(8,128)S(1)} %get-tuple-element.169) | copy-start | bytes 6291460
  237.2 331.5 %reduce-scatter.5.cloned.1.call-start = ((), (), s32[]{:S(2)}) async-start(), calls=%async_computation.4 | async-start | bytes 2129920 | tf_op jit(solution)/shard_map/reduce_scatter | solution.py:123
Sparse Core Ops, SparseCore 0:
  10.2 126.2 all-gather.1
  237.4 102.4 reduce-scatter.2
  342.9 225.8 reduce-scatter.4
where the time goes:
time: 580 us; the launch traced here: 577 us
  blocking collectives  222 us (38%)
  waiting for transfers between devices  193 us (33%)
  local copies, waits for them, and re-layouts  100 us (17%)
  matrix products  33 us (6%)
  between operations  14.6 us (3%)
  other arithmetic  12.6 us (2%)
    reduce_scatter x1, waiting for transfers between devices, body(): lax.psum_scatter(cold_grad, 'wide', scatter_dimension=0, tiled=True)  192 us
    psum x1, blocking collectives, body(): grad_hot = lax.psum(hot_grad_part, ('wide', 'narrow')).astype(jnp.bfloat16)  136 us
    gather x12, local copies, waits for them, and re-layouts, decode_targets(): below = jnp.searchsorted(ordered, targets)  73.8 us
    all_gather x1, blocking collectives, body(): grouped = lax.all_gather(queries, 'narrow', axis=0, tiled=True)  32.5 us
    pmax x1, blocking collectives, body(): top_all = lax.pmax(row_tops, 'narrow')  19.9 us
    dot_general x7, matrix products, scores(): jnp.einsum('rh,ch->rc', query_rows, table, preferred_element_type=jnp.flo...  18.6 us
    unnamed x1, blocking collectives  18.4 us
    psum x1, blocking collectives, body(): sum_all = lax.psum(row_sums, 'narrow')  15.5 us
  transfers between devices with their start and end apart: 3, of which 1 were waited for; matrix products, arithmetic and copies ran while one was open for 19% of the time, Pallas kernels for 0%

commit v1 on v0

v1 whole, which is shorter than its diff:
```python
import functools

import jax
import jax.numpy as jnp
from jax import lax
from jax.experimental import pallas as pl
from jax.experimental.pallas import tpu as pltpu
from jax.sharding import Mesh
from jax.sharding import PartitionSpec as P

AXES = ("z", "yl", "c", "x2", "x1", "yh")
COLS = ("c", "x2", "yh")
NEAR = ("yl", "x1")
PLANE = COLS + NEAR
BF = jnp.bfloat16
F32 = jnp.float32
NT = (((1,), (1,)), ((), ()))
TN = (((0,), (0,)), ((), ()))


def spread(x, axes):
    n = lax.axis_size(axes)
    return lax.all_to_all(jnp.broadcast_to(x[None], (n, *x.shape)), axes, 0, 0)


def stats_kernel(table_ref, rows_ref, col_ref, out_ref):
    chunks, width, _ = table_ref.shape
    rows = rows_ref[...]
    cols = col_ref[...]
    count = rows.shape[0]

    def step(g, carry):
        top, total, hit = carry
        s = lax.dot_general(table_ref[g], rows, NT, preferred_element_type=F32)
        new = jnp.maximum(top, jnp.max(s, axis=0, keepdims=True))
        total = total * jnp.exp(top - new) + jnp.sum(jnp.exp(s - new), axis=0, keepdims=True)
        where = lax.broadcasted_iota(jnp.int32, s.shape, 0) + g * width == cols
        hit = hit + jnp.sum(jnp.where(where, s, 0.0), axis=0, keepdims=True)
        return new, total, hit

    zero = jnp.zeros((1, count), F32)
    top, total, hit = lax.fori_loop(0, chunks, step, (jnp.full((1, count), -1e30, F32), zero, zero))
    out_ref[0:1] = top
    out_ref[1:2] = total
    out_ref[2:3] = hit
    out_ref[3:8] = jnp.zeros((5, count), F32)


def grads_kernel(table_ref, rows_ref, col_ref, stats_ref, query_ref, item_ref, loss_ref, acc_ref):
    chunks, width, _ = table_ref.shape
    rows = rows_ref[...]
    cols = col_ref[...]
    parts = stats_ref.shape[0]
    tops = [stats_ref[k, 0:1] for k in range(parts)]
    top = functools.reduce(jnp.maximum, tops)
    total = sum(stats_ref[k, 1:2] * jnp.exp(tops[k] - top) for k in range(parts))
    logs = top + jnp.log(total)
    loss_ref[...] = logs - sum(stats_ref[k, 2:3] for k in range(parts))
    acc_ref[...] = jnp.zeros_like(acc_ref)

    def step(g, carry):
        table = table_ref[g]
        s = lax.dot_general(table, rows, NT, preferred_element_type=F32)
        where = lax.broadcasted_iota(jnp.int32, s.shape, 0) + g * width == cols
        w = (jnp.exp(s - logs) - jnp.where(where, 1.0, 0.0)).astype(BF)
        item_ref[g] = jnp.dot(w, rows, preferred_element_type=F32).astype(BF)
        acc_ref[...] += lax.dot_general(table, w, TN, preferred_element_type=F32)
        return carry

    lax.fori_loop(0, chunks, step, 0)
    query_ref[...] = acc_ref[...].T.astype(BF)


def body(queries, hot_table, cold_table, hot_ids, targets):
    own, width = queries.shape
    shard = cold_table.shape[0]
    hot = hot_table.shape[0]
    nz, nc, ng = lax.axis_size("z"), lax.axis_size(COLS), lax.axis_size(NEAR)
    k = lax.axis_index(COLS)
    hot_part = hot // nc
    hot_near = hot_part // ng
    hot_own = hot_near // nz
    near_rows = nz * shard + hot_near

    grouped = spread(queries, COLS).reshape(nc * own, width)
    cold = spread(spread(cold_table, ("z",)).reshape(nz * shard, width), NEAR)
    hot_mine = lax.dynamic_slice_in_dim(hot_table, k * hot_part, hot_part, 0)
    table = jnp.concatenate([cold, hot_mine.reshape(ng, hot_near, width)], axis=1)

    sizes = tuple(lax.axis_size(a) for a in AXES)
    aim = targets.reshape(*sizes, own)
    z, yl, x1 = lax.axis_index("z"), lax.axis_index("yl"), lax.axis_index("x1")
    aim = lax.dynamic_slice(aim, (z, yl, 0, 0, x1, 0, 0), (1, 1, *sizes[2:4], 1, sizes[5], own))
    aim = aim.reshape(1, nc * own)
    ids = hot_ids[:, None]
    below = jnp.sum((ids < aim).astype(jnp.int32), axis=0)
    slot = jnp.sum(
        jnp.where(ids == aim, lax.broadcasted_iota(jnp.int32, (hot, 1), 0) + 1, 0), axis=0
    ) - 1
    hot_k, hot_r = slot // hot_part, slot % hot_part
    hot_col = hot_r // hot_near * near_rows + nz * shard + hot_r % hot_near
    cold_row = aim[0] - below
    block = cold_row // shard
    coord = {}
    for a in reversed(AXES):
        n = lax.axis_size(a)
        coord[a] = block % n
        block = block // n
    cold_k = (coord["c"] * lax.axis_size("x2") + coord["x2"]) * lax.axis_size("yh") + coord["yh"]
    cold_g = coord["yl"] * lax.axis_size("x1") + coord["x1"]
    cold_col = cold_g * near_rows + coord["z"] * shard + cold_row % shard
    is_hot = slot >= 0
    column = jnp.where(is_hot, hot_col, cold_col)
    column = jnp.where(jnp.where(is_hot, hot_k, cold_k) == k, column, -1)[None]

    count = nc * own
    params = pltpu.CompilerParams(vmem_limit_bytes=48 << 20)
    stats = pl.pallas_call(
        stats_kernel,
        out_shape=jax.ShapeDtypeStruct((8, count), F32),
        compiler_params=params,
    )(table, grouped, column)
    stats = spread(stats, COLS)
    query_part, item_part, loss = pl.pallas_call(
        grads_kernel,
        out_shape=(
            jax.ShapeDtypeStruct((count, width), BF),
            jax.ShapeDtypeStruct((ng, near_rows, width), BF),
            jax.ShapeDtypeStruct((1, count), F32),
        ),
        scratch_shapes=[pltpu.VMEM((width, count), F32)],
        compiler_params=params,
    )(table, grouped, column, stats)
    row_loss = lax.dynamic_slice_in_dim(loss[0], k * own, own, 0)

    near = lax.all_to_all(item_part, NEAR, 0, 0)
    near = jnp.sum(near.astype(F32), axis=0).astype(BF)
    cold_near = near[: nz * shard].reshape(nz, shard, width)
    hot_z = near[nz * shard :].reshape(nz, hot_own, width)
    far = lax.all_to_all(jnp.concatenate([cold_near, hot_z], axis=1), ("z",), 0, 0)
    far = jnp.sum(far.astype(F32), axis=0).astype(BF)
    grad_cold = far[:shard]
    grad_hot = spread(far[shard:], ("z",)).reshape(hot_near, width)
    grad_hot = spread(grad_hot, PLANE).reshape(hot, width)

    own_query = lax.all_to_all(query_part.reshape(nc, own, width), COLS, 0, 0)
    grad_queries = jnp.sum(own_query.astype(F32), axis=0).astype(BF)
    return grad_queries, grad_hot, grad_cold, row_loss


def solution(mesh):
    fine = Mesh(mesh.devices.reshape(16, 2, 2, 2, 2, 2), AXES)
    rows = P(AXES, None)
    return jax.shard_map(
        body,
        mesh=fine,
        in_specs=(rows, P(), rows, P(), P()),
        out_specs=(rows, P(), rows, P(AXES)),
        check_vma=False,
    )
```

time: 580 us -> 201 us (0.35)
  blocking collectives: 222 us -> 76.8 us
  waiting for transfers between devices: 193 us -> 56.8 us
  local copies, waits for them, and re-layouts: 100 us -> 7.71 us
  starting transfers between devices: 0.12 us -> 43.5 us
  matrix products: 33 us -> 0 us
  between operations: 14.6 us -> 0.77 us
  Pallas kernels: 0 us -> 10.3 us
  other arithmetic: 12.6 us -> 4.61 us
    reduce_scatter x2 -> x0, waiting for transfers between devices: 192 us -> none  [the longest x1 192 us: body(): lax.psum_scatter(cold_grad, 'wide', scatter_dimension=0, tiled=True)]
    psum x2 -> x0, blocking collectives: 151 us -> none  [the longest x1 136 us: body(): grad_hot = lax.psum(hot_grad_part, ('wide', 'narrow')).astype(jnp.bfloat16)]
    gather x15 -> x0, local copies, waits for them, and re-layouts: 97.9 us -> none  [the longest x12 73.8 us: decode_targets(): below = jnp.searchsorted(ordered, targets)]
    all_to_all x0 -> x4, blocking collectives: none -> 76.8 us  [the longest x2 35.7 us: spread(): return lax.all_to_all(jnp.broadcast_to(x[None], (n, *x.shape)), axes, 0, 0)]
    all_to_all x0 -> x5, waiting for transfers between devices: none -> 56.8 us  [the longest x4 44.7 us: spread(): return lax.all_to_all(jnp.broadcast_to(x[None], (n, *x.shape)), axes, 0, 0)]
    all_to_all x0 -> x5, starting transfers between devices: none -> 43.5 us  [the longest x4 37.5 us: spread(): return lax.all_to_all(jnp.broadcast_to(x[None], (n, *x.shape)), axes, 0, 0)]
    dot_general x13 -> x0, matrix products: 33 us -> none  [the longest x7 18.6 us: scores(): jnp.einsum('rh,ch->rc', query_rows, table, preferred_element_type=jnp.flo...]
    all_gather x1 -> x0, blocking collectives: 32.5 us -> none  [body(): grouped = lax.all_gather(queries, 'narrow', axis=0, tiled=True)]
  transfers between devices with their start and end apart: 3 -> 5, of which waited for: 1 -> 5; matrix products, arithmetic and copies ran while one was open for 19% -> 3% of each run, Pallas kernels for 0% -> 0%
where the time goes in v1:
time: 201 us; the launch traced here: 200 us
  blocking collectives  76.8 us (38%)
  waiting for transfers between devices  56.8 us (28%)
  starting transfers between devices  43.5 us (22%)
  Pallas kernels  10.3 us (5%)
  local copies, waits for them, and re-layouts  7.71 us (4%)
  other arithmetic  4.61 us (2%)
    all_to_all x4, waiting for transfers between devices, spread(): return lax.all_to_all(jnp.broadcast_to(x[None], (n, *x.shape)), axes, 0, 0)  44.7 us
    all_to_all x4, starting transfers between devices, spread(): return lax.all_to_all(jnp.broadcast_to(x[None], (n, *x.shape)), axes, 0, 0)  37.5 us
    all_to_all x2, blocking collectives, spread(): return lax.all_to_all(jnp.broadcast_to(x[None], (n, *x.shape)), axes, 0, 0)  35.7 us
    all_to_all x1, blocking collectives, body(): lax.all_to_all(jnp.concatenate([cold_near, hot_z], axis=1), ('z',), 0, 0)  23.8 us
    all_to_all x1, blocking collectives, body(): near = lax.all_to_all(item_part, NEAR, 0, 0)  17.4 us
    all_to_all x1, waiting for transfers between devices, body(): own_query = lax.all_to_all(query_part.reshape(nc, own, width), COLS, 0, 0)  12.1 us
    pallas_call x1, Pallas kernels, body(): pl.pallas_call(grads_kernel, out_shape=(jax.ShapeDtypeStruct((count, widt...  6.37 us
    all_to_all x1, starting transfers between devices, body(): own_query = lax.all_to_all(query_part.reshape(nc, own, width), COLS, 0, 0)  5.91 us
  transfers between devices with their start and end apart: 5, of which 5 were waited for; matrix products, arithmetic and copies ran while one was open for 3% of the time, Pallas kernels for 0%

profile of v1, /device:TPU:1, one launch (start us, length us, event | category | flops | bytes accessed | tf_op | source)
XLA Modules:
  0.0 200.4 jit_solution(5750417632043123958)
XLA Ops:
  0.6 0.0 copy-start
  0.6 1.5 broadcast_in_dim.30
  2.2 15.7 %all-to-all-start = ((bf16[16,32,256]{2,1,0:T(8,128)(2,1)}), bf16[16,32,256]{2,1,0:T(8,128)(2,1)S(1)}, u32[]{:S(2)}, u32[]{:S(2)}) async-start(bf16[16,32,256]{2,1,0:T(8,128)(2,1)} %broadcast_in_dim.30), calls=%async_computation | async-start | bytes 524288 | tf_op jit(solution)/shard_map/all_to_all | solution.py:23
  17.9 13.1 %all-to-all-done = bf16[16,32,256]{2,1,0:T(8,128)(2,1)S(1)} async-done(((bf16[16,32,256]{2,1,0:T(8,128)(2,1)}), bf16[16,32,256]{2,1,0:T(8,128)(2,1)S(1)}, u32[]{:S(2)}, u32[]{:S(2)}) %all-to-all-start) | async-done | bytes 262176 | tf_op jit(solution)/shard_map/all_to_all | solution.py:23
  31.1 1.0 broadcast_in_dim.32
  32.1 3.6 %all-to-all-start.1 = ((bf16[4,512,256]{2,1,0:T(8,128)(2,1)}), bf16[4,512,256]{2,1,0:T(8,128)(2,1)S(1)}, u32[]{:S(2)}, u32[]{:S(2)}) async-start(bf16[4,512,256]{2,1,0:T(8,128)(2,1)} %broadcast_in_dim.32), calls=%async_computation.1 | async-start | bytes 2097152 | tf_op jit(solution)/shard_map/all_to_all | solution.py:23
  35.8 0.7 constant_dynamic-slice_fusion.1
  36.5 1.9 convert_reduce_fusion
  38.4 5.6 %all-to-all-done.1 = bf16[4,512,256]{2,1,0:T(8,128)(2,1)S(1)} async-done(((bf16[4,512,256]{2,1,0:T(8,128)(2,1)}), bf16[4,512,256]{2,1,0:T(8,128)(2,1)S(1)}, u32[]{:S(2)}, u32[]{:S(2)}) %all-to-all-start.1) | async-done | bytes 1048608 | tf_op jit(solution)/shard_map/all_to_all | solution.py:23
  44.0 0.9 broadcast_in_dim.33
  44.9 0.3 copy-done.1
  45.2 14.3 %all-to-all-start.2 = ((bf16[8,128,256]{2,1,0:T(8,128)(2,1)}), bf16[8,128,256]{2,1,0:T(8,128)(2,1)S(1)}, u32[]{:S(2)}, u32[]{:S(2)}) async-start(bf16[8,128,256]{2,1,0:T(8,128)(2,1)} %broadcast_in_dim.33), calls=%async_computation.2 | async-start | bytes 1048576 | tf_op jit(solution)/shard_map/all_to_all | solution.py:23
  59.4 0.3 compare_select_fusion.2.col_ref
  59.7 1.3 pad_maximum_fusion.table_ref
  61.0 10.5 %all-to-all-done.2 = bf16[8,128,256]{2,1,0:T(8,128)(2,1)S(1)} async-done(((bf16[8,128,256]{2,1,0:T(8,128)(2,1)}), bf16[8,128,256]{2,1,0:T(8,128)(2,1)S(1)}, u32[]{:S(2)}, u32[]{:S(2)}) %all-to-all-start.2) | async-done | bytes 524320 | tf_op jit(solution)/shard_map/all_to_all | solution.py:23
  71.5 3.9 %shard_map.84 = f32[8,1024]{1,0:T(8,128)S(1)} custom-call(bf16[4,576,256]{2,1,0:T(8,128)(2,1)S(1)} %pad_maximum_fusion.table_ref, bf16[1024,256]{1,0:T(8,128)(2,1)S(1)} %bitcast.13, s32[1,1024]{1,0:T(1,128)S(1)} %compare_select_fusion.2.col_ref), custom_call_target="tpu_custom_call" | custom-call | tf_op jit(solution)/shard_map/pallas_call | solution.py:118
  75.4 11.9 %all_to_all.45.stats_ref = f32[8,8,1024]{2,1,0:T(8,128)S(1)} all-to-all(f32[8,8,1024]{2,1,0:T(8,128)S(1)} %broadcast_in_dim.60), channel_id=1, replica_groups=mesh['z'=16,'yl'=2,'c'=2,'x2'=2,'x1'=2,'yh'=2] {'c','x2','yh'}, dimensions={0} | all-to-all | bytes 524288 | tf_op jit(solution)/shard_map/all_to_all | solution.py:23
  87.3 6.4 %shard_map.85 = (bf16[1024,256]{1,0:T(8,128)(2,1)}, bf16[4,576,256]{2,1,0:T(8,128)(2,1)S(1)}, f32[1,1024]{1,0:T(1,128)S(1)}) custom-call(bf16[4,576,256]{2,1,0:T(8,128)(2,1)S(1)} %pad_maximum_fusion.table_ref, bf16[1024,256]{1,0:T(8,128)(2,1)S(1)} %bitcast.14, s32[1,1024]{1,0:T(1,128)S(1)} %compare_select_fusion.2.col_ref, ...), custom_call_target="tpu_custom_call" | custom-call | tf_op jit(solution)/shard_map/pallas_call | solution.py:124
  93.7 17.4 %all_to_all.46 = bf16[4,576,256]{2,1,0:T(8,128)(2,1)S(1)} all-to-all(bf16[4,576,256]{2,1,0:T(8,128)(2,1)S(1)} %get-tuple-element.8), channel_id=1, replica_groups=mesh['z'=16,'yl'=2,'c'=2,'x2'=2,'x1'=2,'yh'=2] {'yl','x1'}, dimensions={0} | all-to-all | bytes 2359296 | tf_op jit(solution)/shard_map/all_to_all | solution.py:136
  111.1 0.3 reduce_sum.60
  111.5 23.8 %all_to_all.47 = bf16[16,36,256]{2,1,0:T(8,128)(2,1)S(1)} all-to-all(bf16[16,36,256]{2,1,0:T(8,128)(2,1)S(1)} %pad_maximum_fusion.1), channel_id=1, replica_groups=mesh['z'=16,'yl'=2,'c'=2,'x2'=2,'x1'=2,'yh'=2] {'z'}, dimensions={0} | all-to-all | bytes 589824 | tf_op jit(solution)/shard_map/all_to_all | solution.py:140
  135.2 0.1 reduce_sum.61
  135.3 23.8 %all_to_all.48 = bf16[16,4,256]{2,1,0:T(4,128)(2,1)S(1)} all-to-all(bf16[16,4,256]{2,1,0:T(4,128)(2,1)S(1)} %broadcast_in_dim.61), channel_id=1, replica_groups=mesh['z'=16,'yl'=2,'c'=2,'x2'=2,'x1'=2,'yh'=2] {'z'}, dimensions={0} | all-to-all | bytes 65536 | tf_op jit(solution)/shard_map/all_to_all | solution.py:23
  159.1 5.9 %all-to-all-start.4 = ((bf16[8,128,256]{2,1,0:T(8,128)(2,1)}), bf16[8,128,256]{2,1,0:T(8,128)(2,1)S(1)}, u32[]{:S(2)}, u32[]{:S(2)}) async-start(bf16[8,128,256]{2,1,0:T(8,128)(2,1)} %bitcast.8), calls=%async_computation.4 | async-start | bytes 1048576 | tf_op jit(solution)/shard_map/all_to_all | solution.py:146
  165.1 12.1 %all-to-all-done.4 = bf16[8,128,256]{2,1,0:T(8,128)(2,1)S(1)} async-done(((bf16[8,128,256]{2,1,0:T(8,128)(2,1)}), bf16[8,128,256]{2,1,0:T(8,128)(2,1)S(1)}, u32[]{:S(2)}, u32[]{:S(2)}) %all-to-all-start.4) | async-done | bytes 524320 | tf_op jit(solution)/shard_map/all_to_all | solution.py:146
  177.1 1.1 broadcast_in_dim.63
  178.2 3.9 %all-to-all-start.8 = ((bf16[32,64,256]{2,1,0:T(8,128)(2,1)}), bf16[32,64,256]{2,1,0:T(8,128)(2,1)S(1)}, u32[]{:S(2)}, u32[]{:S(2)}) async-start(bf16[32,64,256]{2,1,0:T(8,128)(2,1)} %broadcast_in_dim.63), calls=%async_computation.8 | async-start | bytes 2097152 | tf_op jit(solution)/shard_map/all_to_all | solution.py:23
  182.1 0.5 fusion.10
  182.6 0.7 reduce_sum.59
  183.3 0.6 slice.19
  183.9 15.5 %all-to-all-done.8 = bf16[32,64,256]{2,1,0:T(8,128)(2,1)S(1)} async-done(((bf16[32,64,256]{2,1,0:T(8,128)(2,1)}), bf16[32,64,256]{2,1,0:T(8,128)(2,1)S(1)}, u32[]{:S(2)}, u32[]{:S(2)}) %all-to-all-start.8) | async-done | bytes 1048608 | tf_op jit(solution)/shard_map/all_to_all | solution.py:23
  199.4 1.0 copy.14
  (17 shorter events, 0.2 us)
Async XLA Ops:
  0.6 58.8 %copy-start = (bf16[2048,256]{1,0:T(8,128)(2,1)S(1)}, bf16[2048,256]{1,0:T(8,128)(2,1)}, u32[]{:S(2)}) copy-start(bf16[2048,256]{1,0:T(8,128)(2,1)} %param.6) | copy-start | bytes 3145732
  2.2 28.9 %all-to-all-start = ((bf16[16,32,256]{2,1,0:T(8,128)(2,1)}), bf16[16,32,256]{2,1,0:T(8,128)(2,1)S(1)}, u32[]{:S(2)}, u32[]{:S(2)}) async-start(bf16[16,32,256]{2,1,0:T(8,128)(2,1)} %broadcast_in_dim.30), calls=%async_computation | async-start | bytes 524288 | tf_op jit(solution)/shard_map/all_to_all | solution.py:23
  32.1 4.4 %copy-start.3 = (s32[2048]{0:T(1024)S(1)}, s32[2048]{0:T(1024)}, u32[]{:S(2)}) copy-start(s32[2048]{0:T(1024)} %param.8) | copy-start | bytes 24580
  32.1 11.9 %copy-start.2 = (bf16[128,256]{1,0:T(8,128)(2,1)S(1)}, bf16[128,256]{1,0:T(8,128)(2,1)}, u32[]{:S(2)}) copy-start(bf16[128,256]{1,0:T(8,128)(2,1)} %param.5) | copy-start | bytes 196612
  32.1 11.9 %all-to-all-start.1 = ((bf16[4,512,256]{2,1,0:T(8,128)(2,1)}), bf16[4,512,256]{2,1,0:T(8,128)(2,1)S(1)}, u32[]{:S(2)}, u32[]{:S(2)}) async-start(bf16[4,512,256]{2,1,0:T(8,128)(2,1)} %broadcast_in_dim.32), calls=%async_computation.1 | async-start | bytes 2097152 | tf_op jit(solution)/shard_map/all_to_all | solution.py:23
  44.0 1.1 copy-start.1
  45.2 26.3 %all-to-all-start.2 = ((bf16[8,128,256]{2,1,0:T(8,128)(2,1)}), bf16[8,128,256]{2,1,0:T(8,128)(2,1)S(1)}, u32[]{:S(2)}, u32[]{:S(2)}) async-start(bf16[8,128,256]{2,1,0:T(8,128)(2,1)} %broadcast_in_dim.33), calls=%async_computation.2 | async-start | bytes 1048576 | tf_op jit(solution)/shard_map/all_to_all | solution.py:23
  159.1 18.0 %all-to-all-start.4 = ((bf16[8,128,256]{2,1,0:T(8,128)(2,1)}), bf16[8,128,256]{2,1,0:T(8,128)(2,1)S(1)}, u32[]{:S(2)}, u32[]{:S(2)}) async-start(bf16[8,128,256]{2,1,0:T(8,128)(2,1)} %bitcast.8), calls=%async_computation.4 | async-start | bytes 1048576 | tf_op jit(solution)/shard_map/all_to_all | solution.py:146
  178.2 21.2 %all-to-all-start.8 = ((bf16[32,64,256]{2,1,0:T(8,128)(2,1)}), bf16[32,64,256]{2,1,0:T(8,128)(2,1)S(1)}, u32[]{:S(2)}, u32[]{:S(2)}) async-start(bf16[32,64,256]{2,1,0:T(8,128)(2,1)} %broadcast_in_dim.63), calls=%async_computation.8 | async-start | bytes 2097152 | tf_op jit(solution)/shard_map/all_to_all | solution.py:23

commit v2 on v1

v2 whole, which is shorter than its diff:
```python
import functools

import jax
import jax.numpy as jnp
from jax import lax
from jax.experimental import pallas as pl
from jax.experimental.pallas import tpu as pltpu
from jax.sharding import Mesh
from jax.sharding import PartitionSpec as P

AXES = ("z8", "z4", "z2", "z1", "yl", "c", "x2", "x1", "yh")
COLS = ("c", "z1", "z2")
NEAR = ("yl", "x2", "x1", "yh")
FAR = ("z8", "z4")
BF = jnp.bfloat16
F32 = jnp.float32
NT = (((1,), (1,)), ((), ()))
TN = (((0,), (0,)), ((), ()))


def spread(x, axes):
    n = lax.axis_size(axes)
    return lax.all_to_all(jnp.broadcast_to(x[None], (n, *x.shape)), axes, 0, 0)


def swap(x, axis):
    return lax.ppermute(x, axis, [(0, 1), (1, 0)])


def coords(index, order):
    found = {}
    for a in reversed(order):
        found[a] = index % 2
        index = index // 2
    return found


def join(found, order):
    index = 0
    for a in order:
        index = index * 2 + found[a]
    return index


def stats_kernel(k_ref, table_ref, rows_ref, col_ref, out_ref):
    chunks, width, _ = table_ref.shape
    parts = out_ref.shape[1] // 128
    rows = rows_ref[...]
    cols = col_ref[...]
    count = rows.shape[0]
    k = k_ref[0]

    def step(g, carry):
        top, total, hit = carry
        s = lax.dot_general(table_ref[g], rows, NT, preferred_element_type=F32)
        new = jnp.maximum(top, jnp.max(s, axis=0, keepdims=True))
        total = total * jnp.exp(top - new) + jnp.sum(jnp.exp(s - new), axis=0, keepdims=True)
        where = lax.broadcasted_iota(jnp.int32, s.shape, 0) + g * width == cols
        hit = hit + jnp.sum(jnp.where(where, s, 0.0), axis=0, keepdims=True)
        return new, total, hit

    zero = jnp.zeros((1, count), F32)
    top, total, hit = lax.fori_loop(0, chunks, step, (jnp.full((1, count), -1e30, F32), zero, zero))
    for p in range(parts):
        here = slice(p * 128, (p + 1) * 128)
        there = pl.ds(pl.multiple_of((k ^ p) * 128, 128), 128)
        out_ref[0:1, there] = top[:, here]
        out_ref[1:2, there] = total[:, here]
        out_ref[2:3, there] = hit[:, here]
        out_ref[3:8, there] = jnp.zeros((5, 128), F32)


def grads_kernel(
    k_ref, table_ref, rows_ref, col_ref, stats_ref, query_ref, item_ref, loss_ref, acc_ref
):
    chunks, width, _ = table_ref.shape
    rows = rows_ref[...]
    cols = col_ref[...]
    parts = stats_ref.shape[0]
    k = k_ref[0]
    pieces = []
    for p in range(parts):
        there = pl.ds(pl.multiple_of((k ^ p) * 128, 128), 128)
        tops = [stats_ref[d, 0:1, there] for d in range(parts)]
        top = functools.reduce(jnp.maximum, tops)
        total = sum(stats_ref[d, 1:2, there] * jnp.exp(tops[d] - top) for d in range(parts))
        pieces.append(top + jnp.log(total))
        if p == 0:
            loss_ref[...] = pieces[0] - sum(stats_ref[d, 2:3, there] for d in range(parts))
    logs = jnp.concatenate(pieces, axis=1)
    acc_ref[...] = jnp.zeros_like(acc_ref)

    def step(g, carry):
        table = table_ref[g]
        s = lax.dot_general(table, rows, NT, preferred_element_type=F32)
        where = lax.broadcasted_iota(jnp.int32, s.shape, 0) + g * width == cols
        w = (jnp.exp(s - logs) - jnp.where(where, 1.0, 0.0)).astype(BF)
        item_ref[g] = jnp.dot(w, rows, preferred_element_type=F32).astype(BF)
        acc_ref[...] += lax.dot_general(table, w, TN, preferred_element_type=F32)
        return carry

    lax.fori_loop(0, chunks, step, 0)
    query_ref[...] = acc_ref[...].T.astype(BF)


def body(queries, hot_table, cold_table, hot_ids, targets):
    own, width = queries.shape
    shard = cold_table.shape[0]
    hot = hot_table.shape[0]
    nc, ng, nf = 2 ** len(COLS), 2 ** len(NEAR), 2 ** len(FAR)
    hot_own = hot // (nc * ng)
    me = {a: lax.axis_index(a) for a in AXES}
    k = join(me, COLS)

    grouped = queries
    for a in reversed(COLS):
        grouped = jnp.concatenate([grouped, swap(grouped, a)], axis=0)

    far = spread(cold_table, FAR).reshape(nf * shard, width)
    cold = spread(far, NEAR)
    mine = lax.dynamic_index_in_dim(hot_table.reshape(ng, nc, hot_own, width), k, 1, False)
    near_rows = nf * shard + hot_own
    table = jnp.concatenate([cold, mine], axis=1)

    base = join(me, AXES)
    blocks = targets.reshape(-1, own)
    picks = []
    for p in range(nc):
        flip = {a: 0 for a in AXES}
        flip.update(coords(p, COLS))
        picks.append(lax.dynamic_slice_in_dim(blocks, base ^ join(flip, AXES), 1, 0))
    aim = jnp.concatenate(picks, axis=1)
    ids = hot_ids[:, None]
    below = jnp.sum((ids < aim).astype(jnp.int32), axis=0)
    slot = jnp.sum(
        jnp.where(ids == aim, lax.broadcasted_iota(jnp.int32, (hot, 1), 0) + 1, 0), axis=0
    ) - 1
    is_hot = slot >= 0
    cold_row = aim[0] - below
    at = coords(cold_row // shard, AXES)
    hot_block = slot // hot_own
    column = jnp.where(
        is_hot,
        hot_block // nc * near_rows + nf * shard + slot % hot_own,
        join(at, NEAR) * near_rows + join(at, FAR) * shard + cold_row % shard,
    )
    column = jnp.where(jnp.where(is_hot, hot_block % nc, join(at, COLS)) == k, column, -1)[None]

    count = nc * own
    params = pltpu.CompilerParams(vmem_limit_bytes=48 << 20)
    chunks = 4
    table = table.reshape(chunks, ng * near_rows // chunks, width)
    vmem = pl.BlockSpec(memory_space=pltpu.VMEM)
    smem = pl.BlockSpec(memory_space=pltpu.SMEM)
    at_k = jnp.reshape(k, (1,)).astype(jnp.int32)
    stats = pl.pallas_call(
        stats_kernel,
        out_shape=jax.ShapeDtypeStruct((8, count), F32),
        in_specs=[smem, vmem, vmem, vmem],
        compiler_params=params,
    )(at_k, table, grouped, column)
    stats = spread(stats, COLS)
    query_part, item_part, loss = pl.pallas_call(
        grads_kernel,
        out_shape=(
            jax.ShapeDtypeStruct((count, width), BF),
            jax.ShapeDtypeStruct(table.shape, BF),
            jax.ShapeDtypeStruct((1, own), F32),
        ),
        in_specs=[smem, vmem, vmem, vmem, vmem],
        scratch_shapes=[pltpu.VMEM((width, count), F32)],
        compiler_params=params,
    )(at_k, table, grouped, column, stats)

    near = lax.all_to_all(item_part.reshape(ng, near_rows, width), NEAR, 0, 0)
    near = jnp.sum(near.astype(F32), axis=0).astype(BF)
    cold_part = near[: nf * shard].reshape(nf, shard, width)
    hot_part = jnp.broadcast_to(near[None, nf * shard :], (nf, hot_own, width))
    far = lax.all_to_all(jnp.concatenate([cold_part, hot_part], axis=1), FAR, 0, 0)
    far = jnp.sum(far.astype(F32), axis=0).astype(BF)
    grad_cold = far[:shard]
    grad_hot = spread(far[shard:], COLS).reshape(nc * hot_own, width)
    grad_hot = spread(grad_hot, NEAR).reshape(hot, width)

    for a in COLS:
        half = query_part.shape[0] // 2
        other = swap(query_part[half:], a)
        query_part = (query_part[:half].astype(F32) + other.astype(F32)).astype(BF)
    return query_part, grad_hot, grad_cold, loss[0]


def solution(mesh):
    fine = Mesh(mesh.devices.reshape((2,) * len(AXES)), AXES)
    rows = P(AXES, None)
    return jax.shard_map(
        body,
        mesh=fine,
        in_specs=(rows, P(), rows, P(), P()),
        out_specs=(rows, P(), rows, P(AXES)),
        check_vma=False,
    )
```

time: 201 us -> 159 us (0.79)
  waiting for transfers between devices: 56.8 us -> 23.5 us
  blocking collectives: 76.8 us -> 59.8 us
  starting transfers between devices: 43.5 us -> 48.3 us
  local copies, waits for them, and re-layouts: 7.71 us -> 11.5 us
    all_to_all x4, waiting for transfers between devices: 44.7 us -> 9.61 us  [spread(): return lax.all_to_all(jnp.broadcast_to(x[None], (n, *x.shape)), axes, 0, 0)]
    all_to_all x2 -> x1, blocking collectives: 35.7 us -> 15.7 us  [spread(): return lax.all_to_all(jnp.broadcast_to(x[None], (n, *x.shape)), axes, 0, 0)]
    ppermute x0 -> x6, starting transfers between devices: none -> 15.8 us  [swap(): return lax.ppermute(x, axis, [(0, 1), (1, 0)])]
    ppermute x0 -> x6, waiting for transfers between devices: none -> 13.9 us  [swap(): return lax.ppermute(x, axis, [(0, 1), (1, 0)])]
    all_to_all x1 -> x0, waiting for transfers between devices: 12.1 us -> none  [body(): own_query = lax.all_to_all(query_part.reshape(nc, own, width), COLS, 0, 0)]
    all_to_all x1 -> x0, starting transfers between devices: 5.91 us -> none  [body(): own_query = lax.all_to_all(query_part.reshape(nc, own, width), COLS, 0, 0)]
    all_to_all x4, starting transfers between devices: 37.5 us -> 32.6 us  [spread(): return lax.all_to_all(jnp.broadcast_to(x[None], (n, *x.shape)), axes, 0, 0)]
    unnamed x9 -> x15, local copies, waits for them, and re-layouts: 1.26 us -> 5.89 us
  transfers between devices with their start and end apart: 5 -> 10, of which waited for: 5 -> 8; matrix products, arithmetic and copies ran while one was open for 3% -> 8% of each run, Pallas kernels for 0% -> 0%
where the time goes in v2:
time: 159 us; the launch traced here: 158 us
  blocking collectives  59.8 us (38%)
  starting transfers between devices  48.3 us (30%)
  waiting for transfers between devices  23.5 us (15%)
  local copies, waits for them, and re-layouts  11.5 us (7%)
  Pallas kernels  9.4 us (6%)
  other arithmetic  4.16 us (3%)
    all_to_all x4, starting transfers between devices, spread(): return lax.all_to_all(jnp.broadcast_to(x[None], (n, *x.shape)), axes, 0, 0)  32.6 us
    all_to_all x1, blocking collectives, body(): lax.all_to_all(jnp.concatenate([cold_part, hot_part], axis=1), FAR, 0, 0)  22.4 us
    all_to_all x1, blocking collectives, body(): near = lax.all_to_all(item_part.reshape(ng, near_rows, width), NEAR, 0, 0)  21.7 us
    ppermute x6, starting transfers between devices, swap(): return lax.ppermute(x, axis, [(0, 1), (1, 0)])  15.8 us
    all_to_all x1, blocking collectives, spread(): return lax.all_to_all(jnp.broadcast_to(x[None], (n, *x.shape)), axes, 0, 0)  15.7 us
    ppermute x6, waiting for transfers between devices, swap(): return lax.ppermute(x, axis, [(0, 1), (1, 0)])  13.9 us
    all_to_all x4, waiting for transfers between devices, spread(): return lax.all_to_all(jnp.broadcast_to(x[None], (n, *x.shape)), axes, 0, 0)  9.61 us
    unnamed x15, local copies, waits for them, and re-layouts  5.89 us
  transfers between devices with their start and end apart: 10, of which 8 were waited for; matrix products, arithmetic and copies ran while one was open for 8% of the time, Pallas kernels for 0%

profile of v2, /device:TPU:1, one launch (start us, length us, event | category | flops | bytes accessed | tf_op | source)
XLA Modules:
  0.0 157.8 jit_solution(7262596718651606620)
XLA Ops:
  0.6 1.4 broadcast_in_dim.30
  2.1 15.6 %all-to-all-start = ((bf16[4,32,256]{2,1,0:T(8,128)(2,1)}), bf16[4,32,256]{2,1,0:T(8,128)(2,1)S(1)}, u32[]{:S(2)}, u32[]{:S(2)}) async-start(bf16[4,32,256]{2,1,0:T(8,128)(2,1)} %broadcast_in_dim.30), calls=%async_computation | async-start | bytes 131072 | tf_op jit(solution)/shard_map/all_to_all | solution.py:23
  17.7 3.1 %collective-permute-start = (bf16[128,256]{1,0:T(8,128)(2,1)}, bf16[128,256]{1,0:T(8,128)(2,1)S(1)}, u32[]{:S(2)}, u32[]{:S(2)}) collective-permute-start(bf16[128,256]{1,0:T(8,128)(2,1)} %param.5), channel_id=1, source_target_pairs={{0,64},{64,0},{1,65},{65,1},{2,66},{66,2},{3,67},{67,3},{4,68},{68... | collective-permute-start | bytes 196616 | tf_op jit(solution)/shard_map/ppermute | solution.py:27
  20.9 0.7 constant_dynamic-update-slice_fusion.11
  21.6 0.7 constant_dynamic-update-slice_fusion.10
  22.3 0.7 constant_dynamic-update-slice_fusion.9
  23.0 0.7 constant_dynamic-update-slice_fusion.8
  26.5 2.7 %convert_reduce_fusion = (s32[1024]{0:T(1024)S(1)}, s32[1024]{0:T(1024)S(1)}) fusion(s32[1024]{0:T(1024)S(1)} %bitcast.25, s32[2048]{0:T(1024)} %param.8, s32[2048]{0:T(1024)S(1)} %iota_add_fusion), kind=kLoop, calls=%fused_computation | loop fusion | flops 12580864 | bytes 28672 | tf_op jit(solution)/shard_map/reduce_sum | solution.py:134
  29.3 0.9 all-to-all-done
  30.2 1.1 broadcast_in_dim.32
  31.3 6.9 %all-to-all-start.1 = ((bf16[16,128,256]{2,1,0:T(8,128)(2,1)}), bf16[16,128,256]{2,1,0:T(8,128)(2,1)S(1)}, u32[]{:S(2)}, u32[]{:S(2)}) async-start(bf16[16,128,256]{2,1,0:T(8,128)(2,1)} %broadcast_in_dim.32), calls=%async_computation.1 | async-start | bytes 2097152 | tf_op jit(solution)/shard_map/all_to_all | solution.py:23
  38.2 2.2 %collective-permute-start.1 = (bf16[256,256]{1,0:T(8,128)(2,1)S(1)}, bf16[256,256]{1,0:T(8,128)(2,1)S(1)}, u32[]{:S(2)}, u32[]{:S(2)}) collective-permute-start(bf16[256,256]{1,0:T(8,128)(2,1)S(1)} %pad_maximum_fusion.2), channel_id=1, source_target_pairs={{0,32},{32,0},{1,33},{33,1},{2,34},{34,2},{3,35},{35,3},{4,36},{36... | collective-permute-start | bytes 393224 | tf_op jit(solution)/shard_map/ppermute | solution.py:27
  40.8 3.4 %collective-permute-done.1 = bf16[256,256]{1,0:T(8,128)(2,1)S(1)} collective-permute-done((bf16[256,256]{1,0:T(8,128)(2,1)S(1)}, bf16[256,256]{1,0:T(8,128)(2,1)S(1)}, u32[]{:S(2)}, u32[]{:S(2)}) %collective-permute-start.1) | collective-permute-done | bytes 131104 | tf_op jit(solution)/shard_map/ppermute | solution.py:27
  44.3 4.6 %collective-permute-start.2 = (bf16[512,256]{1,0:T(8,128)(2,1)S(1)}, bf16[512,256]{1,0:T(8,128)(2,1)S(1)}, u32[]{:S(2)}, u32[]{:S(2)}) collective-permute-start(bf16[512,256]{1,0:T(8,128)(2,1)S(1)} %pad_maximum_fusion.1), channel_id=1, source_target_pairs={{0,8},{8,0},{1,9},{9,1},{2,10},{10,2},{3,11},{11,3},{4,12},{12,4},... | collective-permute-start | bytes 786440 | tf_op jit(solution)/shard_map/ppermute | solution.py:27
  48.9 1.1 collective-permute-done.2
  50.1 2.5 %all-to-all-done.1 = bf16[16,128,256]{2,1,0:T(8,128)(2,1)S(1)} async-done(((bf16[16,128,256]{2,1,0:T(8,128)(2,1)}), bf16[16,128,256]{2,1,0:T(8,128)(2,1)S(1)}, u32[]{:S(2)}, u32[]{:S(2)}) %all-to-all-start.1) | async-done | bytes 1048608 | tf_op jit(solution)/shard_map/all_to_all | solution.py:23
  52.7 3.9 %shard_map.84 = f32[8,1024]{1,0:T(8,128)S(1)} custom-call(s32[1]{0:T(128)} %bitcast.k_ref, bf16[4,576,256]{2,1,0:T(8,128)(2,1)S(1)} %bitcast.16, bf16[1024,256]{1,0:T(8,128)(2,1)S(1)} %constant_dynamic-update-slice_fusion.rows_ref, s32[1,1024]{1,0:T(1,128)S(1)} %compare_select_fusion.2.col_ref), custom_call_target="tpu_custom_call" | custom-call | tf_op jit(solution)/shard_map/pallas_call | solution.py:156
  56.6 15.7 %all_to_all.35.stats_ref = f32[8,8,1024]{2,1,0:T(8,128)S(1)} all-to-all(f32[8,8,1024]{2,1,0:T(8,128)S(1)} %broadcast_in_dim.59), channel_id=1, replica_groups=mesh['z8'=2,'z4'=2,'z2'=2,'z1'=2,'yl'=2,'c'=2,'x2'=2,'x1'=2,'yh'=2] {'c'..., dimensions={0} | all-to-all | bytes 524288 | tf_op jit(solution)/shard_map/all_to_all | solution.py:23
  72.3 5.5 %shard_map.85 = (bf16[1024,256]{1,0:T(8,128)(2,1)S(1)}, bf16[4,576,256]{2,1,0:T(8,128)(2,1)S(1)}, f32[1,128]{1,0:T(1,128)}) custom-call(s32[1]{0:T(128)} %bitcast.k_ref, bf16[4,576,256]{2,1,0:T(8,128)(2,1)S(1)} %bitcast.17, bf16[1024,256]{1,0:T(8,128)(2,1)S(1)} %constant_dynamic-update-slice_fusion.rows_ref, s32[1,1024]{1,0:T(1,128)S(1)} %compare_select_fusion.2.col_ref, ...), custom_call_target="tpu_custom_call" | custom-call | tf_op jit(solution)/shard_map/pallas_call | solution.py:163
  77.9 21.7 %all_to_all.36 = bf16[16,144,256]{2,1,0:T(8,128)(2,1)S(1)} all-to-all(bf16[16,144,256]{2,1,0:T(8,128)(2,1)S(1)} %bitcast.18), channel_id=1, replica_groups=mesh['z8'=2,'z4'=2,'z2'=2,'z1'=2,'yl'=2,'c'=2,'x2'=2,'x1'=2,'yh'=2] {'yl..., dimensions={0} | all-to-all | bytes 2359296 | tf_op jit(solution)/shard_map/all_to_all | solution.py:175
  99.8 22.4 %all_to_all.37 = bf16[4,48,256]{2,1,0:T(8,128)(2,1)S(1)} all-to-all(bf16[4,48,256]{2,1,0:T(8,128)(2,1)S(1)} %pad_maximum_fusion.3), channel_id=1, replica_groups=mesh['z8'=2,'z4'=2,'z2'=2,'z1'=2,'yl'=2,'c'=2,'x2'=2,'x1'=2,'yh'=2] {'z8..., dimensions={0} | all-to-all | bytes 196608 | tf_op jit(solution)/shard_map/all_to_all | solution.py:179
  122.8 6.4 %all-to-all-start.5 = ((bf16[8,16,256]{2,1,0:T(8,128)(2,1)}), bf16[8,16,256]{2,1,0:T(8,128)(2,1)S(1)}, u32[]{:S(2)}, u32[]{:S(2)}) async-start(bf16[8,16,256]{2,1,0:T(8,128)(2,1)} %broadcast_in_dim.61), calls=%async_computation.5 | async-start | bytes 131072 | tf_op jit(solution)/shard_map/all_to_all | solution.py:23
  129.3 1.9 %collective-permute-start.3 = (bf16[512,256]{1,0:T(8,128)(2,1)S(1)}, bf16[512,256]{1,0:T(8,128)(2,1)S(1)}, u32[]{:S(2)}, u32[]{:S(2)}) collective-permute-start(bf16[512,256]{1,0:T(8,128)(2,1)S(1)} %slice.31), channel_id=1, source_target_pairs={{0,8},{8,0},{1,9},{9,1},{2,10},{10,2},{3,11},{11,3},{4,12},{12,4},... | collective-permute-start | bytes 786440 | tf_op jit(solution)/shard_map/ppermute | solution.py:27
  131.2 3.7 %all-to-all-done.5 = bf16[8,16,256]{2,1,0:T(8,128)(2,1)S(1)} async-done(((bf16[8,16,256]{2,1,0:T(8,128)(2,1)}), bf16[8,16,256]{2,1,0:T(8,128)(2,1)S(1)}, u32[]{:S(2)}, u32[]{:S(2)}) %all-to-all-start.5) | async-done | bytes 65568 | tf_op jit(solution)/shard_map/all_to_all | solution.py:23
  134.9 1.1 broadcast_in_dim.63
  135.9 3.7 %all-to-all-start.6 = ((bf16[16,128,256]{2,1,0:T(8,128)(2,1)}), bf16[16,128,256]{2,1,0:T(8,128)(2,1)S(1)}, u32[]{:S(2)}, u32[]{:S(2)}) async-start(bf16[16,128,256]{2,1,0:T(8,128)(2,1)} %broadcast_in_dim.63), calls=%async_computation.6 | async-start | bytes 2097152 | tf_op jit(solution)/shard_map/all_to_all | solution.py:23
  139.7 1.9 %collective-permute-start.4 = (bf16[256,256]{1,0:T(8,128)(2,1)S(1)}, bf16[256,256]{1,0:T(8,128)(2,1)S(1)}, u32[]{:S(2)}, u32[]{:S(2)}) collective-permute-start(bf16[256,256]{1,0:T(8,128)(2,1)S(1)} %slice.41), channel_id=1, source_target_pairs={{0,32},{32,0},{1,33},{33,1},{2,34},{34,2},{3,35},{35,3},{4,36},{36... | collective-permute-start | bytes 393224 | tf_op jit(solution)/shard_map/ppermute | solution.py:27
  141.6 4.6 %collective-permute-done.4 = bf16[256,256]{1,0:T(8,128)(2,1)S(1)} collective-permute-done((bf16[256,256]{1,0:T(8,128)(2,1)S(1)}, bf16[256,256]{1,0:T(8,128)(2,1)S(1)}, u32[]{:S(2)}, u32[]{:S(2)}) %collective-permute-start.4) | collective-permute-done | bytes 131104 | tf_op jit(solution)/shard_map/ppermute | solution.py:27
  146.3 2.0 %collective-permute-start.5 = (bf16[128,256]{1,0:T(8,128)(2,1)S(1)}, bf16[128,256]{1,0:T(8,128)(2,1)S(1)}, u32[]{:S(2)}, u32[]{:S(2)}) collective-permute-start(bf16[128,256]{1,0:T(8,128)(2,1)S(1)} %slice.43), channel_id=1, source_target_pairs={{0,64},{64,0},{1,65},{65,1},{2,66},{66,2},{3,67},{67,3},{4,68},{68... | collective-permute-start | bytes 196616 | tf_op jit(solution)/shard_map/ppermute | solution.py:27
  148.4 4.7 %collective-permute-done.5 = bf16[128,256]{1,0:T(8,128)(2,1)S(1)} collective-permute-done((bf16[128,256]{1,0:T(8,128)(2,1)S(1)}, bf16[128,256]{1,0:T(8,128)(2,1)S(1)}, u32[]{:S(2)}, u32[]{:S(2)}) %collective-permute-start.5) | collective-permute-done | bytes 65568 | tf_op jit(solution)/shard_map/ppermute | solution.py:27
  154.3 2.5 %all-to-all-done.6 = bf16[16,128,256]{2,1,0:T(8,128)(2,1)S(1)} async-done(((bf16[16,128,256]{2,1,0:T(8,128)(2,1)}), bf16[16,128,256]{2,1,0:T(8,128)(2,1)S(1)}, u32[]{:S(2)}, u32[]{:S(2)}) %all-to-all-start.6) | async-done | bytes 1048608 | tf_op jit(solution)/shard_map/all_to_all | solution.py:23
  156.8 1.0 copy.20
  (37 shorter events, 5.6 us)
Async XLA Ops:
  0.6 40.1 %copy-start = (bf16[2048,256]{1,0:T(8,128)(2,1)S(1)}, bf16[2048,256]{1,0:T(8,128)(2,1)}, u32[]{:S(2)}) copy-start(bf16[2048,256]{1,0:T(8,128)(2,1)} %param.6) | copy-start | bytes 3145732
  2.1 28.1 %all-to-all-start = ((bf16[4,32,256]{2,1,0:T(8,128)(2,1)}), bf16[4,32,256]{2,1,0:T(8,128)(2,1)S(1)}, u32[]{:S(2)}, u32[]{:S(2)}) async-start(bf16[4,32,256]{2,1,0:T(8,128)(2,1)} %broadcast_in_dim.30), calls=%async_computation | async-start | bytes 131072 | tf_op jit(solution)/shard_map/all_to_all | solution.py:23
  17.7 20.5 %collective-permute-start = (bf16[128,256]{1,0:T(8,128)(2,1)}, bf16[128,256]{1,0:T(8,128)(2,1)S(1)}, u32[]{:S(2)}, u32[]{:S(2)}) collective-permute-start(bf16[128,256]{1,0:T(8,128)(2,1)} %param.5), channel_id=1, source_target_pairs={{0,64},{64,0},{1,65},{65,1},{2,66},{66,2},{3,67},{67,3},{4,68},{68... | collective-permute-start | bytes 196616 | tf_op jit(solution)/shard_map/ppermute | solution.py:27
  31.3 6.9 %copy-start.1 = (bf16[128,256]{1,0:T(8,128)(2,1)S(1)}, bf16[128,256]{1,0:T(8,128)(2,1)}, u32[]{:S(2)}) copy-start(bf16[128,256]{1,0:T(8,128)(2,1)} %param.5) | copy-start | bytes 196612
  31.3 21.3 %all-to-all-start.1 = ((bf16[16,128,256]{2,1,0:T(8,128)(2,1)}), bf16[16,128,256]{2,1,0:T(8,128)(2,1)S(1)}, u32[]{:S(2)}, u32[]{:S(2)}) async-start(bf16[16,128,256]{2,1,0:T(8,128)(2,1)} %broadcast_in_dim.32), calls=%async_computation.1 | async-start | bytes 2097152 | tf_op jit(solution)/shard_map/all_to_all | solution.py:23
  38.2 6.0 %collective-permute-start.1 = (bf16[256,256]{1,0:T(8,128)(2,1)S(1)}, bf16[256,256]{1,0:T(8,128)(2,1)S(1)}, u32[]{:S(2)}, u32[]{:S(2)}) collective-permute-start(bf16[256,256]{1,0:T(8,128)(2,1)S(1)} %pad_maximum_fusion.2), channel_id=1, source_target_pairs={{0,32},{32,0},{1,33},{33,1},{2,34},{34,2},{3,35},{35,3},{4,36},{36... | collective-permute-start | bytes 393224 | tf_op jit(solution)/shard_map/ppermute | solution.py:27
  44.3 5.8 %collective-permute-start.2 = (bf16[512,256]{1,0:T(8,128)(2,1)S(1)}, bf16[512,256]{1,0:T(8,128)(2,1)S(1)}, u32[]{:S(2)}, u32[]{:S(2)}) collective-permute-start(bf16[512,256]{1,0:T(8,128)(2,1)S(1)} %pad_maximum_fusion.1), channel_id=1, source_target_pairs={{0,8},{8,0},{1,9},{9,1},{2,10},{10,2},{3,11},{11,3},{4,12},{12,4},... | collective-permute-start | bytes 786440 | tf_op jit(solution)/shard_map/ppermute | solution.py:27
  122.8 12.0 %all-to-all-start.5 = ((bf16[8,16,256]{2,1,0:T(8,128)(2,1)}), bf16[8,16,256]{2,1,0:T(8,128)(2,1)S(1)}, u32[]{:S(2)}, u32[]{:S(2)}) async-start(bf16[8,16,256]{2,1,0:T(8,128)(2,1)} %broadcast_in_dim.61), calls=%async_computation.5 | async-start | bytes 131072 | tf_op jit(solution)/shard_map/all_to_all | solution.py:23
  129.3 10.3 %collective-permute-start.3 = (bf16[512,256]{1,0:T(8,128)(2,1)S(1)}, bf16[512,256]{1,0:T(8,128)(2,1)S(1)}, u32[]{:S(2)}, u32[]{:S(2)}) collective-permute-start(bf16[512,256]{1,0:T(8,128)(2,1)S(1)} %slice.31), channel_id=1, source_target_pairs={{0,8},{8,0},{1,9},{9,1},{2,10},{10,2},{3,11},{11,3},{4,12},{12,4},... | collective-permute-start | bytes 786440 | tf_op jit(solution)/shard_map/ppermute | solution.py:27
  135.9 20.8 %all-to-all-start.6 = ((bf16[16,128,256]{2,1,0:T(8,128)(2,1)}), bf16[16,128,256]{2,1,0:T(8,128)(2,1)S(1)}, u32[]{:S(2)}, u32[]{:S(2)}) async-start(bf16[16,128,256]{2,1,0:T(8,128)(2,1)} %broadcast_in_dim.63), calls=%async_computation.6 | async-start | bytes 2097152 | tf_op jit(solution)/shard_map/all_to_all | solution.py:23
  139.7 6.6 %collective-permute-start.4 = (bf16[256,256]{1,0:T(8,128)(2,1)S(1)}, bf16[256,256]{1,0:T(8,128)(2,1)S(1)}, u32[]{:S(2)}, u32[]{:S(2)}) collective-permute-start(bf16[256,256]{1,0:T(8,128)(2,1)S(1)} %slice.41), channel_id=1, source_target_pairs={{0,32},{32,0},{1,33},{33,1},{2,34},{34,2},{3,35},{35,3},{4,36},{36... | collective-permute-start | bytes 393224 | tf_op jit(solution)/shard_map/ppermute | solution.py:27
  146.3 6.7 %collective-permute-start.5 = (bf16[128,256]{1,0:T(8,128)(2,1)S(1)}, bf16[128,256]{1,0:T(8,128)(2,1)S(1)}, u32[]{:S(2)}, u32[]{:S(2)}) collective-permute-start(bf16[128,256]{1,0:T(8,128)(2,1)S(1)} %slice.43), channel_id=1, source_target_pairs={{0,64},{64,0},{1,65},{65,1},{2,66},{66,2},{3,67},{67,3},{4,68},{68... | collective-permute-start | bytes 196616 | tf_op jit(solution)/shard_map/ppermute | solution.py:27

commit v3 on v2

v3 whole, which is shorter than its diff:
```python
import functools

import jax
import jax.numpy as jnp
from jax import lax
from jax.experimental import pallas as pl
from jax.experimental.pallas import tpu as pltpu
from jax.sharding import Mesh
from jax.sharding import PartitionSpec as P

AXES = ("z8", "z4", "z2", "z1", "yl", "c", "x2", "x1", "yh")
COLS = ("c", "z1", "z2")
NEAR = ("yl", "x2", "x1", "yh")
FAR = ("z8", "z4")
NC, NG, NF = 2 ** len(COLS), 2 ** len(NEAR), 2 ** len(FAR)
BF = jnp.bfloat16
F32 = jnp.float32
NT = (((1,), (1,)), ((), ()))
TN = (((0,), (0,)), ((), ()))
CHUNKS = 4


def spread(x, axes):
    n = lax.axis_size(axes)
    return lax.all_to_all(jnp.broadcast_to(x[None], (n, *x.shape)), axes, 0, 0)


def swap(x, axis):
    return lax.ppermute(x, axis, [(0, 1), (1, 0)])


def bit(index, axis):
    return (index >> (len(AXES) - 1 - AXES.index(axis))) & 1


def pick(index, axes):
    out = 0
    for a in axes:
        out = out * 2 + bit(index, a)
    return out


def flip(p):
    mask = 0
    for a in reversed(COLS):
        mask |= (p & 1) << (len(AXES) - 1 - AXES.index(a))
        p >>= 1
    return mask


def decode_kernel(me_ref, ids_ref, targets_ref, out_ref):
    me = me_ref[0]
    k = pick(me, COLS)
    groups, lanes = ids_ref.shape
    own = targets_ref.shape[1]
    hot_own = groups * lanes // (NC * NG)
    shard = 32
    near_chunk = NG // CHUNKS
    width = near_chunk * (NF * shard + hot_own)
    aim = jnp.concatenate([targets_ref[pl.ds(me ^ flip(p), 1)] for p in range(NC)], axis=1)
    below = jnp.zeros(aim.shape, jnp.int32)
    slot = jnp.zeros(aim.shape, jnp.int32)
    for i in range(groups):
        ids = jnp.broadcast_to(ids_ref[i : i + 1], (lanes, lanes)).T
        ids = jnp.concatenate([ids] * NC, axis=1)
        place = lax.broadcasted_iota(jnp.int32, ids.shape, 0) + (i * lanes + 1)
        below += jnp.sum((ids < aim).astype(jnp.int32), axis=0, keepdims=True)
        slot += jnp.sum(jnp.where(ids == aim, place, 0), axis=0, keepdims=True)
    slot -= 1
    is_hot = slot >= 0
    row = aim - below
    block = row >> 5
    near = pick(block, NEAR)
    cold_col = near // near_chunk * width + (near % near_chunk) * (NF * shard)
    cold_col += pick(block, FAR) * shard + (row & (shard - 1))
    hot_block = slot >> 4
    hot_near = hot_block >> 3
    hot_col = hot_near // near_chunk * width + near_chunk * NF * shard
    hot_col += (hot_near % near_chunk) * hot_own + (slot & (hot_own - 1))
    column = jnp.where(is_hot, hot_col, cold_col)
    there = jnp.where(is_hot, hot_block & (NC - 1), pick(block, COLS))
    out_ref[...] = jnp.where(there == k, column, -1)


def chunk_table(cold_ref, hot_ref, g):
    n = NG // CHUNKS
    cold = cold_ref[pl.ds(g * n, n)]
    hot = hot_ref[pl.ds(g * n, n)]
    wide = cold.shape[-1]
    return jnp.concatenate([cold.reshape(-1, wide), hot.reshape(-1, wide)], axis=0)


def stats_kernel(me_ref, cold_ref, hot_ref, col_ref, *refs):
    *row_refs, out_ref = refs
    rows = jnp.concatenate([r[...] for r in row_refs], axis=0)
    cols = col_ref[...]
    count = rows.shape[0]
    k = pick(me_ref[0], COLS)

    def step(g, carry):
        top, total, hit = carry
        table = chunk_table(cold_ref, hot_ref, g)
        s = lax.dot_general(table, rows, NT, preferred_element_type=F32)
        new = jnp.maximum(top, jnp.max(s, axis=0, keepdims=True))
        total = total * jnp.exp(top - new) + jnp.sum(jnp.exp(s - new), axis=0, keepdims=True)
        where = lax.broadcasted_iota(jnp.int32, s.shape, 0) == cols - g * table.shape[0]
        hit = hit + jnp.sum(jnp.where(where, s, 0.0), axis=0, keepdims=True)
        return new, total, hit

    zero = jnp.zeros((1, count), F32)
    top, total, hit = lax.fori_loop(0, CHUNKS, step, (jnp.full((1, count), -1e30, F32), zero, zero))
    for p in range(NC):
        here = slice(p * 128, (p + 1) * 128)
        there = pl.ds(pl.multiple_of((k ^ p) * 128, 128), 128)
        out_ref[0:1, there] = top[:, here]
        out_ref[1:2, there] = total[:, here]
        out_ref[2:3, there] = hit[:, here]
        out_ref[3:4, there] = jnp.zeros((1, 128), F32)


def grads_kernel(me_ref, cold_ref, hot_ref, col_ref, stats_ref, *refs):
    *row_refs, keep_ref, send_ref, item_ref, loss_ref, acc_ref = refs
    rows = jnp.concatenate([r[...] for r in row_refs], axis=0)
    cols = col_ref[...]
    k = pick(me_ref[0], COLS)
    pieces = []
    for p in range(NC):
        there = pl.ds(pl.multiple_of((k ^ p) * 128, 128), 128)
        tops = [stats_ref[d, 0:1, there] for d in range(NC)]
        top = functools.reduce(jnp.maximum, tops)
        total = sum(stats_ref[d, 1:2, there] * jnp.exp(tops[d] - top) for d in range(NC))
        pieces.append(top + jnp.log(total))
        if p == 0:
            loss_ref[...] = pieces[0] - sum(stats_ref[d, 2:3, there] for d in range(NC))
    logs = jnp.concatenate(pieces, axis=1)
    acc_ref[...] = jnp.zeros_like(acc_ref)
    n = NG // CHUNKS
    cold_rows = cold_ref.shape[1]

    def step(g, carry):
        table = chunk_table(cold_ref, hot_ref, g)
        s = lax.dot_general(table, rows, NT, preferred_element_type=F32)
        where = lax.broadcasted_iota(jnp.int32, s.shape, 0) == cols - g * table.shape[0]
        w = (jnp.exp(s - logs) - jnp.where(where, 1.0, 0.0)).astype(BF)
        item = jnp.dot(w, rows, preferred_element_type=F32).astype(BF)
        wide = item.shape[-1]
        item_ref[pl.ds(g * n, n), :cold_rows] = item[: n * cold_rows].reshape(n, -1, wide)
        item_ref[pl.ds(g * n, n), cold_rows:] = item[n * cold_rows :].reshape(n, -1, wide)
        acc_ref[...] += lax.dot_general(table, w, TN, preferred_element_type=F32)
        return carry

    lax.fori_loop(0, CHUNKS, step, 0)
    half = acc_ref.shape[1] // 2
    keep_ref[...] = acc_ref[:, :half].T
    send_ref[...] = acc_ref[:, half:].T


def body(queries, hot_table, cold_table, hot_ids, targets):
    own, width = queries.shape
    shard = cold_table.shape[0]
    hot = hot_table.shape[0]
    hot_own = hot // (NC * NG)
    me = lax.axis_index(AXES)
    at_me = jnp.reshape(me, (1,)).astype(jnp.int32)
    k = pick(me, COLS)
    count = NC * own
    params = pltpu.CompilerParams(vmem_limit_bytes=48 << 20)
    vmem = pl.BlockSpec(memory_space=pltpu.VMEM)
    smem = pl.BlockSpec(memory_space=pltpu.SMEM)

    column = pl.pallas_call(
        decode_kernel,
        out_shape=jax.ShapeDtypeStruct((1, count), jnp.int32),
        in_specs=[smem, vmem, vmem],
        cost_estimate=pl.CostEstimate(flops=6 * hot * count, bytes_accessed=1 << 19, transcendentals=0),
        compiler_params=params,
    )(at_me, hot_ids.reshape(-1, 128), targets.reshape(-1, own))

    rows = [queries]
    for a in reversed(COLS):
        rows.append(swap(jnp.concatenate(rows, axis=0), a))

    far = spread(cold_table, FAR).reshape(NF * shard, width)
    far, rows[1], rows[2] = lax.optimization_barrier((far, rows[1], rows[2]))
    cold = spread(far, NEAR)
    mine = lax.dynamic_index_in_dim(hot_table.reshape(NG, NC, hot_own, width), k, 1, False)

    stats = pl.pallas_call(
        stats_kernel,
        out_shape=jax.ShapeDtypeStruct((4, count), F32),
        in_specs=[smem] + [vmem] * (3 + len(rows)),
        compiler_params=params,
    )(at_me, cold, mine, column, *rows)
    stats = spread(stats, COLS)
    keep, send, item_part, loss = pl.pallas_call(
        grads_kernel,
        out_shape=(
            jax.ShapeDtypeStruct((count // 2, width), F32),
            jax.ShapeDtypeStruct((count // 2, width), F32),
            jax.ShapeDtypeStruct((NG, NF * shard + hot_own, width), BF),
            jax.ShapeDtypeStruct((1, own), F32),
        ),
        in_specs=[smem] + [vmem] * (4 + len(rows)),
        scratch_shapes=[pltpu.VMEM((width, count), F32)],
        compiler_params=params,
    )(at_me, cold, mine, column, stats, *rows)

    near = lax.all_to_all(item_part, NEAR, 0, 0)
    other = swap(send, COLS[0])
    near, other = lax.optimization_barrier((near, other))
    keep = keep + other
    near = jnp.sum(near.astype(F32), axis=0).astype(BF)
    cold_part = near[: NF * shard].reshape(NF, shard, width)
    hot_part = jnp.broadcast_to(near[None, NF * shard :], (NF, hot_own, width))
    far = lax.all_to_all(jnp.concatenate([cold_part, hot_part], axis=1), FAR, 0, 0)
    other = swap(keep[count // 4 :], COLS[1])
    far, other = lax.optimization_barrier((far, other))
    keep = keep[: count // 4] + other
    far = jnp.sum(far.astype(F32), axis=0).astype(BF)
    grad_cold = far[:shard]
    grad_hot = spread(far[shard:], COLS)
    other = swap(keep[own:], COLS[2])
    grad_hot, other = lax.optimization_barrier((grad_hot, other))
    grad_queries = (keep[:own] + other).astype(BF)
    grad_hot = spread(grad_hot.reshape(NC * hot_own, width), NEAR).reshape(hot, width)
    return grad_queries, grad_hot, grad_cold, loss[0]


def solution(mesh):
    fine = Mesh(mesh.devices.reshape((2,) * len(AXES)), AXES)
    rows = P(AXES, None)
    return jax.shard_map(
        body,
        mesh=fine,
        in_specs=(rows, P(), rows, P(), P()),
        out_specs=(rows, P(), rows, P(AXES)),
        check_vma=False,
    )
```

time: 159 us -> 165 us (1.038)
  blocking collectives: 59.8 us -> 14.6 us
  waiting for transfers between devices: 23.5 us -> 61.6 us
  starting transfers between devices: 48.3 us -> 63.8 us
  local copies, waits for them, and re-layouts: 11.5 us -> 6.61 us
  Pallas kernels: 9.4 us -> 12.5 us
    all_to_all x2 -> x0, blocking collectives: 44.1 us -> none  [the longest x1 22.4 us: body(): lax.all_to_all(jnp.concatenate([cold_part, hot_part], axis=1), FAR, 0, 0)]
    all_to_all x0 -> x2, waiting for transfers between devices: none -> 16.6 us  [the longest x1 14.8 us: body(): near = lax.all_to_all(item_part, NEAR, 0, 0)]
    all_to_all x4, waiting for transfers between devices: 9.61 us -> 26.1 us  [spread(): return lax.all_to_all(jnp.broadcast_to(x[None], (n, *x.shape)), axes, 0, 0)]
    all_to_all x0 -> x2, starting transfers between devices: none -> 10.4 us  [the longest x1 6.33 us: body(): lax.all_to_all(jnp.concatenate([cold_part, hot_part], axis=1), FAR, 0, 0)]
    ppermute x6, starting transfers between devices: 15.8 us -> 22 us  [swap(): return lax.ppermute(x, axis, [(0, 1), (1, 0)])]
    ppermute x6, waiting for transfers between devices: 13.9 us -> 18.8 us  [swap(): return lax.ppermute(x, axis, [(0, 1), (1, 0)])]
    unnamed x15 -> x13, local copies, waits for them, and re-layouts: 5.89 us -> 1.79 us
    pallas_call x2 -> x3, Pallas kernels: 9.4 us -> 12.5 us  [the longest x1 6.24 us: body(): pl.pallas_call(grads_kernel, out_shape=(jax.ShapeDtypeStruct((count // 2,...]
  transfers between devices with their start and end apart: 10 -> 12, of which waited for: 8 -> 9; matrix products, arithmetic and copies ran while one was open for 8% -> 3% of each run, Pallas kernels for 0% -> 1%
where the time goes in v3:
time: 165 us; the launch traced here: 163 us
  starting transfers between devices  63.8 us (39%)
  waiting for transfers between devices  61.6 us (37%)
  blocking collectives  14.6 us (9%)
  Pallas kernels  12.5 us (8%)
  local copies, waits for them, and re-layouts  6.61 us (4%)
  other arithmetic  3.48 us (2%)
    all_to_all x4, starting transfers between devices, spread(): return lax.all_to_all(jnp.broadcast_to(x[None], (n, *x.shape)), axes, 0, 0)  31.4 us
    all_to_all x4, waiting for transfers between devices, spread(): return lax.all_to_all(jnp.broadcast_to(x[None], (n, *x.shape)), axes, 0, 0)  26.1 us
    ppermute x6, starting transfers between devices, swap(): return lax.ppermute(x, axis, [(0, 1), (1, 0)])  22 us
    ppermute x6, waiting for transfers between devices, swap(): return lax.ppermute(x, axis, [(0, 1), (1, 0)])  18.8 us
    all_to_all x1, waiting for transfers between devices, body(): near = lax.all_to_all(item_part, NEAR, 0, 0)  14.8 us
    all_to_all x1, blocking collectives, spread(): return lax.all_to_all(jnp.broadcast_to(x[None], (n, *x.shape)), axes, 0, 0)  14.6 us
    all_to_all x1, starting transfers between devices, body(): lax.all_to_all(jnp.concatenate([cold_part, hot_part], axis=1), FAR, 0, 0)  6.33 us
    pallas_call x1, Pallas kernels, body(): pl.pallas_call(grads_kernel, out_shape=(jax.ShapeDtypeStruct((count // 2,...  6.24 us
  transfers between devices with their start and end apart: 12, of which 9 were waited for; matrix products, arithmetic and copies ran while one was open for 3% of the time, Pallas kernels for 1%

profile of v3, /device:TPU:1, one launch (start us, length us, event | category | flops | bytes accessed | tf_op | source)
XLA Modules:
  0.0 163.5 jit_solution(127977907571733012)
XLA Ops:
  0.6 5.9 %collective-permute-start = (bf16[128,256]{1,0:T(8,128)(2,1)}, bf16[128,256]{1,0:T(8,128)(2,1)S(1)}, u32[]{:S(2)}, u32[]{:S(2)}) collective-permute-start(bf16[128,256]{1,0:T(8,128)(2,1)} %refs_0_.3), channel_id=1, source_target_pairs={{0,64},{64,0},{1,65},{65,1},{2,66},{66,2},{3,67},{67,3},{4,68},{68... | collective-permute-start | bytes 196616 | tf_op jit(solution)/shard_map/ppermute | solution.py:29
  6.5 1.4 broadcast_in_dim.14
  7.9 13.0 %all-to-all-start = ((bf16[4,32,256]{2,1,0:T(8,128)(2,1)}), bf16[4,32,256]{2,1,0:T(8,128)(2,1)S(1)}, u32[]{:S(2)}, u32[]{:S(2)}) async-start(bf16[4,32,256]{2,1,0:T(8,128)(2,1)} %broadcast_in_dim.14), calls=%async_computation | async-start | bytes 131072 | tf_op jit(solution)/shard_map/all_to_all | solution.py:25
  20.9 0.8 pad_maximum_fusion.1
  21.7 2.6 %collective-permute-start.1 = (bf16[256,256]{1,0:T(8,128)(2,1)S(1)}, bf16[256,256]{1,0:T(8,128)(2,1)S(1)}, u32[]{:S(2)}, u32[]{:S(2)}) collective-permute-start(bf16[256,256]{1,0:T(8,128)(2,1)S(1)} %pad_maximum_fusion.1), channel_id=1, source_target_pairs={{0,32},{32,0},{1,33},{33,1},{2,34},{34,2},{3,35},{35,3},{4,36},{36... | collective-permute-start | bytes 393224 | tf_op jit(solution)/shard_map/ppermute | solution.py:29
  24.4 3.4 %collective-permute-done.1.refs_2_ = bf16[256,256]{1,0:T(8,128)(2,1)S(1)} collective-permute-done((bf16[256,256]{1,0:T(8,128)(2,1)S(1)}, bf16[256,256]{1,0:T(8,128)(2,1)S(1)}, u32[]{:S(2)}, u32[]{:S(2)}) %collective-permute-start.1) | collective-permute-done | bytes 131104 | tf_op jit(solution)/shard_map/ppermute | solution.py:29
  27.7 4.8 %all-to-all-done = bf16[4,32,256]{2,1,0:T(8,128)(2,1)S(1)} async-done(((bf16[4,32,256]{2,1,0:T(8,128)(2,1)}), bf16[4,32,256]{2,1,0:T(8,128)(2,1)S(1)}, u32[]{:S(2)}, u32[]{:S(2)}) %all-to-all-start) | async-done | bytes 65568 | tf_op jit(solution)/shard_map/all_to_all | solution.py:25
  32.6 1.1 broadcast_in_dim.15
  33.7 6.9 %all-to-all-start.1 = ((bf16[16,128,256]{2,1,0:T(8,128)(2,1)}), bf16[16,128,256]{2,1,0:T(8,128)(2,1)S(1)}, u32[]{:S(2)}, u32[]{:S(2)}) async-start(bf16[16,128,256]{2,1,0:T(8,128)(2,1)} %broadcast_in_dim.15), calls=%async_computation.1 | async-start | bytes 2097152 | tf_op jit(solution)/shard_map/all_to_all | solution.py:25
  40.6 4.8 %collective-permute-start.2 = (bf16[512,256]{1,0:T(8,128)(2,1)S(1)}, bf16[512,256]{1,0:T(8,128)(2,1)S(1)}, u32[]{:S(2)}, u32[]{:S(2)}) collective-permute-start(bf16[512,256]{1,0:T(8,128)(2,1)S(1)} %pad_maximum_fusion), channel_id=1, source_target_pairs={{0,8},{8,0},{1,9},{9,1},{2,10},{10,2},{3,11},{11,3},{4,12},{12,4},... | collective-permute-start | bytes 786440 | tf_op jit(solution)/shard_map/ppermute | solution.py:29
  45.4 2.1 %shard_map.84.col_ref = s32[1,1024]{1,0:T(1,128)S(1)} custom-call(s32[1]{0:T(128)} %bitcast.me_ref, s32[16,128]{1,0:T(8,128)S(1)} %bitcast.15, s32[512,128]{1,0:T(8,128)S(1)} %bitcast.14), custom_call_target="tpu_custom_call" | custom-call | flops 12582912 | bytes 524288 | tf_op jit(solution)/shard_map/pallas_call | solution.py:171
  47.6 6.3 %all-to-all-done.1.cold_ref = bf16[16,128,256]{2,1,0:T(8,128)(2,1)S(1)} async-done(((bf16[16,128,256]{2,1,0:T(8,128)(2,1)}), bf16[16,128,256]{2,1,0:T(8,128)(2,1)S(1)}, u32[]{:S(2)}, u32[]{:S(2)}) %all-to-all-start.1) | async-done | bytes 1048608 | tf_op jit(solution)/shard_map/all_to_all | solution.py:25
  53.9 4.2 %shard_map.85 = f32[4,1024]{1,0:T(4,128)S(1)} custom-call(s32[1]{0:T(128)} %bitcast.me_ref, bf16[16,128,256]{2,1,0:T(8,128)(2,1)S(1)} %all-to-all-done.1.cold_ref, bf16[16,16,256]{2,1,0:T(8,128)(2,1)S(1)} %dynamic-slice_bitcast_fusion.hot_ref, s32[1,1024]{1,0:T(1,128)S(1)} %shard_map.84.col_ref, bf16[128,256]{1,0:T(8,128)(2,1)S(1)} %copy-done.1, ...), custom_call_target="tpu_custom_call" | custom-call | tf_op jit(solution)/shard_map/pallas_call | solution.py:188
  58.1 14.6 %all_to_all.35.stats_ref = f32[8,4,1024]{2,1,0:T(4,128)S(1)} all-to-all(f32[8,4,1024]{2,1,0:T(4,128)S(1)} %broadcast_in_dim.16), channel_id=1, replica_groups=mesh['z8'=2,'z4'=2,'z2'=2,'z1'=2,'yl'=2,'c'=2,'x2'=2,'x1'=2,'yh'=2] {'c'..., dimensions={0} | all-to-all | bytes 262144 | tf_op jit(solution)/shard_map/all_to_all | solution.py:25
  72.7 6.2 %shard_map.86 = (f32[512,256]{1,0:T(8,128)S(1)}, f32[512,256]{1,0:T(8,128)S(1)}, bf16[16,144,256]{2,1,0:T(8,128)(2,1)}, f32[1,128]{1,0:T(1,128)}) custom-call(s32[1]{0:T(128)} %bitcast.me_ref, bf16[16,128,256]{2,1,0:T(8,128)(2,1)S(1)} %all-to-all-done.1.cold_ref, bf16[16,16,256]{2,1,0:T(8,128)(2,1)S(1)} %dynamic-slice_bitcast_fusion.hot_ref, ...), custom_call_target="tpu_custom_call" | custom-call | tf_op jit(solution)/shard_map/pallas_call | solution.py:195
  79.0 0.8 copy-done.4
  79.8 4.1 %all-to-all-start.3 = ((bf16[16,144,256]{2,1,0:T(8,128)(2,1)}), bf16[16,144,256]{2,1,0:T(8,128)(2,1)S(1)}, u32[]{:S(2)}, u32[]{:S(2)}) async-start(bf16[16,144,256]{2,1,0:T(8,128)(2,1)} %get-tuple-element.21), calls=%async_computation.3 | async-start | bytes 2359296 | tf_op jit(solution)/shard_map/all_to_all | solution.py:208
  83.8 2.6 %collective-permute-start.3 = (f32[512,256]{1,0:T(8,128)S(1)}, f32[512,256]{1,0:T(8,128)}, u32[]{:S(2)}, u32[]{:S(2)}) collective-permute-start(f32[512,256]{1,0:T(8,128)S(1)} %copy-done.5), channel_id=1, source_target_pairs={{0,8},{8,0},{1,9},{9,1},{2,10},{10,2},{3,11},{11,3},{4,12},{12,4},... | collective-permute-start | bytes 1572872 | tf_op jit(solution)/shard_map/ppermute | solution.py:29
  86.4 1.6 %collective-permute-done.3 = f32[512,256]{1,0:T(8,128)} collective-permute-done((f32[512,256]{1,0:T(8,128)S(1)}, f32[512,256]{1,0:T(8,128)}, u32[]{:S(2)}, u32[]{:S(2)}) %collective-permute-start.3) | collective-permute-done | bytes 524320 | tf_op jit(solution)/shard_map/ppermute | solution.py:29
  88.1 14.8 %all-to-all-done.3 = bf16[16,144,256]{2,1,0:T(8,128)(2,1)S(1)} async-done(((bf16[16,144,256]{2,1,0:T(8,128)(2,1)}), bf16[16,144,256]{2,1,0:T(8,128)(2,1)S(1)}, u32[]{:S(2)}, u32[]{:S(2)}) %all-to-all-start.3) | async-done | bytes 1179680 | tf_op jit(solution)/shard_map/all_to_all | solution.py:208
  103.7 6.3 %all-to-all-start.4 = ((bf16[4,48,256]{2,1,0:T(8,128)(2,1)}), bf16[4,48,256]{2,1,0:T(8,128)(2,1)S(1)}, u32[]{:S(2)}, u32[]{:S(2)}) async-start(bf16[4,48,256]{2,1,0:T(8,128)(2,1)} %pad_maximum_fusion.2), calls=%async_computation.4 | async-start | bytes 196608 | tf_op jit(solution)/shard_map/all_to_all | solution.py:215
  110.0 1.1 add.54
  111.2 1.9 %collective-permute-start.4 = (f32[256,256]{1,0:T(8,128)S(1)}, f32[256,256]{1,0:T(8,128)S(1)}, u32[]{:S(2)}, u32[]{:S(2)}) collective-permute-start(f32[256,256]{1,0:T(8,128)S(1)} %slice.35), channel_id=1, source_target_pairs={{0,32},{32,0},{1,33},{33,1},{2,34},{34,2},{3,35},{35,3},{4,36},{36... | collective-permute-start | bytes 786440 | tf_op jit(solution)/shard_map/ppermute | solution.py:29
  113.1 7.1 %collective-permute-done.4 = f32[256,256]{1,0:T(8,128)S(1)} collective-permute-done((f32[256,256]{1,0:T(8,128)S(1)}, f32[256,256]{1,0:T(8,128)S(1)}, u32[]{:S(2)}, u32[]{:S(2)}) %collective-permute-start.4) | collective-permute-done | bytes 262176 | tf_op jit(solution)/shard_map/ppermute | solution.py:29
  120.2 1.8 %all-to-all-done.4 = bf16[4,48,256]{2,1,0:T(8,128)(2,1)S(1)} async-done(((bf16[4,48,256]{2,1,0:T(8,128)(2,1)}), bf16[4,48,256]{2,1,0:T(8,128)(2,1)S(1)}, u32[]{:S(2)}, u32[]{:S(2)}) %all-to-all-start.4) | async-done | bytes 98336 | tf_op jit(solution)/shard_map/all_to_all | solution.py:215
  122.7 7.3 %all-to-all-start.5 = ((bf16[8,16,256]{2,1,0:T(8,128)(2,1)}), bf16[8,16,256]{2,1,0:T(8,128)(2,1)S(1)}, u32[]{:S(2)}, u32[]{:S(2)}) async-start(bf16[8,16,256]{2,1,0:T(8,128)(2,1)} %broadcast_in_dim.18), calls=%async_computation.5 | async-start | bytes 131072 | tf_op jit(solution)/shard_map/all_to_all | solution.py:25
  130.0 4.2 %collective-permute-start.5 = (f32[128,256]{1,0:T(8,128)S(1)}, f32[128,256]{1,0:T(8,128)S(1)}, u32[]{:S(2)}, u32[]{:S(2)}) collective-permute-start(f32[128,256]{1,0:T(8,128)S(1)} %slice.38), channel_id=1, source_target_pairs={{0,64},{64,0},{1,65},{65,1},{2,66},{66,2},{3,67},{67,3},{4,68},{68... | collective-permute-start | bytes 393224 | tf_op jit(solution)/shard_map/ppermute | solution.py:29
  134.2 6.7 %collective-permute-done.5 = f32[128,256]{1,0:T(8,128)S(1)} collective-permute-done((f32[128,256]{1,0:T(8,128)S(1)}, f32[128,256]{1,0:T(8,128)S(1)}, u32[]{:S(2)}, u32[]{:S(2)}) %collective-permute-start.5) | collective-permute-done | bytes 131104 | tf_op jit(solution)/shard_map/ppermute | solution.py:29
  140.9 1.1 broadcast_in_dim.20
  142.0 4.3 %all-to-all-start.6 = ((bf16[16,128,256]{2,1,0:T(8,128)(2,1)}), bf16[16,128,256]{2,1,0:T(8,128)(2,1)S(1)}, u32[]{:S(2)}, u32[]{:S(2)}) async-start(bf16[16,128,256]{2,1,0:T(8,128)(2,1)} %broadcast_in_dim.20), calls=%async_computation.6 | async-start | bytes 2097152 | tf_op jit(solution)/shard_map/all_to_all | solution.py:25
  147.5 15.0 %all-to-all-done.6 = bf16[16,128,256]{2,1,0:T(8,128)(2,1)S(1)} async-done(((bf16[16,128,256]{2,1,0:T(8,128)(2,1)}), bf16[16,128,256]{2,1,0:T(8,128)(2,1)S(1)}, u32[]{:S(2)}, u32[]{:S(2)}) %all-to-all-start.6) | async-done | bytes 1048608 | tf_op jit(solution)/shard_map/all_to_all | solution.py:25
  162.5 1.0 copy.12
  (30 shorter events, 2.9 us)
Async XLA Ops:
  0.6 46.9 %copy-start = (bf16[2048,256]{1,0:T(8,128)(2,1)S(1)}, bf16[2048,256]{1,0:T(8,128)(2,1)}, u32[]{:S(2)}) copy-start(bf16[2048,256]{1,0:T(8,128)(2,1)} %param.6) | copy-start | bytes 3145732
  0.6 20.2 %collective-permute-start = (bf16[128,256]{1,0:T(8,128)(2,1)}, bf16[128,256]{1,0:T(8,128)(2,1)S(1)}, u32[]{:S(2)}, u32[]{:S(2)}) collective-permute-start(bf16[128,256]{1,0:T(8,128)(2,1)} %refs_0_.3), channel_id=1, source_target_pairs={{0,64},{64,0},{1,65},{65,1},{2,66},{66,2},{3,67},{67,3},{4,68},{68... | collective-permute-start | bytes 196616 | tf_op jit(solution)/shard_map/ppermute | solution.py:29
  7.9 24.7 %all-to-all-start = ((bf16[4,32,256]{2,1,0:T(8,128)(2,1)}), bf16[4,32,256]{2,1,0:T(8,128)(2,1)S(1)}, u32[]{:S(2)}, u32[]{:S(2)}) async-start(bf16[4,32,256]{2,1,0:T(8,128)(2,1)} %broadcast_in_dim.14), calls=%async_computation | async-start | bytes 131072 | tf_op jit(solution)/shard_map/all_to_all | solution.py:25
  21.7 6.0 %collective-permute-start.1 = (bf16[256,256]{1,0:T(8,128)(2,1)S(1)}, bf16[256,256]{1,0:T(8,128)(2,1)S(1)}, u32[]{:S(2)}, u32[]{:S(2)}) collective-permute-start(bf16[256,256]{1,0:T(8,128)(2,1)S(1)} %pad_maximum_fusion.1), channel_id=1, source_target_pairs={{0,32},{32,0},{1,33},{33,1},{2,34},{34,2},{3,35},{35,3},{4,36},{36... | collective-permute-start | bytes 393224 | tf_op jit(solution)/shard_map/ppermute | solution.py:29
  33.7 6.9 %copy-start.1 = (bf16[128,256]{1,0:T(8,128)(2,1)S(1)}, bf16[128,256]{1,0:T(8,128)(2,1)}, u32[]{:S(2)}) copy-start(bf16[128,256]{1,0:T(8,128)(2,1)} %refs_0_.3) | copy-start | bytes 196612
  33.7 11.8 %copy-start.2 = (s32[65536]{0:T(1024)S(1)}, s32[65536]{0:T(1024)}, u32[]{:S(2)}) copy-start(s32[65536]{0:T(1024)} %param.9) | copy-start | bytes 786436
  33.7 11.8 %copy-start.3 = (s32[2048]{0:T(1024)S(1)}, s32[2048]{0:T(1024)}, u32[]{:S(2)}) copy-start(s32[2048]{0:T(1024)} %param.8) | copy-start | bytes 24580
  33.7 20.2 %all-to-all-start.1 = ((bf16[16,128,256]{2,1,0:T(8,128)(2,1)}), bf16[16,128,256]{2,1,0:T(8,128)(2,1)S(1)}, u32[]{:S(2)}, u32[]{:S(2)}) async-start(bf16[16,128,256]{2,1,0:T(8,128)(2,1)} %broadcast_in_dim.15), calls=%async_computation.1 | async-start | bytes 2097152 | tf_op jit(solution)/shard_map/all_to_all | solution.py:25
  40.6 6.9 %collective-permute-start.2 = (bf16[512,256]{1,0:T(8,128)(2,1)S(1)}, bf16[512,256]{1,0:T(8,128)(2,1)S(1)}, u32[]{:S(2)}, u32[]{:S(2)}) collective-permute-start(bf16[512,256]{1,0:T(8,128)(2,1)S(1)} %pad_maximum_fusion), channel_id=1, source_target_pairs={{0,8},{8,0},{1,9},{9,1},{2,10},{10,2},{3,11},{11,3},{4,12},{12,4},... | collective-permute-start | bytes 786440 | tf_op jit(solution)/shard_map/ppermute | solution.py:29
  79.0 0.8 copy-start.4
  79.8 4.1 %copy-start.5 = (f32[512,256]{1,0:T(8,128)S(1)}, f32[512,256]{1,0:T(8,128)}, u32[]{:S(2)}) copy-start(f32[512,256]{1,0:T(8,128)} %copy-done.4) | copy-start | bytes 1572868
  79.8 23.1 %all-to-all-start.3 = ((bf16[16,144,256]{2,1,0:T(8,128)(2,1)}), bf16[16,144,256]{2,1,0:T(8,128)(2,1)S(1)}, u32[]{:S(2)}, u32[]{:S(2)}) async-start(bf16[16,144,256]{2,1,0:T(8,128)(2,1)} %get-tuple-element.21), calls=%async_computation.3 | async-start | bytes 2359296 | tf_op jit(solution)/shard_map/all_to_all | solution.py:208
  83.8 4.2 %collective-permute-start.3 = (f32[512,256]{1,0:T(8,128)S(1)}, f32[512,256]{1,0:T(8,128)}, u32[]{:S(2)}, u32[]{:S(2)}) collective-permute-start(f32[512,256]{1,0:T(8,128)S(1)} %copy-done.5), channel_id=1, source_target_pairs={{0,8},{8,0},{1,9},{9,1},{2,10},{10,2},{3,11},{11,3},{4,12},{12,4},... | collective-permute-start | bytes 1572872 | tf_op jit(solution)/shard_map/ppermute | solution.py:29
  103.7 18.3 %all-to-all-start.4 = ((bf16[4,48,256]{2,1,0:T(8,128)(2,1)}), bf16[4,48,256]{2,1,0:T(8,128)(2,1)S(1)}, u32[]{:S(2)}, u32[]{:S(2)}) async-start(bf16[4,48,256]{2,1,0:T(8,128)(2,1)} %pad_maximum_fusion.2), calls=%async_computation.4 | async-start | bytes 196608 | tf_op jit(solution)/shard_map/all_to_all | solution.py:215
  111.2 9.0 %collective-permute-start.4 = (f32[256,256]{1,0:T(8,128)S(1)}, f32[256,256]{1,0:T(8,128)S(1)}, u32[]{:S(2)}, u32[]{:S(2)}) collective-permute-start(f32[256,256]{1,0:T(8,128)S(1)} %slice.35), channel_id=1, source_target_pairs={{0,32},{32,0},{1,33},{33,1},{2,34},{34,2},{3,35},{35,3},{4,36},{36... | collective-permute-start | bytes 786440 | tf_op jit(solution)/shard_map/ppermute | solution.py:29
  122.7 18.2 %all-to-all-start.5 = ((bf16[8,16,256]{2,1,0:T(8,128)(2,1)}), bf16[8,16,256]{2,1,0:T(8,128)(2,1)S(1)}, u32[]{:S(2)}, u32[]{:S(2)}) async-start(bf16[8,16,256]{2,1,0:T(8,128)(2,1)} %broadcast_in_dim.18), calls=%async_computation.5 | async-start | bytes 131072 | tf_op jit(solution)/shard_map/all_to_all | solution.py:25
  130.0 10.9 %collective-permute-start.5 = (f32[128,256]{1,0:T(8,128)S(1)}, f32[128,256]{1,0:T(8,128)S(1)}, u32[]{:S(2)}, u32[]{:S(2)}) collective-permute-start(f32[128,256]{1,0:T(8,128)S(1)} %slice.38), channel_id=1, source_target_pairs={{0,64},{64,0},{1,65},{65,1},{2,66},{66,2},{3,67},{67,3},{4,68},{68... | collective-permute-start | bytes 393224 | tf_op jit(solution)/shard_map/ppermute | solution.py:29
  142.0 20.5 %all-to-all-start.6 = ((bf16[16,128,256]{2,1,0:T(8,128)(2,1)}), bf16[16,128,256]{2,1,0:T(8,128)(2,1)S(1)}, u32[]{:S(2)}, u32[]{:S(2)}) async-start(bf16[16,128,256]{2,1,0:T(8,128)(2,1)} %broadcast_in_dim.20), calls=%async_computation.6 | async-start | bytes 2097152 | tf_op jit(solution)/shard_map/all_to_all | solution.py:25

commit v4 on v3

--- a/solution.py
+++ b/solution.py
@@ -9,8 +9,9 @@
 from jax.sharding import PartitionSpec as P
 
 AXES = ("z8", "z4", "z2", "z1", "yl", "c", "x2", "x1", "yh")
-COLS = ("c", "z1", "z2")
-NEAR = ("yl", "x2", "x1", "yh")
+COLS = ("z1", "z2", "yl", "c")
+HALF = ("z1", "z2", "yl")
+NEAR = ("x2", "x1", "yh")
 FAR = ("z8", "z4")
 NC, NG, NF = 2 ** len(COLS), 2 ** len(NEAR), 2 ** len(FAR)
 BF = jnp.bfloat16
@@ -73,12 +74,12 @@
     near = pick(block, NEAR)
     cold_col = near // near_chunk * width + (near % near_chunk) * (NF * shard)
     cold_col += pick(block, FAR) * shard + (row & (shard - 1))
-    hot_block = slot >> 4
-    hot_near = hot_block >> 3
+    hot_near = (slot >> 7) & (NG - 1)
+    hot_k = (((slot >> 4) & 7) << 1) | (slot >> 10)
     hot_col = hot_near // near_chunk * width + near_chunk * NF * shard
     hot_col += (hot_near % near_chunk) * hot_own + (slot & (hot_own - 1))
     column = jnp.where(is_hot, hot_col, cold_col)
-    there = jnp.where(is_hot, hot_block & (NC - 1), pick(block, COLS))
+    there = jnp.where(is_hot, hot_k, pick(block, COLS))
     out_ref[...] = jnp.where(there == k, column, -1)
 
 
@@ -109,13 +110,12 @@
 
     zero = jnp.zeros((1, count), F32)
     top, total, hit = lax.fori_loop(0, CHUNKS, step, (jnp.full((1, count), -1e30, F32), zero, zero))
+    logs = top + jnp.log(total)
     for p in range(NC):
         here = slice(p * 128, (p + 1) * 128)
         there = pl.ds(pl.multiple_of((k ^ p) * 128, 128), 128)
-        out_ref[0:1, there] = top[:, here]
-        out_ref[1:2, there] = total[:, here]
-        out_ref[2:3, there] = hit[:, here]
-        out_ref[3:4, there] = jnp.zeros((1, 128), F32)
+        out_ref[0:1, there] = logs[:, here]
+        out_ref[1:2, there] = hit[:, here]
 
 
 def grads_kernel(me_ref, cold_ref, hot_ref, col_ref, stats_ref, *refs):
@@ -128,10 +128,10 @@
         there = pl.ds(pl.multiple_of((k ^ p) * 128, 128), 128)
         tops = [stats_ref[d, 0:1, there] for d in range(NC)]
         top = functools.reduce(jnp.maximum, tops)
-        total = sum(stats_ref[d, 1:2, there] * jnp.exp(tops[d] - top) for d in range(NC))
+        total = sum(jnp.exp(t - top) for t in tops)
         pieces.append(top + jnp.log(total))
         if p == 0:
-            loss_ref[...] = pieces[0] - sum(stats_ref[d, 2:3, there] for d in range(NC))
+            loss_ref[...] = pieces[0] - sum(stats_ref[d, 1:2, there] for d in range(NC))
     logs = jnp.concatenate(pieces, axis=1)
     acc_ref[...] = jnp.zeros_like(acc_ref)
     n = NG // CHUNKS
@@ -150,9 +150,23 @@
         return carry
 
     lax.fori_loop(0, CHUNKS, step, 0)
-    half = acc_ref.shape[1] // 2
-    keep_ref[...] = acc_ref[:, :half].T
-    send_ref[...] = acc_ref[:, half:].T
+    for j in range(NC // 2):
+        out = slice(j * 128, (j + 1) * 128)
+        keep_ref[out] = acc_ref[:, 2 * j * 128 : (2 * j + 1) * 128].T
+        send_ref[out] = acc_ref[:, (2 * j + 1) * 128 : (2 * j + 2) * 128].T.astype(BF)
+
+
+def place_kernel(me_ref, own_ref, other_ref, out_ref, sems):
+    core = bit(me_ref[0], "c")
+    half = own_ref.shape[0]
+    first = pltpu.make_async_copy(own_ref, out_ref.at[pl.ds(core * half, half)], sems.at[0])
+    second = pltpu.make_async_copy(
+        other_ref, out_ref.at[pl.ds((1 - core) * half, half)], sems.at[1]
+    )
+    first.start()
+    second.start()
+    first.wait()
+    second.wait()
 
 
 def body(queries, hot_table, cold_table, hot_ids, targets):
@@ -164,7 +178,7 @@
     at_me = jnp.reshape(me, (1,)).astype(jnp.int32)
     k = pick(me, COLS)
     count = NC * own
-    params = pltpu.CompilerParams(vmem_limit_bytes=48 << 20)
+    params = pltpu.CompilerParams(vmem_limit_bytes=24 << 20)
     vmem = pl.BlockSpec(memory_space=pltpu.VMEM)
     smem = pl.BlockSpec(memory_space=pltpu.SMEM)
 
@@ -176,18 +190,21 @@
         compiler_params=params,
     )(at_me, hot_ids.reshape(-1, 128), targets.reshape(-1, own))
 
-    rows = [queries]
-    for a in reversed(COLS):
-        rows.append(swap(jnp.concatenate(rows, axis=0), a))
+    pair = jnp.concatenate([queries, swap(queries, "c")], axis=0)
+    rows = [pair, swap(pair, "yl"), swap(pair, "z2")]
+    rows.append(lax.ppermute(pair, ("z2", "yl"), [(i, 3 - i) for i in range(4)]))
 
     far = spread(cold_table, FAR).reshape(NF * shard, width)
-    far, rows[1], rows[2] = lax.optimization_barrier((far, rows[1], rows[2]))
+    far, rows = lax.optimization_barrier((far, jnp.concatenate(rows, axis=0)))
     cold = spread(far, NEAR)
-    mine = lax.dynamic_index_in_dim(hot_table.reshape(NG, NC, hot_own, width), k, 1, False)
+    rows = [rows, swap(rows, "z1")]
+    mine = hot_table.reshape(2, NG, NC // 2, hot_own, width)
+    mine = lax.dynamic_slice(mine, (k & 1, 0, k >> 1, 0, 0), (1, NG, 1, hot_own, width))
+    mine = mine.reshape(NG, hot_own, width)
 
     stats = pl.pallas_call(
         stats_kernel,
-        out_shape=jax.ShapeDtypeStruct((4, count), F32),
+        out_shape=jax.ShapeDtypeStruct((2, count), F32),
         in_specs=[smem] + [vmem] * (3 + len(rows)),
         compiler_params=params,
     )(at_me, cold, mine, column, *rows)
@@ -196,7 +213,7 @@
         grads_kernel,
         out_shape=(
             jax.ShapeDtypeStruct((count // 2, width), F32),
-            jax.ShapeDtypeStruct((count // 2, width), F32),
+            jax.ShapeDtypeStruct((count // 2, width), BF),
             jax.ShapeDtypeStruct((NG, NF * shard + hot_own, width), BF),
             jax.ShapeDtypeStruct((1, own), F32),
         ),
@@ -206,24 +223,32 @@
     )(at_me, cold, mine, column, stats, *rows)
 
     near = lax.all_to_all(item_part, NEAR, 0, 0)
-    other = swap(send, COLS[0])
+    keep = keep + swap(send, "c").astype(F32)
+    other = swap(keep[count // 4 :].astype(BF), "z1")
     near, other = lax.optimization_barrier((near, other))
-    keep = keep + other
     near = jnp.sum(near.astype(F32), axis=0).astype(BF)
     cold_part = near[: NF * shard].reshape(NF, shard, width)
     hot_part = jnp.broadcast_to(near[None, NF * shard :], (NF, hot_own, width))
     far = lax.all_to_all(jnp.concatenate([cold_part, hot_part], axis=1), FAR, 0, 0)
-    other = swap(keep[count // 4 :], COLS[1])
-    far, other = lax.optimization_barrier((far, other))
-    keep = keep[: count // 4] + other
     far = jnp.sum(far.astype(F32), axis=0).astype(BF)
     grad_cold = far[:shard]
-    grad_hot = spread(far[shard:], COLS)
-    other = swap(keep[own:], COLS[2])
-    grad_hot, other = lax.optimization_barrier((grad_hot, other))
-    grad_queries = (keep[:own] + other).astype(BF)
-    grad_hot = spread(grad_hot.reshape(NC * hot_own, width), NEAR).reshape(hot, width)
-    return grad_queries, grad_hot, grad_cold, loss[0]
+    keep = keep[: count // 4] + other.astype(F32)
+    for a in ("z2", "yl"):
+        half = keep.shape[0] // 2
+        keep = keep[:half] + swap(keep[half:].astype(BF), a).astype(F32)
+    grad_hot = spread(far[shard:], HALF).reshape(-1, width)
+    grad_hot = spread(grad_hot, NEAR)
+    grad_hot, keep = lax.optimization_barrier((grad_hot, keep))
+    grad_hot = grad_hot.reshape(hot // 2, width)
+    grad_hot = pl.pallas_call(
+        place_kernel,
+        out_shape=jax.ShapeDtypeStruct((hot, width), BF),
+        in_specs=[smem, vmem, vmem],
+        out_specs=pl.BlockSpec(memory_space=pl.ANY),
+        scratch_shapes=[pltpu.SemaphoreType.DMA((2,))],
+        compiler_params=params,
+    )(at_me, grad_hot, swap(grad_hot, "c"))
+    return keep.astype(BF), grad_hot, grad_cold, loss[0]
 
 
 def solution(mesh):

time: 165 us -> 165 us (level)
  waiting for transfers between devices: 61.6 us -> 29.6 us
  blocking collectives: 14.6 us -> 38.8 us
  starting transfers between devices: 63.8 us -> 68.8 us
  Pallas kernels: 12.5 us -> 16.2 us
    all_to_all x0 -> x1, blocking collectives: none -> 22.2 us  [body(): lax.all_to_all(jnp.concatenate([cold_part, hot_part], axis=1), FAR, 0, 0)]
    all_to_all x4, waiting for transfers between devices: 26.1 us -> 7.37 us  [spread(): return lax.all_to_all(jnp.broadcast_to(x[None], (n, *x.shape)), axes, 0, 0)]
    ppermute x6 -> x9, waiting for transfers between devices: 18.8 us -> 5.01 us  [swap(): return lax.ppermute(x, axis, [(0, 1), (1, 0)])]
    ppermute x6 -> x9, starting transfers between devices: 22 us -> 33.9 us  [swap(): return lax.ppermute(x, axis, [(0, 1), (1, 0)])]
    ppermute x0 -> x1, waiting for transfers between devices: none -> 10 us  [body(): lax.ppermute(pair, ('z2', 'yl'), [(i, 3 - i) for i in range(4)])]
    all_to_all x1, waiting for transfers between devices: 14.8 us -> 7.19 us  [body(): near = lax.all_to_all(item_part, NEAR, 0, 0)]
    all_to_all x1 -> x0, starting transfers between devices: 6.33 us -> none  [body(): lax.all_to_all(jnp.concatenate([cold_part, hot_part], axis=1), FAR, 0, 0)]
    all_to_all x4, starting transfers between devices: 31.4 us -> 27.7 us  [spread(): return lax.all_to_all(jnp.broadcast_to(x[None], (n, *x.shape)), axes, 0, 0)]
  transfers between devices with their start and end apart: 12 -> 15, of which waited for: 9 -> 8; matrix products, arithmetic and copies ran while one was open for 3% -> 3% of each run, Pallas kernels for 1% -> 3%
where the time goes in v4:
time: 165 us; the launch traced here: 164 us
  starting transfers between devices  68.8 us (42%)
  blocking collectives  38.8 us (24%)
  waiting for transfers between devices  29.6 us (18%)
  Pallas kernels  16.2 us (10%)
  local copies, waits for them, and re-layouts  6.28 us (4%)
  other arithmetic  3.05 us (2%)
    ppermute x9, starting transfers between devices, swap(): return lax.ppermute(x, axis, [(0, 1), (1, 0)])  33.9 us
    all_to_all x4, starting transfers between devices, spread(): return lax.all_to_all(jnp.broadcast_to(x[None], (n, *x.shape)), axes, 0, 0)  27.7 us
    all_to_all x1, blocking collectives, body(): lax.all_to_all(jnp.concatenate([cold_part, hot_part], axis=1), FAR, 0, 0)  22.2 us
    all_to_all x1, blocking collectives, spread(): return lax.all_to_all(jnp.broadcast_to(x[None], (n, *x.shape)), axes, 0, 0)  16.6 us
    ppermute x1, waiting for transfers between devices, body(): lax.ppermute(pair, ('z2', 'yl'), [(i, 3 - i) for i in range(4)])  10 us
    all_to_all x4, waiting for transfers between devices, spread(): return lax.all_to_all(jnp.broadcast_to(x[None], (n, *x.shape)), axes, 0, 0)  7.37 us
    all_to_all x1, waiting for transfers between devices, body(): near = lax.all_to_all(item_part, NEAR, 0, 0)  7.19 us
    pallas_call x1, Pallas kernels, body(): pl.pallas_call(grads_kernel, out_shape=(jax.ShapeDtypeStruct((count // 2,...  6.95 us
  transfers between devices with their start and end apart: 15, of which 8 were waited for; matrix products, arithmetic and copies ran while one was open for 3% of the time, Pallas kernels for 3%

profile of v4, /device:TPU:1, one launch (start us, length us, event | category | flops | bytes accessed | tf_op | source)
XLA Modules:
  0.0 163.7 jit_solution(14447718566046706960)
XLA Ops:
  0.6 8.9 %collective-permute-start = (bf16[128,256]{1,0:T(8,128)(2,1)}, bf16[128,256]{1,0:T(8,128)(2,1)S(1)}, u32[]{:S(2)}, u32[]{:S(2)}) collective-permute-start(bf16[128,256]{1,0:T(8,128)(2,1)} %param.5), channel_id=1, source_target_pairs={{0,8},{8,0},{1,9},{9,1},{2,10},{10,2},{3,11},{11,3},{4,12},{12,4},... | collective-permute-start | bytes 196616 | tf_op jit(solution)/shard_map/ppermute | solution.py:30
  9.6 0.8 constant_dynamic-update-slice_fusion.1
  10.7 1.9 %collective-permute-start.1 = (bf16[256,256]{1,0:T(8,128)(2,1)S(1)}, bf16[256,256]{1,0:T(8,128)(2,1)S(1)}, u32[]{:S(2)}, u32[]{:S(2)}) collective-permute-start(bf16[256,256]{1,0:T(8,128)(2,1)S(1)} %get-tuple-element.24), channel_id=1, source_target_pairs={{0,16},{16,0},{1,17},{17,1},{2,18},{18,2},{3,19},{19,3},{4,20},{20... | collective-permute-start | bytes 393224 | tf_op jit(solution)/shard_map/ppermute | solution.py:30
  12.6 1.9 %collective-permute-start.2 = (bf16[256,256]{1,0:T(8,128)(2,1)S(1)}, bf16[256,256]{1,0:T(8,128)(2,1)S(1)}, u32[]{:S(2)}, u32[]{:S(2)}) collective-permute-start(bf16[256,256]{1,0:T(8,128)(2,1)S(1)} %get-tuple-element.24), channel_id=1, source_target_pairs={{0,64},{64,0},{1,65},{65,1},{2,66},{66,2},{3,67},{67,3},{4,68},{68... | collective-permute-start | bytes 393224 | tf_op jit(solution)/shard_map/ppermute | solution.py:30
  15.2 11.9 %all-to-all-start = ((bf16[4,32,256]{2,1,0:T(8,128)(2,1)}), bf16[4,32,256]{2,1,0:T(8,128)(2,1)S(1)}, u32[]{:S(2)}, u32[]{:S(2)}) async-start(bf16[4,32,256]{2,1,0:T(8,128)(2,1)} %broadcast_in_dim.14), calls=%async_computation | async-start | bytes 131072 | tf_op jit(solution)/shard_map/all_to_all | solution.py:26
  27.1 3.0 %collective-permute-start.3 = (bf16[256,256]{1,0:T(8,128)(2,1)S(1)}, bf16[256,256]{1,0:T(8,128)(2,1)S(1)}, u32[]{:S(2)}, u32[]{:S(2)}) collective-permute-start(bf16[256,256]{1,0:T(8,128)(2,1)S(1)} %get-tuple-element.24), channel_id=1, source_target_pairs={{0,80},{16,64},{64,16},{80,0},{1,81},{17,65},{65,17},{81,1},{2,82}... | collective-permute-start | bytes 393224 | tf_op jit(solution)/shard_map/ppermute | solution.py:195
  30.1 10.0 %collective-permute-done.3 = bf16[256,256]{1,0:T(8,128)(2,1)S(1)} collective-permute-done((bf16[256,256]{1,0:T(8,128)(2,1)S(1)}, bf16[256,256]{1,0:T(8,128)(2,1)S(1)}, u32[]{:S(2)}, u32[]{:S(2)}) %collective-permute-start.3) | collective-permute-done | bytes 131104 | tf_op jit(solution)/shard_map/ppermute | solution.py:195
  40.1 1.9 %collective-permute-start.4 = (bf16[1024,256]{1,0:T(8,128)(2,1)S(1)}, bf16[1024,256]{1,0:T(8,128)(2,1)S(1)}, u32[]{:S(2)}, u32[]{:S(2)}) collective-permute-start(bf16[1024,256]{1,0:T(8,128)(2,1)S(1)} %constant_dynamic-update-slice_fusion.2.refs_0_), channel_id=1, source_target_pairs={{0,32},{32,0},{1,33},{33,1},{2,34},{34,2},{3,35},{35,3},{4,36},{36... | collective-permute-start | bytes 1572872 | tf_op jit(solution)/shard_map/ppermute | solution.py:30
  42.9 6.3 %all-to-all-start.1 = ((bf16[8,128,256]{2,1,0:T(8,128)(2,1)}), bf16[8,128,256]{2,1,0:T(8,128)(2,1)S(1)}, u32[]{:S(2)}, u32[]{:S(2)}) async-start(bf16[8,128,256]{2,1,0:T(8,128)(2,1)} %broadcast_in_dim.15), calls=%async_computation.1 | async-start | bytes 1048576 | tf_op jit(solution)/shard_map/all_to_all | solution.py:26
  49.9 4.1 %shard_map.84.col_ref = s32[1,2048]{1,0:T(1,128)S(1)} custom-call(s32[1]{0:T(128)} %bitcast.me_ref, s32[16,128]{1,0:T(8,128)S(1)} %bitcast.17, s32[512,128]{1,0:T(8,128)S(1)} %bitcast.16), custom_call_target="tpu_custom_call" | custom-call | flops 25165824 | bytes 524288 | tf_op jit(solution)/shard_map/pallas_call | solution.py:185
  54.1 3.8 %all-to-all-done.1.cold_ref = bf16[8,128,256]{2,1,0:T(8,128)(2,1)S(1)} async-done(((bf16[8,128,256]{2,1,0:T(8,128)(2,1)}), bf16[8,128,256]{2,1,0:T(8,128)(2,1)S(1)}, u32[]{:S(2)}, u32[]{:S(2)}) %all-to-all-start.1) | async-done | bytes 524320 | tf_op jit(solution)/shard_map/all_to_all | solution.py:26
  57.8 4.2 %shard_map.85 = f32[2,2048]{1,0:T(2,128)S(1)} custom-call(s32[1]{0:T(128)} %bitcast.me_ref, bf16[8,128,256]{2,1,0:T(8,128)(2,1)S(1)} %all-to-all-done.1.cold_ref, bf16[8,16,256]{2,1,0:T(8,128)(2,1)S(1)} %dynamic-slice_bitcast_fusion.hot_ref, s32[1,2048]{1,0:T(1,128)S(1)} %shard_map.84.col_ref, ...), custom_call_target="tpu_custom_call" | custom-call | tf_op jit(solution)/shard_map/pallas_call | solution.py:205
  62.1 16.6 %all_to_all.35.stats_ref = f32[16,2,2048]{2,1,0:T(2,128)S(1)} all-to-all(f32[16,2,2048]{2,1,0:T(2,128)S(1)} %broadcast_in_dim.16), channel_id=1, replica_groups=mesh['z8'=2,'z4'=2,'z2'=2,'z1'=2,'yl'=2,'c'=2,'x2'=2,'x1'=2,'yh'=2] {'z1..., dimensions={0} | all-to-all | bytes 524288 | tf_op jit(solution)/shard_map/all_to_all | solution.py:26
  78.7 6.9 %shard_map.86 = (f32[1024,256]{1,0:T(8,128)S(1)}, bf16[1024,256]{1,0:T(8,128)(2,1)S(1)}, bf16[8,144,256]{2,1,0:T(8,128)(2,1)}, f32[1,128]{1,0:T(1,128)}) custom-call(s32[1]{0:T(128)} %bitcast.me_ref, bf16[8,128,256]{2,1,0:T(8,128)(2,1)S(1)} %all-to-all-done.1.cold_ref, bf16[8,16,256]{2,1,0:T(8,128)(2,1)S(1)} %dynamic-slice_bitcast_fusion.hot_ref, ...), custom_call_target="tpu_custom_call" | custom-call | tf_op jit(solution)/shard_map/pallas_call | solution.py:212
  85.7 1.0 copy-done.1
  86.6 2.4 %collective-permute-start.5 = (bf16[1024,256]{1,0:T(8,128)(2,1)S(1)}, bf16[1024,256]{1,0:T(8,128)(2,1)}, u32[]{:S(2)}, u32[]{:S(2)}) collective-permute-start(bf16[1024,256]{1,0:T(8,128)(2,1)S(1)} %get-tuple-element.18), channel_id=1, source_target_pairs={{0,8},{8,0},{1,9},{9,1},{2,10},{10,2},{3,11},{11,3},{4,12},{12,4},... | collective-permute-start | bytes 1572872 | tf_op jit(solution)/shard_map/ppermute | solution.py:30
  89.1 4.2 %all-to-all-start.3 = ((bf16[8,144,256]{2,1,0:T(8,128)(2,1)}), bf16[8,144,256]{2,1,0:T(8,128)(2,1)}, u32[]{:S(2)}, u32[]{:S(2)}) async-start(bf16[8,144,256]{2,1,0:T(8,128)(2,1)} %get-tuple-element.16), calls=%async_computation.3 | async-start | bytes 1179648 | tf_op jit(solution)/shard_map/all_to_all | solution.py:225
  93.3 1.1 convert_add_fusion
  94.5 2.7 %collective-permute-start.6 = (bf16[512,256]{1,0:T(8,128)(2,1)S(1)}, bf16[512,256]{1,0:T(8,128)(2,1)S(1)}, u32[]{:S(2)}, u32[]{:S(2)}) collective-permute-start(bf16[512,256]{1,0:T(8,128)(2,1)S(1)} %slice.59), channel_id=1, source_target_pairs={{0,32},{32,0},{1,33},{33,1},{2,34},{34,2},{3,35},{35,3},{4,36},{36... | collective-permute-start | bytes 786440 | tf_op jit(solution)/shard_map/ppermute | solution.py:30
  97.2 7.2 %all-to-all-done.3 = bf16[8,144,256]{2,1,0:T(8,128)(2,1)} async-done(((bf16[8,144,256]{2,1,0:T(8,128)(2,1)}), bf16[8,144,256]{2,1,0:T(8,128)(2,1)}, u32[]{:S(2)}, u32[]{:S(2)}) %all-to-all-start.3) | async-done | bytes 589856 | tf_op jit(solution)/shard_map/all_to_all | solution.py:225
  104.4 1.1 reduce_sum.24
  105.6 22.2 %all_to_all.36 = bf16[4,48,256]{2,1,0:T(8,128)(2,1)S(1)} all-to-all(bf16[4,48,256]{2,1,0:T(8,128)(2,1)S(1)} %pad_maximum_fusion), channel_id=1, replica_groups=mesh['z8'=2,'z4'=2,'z2'=2,'z1'=2,'yl'=2,'c'=2,'x2'=2,'x1'=2,'yh'=2] {'z8..., dimensions={0} | all-to-all | bytes 196608 | tf_op jit(solution)/shard_map/all_to_all | solution.py:232
  128.5 3.4 %all-to-all-start.5 = ((bf16[8,16,256]{2,1,0:T(8,128)(2,1)}), bf16[8,16,256]{2,1,0:T(8,128)(2,1)S(1)}, u32[]{:S(2)}, u32[]{:S(2)}) async-start(bf16[8,16,256]{2,1,0:T(8,128)(2,1)} %broadcast_in_dim.18), calls=%async_computation.5 | async-start | bytes 131072 | tf_op jit(solution)/shard_map/all_to_all | solution.py:26
  131.9 4.2 %collective-permute-start.7 = (bf16[256,256]{1,0:T(8,128)(2,1)S(1)}, bf16[256,256]{1,0:T(8,128)(2,1)S(1)}, u32[]{:S(2)}, u32[]{:S(2)}) collective-permute-start(bf16[256,256]{1,0:T(8,128)(2,1)S(1)} %slice.60), channel_id=1, source_target_pairs={{0,64},{64,0},{1,65},{65,1},{2,66},{66,2},{3,67},{67,3},{4,68},{68... | collective-permute-start | bytes 393224 | tf_op jit(solution)/shard_map/ppermute | solution.py:30
  136.1 1.5 all-to-all-done.5
  138.4 6.2 %all-to-all-start.6 = ((bf16[8,128,256]{2,1,0:T(8,128)(2,1)}), bf16[8,128,256]{2,1,0:T(8,128)(2,1)S(1)}, u32[]{:S(2)}, u32[]{:S(2)}) async-start(bf16[8,128,256]{2,1,0:T(8,128)(2,1)} %broadcast_in_dim.20), calls=%async_computation.6 | async-start | bytes 1048576 | tf_op jit(solution)/shard_map/all_to_all | solution.py:26
  144.6 1.9 %collective-permute-start.8 = (bf16[128,256]{1,0:T(8,128)(2,1)S(1)}, bf16[128,256]{1,0:T(8,128)(2,1)S(1)}, u32[]{:S(2)}, u32[]{:S(2)}) collective-permute-start(bf16[128,256]{1,0:T(8,128)(2,1)S(1)} %slice.61), channel_id=1, source_target_pairs={{0,16},{16,0},{1,17},{17,1},{2,18},{18,2},{3,19},{19,3},{4,20},{20... | collective-permute-start | bytes 196616 | tf_op jit(solution)/shard_map/ppermute | solution.py:30
  146.5 3.9 %collective-permute-done.8 = bf16[128,256]{1,0:T(8,128)(2,1)S(1)} collective-permute-done((bf16[128,256]{1,0:T(8,128)(2,1)S(1)}, bf16[128,256]{1,0:T(8,128)(2,1)S(1)}, u32[]{:S(2)}, u32[]{:S(2)}) %collective-permute-start.8) | collective-permute-done | bytes 65568 | tf_op jit(solution)/shard_map/ppermute | solution.py:30
  151.1 2.1 %all-to-all-done.6 = bf16[8,128,256]{2,1,0:T(8,128)(2,1)S(1)} async-done(((bf16[8,128,256]{2,1,0:T(8,128)(2,1)}), bf16[8,128,256]{2,1,0:T(8,128)(2,1)S(1)}, u32[]{:S(2)}, u32[]{:S(2)}) %all-to-all-start.6) | async-done | bytes 524320 | tf_op jit(solution)/shard_map/all_to_all | solution.py:26
  153.2 8.0 %collective-permute-start.9 = (bf16[1024,256]{1,0:T(8,128)(2,1)S(1)}, bf16[1024,256]{1,0:T(8,128)(2,1)S(1)}, u32[]{:S(2)}, u32[]{:S(2)}) collective-permute-start(bf16[1024,256]{1,0:T(8,128)(2,1)S(1)} %bitcast.14), channel_id=1, source_target_pairs={{0,8},{8,0},{1,9},{9,1},{2,10},{10,2},{3,11},{11,3},{4,12},{12,4},... | collective-permute-start | bytes 1572872 | tf_op jit(solution)/shard_map/ppermute | solution.py:30
  161.8 0.9 collective-permute-done.9.other_ref
  162.7 1.0 shard_map.87
  (42 shorter events, 5.5 us)
Async XLA Ops:
  0.6 53.4 %copy-start = (bf16[2048,256]{1,0:T(8,128)(2,1)S(1)}, bf16[2048,256]{1,0:T(8,128)(2,1)}, u32[]{:S(2)}) copy-start(bf16[2048,256]{1,0:T(8,128)(2,1)} %param.6) | copy-start | bytes 3145732
  0.6 10.0 %collective-permute-start = (bf16[128,256]{1,0:T(8,128)(2,1)}, bf16[128,256]{1,0:T(8,128)(2,1)S(1)}, u32[]{:S(2)}, u32[]{:S(2)}) collective-permute-start(bf16[128,256]{1,0:T(8,128)(2,1)} %param.5), channel_id=1, source_target_pairs={{0,8},{8,0},{1,9},{9,1},{2,10},{10,2},{3,11},{11,3},{4,12},{12,4},... | collective-permute-start | bytes 196616 | tf_op jit(solution)/shard_map/ppermute | solution.py:30
  10.7 3.9 %copy-start.5 = (bf16[32,256]{1,0:T(8,128)(2,1)S(1)}, bf16[32,256]{1,0:T(8,128)(2,1)}, u32[]{:S(2)}) copy-start(bf16[32,256]{1,0:T(8,128)(2,1)} %param.7) | copy-start | bytes 49156
  10.7 19.4 %collective-permute-start.1 = (bf16[256,256]{1,0:T(8,128)(2,1)S(1)}, bf16[256,256]{1,0:T(8,128)(2,1)S(1)}, u32[]{:S(2)}, u32[]{:S(2)}) collective-permute-start(bf16[256,256]{1,0:T(8,128)(2,1)S(1)} %get-tuple-element.24), channel_id=1, source_target_pairs={{0,16},{16,0},{1,17},{17,1},{2,18},{18,2},{3,19},{19,3},{4,20},{20... | collective-permute-start | bytes 393224 | tf_op jit(solution)/shard_map/ppermute | solution.py:30
  12.6 17.5 %collective-permute-start.2 = (bf16[256,256]{1,0:T(8,128)(2,1)S(1)}, bf16[256,256]{1,0:T(8,128)(2,1)S(1)}, u32[]{:S(2)}, u32[]{:S(2)}) collective-permute-start(bf16[256,256]{1,0:T(8,128)(2,1)S(1)} %get-tuple-element.24), channel_id=1, source_target_pairs={{0,64},{64,0},{1,65},{65,1},{2,66},{66,2},{3,67},{67,3},{4,68},{68... | collective-permute-start | bytes 393224 | tf_op jit(solution)/shard_map/ppermute | solution.py:30
  15.2 24.9 %all-to-all-start = ((bf16[4,32,256]{2,1,0:T(8,128)(2,1)}), bf16[4,32,256]{2,1,0:T(8,128)(2,1)S(1)}, u32[]{:S(2)}, u32[]{:S(2)}) async-start(bf16[4,32,256]{2,1,0:T(8,128)(2,1)} %broadcast_in_dim.14), calls=%async_computation | async-start | bytes 131072 | tf_op jit(solution)/shard_map/all_to_all | solution.py:26
  27.1 13.0 %collective-permute-start.3 = (bf16[256,256]{1,0:T(8,128)(2,1)S(1)}, bf16[256,256]{1,0:T(8,128)(2,1)S(1)}, u32[]{:S(2)}, u32[]{:S(2)}) collective-permute-start(bf16[256,256]{1,0:T(8,128)(2,1)S(1)} %get-tuple-element.24), channel_id=1, source_target_pairs={{0,80},{16,64},{64,16},{80,0},{1,81},{17,65},{65,17},{81,1},{2,82}... | collective-permute-start | bytes 393224 | tf_op jit(solution)/shard_map/ppermute | solution.py:195
  40.1 17.7 %collective-permute-start.4 = (bf16[1024,256]{1,0:T(8,128)(2,1)S(1)}, bf16[1024,256]{1,0:T(8,128)(2,1)S(1)}, u32[]{:S(2)}, u32[]{:S(2)}) collective-permute-start(bf16[1024,256]{1,0:T(8,128)(2,1)S(1)} %constant_dynamic-update-slice_fusion.2.refs_0_), channel_id=1, source_target_pairs={{0,32},{32,0},{1,33},{33,1},{2,34},{34,2},{3,35},{35,3},{4,36},{36... | collective-permute-start | bytes 1572872 | tf_op jit(solution)/shard_map/ppermute | solution.py:30
  42.9 6.3 %copy-start.3 = (s32[65536]{0:T(1024)S(1)}, s32[65536]{0:T(1024)}, u32[]{:S(2)}) copy-start(s32[65536]{0:T(1024)} %param.9) | copy-start | bytes 786436
  42.9 15.0 %all-to-all-start.1 = ((bf16[8,128,256]{2,1,0:T(8,128)(2,1)}), bf16[8,128,256]{2,1,0:T(8,128)(2,1)S(1)}, u32[]{:S(2)}, u32[]{:S(2)}) async-start(bf16[8,128,256]{2,1,0:T(8,128)(2,1)} %broadcast_in_dim.15), calls=%async_computation.1 | async-start | bytes 1048576 | tf_op jit(solution)/shard_map/all_to_all | solution.py:26
  49.2 0.7 copy-start.4
  85.7 1.0 copy-start.1
  86.6 6.7 %copy-start.2 = (f32[1024,256]{1,0:T(8,128)S(1)}, f32[1024,256]{1,0:T(8,128)}, u32[]{:S(2)}) copy-start(f32[1024,256]{1,0:T(8,128)} %copy-done.1) | copy-start | bytes 3145732
  86.6 6.7 %collective-permute-start.5 = (bf16[1024,256]{1,0:T(8,128)(2,1)S(1)}, bf16[1024,256]{1,0:T(8,128)(2,1)}, u32[]{:S(2)}, u32[]{:S(2)}) collective-permute-start(bf16[1024,256]{1,0:T(8,128)(2,1)S(1)} %get-tuple-element.18), channel_id=1, source_target_pairs={{0,8},{8,0},{1,9},{9,1},{2,10},{10,2},{3,11},{11,3},{4,12},{12,4},... | collective-permute-start | bytes 1572872 | tf_op jit(solution)/shard_map/ppermute | solution.py:30
  89.1 15.3 %all-to-all-start.3 = ((bf16[8,144,256]{2,1,0:T(8,128)(2,1)}), bf16[8,144,256]{2,1,0:T(8,128)(2,1)}, u32[]{:S(2)}, u32[]{:S(2)}) async-start(bf16[8,144,256]{2,1,0:T(8,128)(2,1)} %get-tuple-element.16), calls=%async_computation.3 | async-start | bytes 1179648 | tf_op jit(solution)/shard_map/all_to_all | solution.py:225
  94.5 9.9 %collective-permute-start.6 = (bf16[512,256]{1,0:T(8,128)(2,1)S(1)}, bf16[512,256]{1,0:T(8,128)(2,1)S(1)}, u32[]{:S(2)}, u32[]{:S(2)}) collective-permute-start(bf16[512,256]{1,0:T(8,128)(2,1)S(1)} %slice.59), channel_id=1, source_target_pairs={{0,32},{32,0},{1,33},{33,1},{2,34},{34,2},{3,35},{35,3},{4,36},{36... | collective-permute-start | bytes 786440 | tf_op jit(solution)/shard_map/ppermute | solution.py:30
  128.5 9.1 %all-to-all-start.5 = ((bf16[8,16,256]{2,1,0:T(8,128)(2,1)}), bf16[8,16,256]{2,1,0:T(8,128)(2,1)S(1)}, u32[]{:S(2)}, u32[]{:S(2)}) async-start(bf16[8,16,256]{2,1,0:T(8,128)(2,1)} %broadcast_in_dim.18), calls=%async_computation.5 | async-start | bytes 131072 | tf_op jit(solution)/shard_map/all_to_all | solution.py:26
  131.9 12.6 %collective-permute-start.7 = (bf16[256,256]{1,0:T(8,128)(2,1)S(1)}, bf16[256,256]{1,0:T(8,128)(2,1)S(1)}, u32[]{:S(2)}, u32[]{:S(2)}) collective-permute-start(bf16[256,256]{1,0:T(8,128)(2,1)S(1)} %slice.60), channel_id=1, source_target_pairs={{0,64},{64,0},{1,65},{65,1},{2,66},{66,2},{3,67},{67,3},{4,68},{68... | collective-permute-start | bytes 393224 | tf_op jit(solution)/shard_map/ppermute | solution.py:30
  138.4 14.8 %all-to-all-start.6 = ((bf16[8,128,256]{2,1,0:T(8,128)(2,1)}), bf16[8,128,256]{2,1,0:T(8,128)(2,1)S(1)}, u32[]{:S(2)}, u32[]{:S(2)}) async-start(bf16[8,128,256]{2,1,0:T(8,128)(2,1)} %broadcast_in_dim.20), calls=%async_computation.6 | async-start | bytes 1048576 | tf_op jit(solution)/shard_map/all_to_all | solution.py:26
  144.6 5.8 %collective-permute-start.8 = (bf16[128,256]{1,0:T(8,128)(2,1)S(1)}, bf16[128,256]{1,0:T(8,128)(2,1)S(1)}, u32[]{:S(2)}, u32[]{:S(2)}) collective-permute-start(bf16[128,256]{1,0:T(8,128)(2,1)S(1)} %slice.61), channel_id=1, source_target_pairs={{0,16},{16,0},{1,17},{17,1},{2,18},{18,2},{3,19},{19,3},{4,20},{20... | collective-permute-start | bytes 196616 | tf_op jit(solution)/shard_map/ppermute | solution.py:30
  153.2 9.5 %collective-permute-start.9 = (bf16[1024,256]{1,0:T(8,128)(2,1)S(1)}, bf16[1024,256]{1,0:T(8,128)(2,1)S(1)}, u32[]{:S(2)}, u32[]{:S(2)}) collective-permute-start(bf16[1024,256]{1,0:T(8,128)(2,1)S(1)} %bitcast.14), channel_id=1, source_target_pairs={{0,8},{8,0},{1,9},{9,1},{2,10},{10,2},{3,11},{11,3},{4,12},{12,4},... | collective-permute-start | bytes 1572872 | tf_op jit(solution)/shard_map/ppermute | solution.py:30

commit v5 on v4

--- a/solution.py
+++ b/solution.py
@@ -9,9 +9,9 @@
 from jax.sharding import PartitionSpec as P
 
 AXES = ("z8", "z4", "z2", "z1", "yl", "c", "x2", "x1", "yh")
-COLS = ("z1", "z2", "yl", "c")
-HALF = ("z1", "z2", "yl")
-NEAR = ("x2", "x1", "yh")
+COLS = ("c", "z1", "z2")
+HALF = ("z1", "z2")
+NEAR = ("yl", "x2", "x1", "yh")
 FAR = ("z8", "z4")
 NC, NG, NF = 2 ** len(COLS), 2 ** len(NEAR), 2 ** len(FAR)
 BF = jnp.bfloat16
@@ -74,8 +74,8 @@
     near = pick(block, NEAR)
     cold_col = near // near_chunk * width + (near % near_chunk) * (NF * shard)
     cold_col += pick(block, FAR) * shard + (row & (shard - 1))
-    hot_near = (slot >> 7) & (NG - 1)
-    hot_k = (((slot >> 4) & 7) << 1) | (slot >> 10)
+    hot_near = (slot >> 6) & (NG - 1)
+    hot_k = ((slot >> 10) << 2) | ((slot >> 4) & 3)
     hot_col = hot_near // near_chunk * width + near_chunk * NF * shard
     hot_col += (hot_near % near_chunk) * hot_own + (slot & (hot_own - 1))
     column = jnp.where(is_hot, hot_col, cold_col)
@@ -150,10 +150,9 @@
         return carry
 
     lax.fori_loop(0, CHUNKS, step, 0)
-    for j in range(NC // 2):
-        out = slice(j * 128, (j + 1) * 128)
-        keep_ref[out] = acc_ref[:, 2 * j * 128 : (2 * j + 1) * 128].T
-        send_ref[out] = acc_ref[:, (2 * j + 1) * 128 : (2 * j + 2) * 128].T.astype(BF)
+    half = acc_ref.shape[1] // 2
+    keep_ref[...] = acc_ref[:, :half].T
+    send_ref[...] = acc_ref[:, half:].T.astype(BF)
 
 
 def place_kernel(me_ref, own_ref, other_ref, out_ref, sems):
@@ -190,16 +189,15 @@
         compiler_params=params,
     )(at_me, hot_ids.reshape(-1, 128), targets.reshape(-1, own))
 
-    pair = jnp.concatenate([queries, swap(queries, "c")], axis=0)
-    rows = [pair, swap(pair, "yl"), swap(pair, "z2")]
-    rows.append(lax.ppermute(pair, ("z2", "yl"), [(i, 3 - i) for i in range(4)]))
+    rows = [queries, swap(queries, "z2")]
 
     far = spread(cold_table, FAR).reshape(NF * shard, width)
-    far, rows = lax.optimization_barrier((far, jnp.concatenate(rows, axis=0)))
+    far, rows[1], column = lax.optimization_barrier((far, rows[1], column))
     cold = spread(far, NEAR)
-    rows = [rows, swap(rows, "z1")]
+    for a in ("z1", "c"):
+        rows.append(swap(jnp.concatenate(rows, axis=0), a))
     mine = hot_table.reshape(2, NG, NC // 2, hot_own, width)
-    mine = lax.dynamic_slice(mine, (k & 1, 0, k >> 1, 0, 0), (1, NG, 1, hot_own, width))
+    mine = lax.dynamic_slice(mine, (k >> 2, 0, k & 3, 0, 0), (1, NG, 1, hot_own, width))
     mine = mine.reshape(NG, hot_own, width)
 
     stats = pl.pallas_call(
@@ -233,7 +231,7 @@
     far = jnp.sum(far.astype(F32), axis=0).astype(BF)
     grad_cold = far[:shard]
     keep = keep[: count // 4] + other.astype(F32)
-    for a in ("z2", "yl"):
+    for a in ("z2",):
         half = keep.shape[0] // 2
         keep = keep[:half] + swap(keep[half:].astype(BF), a).astype(F32)
     grad_hot = spread(far[shard:], HALF).reshape(-1, width)

time: 165 us -> 149 us (0.903)
  starting transfers between devices: 68.8 us -> 55.6 us
  waiting for transfers between devices: 29.6 us -> 34.3 us
  Pallas kernels: 16.2 us -> 13.6 us
  other arithmetic: 3.05 us -> 0.96 us
    ppermute x9 -> x7, waiting for transfers between devices: 5.01 us -> 16.9 us  [swap(): return lax.ppermute(x, axis, [(0, 1), (1, 0)])]
    ppermute x9 -> x7, starting transfers between devices: 33.9 us -> 23.8 us  [swap(): return lax.ppermute(x, axis, [(0, 1), (1, 0)])]
    ppermute x1 -> x0, waiting for transfers between devices: 10 us -> none  [body(): lax.ppermute(pair, ('z2', 'yl'), [(i, 3 - i) for i in range(4)])]
    all_to_all x1, blocking collectives: 22.2 us -> 17.8 us  [body(): lax.all_to_all(jnp.concatenate([cold_part, hot_part], axis=1), FAR, 0, 0)]
    all_to_all x1 -> x2, blocking collectives: 16.6 us -> 19.6 us  [spread(): return lax.all_to_all(jnp.broadcast_to(x[None], (n, *x.shape)), axes, 0, 0)]
    ppermute x1 -> x0, starting transfers between devices: 2.95 us -> none  [body(): lax.ppermute(pair, ('z2', 'yl'), [(i, 3 - i) for i in range(4)])]
    pallas_call x1, Pallas kernels: 4.13 us -> 2.07 us  [body(): pl.pallas_call(decode_kernel, out_shape=jax.ShapeDtypeStruct((1, count),...]
    all_to_all x4 -> x3, waiting for transfers between devices: 7.37 us -> 8.84 us  [spread(): return lax.all_to_all(jnp.broadcast_to(x[None], (n, *x.shape)), axes, 0, 0)]
  transfers between devices with their start and end apart: 15 -> 11, of which waited for: 8 -> 11; matrix products, arithmetic and copies ran while one was open for 3% -> 1% of each run, Pallas kernels for 3% -> 1%
where the time goes in v5:
time: 149 us; the launch traced here: 148 us
  starting transfers between devices  55.6 us (37%)
  blocking collectives  37.4 us (25%)
  waiting for transfers between devices  34.3 us (23%)
  Pallas kernels  13.6 us (9%)
  local copies, waits for them, and re-layouts  5.71 us (4%)
    all_to_all x3, starting transfers between devices, spread(): return lax.all_to_all(jnp.broadcast_to(x[None], (n, *x.shape)), axes, 0, 0)  28 us
    ppermute x7, starting transfers between devices, swap(): return lax.ppermute(x, axis, [(0, 1), (1, 0)])  23.8 us
    all_to_all x2, blocking collectives, spread(): return lax.all_to_all(jnp.broadcast_to(x[None], (n, *x.shape)), axes, 0, 0)  19.6 us
    all_to_all x1, blocking collectives, body(): lax.all_to_all(jnp.concatenate([cold_part, hot_part], axis=1), FAR, 0, 0)  17.8 us
    ppermute x7, waiting for transfers between devices, swap(): return lax.ppermute(x, axis, [(0, 1), (1, 0)])  16.9 us
    all_to_all x3, waiting for transfers between devices, spread(): return lax.all_to_all(jnp.broadcast_to(x[None], (n, *x.shape)), axes, 0, 0)  8.84 us
    all_to_all x1, waiting for transfers between devices, body(): near = lax.all_to_all(item_part, NEAR, 0, 0)  8.6 us
    pallas_call x1, Pallas kernels, body(): pl.pallas_call(grads_kernel, out_shape=(jax.ShapeDtypeStruct((count // 2,...  6.29 us
  transfers between devices with their start and end apart: 11, of which 11 were waited for; matrix products, arithmetic and copies ran while one was open for 1% of the time, Pallas kernels for 1%

profile of v5, /device:TPU:1, one launch (start us, length us, event | category | flops | bytes accessed | tf_op | source)
XLA Modules:
  0.0 148.4 jit_solution(3737830988279753785)
XLA Ops:
  0.6 1.4 broadcast_in_dim.14
  2.1 15.6 %all-to-all-start = ((bf16[4,32,256]{2,1,0:T(8,128)(2,1)}), bf16[4,32,256]{2,1,0:T(8,128)(2,1)S(1)}, u32[]{:S(2)}, u32[]{:S(2)}) async-start(bf16[4,32,256]{2,1,0:T(8,128)(2,1)} %broadcast_in_dim.14), calls=%async_computation | async-start | bytes 131072 | tf_op jit(solution)/shard_map/all_to_all | solution.py:26
  17.7 3.1 %collective-permute-start = (bf16[128,256]{1,0:T(8,128)(2,1)}, bf16[128,256]{1,0:T(8,128)(2,1)S(1)}, u32[]{:S(2)}, u32[]{:S(2)}) collective-permute-start(bf16[128,256]{1,0:T(8,128)(2,1)} %refs_0_.3), channel_id=1, source_target_pairs={{0,64},{64,0},{1,65},{65,1},{2,66},{66,2},{3,67},{67,3},{4,68},{68... | collective-permute-start | bytes 196616 | tf_op jit(solution)/shard_map/ppermute | solution.py:30
  20.9 0.9 copy-done.2
  22.5 2.1 %shard_map.84.col_ref = s32[1,1024]{1,0:T(1,128)S(1)} custom-call(s32[1]{0:T(128)} %bitcast.me_ref, s32[16,128]{1,0:T(8,128)S(1)} %bitcast.17, s32[512,128]{1,0:T(8,128)S(1)} %bitcast.16), custom_call_target="tpu_custom_call" | custom-call | flops 12582912 | bytes 524288 | tf_op jit(solution)/shard_map/pallas_call | solution.py:184
  24.6 1.0 collective-permute-done.refs_1_
  25.5 4.7 %all-to-all-done = bf16[4,32,256]{2,1,0:T(8,128)(2,1)S(1)} async-done(((bf16[4,32,256]{2,1,0:T(8,128)(2,1)}), bf16[4,32,256]{2,1,0:T(8,128)(2,1)S(1)}, u32[]{:S(2)}, u32[]{:S(2)}) %all-to-all-start) | async-done | bytes 65568 | tf_op jit(solution)/shard_map/all_to_all | solution.py:26
  30.2 1.1 broadcast_in_dim.15
  31.3 6.9 %all-to-all-start.1 = ((bf16[16,128,256]{2,1,0:T(8,128)(2,1)}), bf16[16,128,256]{2,1,0:T(8,128)(2,1)S(1)}, u32[]{:S(2)}, u32[]{:S(2)}) async-start(bf16[16,128,256]{2,1,0:T(8,128)(2,1)} %broadcast_in_dim.15), calls=%async_computation.1 | async-start | bytes 2097152 | tf_op jit(solution)/shard_map/all_to_all | solution.py:26
  38.2 2.2 %collective-permute-start.1 = (bf16[256,256]{1,0:T(8,128)(2,1)S(1)}, bf16[256,256]{1,0:T(8,128)(2,1)S(1)}, u32[]{:S(2)}, u32[]{:S(2)}) collective-permute-start(bf16[256,256]{1,0:T(8,128)(2,1)S(1)} %pad_maximum_fusion.1), channel_id=1, source_target_pairs={{0,32},{32,0},{1,33},{33,1},{2,34},{34,2},{3,35},{35,3},{4,36},{36... | collective-permute-start | bytes 393224 | tf_op jit(solution)/shard_map/ppermute | solution.py:30
  40.4 3.8 %collective-permute-done.1.refs_2_ = bf16[256,256]{1,0:T(8,128)(2,1)S(1)} collective-permute-done((bf16[256,256]{1,0:T(8,128)(2,1)S(1)}, bf16[256,256]{1,0:T(8,128)(2,1)S(1)}, u32[]{:S(2)}, u32[]{:S(2)}) %collective-permute-start.1) | collective-permute-done | bytes 131104 | tf_op jit(solution)/shard_map/ppermute | solution.py:30
  44.2 4.6 %collective-permute-start.2 = (bf16[512,256]{1,0:T(8,128)(2,1)S(1)}, bf16[512,256]{1,0:T(8,128)(2,1)S(1)}, u32[]{:S(2)}, u32[]{:S(2)}) collective-permute-start(bf16[512,256]{1,0:T(8,128)(2,1)S(1)} %pad_maximum_fusion), channel_id=1, source_target_pairs={{0,8},{8,0},{1,9},{9,1},{2,10},{10,2},{3,11},{11,3},{4,12},{12,4},... | collective-permute-start | bytes 786440 | tf_op jit(solution)/shard_map/ppermute | solution.py:30
  48.9 1.1 collective-permute-done.2.refs_3_
  50.0 2.6 %all-to-all-done.1.cold_ref = bf16[16,128,256]{2,1,0:T(8,128)(2,1)S(1)} async-done(((bf16[16,128,256]{2,1,0:T(8,128)(2,1)}), bf16[16,128,256]{2,1,0:T(8,128)(2,1)S(1)}, u32[]{:S(2)}, u32[]{:S(2)}) %all-to-all-start.1) | async-done | bytes 1048608 | tf_op jit(solution)/shard_map/all_to_all | solution.py:26
  52.6 4.2 %shard_map.85 = f32[2,1024]{1,0:T(2,128)S(1)} custom-call(s32[1]{0:T(128)} %bitcast.me_ref, bf16[16,128,256]{2,1,0:T(8,128)(2,1)S(1)} %all-to-all-done.1.cold_ref, bf16[16,16,256]{2,1,0:T(8,128)(2,1)S(1)} %dynamic-slice_bitcast_fusion.hot_ref, s32[1,1024]{1,0:T(1,128)S(1)} %shard_map.84.col_ref, bf16[128,256]{1,0:T(8,128)(2,1)S(1)} %copy-done.1, ...), custom_call_target="tpu_custom_call" | custom-call | tf_op jit(solution)/shard_map/pallas_call | solution.py:203
  56.8 12.7 %all_to_all.35.stats_ref = f32[8,2,1024]{2,1,0:T(2,128)S(1)} all-to-all(f32[8,2,1024]{2,1,0:T(2,128)S(1)} %broadcast_in_dim.16), channel_id=1, replica_groups=mesh['z8'=2,'z4'=2,'z2'=2,'z1'=2,'yl'=2,'c'=2,'x2'=2,'x1'=2,'yh'=2] {'c'..., dimensions={0} | all-to-all | bytes 131072 | tf_op jit(solution)/shard_map/all_to_all | solution.py:26
  69.5 6.3 %shard_map.86 = (f32[512,256]{1,0:T(8,128)S(1)}, bf16[512,256]{1,0:T(8,128)(2,1)S(1)}, bf16[16,144,256]{2,1,0:T(8,128)(2,1)}, f32[1,128]{1,0:T(1,128)}) custom-call(s32[1]{0:T(128)} %bitcast.me_ref, bf16[16,128,256]{2,1,0:T(8,128)(2,1)S(1)} %all-to-all-done.1.cold_ref, bf16[16,16,256]{2,1,0:T(8,128)(2,1)S(1)} %dynamic-slice_bitcast_fusion.hot_ref, ...), custom_call_target="tpu_custom_call" | custom-call | tf_op jit(solution)/shard_map/pallas_call | solution.py:210
  75.8 3.8 %all-to-all-start.3 = ((bf16[16,144,256]{2,1,0:T(8,128)(2,1)}), bf16[16,144,256]{2,1,0:T(8,128)(2,1)S(1)}, u32[]{:S(2)}, u32[]{:S(2)}) async-start(bf16[16,144,256]{2,1,0:T(8,128)(2,1)} %get-tuple-element.18), calls=%async_computation.3 | async-start | bytes 2359296 | tf_op jit(solution)/shard_map/all_to_all | solution.py:223
  79.6 2.6 %collective-permute-start.3 = (bf16[512,256]{1,0:T(8,128)(2,1)S(1)}, bf16[512,256]{1,0:T(8,128)(2,1)S(1)}, u32[]{:S(2)}, u32[]{:S(2)}) collective-permute-start(bf16[512,256]{1,0:T(8,128)(2,1)S(1)} %get-tuple-element.20), channel_id=1, source_target_pairs={{0,8},{8,0},{1,9},{9,1},{2,10},{10,2},{3,11},{11,3},{4,12},{12,4},... | collective-permute-start | bytes 786440 | tf_op jit(solution)/shard_map/ppermute | solution.py:30
  82.2 1.1 collective-permute-done.3
  83.5 1.9 %collective-permute-start.4 = (bf16[256,256]{1,0:T(8,128)(2,1)S(1)}, bf16[256,256]{1,0:T(8,128)(2,1)S(1)}, u32[]{:S(2)}, u32[]{:S(2)}) collective-permute-start(bf16[256,256]{1,0:T(8,128)(2,1)S(1)} %slice.46), channel_id=1, source_target_pairs={{0,32},{32,0},{1,33},{33,1},{2,34},{34,2},{3,35},{35,3},{4,36},{36... | collective-permute-start | bytes 393224 | tf_op jit(solution)/shard_map/ppermute | solution.py:30
  85.4 4.7 %collective-permute-done.4 = bf16[256,256]{1,0:T(8,128)(2,1)S(1)} collective-permute-done((bf16[256,256]{1,0:T(8,128)(2,1)S(1)}, bf16[256,256]{1,0:T(8,128)(2,1)S(1)}, u32[]{:S(2)}, u32[]{:S(2)}) %collective-permute-start.4) | collective-permute-done | bytes 131104 | tf_op jit(solution)/shard_map/ppermute | solution.py:30
  90.1 8.6 %all-to-all-done.3 = bf16[16,144,256]{2,1,0:T(8,128)(2,1)S(1)} async-done(((bf16[16,144,256]{2,1,0:T(8,128)(2,1)}), bf16[16,144,256]{2,1,0:T(8,128)(2,1)S(1)}, u32[]{:S(2)}, u32[]{:S(2)}) %all-to-all-start.3) | async-done | bytes 1179680 | tf_op jit(solution)/shard_map/all_to_all | solution.py:223
  98.9 17.8 %all_to_all.36 = bf16[4,48,256]{2,1,0:T(8,128)(2,1)S(1)} all-to-all(bf16[4,48,256]{2,1,0:T(8,128)(2,1)S(1)} %pad_maximum_fusion.2), channel_id=1, replica_groups=mesh['z8'=2,'z4'=2,'z2'=2,'z1'=2,'yl'=2,'c'=2,'x2'=2,'x1'=2,'yh'=2] {'z8..., dimensions={0} | all-to-all | bytes 196608 | tf_op jit(solution)/shard_map/all_to_all | solution.py:230
  116.8 6.9 %all_to_all.37 = bf16[4,16,256]{2,1,0:T(8,128)(2,1)S(1)} all-to-all(bf16[4,16,256]{2,1,0:T(8,128)(2,1)S(1)} %broadcast_in_dim.18), channel_id=1, replica_groups=mesh['z8'=2,'z4'=2,'z2'=2,'z1'=2,'yl'=2,'c'=2,'x2'=2,'x1'=2,'yh'=2] {'z1..., dimensions={0} | all-to-all | bytes 65536 | tf_op jit(solution)/shard_map/all_to_all | solution.py:26
  124.5 5.5 %all-to-all-start.6 = ((bf16[16,64,256]{2,1,0:T(8,128)(2,1)}), bf16[16,64,256]{2,1,0:T(8,128)(2,1)S(1)}, u32[]{:S(2)}, u32[]{:S(2)}) async-start(bf16[16,64,256]{2,1,0:T(8,128)(2,1)} %broadcast_in_dim.20), calls=%async_computation.6 | async-start | bytes 1048576 | tf_op jit(solution)/shard_map/all_to_all | solution.py:26
  130.0 2.4 %collective-permute-start.5 = (bf16[128,256]{1,0:T(8,128)(2,1)S(1)}, bf16[128,256]{1,0:T(8,128)(2,1)S(1)}, u32[]{:S(2)}, u32[]{:S(2)}) collective-permute-start(bf16[128,256]{1,0:T(8,128)(2,1)S(1)} %slice.47), channel_id=1, source_target_pairs={{0,64},{64,0},{1,65},{65,1},{2,66},{66,2},{3,67},{67,3},{4,68},{68... | collective-permute-start | bytes 196616 | tf_op jit(solution)/shard_map/ppermute | solution.py:30
  132.4 4.2 %collective-permute-done.5 = bf16[128,256]{1,0:T(8,128)(2,1)S(1)} collective-permute-done((bf16[128,256]{1,0:T(8,128)(2,1)S(1)}, bf16[128,256]{1,0:T(8,128)(2,1)S(1)}, u32[]{:S(2)}, u32[]{:S(2)}) %collective-permute-start.5) | collective-permute-done | bytes 65568 | tf_op jit(solution)/shard_map/ppermute | solution.py:30
  137.3 1.6 %all-to-all-done.6 = bf16[16,64,256]{2,1,0:T(8,128)(2,1)S(1)} async-done(((bf16[16,64,256]{2,1,0:T(8,128)(2,1)}), bf16[16,64,256]{2,1,0:T(8,128)(2,1)S(1)}, u32[]{:S(2)}, u32[]{:S(2)}) %all-to-all-start.6) | async-done | bytes 524320 | tf_op jit(solution)/shard_map/all_to_all | solution.py:26
  138.9 7.0 %collective-permute-start.6 = (bf16[1024,256]{1,0:T(8,128)(2,1)S(1)}, bf16[1024,256]{1,0:T(8,128)(2,1)S(1)}, u32[]{:S(2)}, u32[]{:S(2)}) collective-permute-start(bf16[1024,256]{1,0:T(8,128)(2,1)S(1)} %bitcast.14), channel_id=1, source_target_pairs={{0,8},{8,0},{1,9},{9,1},{2,10},{10,2},{3,11},{11,3},{4,12},{12,4},... | collective-permute-start | bytes 1572872 | tf_op jit(solution)/shard_map/ppermute | solution.py:30
  146.5 0.9 collective-permute-done.6.other_ref
  147.4 1.0 shard_map.87
  (30 shorter events, 3.2 us)
Async XLA Ops:
  0.6 48.3 %copy-start = (bf16[2048,256]{1,0:T(8,128)(2,1)S(1)}, bf16[2048,256]{1,0:T(8,128)(2,1)}, u32[]{:S(2)}) copy-start(bf16[2048,256]{1,0:T(8,128)(2,1)} %param.6) | copy-start | bytes 3145732
  2.1 28.1 %all-to-all-start = ((bf16[4,32,256]{2,1,0:T(8,128)(2,1)}), bf16[4,32,256]{2,1,0:T(8,128)(2,1)S(1)}, u32[]{:S(2)}, u32[]{:S(2)}) async-start(bf16[4,32,256]{2,1,0:T(8,128)(2,1)} %broadcast_in_dim.14), calls=%async_computation | async-start | bytes 131072 | tf_op jit(solution)/shard_map/all_to_all | solution.py:26
  17.7 7.8 %collective-permute-start = (bf16[128,256]{1,0:T(8,128)(2,1)}, bf16[128,256]{1,0:T(8,128)(2,1)S(1)}, u32[]{:S(2)}, u32[]{:S(2)}) collective-permute-start(bf16[128,256]{1,0:T(8,128)(2,1)} %refs_0_.3), channel_id=1, source_target_pairs={{0,64},{64,0},{1,65},{65,1},{2,66},{66,2},{3,67},{67,3},{4,68},{68... | collective-permute-start | bytes 196616 | tf_op jit(solution)/shard_map/ppermute | solution.py:30
  20.8 1.0 copy-start.2
  21.8 0.7 copy-start.3
  31.3 6.9 %copy-start.1 = (bf16[128,256]{1,0:T(8,128)(2,1)S(1)}, bf16[128,256]{1,0:T(8,128)(2,1)}, u32[]{:S(2)}) copy-start(bf16[128,256]{1,0:T(8,128)(2,1)} %refs_0_.3) | copy-start | bytes 196612
  31.3 21.3 %all-to-all-start.1 = ((bf16[16,128,256]{2,1,0:T(8,128)(2,1)}), bf16[16,128,256]{2,1,0:T(8,128)(2,1)S(1)}, u32[]{:S(2)}, u32[]{:S(2)}) async-start(bf16[16,128,256]{2,1,0:T(8,128)(2,1)} %broadcast_in_dim.15), calls=%async_computation.1 | async-start | bytes 2097152 | tf_op jit(solution)/shard_map/all_to_all | solution.py:26
  38.2 6.0 %collective-permute-start.1 = (bf16[256,256]{1,0:T(8,128)(2,1)S(1)}, bf16[256,256]{1,0:T(8,128)(2,1)S(1)}, u32[]{:S(2)}, u32[]{:S(2)}) collective-permute-start(bf16[256,256]{1,0:T(8,128)(2,1)S(1)} %pad_maximum_fusion.1), channel_id=1, source_target_pairs={{0,32},{32,0},{1,33},{33,1},{2,34},{34,2},{3,35},{35,3},{4,36},{36... | collective-permute-start | bytes 393224 | tf_op jit(solution)/shard_map/ppermute | solution.py:30
  44.2 5.8 %collective-permute-start.2 = (bf16[512,256]{1,0:T(8,128)(2,1)S(1)}, bf16[512,256]{1,0:T(8,128)(2,1)S(1)}, u32[]{:S(2)}, u32[]{:S(2)}) collective-permute-start(bf16[512,256]{1,0:T(8,128)(2,1)S(1)} %pad_maximum_fusion), channel_id=1, source_target_pairs={{0,8},{8,0},{1,9},{9,1},{2,10},{10,2},{3,11},{11,3},{4,12},{12,4},... | collective-permute-start | bytes 786440 | tf_op jit(solution)/shard_map/ppermute | solution.py:30
  75.8 22.9 %all-to-all-start.3 = ((bf16[16,144,256]{2,1,0:T(8,128)(2,1)}), bf16[16,144,256]{2,1,0:T(8,128)(2,1)S(1)}, u32[]{:S(2)}, u32[]{:S(2)}) async-start(bf16[16,144,256]{2,1,0:T(8,128)(2,1)} %get-tuple-element.18), calls=%async_computation.3 | async-start | bytes 2359296 | tf_op jit(solution)/shard_map/all_to_all | solution.py:223
  79.6 3.7 %collective-permute-start.3 = (bf16[512,256]{1,0:T(8,128)(2,1)S(1)}, bf16[512,256]{1,0:T(8,128)(2,1)S(1)}, u32[]{:S(2)}, u32[]{:S(2)}) collective-permute-start(bf16[512,256]{1,0:T(8,128)(2,1)S(1)} %get-tuple-element.20), channel_id=1, source_target_pairs={{0,8},{8,0},{1,9},{9,1},{2,10},{10,2},{3,11},{11,3},{4,12},{12,4},... | collective-permute-start | bytes 786440 | tf_op jit(solution)/shard_map/ppermute | solution.py:30
  83.4 2.0 %copy-start.4 = (f32[512,256]{1,0:T(8,128)}, f32[512,256]{1,0:T(8,128)S(1)}, u32[]{:S(2)}) copy-start(f32[512,256]{1,0:T(8,128)S(1)} %convert_add_fusion) | copy-start | bytes 1572868
  83.5 6.6 %collective-permute-start.4 = (bf16[256,256]{1,0:T(8,128)(2,1)S(1)}, bf16[256,256]{1,0:T(8,128)(2,1)S(1)}, u32[]{:S(2)}, u32[]{:S(2)}) collective-permute-start(bf16[256,256]{1,0:T(8,128)(2,1)S(1)} %slice.46), channel_id=1, source_target_pairs={{0,32},{32,0},{1,33},{33,1},{2,34},{34,2},{3,35},{35,3},{4,36},{36... | collective-permute-start | bytes 393224 | tf_op jit(solution)/shard_map/ppermute | solution.py:30
  98.9 31.1 %copy-start.5 = (f32[512,256]{1,0:T(8,128)S(1)}, f32[512,256]{1,0:T(8,128)}, u32[]{:S(2)}) copy-start(f32[512,256]{1,0:T(8,128)} %copy-done.4) | copy-start | bytes 1572868
  124.5 14.4 %all-to-all-start.6 = ((bf16[16,64,256]{2,1,0:T(8,128)(2,1)}), bf16[16,64,256]{2,1,0:T(8,128)(2,1)S(1)}, u32[]{:S(2)}, u32[]{:S(2)}) async-start(bf16[16,64,256]{2,1,0:T(8,128)(2,1)} %broadcast_in_dim.20), calls=%async_computation.6 | async-start | bytes 1048576 | tf_op jit(solution)/shard_map/all_to_all | solution.py:26
  130.0 6.6 %collective-permute-start.5 = (bf16[128,256]{1,0:T(8,128)(2,1)S(1)}, bf16[128,256]{1,0:T(8,128)(2,1)S(1)}, u32[]{:S(2)}, u32[]{:S(2)}) collective-permute-start(bf16[128,256]{1,0:T(8,128)(2,1)S(1)} %slice.47), channel_id=1, source_target_pairs={{0,64},{64,0},{1,65},{65,1},{2,66},{66,2},{3,67},{67,3},{4,68},{68... | collective-permute-start | bytes 196616 | tf_op jit(solution)/shard_map/ppermute | solution.py:30
  138.9 8.5 %collective-permute-start.6 = (bf16[1024,256]{1,0:T(8,128)(2,1)S(1)}, bf16[1024,256]{1,0:T(8,128)(2,1)S(1)}, u32[]{:S(2)}, u32[]{:S(2)}) collective-permute-start(bf16[1024,256]{1,0:T(8,128)(2,1)S(1)} %bitcast.14), channel_id=1, source_target_pairs={{0,8},{8,0},{1,9},{9,1},{2,10},{10,2},{3,11},{11,3},{4,12},{12,4},... | collective-permute-start | bytes 1572872 | tf_op jit(solution)/shard_map/ppermute | solution.py:30

commit v6 on v5

--- a/solution.py
+++ b/solution.py
@@ -9,8 +9,8 @@
 from jax.sharding import PartitionSpec as P
 
 AXES = ("z8", "z4", "z2", "z1", "yl", "c", "x2", "x1", "yh")
-COLS = ("c", "z1", "z2")
-HALF = ("z1", "z2")
+COLS = ("c", "z2", "z1")
+HALF = ("z2", "z1")
 NEAR = ("yl", "x2", "x1", "yh")
 FAR = ("z8", "z4")
 NC, NG, NF = 2 ** len(COLS), 2 ** len(NEAR), 2 ** len(FAR)
@@ -49,16 +49,22 @@
     return mask
 
 
-def decode_kernel(me_ref, ids_ref, targets_ref, out_ref):
+def decode_kernel(me_ref, ids_ref, targets_ref, out_ref, aim_ref, sems):
     me = me_ref[0]
     k = pick(me, COLS)
     groups, lanes = ids_ref.shape
-    own = targets_ref.shape[1]
+    copies = []
+    for p in range(NC):
+        here = aim_ref.at[:, pl.ds(p * lanes, lanes)]
+        copies.append(pltpu.make_async_copy(targets_ref.at[me ^ flip(p)], here, sems.at[p]))
+        copies[p].start()
     hot_own = groups * lanes // (NC * NG)
     shard = 32
     near_chunk = NG // CHUNKS
     width = near_chunk * (NF * shard + hot_own)
-    aim = jnp.concatenate([targets_ref[pl.ds(me ^ flip(p), 1)] for p in range(NC)], axis=1)
+    for copy in copies:
+        copy.wait()
+    aim = aim_ref[...]
     below = jnp.zeros(aim.shape, jnp.int32)
     slot = jnp.zeros(aim.shape, jnp.int32)
     for i in range(groups):
@@ -109,13 +115,15 @@
         return new, total, hit
 
     zero = jnp.zeros((1, count), F32)
-    top, total, hit = lax.fori_loop(0, CHUNKS, step, (jnp.full((1, count), -1e30, F32), zero, zero))
+    start = (jnp.full((1, count), -1e30, F32), zero, zero)
+    top, total, hit = lax.fori_loop(0, CHUNKS, step, start, unroll=True)
     logs = top + jnp.log(total)
     for p in range(NC):
         here = slice(p * 128, (p + 1) * 128)
         there = pl.ds(pl.multiple_of((k ^ p) * 128, 128), 128)
-        out_ref[0:1, there] = logs[:, here]
-        out_ref[1:2, there] = hit[:, here]
+        for d in range(NC):
+            out_ref[d, 0:1, there] = logs[:, here]
+            out_ref[d, 1:2, there] = hit[:, here]
 
 
 def grads_kernel(me_ref, cold_ref, hot_ref, col_ref, stats_ref, *refs):
@@ -149,7 +157,7 @@
         acc_ref[...] += lax.dot_general(table, w, TN, preferred_element_type=F32)
         return carry
 
-    lax.fori_loop(0, CHUNKS, step, 0)
+    lax.fori_loop(0, CHUNKS, step, 0, unroll=True)
     half = acc_ref.shape[1] // 2
     keep_ref[...] = acc_ref[:, :half].T
     send_ref[...] = acc_ref[:, half:].T.astype(BF)
@@ -181,20 +189,24 @@
     vmem = pl.BlockSpec(memory_space=pltpu.VMEM)
     smem = pl.BlockSpec(memory_space=pltpu.SMEM)
 
+    rows = [queries, swap(queries, "z1")]
+    late_me, rows[1] = lax.optimization_barrier((at_me, rows[1]))
+
     column = pl.pallas_call(
         decode_kernel,
         out_shape=jax.ShapeDtypeStruct((1, count), jnp.int32),
-        in_specs=[smem, vmem, vmem],
-        cost_estimate=pl.CostEstimate(flops=6 * hot * count, bytes_accessed=1 << 19, transcendentals=0),
-        compiler_params=params,
-    )(at_me, hot_ids.reshape(-1, 128), targets.reshape(-1, own))
-
-    rows = [queries, swap(queries, "z2")]
+        in_specs=[smem, vmem, pl.BlockSpec(memory_space=pltpu.HBM)],
+        scratch_shapes=[pltpu.VMEM((1, count), jnp.int32), pltpu.SemaphoreType.DMA((NC,))],
+        cost_estimate=pl.CostEstimate(
+            flops=hot * count << 11, bytes_accessed=1 << 20, transcendentals=0
+        ),
+        compiler_params=params,
+    )(late_me, hot_ids.reshape(-1, 128), targets.reshape(-1, 1, own))
 
     far = spread(cold_table, FAR).reshape(NF * shard, width)
-    far, rows[1], column = lax.optimization_barrier((far, rows[1], column))
+    far, column = lax.optimization_barrier((far, column))
     cold = spread(far, NEAR)
-    for a in ("z1", "c"):
+    for a in ("z2", "c"):
         rows.append(swap(jnp.concatenate(rows, axis=0), a))
     mine = hot_table.reshape(2, NG, NC // 2, hot_own, width)
     mine = lax.dynamic_slice(mine, (k >> 2, 0, k & 3, 0, 0), (1, NG, 1, hot_own, width))
@@ -202,11 +214,11 @@
 
     stats = pl.pallas_call(
         stats_kernel,
-        out_shape=jax.ShapeDtypeStruct((2, count), F32),
+        out_shape=jax.ShapeDtypeStruct((NC, 2, count), F32),
         in_specs=[smem] + [vmem] * (3 + len(rows)),
         compiler_params=params,
     )(at_me, cold, mine, column, *rows)
-    stats = spread(stats, COLS)
+    stats = lax.all_to_all(stats, COLS, 0, 0)
     keep, send, item_part, loss = pl.pallas_call(
         grads_kernel,
         out_shape=(
@@ -222,21 +234,21 @@
 
     near = lax.all_to_all(item_part, NEAR, 0, 0)
     keep = keep + swap(send, "c").astype(F32)
-    other = swap(keep[count // 4 :].astype(BF), "z1")
+    other = swap(keep[count // 4 :].astype(BF), "z2")
     near, other = lax.optimization_barrier((near, other))
+    keep = keep[: count // 4] + other.astype(F32)
     near = jnp.sum(near.astype(F32), axis=0).astype(BF)
     cold_part = near[: NF * shard].reshape(NF, shard, width)
     hot_part = jnp.broadcast_to(near[None, NF * shard :], (NF, hot_own, width))
     far = lax.all_to_all(jnp.concatenate([cold_part, hot_part], axis=1), FAR, 0, 0)
+    other = swap(keep[own:].astype(BF), "z1")
+    far, other = lax.optimization_barrier((far, other))
+    grad_queries = (keep[:own] + other.astype(F32)).astype(BF)
     far = jnp.sum(far.astype(F32), axis=0).astype(BF)
     grad_cold = far[:shard]
-    keep = keep[: count // 4] + other.astype(F32)
-    for a in ("z2",):
-        half = keep.shape[0] // 2
-        keep = keep[:half] + swap(keep[half:].astype(BF), a).astype(F32)
     grad_hot = spread(far[shard:], HALF).reshape(-1, width)
     grad_hot = spread(grad_hot, NEAR)
-    grad_hot, keep = lax.optimization_barrier((grad_hot, keep))
+    grad_hot, grad_queries = lax.optimization_barrier((grad_hot, grad_queries))
     grad_hot = grad_hot.reshape(hot // 2, width)
     grad_hot = pl.pallas_call(
         place_kernel,
@@ -246,7 +258,7 @@
         scratch_shapes=[pltpu.SemaphoreType.DMA((2,))],
         compiler_params=params,
     )(at_me, grad_hot, swap(grad_hot, "c"))
-    return keep.astype(BF), grad_hot, grad_cold, loss[0]
+    return grad_queries, grad_hot, grad_cold, loss[0]
 
 
 def solution(mesh):

time: 149 us -> 149 us (level)
  blocking collectives: 37.4 us -> 18.7 us
  waiting for transfers between devices: 34.3 us -> 47.4 us
  starting transfers between devices: 55.6 us -> 61.3 us
    all_to_all x2 -> x1, blocking collectives: 19.6 us -> 6.86 us  [spread(): return lax.all_to_all(jnp.broadcast_to(x[None], (n, *x.shape)), axes, 0, 0)]
    all_to_all x3, waiting for transfers between devices: 8.84 us -> 16.1 us  [spread(): return lax.all_to_all(jnp.broadcast_to(x[None], (n, *x.shape)), axes, 0, 0)]
    all_to_all x0 -> x1, waiting for transfers between devices: none -> 6.18 us  [body(): lax.all_to_all(jnp.concatenate([cold_part, hot_part], axis=1), FAR, 0, 0)]
    all_to_all x1, blocking collectives: 17.8 us -> 11.8 us  [body(): stats = lax.all_to_all(stats, COLS, 0, 0)]
    ppermute x7, starting transfers between devices: 23.8 us -> 28.2 us  [swap(): return lax.ppermute(x, axis, [(0, 1), (1, 0)])]
    all_to_all x1, waiting for transfers between devices: 8.6 us -> 4.36 us  [body(): near = lax.all_to_all(item_part, NEAR, 0, 0)]
    ppermute x7, waiting for transfers between devices: 16.9 us -> 20.8 us  [swap(): return lax.ppermute(x, axis, [(0, 1), (1, 0)])]
    all_to_all x0 -> x1, starting transfers between devices: none -> 3.51 us  [body(): lax.all_to_all(jnp.concatenate([cold_part, hot_part], axis=1), FAR, 0, 0)]
  transfers between devices with their start and end apart: 11 -> 12, of which waited for: 11 -> 10; matrix products, arithmetic and copies ran while one was open for 1% -> 2% of each run, Pallas kernels for 1% -> 2%
where the time goes in v6:
time: 149 us; the launch traced here: 148 us
  starting transfers between devices  61.3 us (41%)
  waiting for transfers between devices  47.4 us (32%)
  blocking collectives  18.7 us (13%)
  Pallas kernels  12.6 us (8%)
  local copies, waits for them, and re-layouts  5.61 us (4%)
  other arithmetic  1.6 us (1%)
    ppermute x7, starting transfers between devices, swap(): return lax.ppermute(x, axis, [(0, 1), (1, 0)])  28.2 us
    all_to_all x3, starting transfers between devices, spread(): return lax.all_to_all(jnp.broadcast_to(x[None], (n, *x.shape)), axes, 0, 0)  25.6 us
    ppermute x7, waiting for transfers between devices, swap(): return lax.ppermute(x, axis, [(0, 1), (1, 0)])  20.8 us
    all_to_all x3, waiting for transfers between devices, spread(): return lax.all_to_all(jnp.broadcast_to(x[None], (n, *x.shape)), axes, 0, 0)  16.1 us
    all_to_all x1, blocking collectives, body(): stats = lax.all_to_all(stats, COLS, 0, 0)  11.8 us
    all_to_all x1, blocking collectives, spread(): return lax.all_to_all(jnp.broadcast_to(x[None], (n, *x.shape)), axes, 0, 0)  6.86 us
    all_to_all x1, waiting for transfers between devices, body(): lax.all_to_all(jnp.concatenate([cold_part, hot_part], axis=1), FAR, 0, 0)  6.18 us
    pallas_call x1, Pallas kernels, body(): pl.pallas_call(grads_kernel, out_shape=(jax.ShapeDtypeStruct((count // 2,...  5.66 us
  transfers between devices with their start and end apart: 12, of which 10 were waited for; matrix products, arithmetic and copies ran while one was open for 2% of the time, Pallas kernels for 2%

profile of v6, /device:TPU:1, one launch (start us, length us, event | category | flops | bytes accessed | tf_op | source)
XLA Modules:
  0.0 148.0 jit_solution(14620602931356832876)
XLA Ops:
  0.6 4.5 %collective-permute-start = (bf16[128,256]{1,0:T(8,128)(2,1)}, bf16[128,256]{1,0:T(8,128)(2,1)S(1)}, u32[]{:S(2)}, u32[]{:S(2)}) collective-permute-start(bf16[128,256]{1,0:T(8,128)(2,1)} %refs_0_.3), channel_id=1, source_target_pairs={{0,32},{32,0},{1,33},{33,1},{2,34},{34,2},{3,35},{35,3},{4,36},{36... | collective-permute-start | bytes 196616 | tf_op jit(solution)/shard_map/ppermute | solution.py:30
  5.2 1.4 broadcast_in_dim.12
  6.5 13.9 %all-to-all-start = ((bf16[4,32,256]{2,1,0:T(8,128)(2,1)}), bf16[4,32,256]{2,1,0:T(8,128)(2,1)S(1)}, u32[]{:S(2)}, u32[]{:S(2)}) async-start(bf16[4,32,256]{2,1,0:T(8,128)(2,1)} %broadcast_in_dim.12), calls=%async_computation | async-start | bytes 131072 | tf_op jit(solution)/shard_map/all_to_all | solution.py:26
  20.4 0.9 copy-done.2
  22.1 2.2 %shard_map.84.col_ref = s32[1,1024]{1,0:T(1,128)S(1)} custom-call(s32[1]{0:T(128)} %bitcast.me_ref, s32[16,128]{1,0:T(8,128)S(1)} %bitcast.17, s32[512,1,128]{2,1,0:T(1,128)S(1)} %bitcast.16), custom_call_target="tpu_custom_call" | custom-call | flops 4294967296 | bytes 1048576 | tf_op jit(solution)/shard_map/pallas_call | solution.py:195
  24.3 7.8 %all-to-all-done = bf16[4,32,256]{2,1,0:T(8,128)(2,1)S(1)} async-done(((bf16[4,32,256]{2,1,0:T(8,128)(2,1)}), bf16[4,32,256]{2,1,0:T(8,128)(2,1)S(1)}, u32[]{:S(2)}, u32[]{:S(2)}) %all-to-all-start) | async-done | bytes 65568 | tf_op jit(solution)/shard_map/all_to_all | solution.py:26
  32.1 1.1 broadcast_in_dim.13
  33.2 6.9 %all-to-all-start.1 = ((bf16[16,128,256]{2,1,0:T(8,128)(2,1)}), bf16[16,128,256]{2,1,0:T(8,128)(2,1)S(1)}, u32[]{:S(2)}, u32[]{:S(2)}) async-start(bf16[16,128,256]{2,1,0:T(8,128)(2,1)} %broadcast_in_dim.13), calls=%async_computation.1 | async-start | bytes 2097152 | tf_op jit(solution)/shard_map/all_to_all | solution.py:26
  40.1 3.5 %collective-permute-start.1 = (bf16[256,256]{1,0:T(8,128)(2,1)S(1)}, bf16[256,256]{1,0:T(8,128)(2,1)S(1)}, u32[]{:S(2)}, u32[]{:S(2)}) collective-permute-start(bf16[256,256]{1,0:T(8,128)(2,1)S(1)} %pad_maximum_fusion.1), channel_id=1, source_target_pairs={{0,64},{64,0},{1,65},{65,1},{2,66},{66,2},{3,67},{67,3},{4,68},{68... | collective-permute-start | bytes 393224 | tf_op jit(solution)/shard_map/ppermute | solution.py:30
  43.6 4.8 %collective-permute-done.1.refs_2_ = bf16[256,256]{1,0:T(8,128)(2,1)S(1)} collective-permute-done((bf16[256,256]{1,0:T(8,128)(2,1)S(1)}, bf16[256,256]{1,0:T(8,128)(2,1)S(1)}, u32[]{:S(2)}, u32[]{:S(2)}) %collective-permute-start.1) | collective-permute-done | bytes 131104 | tf_op jit(solution)/shard_map/ppermute | solution.py:30
  48.4 5.7 %collective-permute-start.2 = (bf16[512,256]{1,0:T(8,128)(2,1)S(1)}, bf16[512,256]{1,0:T(8,128)(2,1)S(1)}, u32[]{:S(2)}, u32[]{:S(2)}) collective-permute-start(bf16[512,256]{1,0:T(8,128)(2,1)S(1)} %pad_maximum_fusion), channel_id=1, source_target_pairs={{0,8},{8,0},{1,9},{9,1},{2,10},{10,2},{3,11},{11,3},{4,12},{12,4},... | collective-permute-start | bytes 786440 | tf_op jit(solution)/shard_map/ppermute | solution.py:30
  54.2 1.1 collective-permute-done.2.refs_3_
  55.3 3.7 %shard_map.85 = f32[8,2,1024]{2,1,0:T(2,128)S(1)} custom-call(s32[1]{0:T(128)} %bitcast.me_ref, bf16[16,128,256]{2,1,0:T(8,128)(2,1)S(1)} %all-to-all-done.1.cold_ref, bf16[16,16,256]{2,1,0:T(8,128)(2,1)S(1)} %dynamic-slice_bitcast_fusion.hot_ref, s32[1,1024]{1,0:T(1,128)S(1)} %shard_map.84.col_ref, bf16[128,256]{1,0:T(8,128)(2,1)S(1)} %copy-done.1, ...), custom_call_target="tpu_custom_call" | custom-call | tf_op jit(solution)/shard_map/pallas_call | solution.py:215
  59.0 11.8 %all_to_all.35.stats_ref = f32[8,2,1024]{2,1,0:T(2,128)S(1)} all-to-all(f32[8,2,1024]{2,1,0:T(2,128)S(1)} %shard_map.85), channel_id=1, replica_groups=mesh['z8'=2,'z4'=2,'z2'=2,'z1'=2,'yl'=2,'c'=2,'x2'=2,'x1'=2,'yh'=2] {'c'..., dimensions={0} | all-to-all | bytes 131072 | tf_op jit(solution)/shard_map/all_to_all | solution.py:221
  70.8 5.7 %shard_map.86 = (f32[512,256]{1,0:T(8,128)S(1)}, bf16[512,256]{1,0:T(8,128)(2,1)S(1)}, bf16[16,144,256]{2,1,0:T(8,128)(2,1)}, f32[1,128]{1,0:T(1,128)}) custom-call(s32[1]{0:T(128)} %bitcast.me_ref, bf16[16,128,256]{2,1,0:T(8,128)(2,1)S(1)} %all-to-all-done.1.cold_ref, bf16[16,16,256]{2,1,0:T(8,128)(2,1)S(1)} %dynamic-slice_bitcast_fusion.hot_ref, ...), custom_call_target="tpu_custom_call" | custom-call | tf_op jit(solution)/shard_map/pallas_call | solution.py:222
  76.4 4.1 %all-to-all-start.3 = ((bf16[16,144,256]{2,1,0:T(8,128)(2,1)}), bf16[16,144,256]{2,1,0:T(8,128)(2,1)S(1)}, u32[]{:S(2)}, u32[]{:S(2)}) async-start(bf16[16,144,256]{2,1,0:T(8,128)(2,1)} %get-tuple-element.22), calls=%async_computation.3 | async-start | bytes 2359296 | tf_op jit(solution)/shard_map/all_to_all | solution.py:235
  80.5 2.6 %collective-permute-start.3 = (bf16[512,256]{1,0:T(8,128)(2,1)S(1)}, bf16[512,256]{1,0:T(8,128)(2,1)S(1)}, u32[]{:S(2)}, u32[]{:S(2)}) collective-permute-start(bf16[512,256]{1,0:T(8,128)(2,1)S(1)} %get-tuple-element.24), channel_id=1, source_target_pairs={{0,8},{8,0},{1,9},{9,1},{2,10},{10,2},{3,11},{11,3},{4,12},{12,4},... | collective-permute-start | bytes 786440 | tf_op jit(solution)/shard_map/ppermute | solution.py:30
  83.1 1.1 collective-permute-done.3
  84.3 1.9 %collective-permute-start.4 = (bf16[256,256]{1,0:T(8,128)(2,1)S(1)}, bf16[256,256]{1,0:T(8,128)(2,1)S(1)}, u32[]{:S(2)}, u32[]{:S(2)}) collective-permute-start(bf16[256,256]{1,0:T(8,128)(2,1)S(1)} %slice.48), channel_id=1, source_target_pairs={{0,64},{64,0},{1,65},{65,1},{2,66},{66,2},{3,67},{67,3},{4,68},{68... | collective-permute-start | bytes 393224 | tf_op jit(solution)/shard_map/ppermute | solution.py:30
  86.3 8.9 %collective-permute-done.4 = bf16[256,256]{1,0:T(8,128)(2,1)S(1)} collective-permute-done((bf16[256,256]{1,0:T(8,128)(2,1)S(1)}, bf16[256,256]{1,0:T(8,128)(2,1)S(1)}, u32[]{:S(2)}, u32[]{:S(2)}) %collective-permute-start.4) | collective-permute-done | bytes 131104 | tf_op jit(solution)/shard_map/ppermute | solution.py:30
  95.2 4.4 %all-to-all-done.3 = bf16[16,144,256]{2,1,0:T(8,128)(2,1)S(1)} async-done(((bf16[16,144,256]{2,1,0:T(8,128)(2,1)}), bf16[16,144,256]{2,1,0:T(8,128)(2,1)S(1)}, u32[]{:S(2)}, u32[]{:S(2)}) %all-to-all-start.3) | async-done | bytes 1179680 | tf_op jit(solution)/shard_map/all_to_all | solution.py:235
  100.4 3.5 %all-to-all-start.4 = ((bf16[4,48,256]{2,1,0:T(8,128)(2,1)}), bf16[4,48,256]{2,1,0:T(8,128)(2,1)S(1)}, u32[]{:S(2)}, u32[]{:S(2)}) async-start(bf16[4,48,256]{2,1,0:T(8,128)(2,1)} %pad_maximum_fusion.2), calls=%async_computation.4 | async-start | bytes 196608 | tf_op jit(solution)/shard_map/all_to_all | solution.py:243
  104.0 2.0 %collective-permute-start.5 = (bf16[128,256]{1,0:T(8,128)(2,1)S(1)}, bf16[128,256]{1,0:T(8,128)(2,1)S(1)}, u32[]{:S(2)}, u32[]{:S(2)}) collective-permute-start(bf16[128,256]{1,0:T(8,128)(2,1)S(1)} %slice.49), channel_id=1, source_target_pairs={{0,32},{32,0},{1,33},{33,1},{2,34},{34,2},{3,35},{35,3},{4,36},{36... | collective-permute-start | bytes 196616 | tf_op jit(solution)/shard_map/ppermute | solution.py:30
  106.0 3.9 %collective-permute-done.5 = bf16[128,256]{1,0:T(8,128)(2,1)S(1)} collective-permute-done((bf16[128,256]{1,0:T(8,128)(2,1)S(1)}, bf16[128,256]{1,0:T(8,128)(2,1)S(1)}, u32[]{:S(2)}, u32[]{:S(2)}) %collective-permute-start.5) | collective-permute-done | bytes 65568 | tf_op jit(solution)/shard_map/ppermute | solution.py:30
  109.9 6.2 %all-to-all-done.4 = bf16[4,48,256]{2,1,0:T(8,128)(2,1)S(1)} async-done(((bf16[4,48,256]{2,1,0:T(8,128)(2,1)}), bf16[4,48,256]{2,1,0:T(8,128)(2,1)S(1)}, u32[]{:S(2)}, u32[]{:S(2)}) %all-to-all-start.4) | async-done | bytes 98336 | tf_op jit(solution)/shard_map/all_to_all | solution.py:243
  116.1 6.9 %all_to_all.36 = bf16[4,16,256]{2,1,0:T(8,128)(2,1)S(1)} all-to-all(bf16[4,16,256]{2,1,0:T(8,128)(2,1)S(1)} %broadcast_in_dim.15), channel_id=1, replica_groups=mesh['z8'=2,'z4'=2,'z2'=2,'z1'=2,'yl'=2,'c'=2,'x2'=2,'x1'=2,'yh'=2] {'z2..., dimensions={0} | all-to-all | bytes 65536 | tf_op jit(solution)/shard_map/all_to_all | solution.py:26
  123.0 0.8 broadcast_in_dim.17
  123.8 4.8 %all-to-all-start.6 = ((bf16[16,64,256]{2,1,0:T(8,128)(2,1)}), bf16[16,64,256]{2,1,0:T(8,128)(2,1)S(1)}, u32[]{:S(2)}, u32[]{:S(2)}) async-start(bf16[16,64,256]{2,1,0:T(8,128)(2,1)} %broadcast_in_dim.17), calls=%async_computation.6 | async-start | bytes 1048576 | tf_op jit(solution)/shard_map/all_to_all | solution.py:26
  129.3 8.2 %all-to-all-done.6 = bf16[16,64,256]{2,1,0:T(8,128)(2,1)S(1)} async-done(((bf16[16,64,256]{2,1,0:T(8,128)(2,1)}), bf16[16,64,256]{2,1,0:T(8,128)(2,1)S(1)}, u32[]{:S(2)}, u32[]{:S(2)}) %all-to-all-start.6) | async-done | bytes 524320 | tf_op jit(solution)/shard_map/all_to_all | solution.py:26
  137.5 8.0 %collective-permute-start.6 = (bf16[1024,256]{1,0:T(8,128)(2,1)S(1)}, bf16[1024,256]{1,0:T(8,128)(2,1)S(1)}, u32[]{:S(2)}, u32[]{:S(2)}) collective-permute-start(bf16[1024,256]{1,0:T(8,128)(2,1)S(1)} %bitcast.14), channel_id=1, source_target_pairs={{0,8},{8,0},{1,9},{9,1},{2,10},{10,2},{3,11},{11,3},{4,12},{12,4},... | collective-permute-start | bytes 1572872 | tf_op jit(solution)/shard_map/ppermute | solution.py:30
  146.1 0.9 collective-permute-done.6.other_ref
  147.1 1.0 shard_map.87
  (30 shorter events, 3.0 us)
Async XLA Ops:
  0.6 53.5 %copy-start = (bf16[2048,256]{1,0:T(8,128)(2,1)S(1)}, bf16[2048,256]{1,0:T(8,128)(2,1)}, u32[]{:S(2)}) copy-start(bf16[2048,256]{1,0:T(8,128)(2,1)} %param.6) | copy-start | bytes 3145732
  0.6 19.8 %collective-permute-start = (bf16[128,256]{1,0:T(8,128)(2,1)}, bf16[128,256]{1,0:T(8,128)(2,1)S(1)}, u32[]{:S(2)}, u32[]{:S(2)}) collective-permute-start(bf16[128,256]{1,0:T(8,128)(2,1)} %refs_0_.3), channel_id=1, source_target_pairs={{0,32},{32,0},{1,33},{33,1},{2,34},{34,2},{3,35},{35,3},{4,36},{36... | collective-permute-start | bytes 196616 | tf_op jit(solution)/shard_map/ppermute | solution.py:30
  6.5 25.6 %all-to-all-start = ((bf16[4,32,256]{2,1,0:T(8,128)(2,1)}), bf16[4,32,256]{2,1,0:T(8,128)(2,1)S(1)}, u32[]{:S(2)}, u32[]{:S(2)}) async-start(bf16[4,32,256]{2,1,0:T(8,128)(2,1)} %broadcast_in_dim.12), calls=%async_computation | async-start | bytes 131072 | tf_op jit(solution)/shard_map/all_to_all | solution.py:26
  20.4 1.0 copy-start.2
  21.4 0.7 copy-start.3
  33.2 6.9 %copy-start.1 = (bf16[128,256]{1,0:T(8,128)(2,1)S(1)}, bf16[128,256]{1,0:T(8,128)(2,1)}, u32[]{:S(2)}) copy-start(bf16[128,256]{1,0:T(8,128)(2,1)} %refs_0_.3) | copy-start | bytes 196612
  33.2 22.1 %all-to-all-start.1 = ((bf16[16,128,256]{2,1,0:T(8,128)(2,1)}), bf16[16,128,256]{2,1,0:T(8,128)(2,1)S(1)}, u32[]{:S(2)}, u32[]{:S(2)}) async-start(bf16[16,128,256]{2,1,0:T(8,128)(2,1)} %broadcast_in_dim.13), calls=%async_computation.1 | async-start | bytes 2097152 | tf_op jit(solution)/shard_map/all_to_all | solution.py:26
  40.1 8.3 %collective-permute-start.1 = (bf16[256,256]{1,0:T(8,128)(2,1)S(1)}, bf16[256,256]{1,0:T(8,128)(2,1)S(1)}, u32[]{:S(2)}, u32[]{:S(2)}) collective-permute-start(bf16[256,256]{1,0:T(8,128)(2,1)S(1)} %pad_maximum_fusion.1), channel_id=1, source_target_pairs={{0,64},{64,0},{1,65},{65,1},{2,66},{66,2},{3,67},{67,3},{4,68},{68... | collective-permute-start | bytes 393224 | tf_op jit(solution)/shard_map/ppermute | solution.py:30
  48.4 6.8 %collective-permute-start.2 = (bf16[512,256]{1,0:T(8,128)(2,1)S(1)}, bf16[512,256]{1,0:T(8,128)(2,1)S(1)}, u32[]{:S(2)}, u32[]{:S(2)}) collective-permute-start(bf16[512,256]{1,0:T(8,128)(2,1)S(1)} %pad_maximum_fusion), channel_id=1, source_target_pairs={{0,8},{8,0},{1,9},{9,1},{2,10},{10,2},{3,11},{11,3},{4,12},{12,4},... | collective-permute-start | bytes 786440 | tf_op jit(solution)/shard_map/ppermute | solution.py:30
  76.4 23.1 %all-to-all-start.3 = ((bf16[16,144,256]{2,1,0:T(8,128)(2,1)}), bf16[16,144,256]{2,1,0:T(8,128)(2,1)S(1)}, u32[]{:S(2)}, u32[]{:S(2)}) async-start(bf16[16,144,256]{2,1,0:T(8,128)(2,1)} %get-tuple-element.22), calls=%async_computation.3 | async-start | bytes 2359296 | tf_op jit(solution)/shard_map/all_to_all | solution.py:235
  80.5 3.7 %collective-permute-start.3 = (bf16[512,256]{1,0:T(8,128)(2,1)S(1)}, bf16[512,256]{1,0:T(8,128)(2,1)S(1)}, u32[]{:S(2)}, u32[]{:S(2)}) collective-permute-start(bf16[512,256]{1,0:T(8,128)(2,1)S(1)} %get-tuple-element.24), channel_id=1, source_target_pairs={{0,8},{8,0},{1,9},{9,1},{2,10},{10,2},{3,11},{11,3},{4,12},{12,4},... | collective-permute-start | bytes 786440 | tf_op jit(solution)/shard_map/ppermute | solution.py:30
  84.3 2.0 %copy-start.4 = (f32[512,256]{1,0:T(8,128)}, f32[512,256]{1,0:T(8,128)S(1)}, u32[]{:S(2)}) copy-start(f32[512,256]{1,0:T(8,128)S(1)} %convert_add_fusion) | copy-start | bytes 1572868
  84.3 10.9 %collective-permute-start.4 = (bf16[256,256]{1,0:T(8,128)(2,1)S(1)}, bf16[256,256]{1,0:T(8,128)(2,1)S(1)}, u32[]{:S(2)}, u32[]{:S(2)}) collective-permute-start(bf16[256,256]{1,0:T(8,128)(2,1)S(1)} %slice.48), channel_id=1, source_target_pairs={{0,64},{64,0},{1,65},{65,1},{2,66},{66,2},{3,67},{67,3},{4,68},{68... | collective-permute-start | bytes 393224 | tf_op jit(solution)/shard_map/ppermute | solution.py:30
  95.2 8.7 %copy-start.5 = (f32[512,256]{1,0:T(8,128)S(1)}, f32[512,256]{1,0:T(8,128)}, u32[]{:S(2)}) copy-start(f32[512,256]{1,0:T(8,128)} %copy-done.4) | copy-start | bytes 1572868
  100.4 15.7 %all-to-all-start.4 = ((bf16[4,48,256]{2,1,0:T(8,128)(2,1)}), bf16[4,48,256]{2,1,0:T(8,128)(2,1)S(1)}, u32[]{:S(2)}, u32[]{:S(2)}) async-start(bf16[4,48,256]{2,1,0:T(8,128)(2,1)} %pad_maximum_fusion.2), calls=%async_computation.4 | async-start | bytes 196608 | tf_op jit(solution)/shard_map/all_to_all | solution.py:243
  104.0 5.9 %collective-permute-start.5 = (bf16[128,256]{1,0:T(8,128)(2,1)S(1)}, bf16[128,256]{1,0:T(8,128)(2,1)S(1)}, u32[]{:S(2)}, u32[]{:S(2)}) collective-permute-start(bf16[128,256]{1,0:T(8,128)(2,1)S(1)} %slice.49), channel_id=1, source_target_pairs={{0,32},{32,0},{1,33},{33,1},{2,34},{34,2},{3,35},{35,3},{4,36},{36... | collective-permute-start | bytes 196616 | tf_op jit(solution)/shard_map/ppermute | solution.py:30
  123.8 13.7 %all-to-all-start.6 = ((bf16[16,64,256]{2,1,0:T(8,128)(2,1)}), bf16[16,64,256]{2,1,0:T(8,128)(2,1)S(1)}, u32[]{:S(2)}, u32[]{:S(2)}) async-start(bf16[16,64,256]{2,1,0:T(8,128)(2,1)} %broadcast_in_dim.17), calls=%async_computation.6 | async-start | bytes 1048576 | tf_op jit(solution)/shard_map/all_to_all | solution.py:26
  137.5 9.5 %collective-permute-start.6 = (bf16[1024,256]{1,0:T(8,128)(2,1)S(1)}, bf16[1024,256]{1,0:T(8,128)(2,1)S(1)}, u32[]{:S(2)}, u32[]{:S(2)}) collective-permute-start(bf16[1024,256]{1,0:T(8,128)(2,1)S(1)} %bitcast.14), channel_id=1, source_target_pairs={{0,8},{8,0},{1,9},{9,1},{2,10},{10,2},{3,11},{11,3},{4,12},{12,4},... | collective-permute-start | bytes 1572872 | tf_op jit(solution)/shard_map/ppermute | solution.py:30

commit v7 on v6

--- a/solution.py
+++ b/solution.py
@@ -190,7 +190,6 @@
     smem = pl.BlockSpec(memory_space=pltpu.SMEM)
 
     rows = [queries, swap(queries, "z1")]
-    late_me, rows[1] = lax.optimization_barrier((at_me, rows[1]))
 
     column = pl.pallas_call(
         decode_kernel,
@@ -198,16 +197,18 @@
         in_specs=[smem, vmem, pl.BlockSpec(memory_space=pltpu.HBM)],
         scratch_shapes=[pltpu.VMEM((1, count), jnp.int32), pltpu.SemaphoreType.DMA((NC,))],
         cost_estimate=pl.CostEstimate(
-            flops=hot * count << 11, bytes_accessed=1 << 20, transcendentals=0
+            flops=6 * hot * count, bytes_accessed=1 << 20, transcendentals=0
         ),
         compiler_params=params,
-    )(late_me, hot_ids.reshape(-1, 128), targets.reshape(-1, 1, own))
+    )(at_me, hot_ids.reshape(-1, 128), targets.reshape(-1, 1, own))
 
     far = spread(cold_table, FAR).reshape(NF * shard, width)
-    far, column = lax.optimization_barrier((far, column))
+    far, rows[1] = lax.optimization_barrier((far, rows[1]))
     cold = spread(far, NEAR)
-    for a in ("z2", "c"):
-        rows.append(swap(jnp.concatenate(rows, axis=0), a))
+    rows = jnp.concatenate(rows, axis=0)
+    other, column = lax.optimization_barrier((swap(rows, "z2"), column))
+    rows = jnp.concatenate([rows, other], axis=0)
+    rows = [rows, swap(rows, "c")]
     mine = hot_table.reshape(2, NG, NC // 2, hot_own, width)
     mine = lax.dynamic_slice(mine, (k >> 2, 0, k & 3, 0, 0), (1, NG, 1, hot_own, width))
     mine = mine.reshape(NG, hot_own, width)
@@ -233,22 +234,20 @@
     )(at_me, cold, mine, column, stats, *rows)
 
     near = lax.all_to_all(item_part, NEAR, 0, 0)
-    keep = keep + swap(send, "c").astype(F32)
-    other = swap(keep[count // 4 :].astype(BF), "z2")
-    near, other = lax.optimization_barrier((near, other))
-    keep = keep[: count // 4] + other.astype(F32)
+    keep = (keep + swap(send, "c").astype(F32)).reshape(4, own, width)
+    sends = keep.astype(BF)
+    others = [swap(sends[1], "z1"), swap(sends[2], "z2")]
+    others.append(lax.ppermute(sends[3], ("z2", "z1"), [(i, 3 - i) for i in range(4)]))
+    near, *others = lax.optimization_barrier((near, *others))
+    grad_queries = (keep[0] + sum(x.astype(F32) for x in others)).astype(BF)
     near = jnp.sum(near.astype(F32), axis=0).astype(BF)
     cold_part = near[: NF * shard].reshape(NF, shard, width)
     hot_part = jnp.broadcast_to(near[None, NF * shard :], (NF, hot_own, width))
     far = lax.all_to_all(jnp.concatenate([cold_part, hot_part], axis=1), FAR, 0, 0)
-    other = swap(keep[own:].astype(BF), "z1")
-    far, other = lax.optimization_barrier((far, other))
-    grad_queries = (keep[:own] + other.astype(F32)).astype(BF)
     far = jnp.sum(far.astype(F32), axis=0).astype(BF)
     grad_cold = far[:shard]
     grad_hot = spread(far[shard:], HALF).reshape(-1, width)
     grad_hot = spread(grad_hot, NEAR)
-    grad_hot, grad_queries = lax.optimization_barrier((grad_hot, grad_queries))
     grad_hot = grad_hot.reshape(hot // 2, width)
     grad_hot = pl.pallas_call(
         place_kernel,

time: 149 us -> 146 us (0.980)
  blocking collectives: 18.7 us -> 49.3 us
  waiting for transfers between devices: 47.4 us -> 22 us
  starting transfers between devices: 61.3 us -> 56.3 us
  local copies, waits for them, and re-layouts: 5.61 us -> 3.26 us
    all_to_all x0 -> x1, blocking collectives: none -> 17 us  [body(): lax.all_to_all(jnp.concatenate([cold_part, hot_part], axis=1), FAR, 0, 0)]
    all_to_all x1 -> x2, blocking collectives: 6.86 us -> 19.9 us  [spread(): return lax.all_to_all(jnp.broadcast_to(x[None], (n, *x.shape)), axes, 0, 0)]
    ppermute x7, waiting for transfers between devices: 20.8 us -> 10.9 us  [swap(): return lax.ppermute(x, axis, [(0, 1), (1, 0)])]
    all_to_all x3 -> x2, waiting for transfers between devices: 16.1 us -> 7.29 us  [spread(): return lax.all_to_all(jnp.broadcast_to(x[None], (n, *x.shape)), axes, 0, 0)]
    all_to_all x1 -> x0, waiting for transfers between devices: 6.18 us -> none  [body(): lax.all_to_all(jnp.concatenate([cold_part, hot_part], axis=1), FAR, 0, 0)]
    all_to_all x1 -> x0, starting transfers between devices: 3.51 us -> none  [body(): lax.all_to_all(jnp.concatenate([cold_part, hot_part], axis=1), FAR, 0, 0)]
    all_to_all x3 -> x2, starting transfers between devices: 25.6 us -> 22.5 us  [spread(): return lax.all_to_all(jnp.broadcast_to(x[None], (n, *x.shape)), axes, 0, 0)]
    ppermute x0 -> x1, starting transfers between devices: none -> 2.18 us  [body(): lax.ppermute(sends[3], ('z2', 'z1'), [(i, 3 - i) for i in range(4)])]
  transfers between devices with their start and end apart: 12 -> 11, of which waited for: 10 -> 9; matrix products, arithmetic and copies ran while one was open for 2% -> 1% of each run, Pallas kernels for 2% -> 2%
where the time goes in v7:
time: 146 us; the launch traced here: 145 us
  starting transfers between devices  56.3 us (39%)
  blocking collectives  49.3 us (34%)
  waiting for transfers between devices  22 us (15%)
  Pallas kernels  12.4 us (8%)
  local copies, waits for them, and re-layouts  3.26 us (2%)
    ppermute x7, starting transfers between devices, swap(): return lax.ppermute(x, axis, [(0, 1), (1, 0)])  27.8 us
    all_to_all x2, starting transfers between devices, spread(): return lax.all_to_all(jnp.broadcast_to(x[None], (n, *x.shape)), axes, 0, 0)  22.5 us
    all_to_all x2, blocking collectives, spread(): return lax.all_to_all(jnp.broadcast_to(x[None], (n, *x.shape)), axes, 0, 0)  19.9 us
    all_to_all x1, blocking collectives, body(): lax.all_to_all(jnp.concatenate([cold_part, hot_part], axis=1), FAR, 0, 0)  17 us
    all_to_all x1, blocking collectives, body(): stats = lax.all_to_all(stats, COLS, 0, 0)  12.5 us
    ppermute x7, waiting for transfers between devices, swap(): return lax.ppermute(x, axis, [(0, 1), (1, 0)])  10.9 us
    all_to_all x2, waiting for transfers between devices, spread(): return lax.all_to_all(jnp.broadcast_to(x[None], (n, *x.shape)), axes, 0, 0)  7.29 us
    pallas_call x1, Pallas kernels, body(): pl.pallas_call(grads_kernel, out_shape=(jax.ShapeDtypeStruct((count // 2,...  5.56 us
  transfers between devices with their start and end apart: 11, of which 9 were waited for; matrix products, arithmetic and copies ran while one was open for 1% of the time, Pallas kernels for 2%

profile of v7, /device:TPU:1, one launch (start us, length us, event | category | flops | bytes accessed | tf_op | source)
XLA Modules:
  0.0 145.1 jit_solution(17804778964031746923)
XLA Ops:
  0.6 1.4 broadcast_in_dim.12
  2.1 15.6 %all-to-all-start = ((bf16[4,32,256]{2,1,0:T(8,128)(2,1)}), bf16[4,32,256]{2,1,0:T(8,128)(2,1)S(1)}, u32[]{:S(2)}, u32[]{:S(2)}) async-start(bf16[4,32,256]{2,1,0:T(8,128)(2,1)} %broadcast_in_dim.12), calls=%async_computation | async-start | bytes 131072 | tf_op jit(solution)/shard_map/all_to_all | solution.py:26
  17.7 2.6 %collective-permute-start = (bf16[128,256]{1,0:T(8,128)(2,1)}, bf16[128,256]{1,0:T(8,128)(2,1)S(1)}, u32[]{:S(2)}, u32[]{:S(2)}) collective-permute-start(bf16[128,256]{1,0:T(8,128)(2,1)} %param.5), channel_id=1, source_target_pairs={{0,32},{32,0},{1,33},{33,1},{2,34},{34,2},{3,35},{35,3},{4,36},{36... | collective-permute-start | bytes 196616 | tf_op jit(solution)/shard_map/ppermute | solution.py:30
  20.4 2.6 %collective-permute-done = bf16[128,256]{1,0:T(8,128)(2,1)S(1)} collective-permute-done((bf16[128,256]{1,0:T(8,128)(2,1)}, bf16[128,256]{1,0:T(8,128)(2,1)S(1)}, u32[]{:S(2)}, u32[]{:S(2)}) %collective-permute-start) | collective-permute-done | bytes 65568 | tf_op jit(solution)/shard_map/ppermute | solution.py:30
  22.9 7.3 %all-to-all-done = bf16[4,32,256]{2,1,0:T(8,128)(2,1)S(1)} async-done(((bf16[4,32,256]{2,1,0:T(8,128)(2,1)}), bf16[4,32,256]{2,1,0:T(8,128)(2,1)S(1)}, u32[]{:S(2)}, u32[]{:S(2)}) %all-to-all-start) | async-done | bytes 65568 | tf_op jit(solution)/shard_map/all_to_all | solution.py:26
  30.2 1.1 broadcast_in_dim.13
  31.3 6.9 %all-to-all-start.1 = ((bf16[16,128,256]{2,1,0:T(8,128)(2,1)}), bf16[16,128,256]{2,1,0:T(8,128)(2,1)S(1)}, u32[]{:S(2)}, u32[]{:S(2)}) async-start(bf16[16,128,256]{2,1,0:T(8,128)(2,1)} %broadcast_in_dim.13), calls=%async_computation.1 | async-start | bytes 2097152 | tf_op jit(solution)/shard_map/all_to_all | solution.py:26
  38.2 2.7 %collective-permute-start.1 = (bf16[256,256]{1,0:T(8,128)(2,1)S(1)}, bf16[256,256]{1,0:T(8,128)(2,1)S(1)}, u32[]{:S(2)}, u32[]{:S(2)}) collective-permute-start(bf16[256,256]{1,0:T(8,128)(2,1)S(1)} %pad_maximum_fusion), channel_id=1, source_target_pairs={{0,64},{64,0},{1,65},{65,1},{2,66},{66,2},{3,67},{67,3},{4,68},{68... | collective-permute-start | bytes 393224 | tf_op jit(solution)/shard_map/ppermute | solution.py:30
  40.9 2.2 %shard_map.84.col_ref = s32[1,1024]{1,0:T(1,128)S(1)} custom-call(s32[1]{0:T(128)} %bitcast.me_ref, s32[16,128]{1,0:T(8,128)S(1)} %bitcast.17, s32[512,1,128]{2,1,0:T(1,128)S(1)} %bitcast.16), custom_call_target="tpu_custom_call" | custom-call | flops 12582912 | bytes 1048576 | tf_op jit(solution)/shard_map/pallas_call | solution.py:194
  43.2 3.8 %collective-permute-done.1 = bf16[256,256]{1,0:T(8,128)(2,1)S(1)} collective-permute-done((bf16[256,256]{1,0:T(8,128)(2,1)S(1)}, bf16[256,256]{1,0:T(8,128)(2,1)S(1)}, u32[]{:S(2)}, u32[]{:S(2)}) %collective-permute-start.1) | collective-permute-done | bytes 131104 | tf_op jit(solution)/shard_map/ppermute | solution.py:30
  47.0 4.7 %collective-permute-start.2 = (bf16[512,256]{1,0:T(8,128)(2,1)S(1)}, bf16[512,256]{1,0:T(8,128)(2,1)S(1)}, u32[]{:S(2)}, u32[]{:S(2)}) collective-permute-start(bf16[512,256]{1,0:T(8,128)(2,1)S(1)} %constant_dynamic-update-slice_fusion.refs_0_), channel_id=1, source_target_pairs={{0,8},{8,0},{1,9},{9,1},{2,10},{10,2},{3,11},{11,3},{4,12},{12,4},... | collective-permute-start | bytes 786440 | tf_op jit(solution)/shard_map/ppermute | solution.py:30
  51.7 1.1 collective-permute-done.2.refs_1_
  52.8 3.6 %shard_map.85 = f32[8,2,1024]{2,1,0:T(2,128)S(1)} custom-call(s32[1]{0:T(128)} %bitcast.me_ref, bf16[16,128,256]{2,1,0:T(8,128)(2,1)S(1)} %all-to-all-done.1.cold_ref, bf16[16,16,256]{2,1,0:T(8,128)(2,1)S(1)} %dynamic-slice_bitcast_fusion.hot_ref, s32[1,1024]{1,0:T(1,128)S(1)} %shard_map.84.col_ref, ...), custom_call_target="tpu_custom_call" | custom-call | tf_op jit(solution)/shard_map/pallas_call | solution.py:216
  56.4 12.5 %all_to_all.35.stats_ref = f32[8,2,1024]{2,1,0:T(2,128)S(1)} all-to-all(f32[8,2,1024]{2,1,0:T(2,128)S(1)} %shard_map.85), channel_id=1, replica_groups=mesh['z8'=2,'z4'=2,'z2'=2,'z1'=2,'yl'=2,'c'=2,'x2'=2,'x1'=2,'yh'=2] {'c'..., dimensions={0} | all-to-all | bytes 131072 | tf_op jit(solution)/shard_map/all_to_all | solution.py:222
  68.9 5.6 %shard_map.86 = (f32[512,256]{1,0:T(8,128)S(1)}, bf16[512,256]{1,0:T(8,128)(2,1)S(1)}, bf16[16,144,256]{2,1,0:T(8,128)(2,1)}, f32[1,128]{1,0:T(1,128)}) custom-call(s32[1]{0:T(128)} %bitcast.me_ref, bf16[16,128,256]{2,1,0:T(8,128)(2,1)S(1)} %all-to-all-done.1.cold_ref, bf16[16,16,256]{2,1,0:T(8,128)(2,1)S(1)} %dynamic-slice_bitcast_fusion.hot_ref, ...), custom_call_target="tpu_custom_call" | custom-call | tf_op jit(solution)/shard_map/pallas_call | solution.py:223
  74.5 3.8 %all-to-all-start.3 = ((bf16[16,144,256]{2,1,0:T(8,128)(2,1)}), bf16[16,144,256]{2,1,0:T(8,128)(2,1)S(1)}, u32[]{:S(2)}, u32[]{:S(2)}) async-start(bf16[16,144,256]{2,1,0:T(8,128)(2,1)} %get-tuple-element.22), calls=%async_computation.3 | async-start | bytes 2359296 | tf_op jit(solution)/shard_map/all_to_all | solution.py:236
  78.3 2.6 %collective-permute-start.3 = (bf16[512,256]{1,0:T(8,128)(2,1)S(1)}, bf16[512,256]{1,0:T(8,128)(2,1)S(1)}, u32[]{:S(2)}, u32[]{:S(2)}) collective-permute-start(bf16[512,256]{1,0:T(8,128)(2,1)S(1)} %get-tuple-element.21), channel_id=1, source_target_pairs={{0,8},{8,0},{1,9},{9,1},{2,10},{10,2},{3,11},{11,3},{4,12},{12,4},... | collective-permute-start | bytes 786440 | tf_op jit(solution)/shard_map/ppermute | solution.py:30
  80.9 1.1 collective-permute-done.3
  82.1 2.2 %collective-permute-start.6 = (bf16[128,256]{1,0:T(8,128)(2,1)S(1)}, bf16[128,256]{1,0:T(8,128)(2,1)S(1)}, u32[]{:S(2)}, u32[]{:S(2)}) collective-permute-start(bf16[128,256]{1,0:T(8,128)(2,1)S(1)} %get-tuple-element.30), channel_id=1, source_target_pairs={{0,96},{32,64},{64,32},{96,0},{1,97},{33,65},{65,33},{97,1},{2,98}... | collective-permute-start | bytes 196616 | tf_op jit(solution)/shard_map/ppermute | solution.py:240
  84.3 2.9 %collective-permute-start.5 = (bf16[128,256]{1,0:T(8,128)(2,1)S(1)}, bf16[128,256]{1,0:T(8,128)(2,1)S(1)}, u32[]{:S(2)}, u32[]{:S(2)}) collective-permute-start(bf16[128,256]{1,0:T(8,128)(2,1)S(1)} %get-tuple-element.31), channel_id=1, source_target_pairs={{0,64},{64,0},{1,65},{65,1},{2,66},{66,2},{3,67},{67,3},{4,68},{68... | collective-permute-start | bytes 196616 | tf_op jit(solution)/shard_map/ppermute | solution.py:30
  87.2 4.2 %collective-permute-start.4 = (bf16[128,256]{1,0:T(8,128)(2,1)S(1)}, bf16[128,256]{1,0:T(8,128)(2,1)S(1)}, u32[]{:S(2)}, u32[]{:S(2)}) collective-permute-start(bf16[128,256]{1,0:T(8,128)(2,1)S(1)} %get-tuple-element.32), channel_id=1, source_target_pairs={{0,32},{32,0},{1,33},{33,1},{2,34},{34,2},{3,35},{35,3},{4,36},{36... | collective-permute-start | bytes 196616 | tf_op jit(solution)/shard_map/ppermute | solution.py:30
  91.4 1.0 collective-permute-done.5
  92.5 1.1 collective-permute-done.4
  93.6 3.8 %all-to-all-done.3 = bf16[16,144,256]{2,1,0:T(8,128)(2,1)S(1)} async-done(((bf16[16,144,256]{2,1,0:T(8,128)(2,1)}), bf16[16,144,256]{2,1,0:T(8,128)(2,1)S(1)}, u32[]{:S(2)}, u32[]{:S(2)}) %all-to-all-start.3) | async-done | bytes 1179680 | tf_op jit(solution)/shard_map/all_to_all | solution.py:236
  97.5 17.0 %all_to_all.36 = bf16[4,48,256]{2,1,0:T(8,128)(2,1)S(1)} all-to-all(bf16[4,48,256]{2,1,0:T(8,128)(2,1)S(1)} %pad_maximum_fusion.1), channel_id=1, replica_groups=mesh['z8'=2,'z4'=2,'z2'=2,'z1'=2,'yl'=2,'c'=2,'x2'=2,'x1'=2,'yh'=2] {'z8..., dimensions={0} | all-to-all | bytes 196608 | tf_op jit(solution)/shard_map/all_to_all | solution.py:246
  114.6 6.9 %all_to_all.37 = bf16[4,16,256]{2,1,0:T(8,128)(2,1)S(1)} all-to-all(bf16[4,16,256]{2,1,0:T(8,128)(2,1)S(1)} %broadcast_in_dim.15), channel_id=1, replica_groups=mesh['z8'=2,'z4'=2,'z2'=2,'z1'=2,'yl'=2,'c'=2,'x2'=2,'x1'=2,'yh'=2] {'z2..., dimensions={0} | all-to-all | bytes 65536 | tf_op jit(solution)/shard_map/all_to_all | solution.py:26
  121.5 13.0 %all_to_all.38 = bf16[16,64,256]{2,1,0:T(8,128)(2,1)S(1)} all-to-all(bf16[16,64,256]{2,1,0:T(8,128)(2,1)S(1)} %broadcast_in_dim.17), channel_id=1, replica_groups=mesh['z8'=2,'z4'=2,'z2'=2,'z1'=2,'yl'=2,'c'=2,'x2'=2,'x1'=2,'yh'=2] {'yl..., dimensions={0} | all-to-all | bytes 1048576 | tf_op jit(solution)/shard_map/all_to_all | solution.py:26
  134.5 8.2 %collective-permute-start.7 = (bf16[1024,256]{1,0:T(8,128)(2,1)S(1)}, bf16[1024,256]{1,0:T(8,128)(2,1)S(1)}, u32[]{:S(2)}, u32[]{:S(2)}) collective-permute-start(bf16[1024,256]{1,0:T(8,128)(2,1)S(1)} %bitcast.14), channel_id=1, source_target_pairs={{0,8},{8,0},{1,9},{9,1},{2,10},{10,2},{3,11},{11,3},{4,12},{12,4},... | collective-permute-start | bytes 1572872 | tf_op jit(solution)/shard_map/ppermute | solution.py:30
  142.6 0.7 fusion
  143.3 0.6 slice.43
  143.9 0.2 collective-permute-done.7.other_ref
  144.1 1.0 shard_map.87
  (26 shorter events, 0.4 us)
Async XLA Ops:
  0.6 51.0 %copy-start = (bf16[2048,256]{1,0:T(8,128)(2,1)S(1)}, bf16[2048,256]{1,0:T(8,128)(2,1)}, u32[]{:S(2)}) copy-start(bf16[2048,256]{1,0:T(8,128)(2,1)} %param.6) | copy-start | bytes 3145732
  2.1 28.1 %all-to-all-start = ((bf16[4,32,256]{2,1,0:T(8,128)(2,1)}), bf16[4,32,256]{2,1,0:T(8,128)(2,1)S(1)}, u32[]{:S(2)}, u32[]{:S(2)}) async-start(bf16[4,32,256]{2,1,0:T(8,128)(2,1)} %broadcast_in_dim.12), calls=%async_computation | async-start | bytes 131072 | tf_op jit(solution)/shard_map/all_to_all | solution.py:26
  17.7 5.2 %collective-permute-start = (bf16[128,256]{1,0:T(8,128)(2,1)}, bf16[128,256]{1,0:T(8,128)(2,1)S(1)}, u32[]{:S(2)}, u32[]{:S(2)}) collective-permute-start(bf16[128,256]{1,0:T(8,128)(2,1)} %param.5), channel_id=1, source_target_pairs={{0,32},{32,0},{1,33},{33,1},{2,34},{34,2},{3,35},{35,3},{4,36},{36... | collective-permute-start | bytes 196616 | tf_op jit(solution)/shard_map/ppermute | solution.py:30
  31.3 6.9 %copy-start.3 = (bf16[128,256]{1,0:T(8,128)(2,1)S(1)}, bf16[128,256]{1,0:T(8,128)(2,1)}, u32[]{:S(2)}) copy-start(bf16[128,256]{1,0:T(8,128)(2,1)} %param.5) | copy-start | bytes 196612
  31.3 9.6 %copy-start.1 = (s32[65536]{0:T(1024)S(1)}, s32[65536]{0:T(1024)}, u32[]{:S(2)}) copy-start(s32[65536]{0:T(1024)} %param.9) | copy-start | bytes 786436
  31.3 9.6 %copy-start.2 = (s32[2048]{0:T(1024)S(1)}, s32[2048]{0:T(1024)}, u32[]{:S(2)}) copy-start(s32[2048]{0:T(1024)} %param.8) | copy-start | bytes 24580
  31.3 21.5 %all-to-all-start.1 = ((bf16[16,128,256]{2,1,0:T(8,128)(2,1)}), bf16[16,128,256]{2,1,0:T(8,128)(2,1)S(1)}, u32[]{:S(2)}, u32[]{:S(2)}) async-start(bf16[16,128,256]{2,1,0:T(8,128)(2,1)} %broadcast_in_dim.13), calls=%async_computation.1 | async-start | bytes 2097152 | tf_op jit(solution)/shard_map/all_to_all | solution.py:26
  38.2 8.7 %collective-permute-start.1 = (bf16[256,256]{1,0:T(8,128)(2,1)S(1)}, bf16[256,256]{1,0:T(8,128)(2,1)S(1)}, u32[]{:S(2)}, u32[]{:S(2)}) collective-permute-start(bf16[256,256]{1,0:T(8,128)(2,1)S(1)} %pad_maximum_fusion), channel_id=1, source_target_pairs={{0,64},{64,0},{1,65},{65,1},{2,66},{66,2},{3,67},{67,3},{4,68},{68... | collective-permute-start | bytes 393224 | tf_op jit(solution)/shard_map/ppermute | solution.py:30
  47.0 5.8 %collective-permute-start.2 = (bf16[512,256]{1,0:T(8,128)(2,1)S(1)}, bf16[512,256]{1,0:T(8,128)(2,1)S(1)}, u32[]{:S(2)}, u32[]{:S(2)}) collective-permute-start(bf16[512,256]{1,0:T(8,128)(2,1)S(1)} %constant_dynamic-update-slice_fusion.refs_0_), channel_id=1, source_target_pairs={{0,8},{8,0},{1,9},{9,1},{2,10},{10,2},{3,11},{11,3},{4,12},{12,4},... | collective-permute-start | bytes 786440 | tf_op jit(solution)/shard_map/ppermute | solution.py:30
  74.5 22.9 %all-to-all-start.3 = ((bf16[16,144,256]{2,1,0:T(8,128)(2,1)}), bf16[16,144,256]{2,1,0:T(8,128)(2,1)S(1)}, u32[]{:S(2)}, u32[]{:S(2)}) async-start(bf16[16,144,256]{2,1,0:T(8,128)(2,1)} %get-tuple-element.22), calls=%async_computation.3 | async-start | bytes 2359296 | tf_op jit(solution)/shard_map/all_to_all | solution.py:236
  78.3 3.7 %collective-permute-start.3 = (bf16[512,256]{1,0:T(8,128)(2,1)S(1)}, bf16[512,256]{1,0:T(8,128)(2,1)S(1)}, u32[]{:S(2)}, u32[]{:S(2)}) collective-permute-start(bf16[512,256]{1,0:T(8,128)(2,1)S(1)} %get-tuple-element.21), channel_id=1, source_target_pairs={{0,8},{8,0},{1,9},{9,1},{2,10},{10,2},{3,11},{11,3},{4,12},{12,4},... | collective-permute-start | bytes 786440 | tf_op jit(solution)/shard_map/ppermute | solution.py:30
  82.1 9.3 %collective-permute-start.6 = (bf16[128,256]{1,0:T(8,128)(2,1)S(1)}, bf16[128,256]{1,0:T(8,128)(2,1)S(1)}, u32[]{:S(2)}, u32[]{:S(2)}) collective-permute-start(bf16[128,256]{1,0:T(8,128)(2,1)S(1)} %get-tuple-element.30), channel_id=1, source_target_pairs={{0,96},{32,64},{64,32},{96,0},{1,97},{33,65},{65,33},{97,1},{2,98}... | collective-permute-start | bytes 196616 | tf_op jit(solution)/shard_map/ppermute | solution.py:240
  84.3 8.2 %collective-permute-start.5 = (bf16[128,256]{1,0:T(8,128)(2,1)S(1)}, bf16[128,256]{1,0:T(8,128)(2,1)S(1)}, u32[]{:S(2)}, u32[]{:S(2)}) collective-permute-start(bf16[128,256]{1,0:T(8,128)(2,1)S(1)} %get-tuple-element.31), channel_id=1, source_target_pairs={{0,64},{64,0},{1,65},{65,1},{2,66},{66,2},{3,67},{67,3},{4,68},{68... | collective-permute-start | bytes 196616 | tf_op jit(solution)/shard_map/ppermute | solution.py:30
  87.2 6.3 %collective-permute-start.4 = (bf16[128,256]{1,0:T(8,128)(2,1)S(1)}, bf16[128,256]{1,0:T(8,128)(2,1)S(1)}, u32[]{:S(2)}, u32[]{:S(2)}) collective-permute-start(bf16[128,256]{1,0:T(8,128)(2,1)S(1)} %get-tuple-element.32), channel_id=1, source_target_pairs={{0,32},{32,0},{1,33},{33,1},{2,34},{34,2},{3,35},{35,3},{4,36},{36... | collective-permute-start | bytes 196616 | tf_op jit(solution)/shard_map/ppermute | solution.py:30
  134.5 9.7 %collective-permute-start.7 = (bf16[1024,256]{1,0:T(8,128)(2,1)S(1)}, bf16[1024,256]{1,0:T(8,128)(2,1)S(1)}, u32[]{:S(2)}, u32[]{:S(2)}) collective-permute-start(bf16[1024,256]{1,0:T(8,128)(2,1)S(1)} %bitcast.14), channel_id=1, source_target_pairs={{0,8},{8,0},{1,9},{9,1},{2,10},{10,2},{3,11},{11,3},{4,12},{12,4},... | collective-permute-start | bytes 1572872 | tf_op jit(solution)/shard_map/ppermute | solution.py:30

commit v8 on v7

--- a/solution.py
+++ b/solution.py
@@ -238,8 +238,7 @@
     sends = keep.astype(BF)
     others = [swap(sends[1], "z1"), swap(sends[2], "z2")]
     others.append(lax.ppermute(sends[3], ("z2", "z1"), [(i, 3 - i) for i in range(4)]))
-    near, *others = lax.optimization_barrier((near, *others))
-    grad_queries = (keep[0] + sum(x.astype(F32) for x in others)).astype(BF)
+    near, others[0] = lax.optimization_barrier((near, others[0]))
     near = jnp.sum(near.astype(F32), axis=0).astype(BF)
     cold_part = near[: NF * shard].reshape(NF, shard, width)
     hot_part = jnp.broadcast_to(near[None, NF * shard :], (NF, hot_own, width))
@@ -248,6 +247,8 @@
     grad_cold = far[:shard]
     grad_hot = spread(far[shard:], HALF).reshape(-1, width)
     grad_hot = spread(grad_hot, NEAR)
+    grad_hot, *others = lax.optimization_barrier((grad_hot, *others))
+    grad_queries = (keep[0] + sum(x.astype(F32) for x in others)).astype(BF)
     grad_hot = grad_hot.reshape(hot // 2, width)
     grad_hot = pl.pallas_call(
         place_kernel,

time: 146 us -> 148 us (1.014)
  blocking collectives: 49.3 us -> 36.2 us
  waiting for transfers between devices: 22 us -> 31.7 us
  starting transfers between devices: 56.3 us -> 58.9 us
  other arithmetic: 0.94 us -> 2.65 us
    all_to_all x2 -> x1, blocking collectives: 19.9 us -> 6.86 us  [spread(): return lax.all_to_all(jnp.broadcast_to(x[None], (n, *x.shape)), axes, 0, 0)]
    all_to_all x1, waiting for transfers between devices: 3.76 us -> 9.1 us  [body(): near = lax.all_to_all(item_part, NEAR, 0, 0)]
    all_to_all x2 -> x3, starting transfers between devices: 22.5 us -> 26.9 us  [spread(): return lax.all_to_all(jnp.broadcast_to(x[None], (n, *x.shape)), axes, 0, 0)]
    ppermute x7, waiting for transfers between devices: 10.9 us -> 13.9 us  [swap(): return lax.ppermute(x, axis, [(0, 1), (1, 0)])]
    ppermute x7, starting transfers between devices: 27.8 us -> 25.9 us  [swap(): return lax.ppermute(x, axis, [(0, 1), (1, 0)])]
    all_to_all x2 -> x3, waiting for transfers between devices: 7.29 us -> 7.3 us  [spread(): return lax.all_to_all(jnp.broadcast_to(x[None], (n, *x.shape)), axes, 0, 0)]
  transfers between devices with their start and end apart: 11 -> 12, of which waited for: 9 -> 9; matrix products, arithmetic and copies ran while one was open for 1% -> 2% of each run, Pallas kernels for 2% -> 2%
where the time goes in v8:
time: 148 us; the launch traced here: 147 us
  starting transfers between devices  58.9 us (40%)
  blocking collectives  36.2 us (24%)
  waiting for transfers between devices  31.7 us (21%)
  Pallas kernels  12.4 us (8%)
  local copies, waits for them, and re-layouts  4.05 us (3%)
  other arithmetic  2.65 us (2%)
    all_to_all x3, starting transfers between devices, spread(): return lax.all_to_all(jnp.broadcast_to(x[None], (n, *x.shape)), axes, 0, 0)  26.9 us
    ppermute x7, starting transfers between devices, swap(): return lax.ppermute(x, axis, [(0, 1), (1, 0)])  25.9 us
    all_to_all x1, blocking collectives, body(): lax.all_to_all(jnp.concatenate([cold_part, hot_part], axis=1), FAR, 0, 0)  16.9 us
    ppermute x7, waiting for transfers between devices, swap(): return lax.ppermute(x, axis, [(0, 1), (1, 0)])  13.9 us
    all_to_all x1, blocking collectives, body(): stats = lax.all_to_all(stats, COLS, 0, 0)  12.5 us
    all_to_all x1, waiting for transfers between devices, body(): near = lax.all_to_all(item_part, NEAR, 0, 0)  9.1 us
    all_to_all x3, waiting for transfers between devices, spread(): return lax.all_to_all(jnp.broadcast_to(x[None], (n, *x.shape)), axes, 0, 0)  7.3 us
    all_to_all x1, blocking collectives, spread(): return lax.all_to_all(jnp.broadcast_to(x[None], (n, *x.shape)), axes, 0, 0)  6.86 us
  transfers between devices with their start and end apart: 12, of which 9 were waited for; matrix products, arithmetic and copies ran while one was open for 2% of the time, Pallas kernels for 2%

profile of v8, /device:TPU:1, one launch (start us, length us, event | category | flops | bytes accessed | tf_op | source)
XLA Modules:
  0.0 146.8 jit_solution(13915251709010604744)
XLA Ops:
  0.6 1.4 broadcast_in_dim.12
  2.1 15.6 %all-to-all-start = ((bf16[4,32,256]{2,1,0:T(8,128)(2,1)}), bf16[4,32,256]{2,1,0:T(8,128)(2,1)S(1)}, u32[]{:S(2)}, u32[]{:S(2)}) async-start(bf16[4,32,256]{2,1,0:T(8,128)(2,1)} %broadcast_in_dim.12), calls=%async_computation | async-start | bytes 131072 | tf_op jit(solution)/shard_map/all_to_all | solution.py:26
  17.7 2.6 %collective-permute-start = (bf16[128,256]{1,0:T(8,128)(2,1)}, bf16[128,256]{1,0:T(8,128)(2,1)S(1)}, u32[]{:S(2)}, u32[]{:S(2)}) collective-permute-start(bf16[128,256]{1,0:T(8,128)(2,1)} %param.5), channel_id=1, source_target_pairs={{0,32},{32,0},{1,33},{33,1},{2,34},{34,2},{3,35},{35,3},{4,36},{36... | collective-permute-start | bytes 196616 | tf_op jit(solution)/shard_map/ppermute | solution.py:30
  20.4 2.6 %collective-permute-done = bf16[128,256]{1,0:T(8,128)(2,1)S(1)} collective-permute-done((bf16[128,256]{1,0:T(8,128)(2,1)}, bf16[128,256]{1,0:T(8,128)(2,1)S(1)}, u32[]{:S(2)}, u32[]{:S(2)}) %collective-permute-start) | collective-permute-done | bytes 65568 | tf_op jit(solution)/shard_map/ppermute | solution.py:30
  22.9 7.3 %all-to-all-done = bf16[4,32,256]{2,1,0:T(8,128)(2,1)S(1)} async-done(((bf16[4,32,256]{2,1,0:T(8,128)(2,1)}), bf16[4,32,256]{2,1,0:T(8,128)(2,1)S(1)}, u32[]{:S(2)}, u32[]{:S(2)}) %all-to-all-start) | async-done | bytes 65568 | tf_op jit(solution)/shard_map/all_to_all | solution.py:26
  30.2 1.1 broadcast_in_dim.13
  31.3 6.9 %all-to-all-start.1 = ((bf16[16,128,256]{2,1,0:T(8,128)(2,1)}), bf16[16,128,256]{2,1,0:T(8,128)(2,1)S(1)}, u32[]{:S(2)}, u32[]{:S(2)}) async-start(bf16[16,128,256]{2,1,0:T(8,128)(2,1)} %broadcast_in_dim.13), calls=%async_computation.1 | async-start | bytes 2097152 | tf_op jit(solution)/shard_map/all_to_all | solution.py:26
  38.2 2.7 %collective-permute-start.1 = (bf16[256,256]{1,0:T(8,128)(2,1)S(1)}, bf16[256,256]{1,0:T(8,128)(2,1)S(1)}, u32[]{:S(2)}, u32[]{:S(2)}) collective-permute-start(bf16[256,256]{1,0:T(8,128)(2,1)S(1)} %pad_maximum_fusion), channel_id=1, source_target_pairs={{0,64},{64,0},{1,65},{65,1},{2,66},{66,2},{3,67},{67,3},{4,68},{68... | collective-permute-start | bytes 393224 | tf_op jit(solution)/shard_map/ppermute | solution.py:30
  40.9 2.2 %shard_map.84.col_ref = s32[1,1024]{1,0:T(1,128)S(1)} custom-call(s32[1]{0:T(128)} %bitcast.me_ref, s32[16,128]{1,0:T(8,128)S(1)} %bitcast.17, s32[512,1,128]{2,1,0:T(1,128)S(1)} %bitcast.16), custom_call_target="tpu_custom_call" | custom-call | flops 12582912 | bytes 1048576 | tf_op jit(solution)/shard_map/pallas_call | solution.py:194
  43.2 3.8 %collective-permute-done.1 = bf16[256,256]{1,0:T(8,128)(2,1)S(1)} collective-permute-done((bf16[256,256]{1,0:T(8,128)(2,1)S(1)}, bf16[256,256]{1,0:T(8,128)(2,1)S(1)}, u32[]{:S(2)}, u32[]{:S(2)}) %collective-permute-start.1) | collective-permute-done | bytes 131104 | tf_op jit(solution)/shard_map/ppermute | solution.py:30
  47.0 4.7 %collective-permute-start.2 = (bf16[512,256]{1,0:T(8,128)(2,1)S(1)}, bf16[512,256]{1,0:T(8,128)(2,1)S(1)}, u32[]{:S(2)}, u32[]{:S(2)}) collective-permute-start(bf16[512,256]{1,0:T(8,128)(2,1)S(1)} %constant_dynamic-update-slice_fusion.refs_0_), channel_id=1, source_target_pairs={{0,8},{8,0},{1,9},{9,1},{2,10},{10,2},{3,11},{11,3},{4,12},{12,4},... | collective-permute-start | bytes 786440 | tf_op jit(solution)/shard_map/ppermute | solution.py:30
  51.7 1.1 collective-permute-done.2.refs_1_
  52.8 3.6 %shard_map.85 = f32[8,2,1024]{2,1,0:T(2,128)S(1)} custom-call(s32[1]{0:T(128)} %bitcast.me_ref, bf16[16,128,256]{2,1,0:T(8,128)(2,1)S(1)} %all-to-all-done.1.cold_ref, bf16[16,16,256]{2,1,0:T(8,128)(2,1)S(1)} %dynamic-slice_bitcast_fusion.hot_ref, s32[1,1024]{1,0:T(1,128)S(1)} %shard_map.84.col_ref, ...), custom_call_target="tpu_custom_call" | custom-call | tf_op jit(solution)/shard_map/pallas_call | solution.py:216
  56.4 12.5 %all_to_all.35.stats_ref = f32[8,2,1024]{2,1,0:T(2,128)S(1)} all-to-all(f32[8,2,1024]{2,1,0:T(2,128)S(1)} %shard_map.85), channel_id=1, replica_groups=mesh['z8'=2,'z4'=2,'z2'=2,'z1'=2,'yl'=2,'c'=2,'x2'=2,'x1'=2,'yh'=2] {'c'..., dimensions={0} | all-to-all | bytes 131072 | tf_op jit(solution)/shard_map/all_to_all | solution.py:222
  68.9 5.6 %shard_map.86 = (f32[512,256]{1,0:T(8,128)S(1)}, bf16[512,256]{1,0:T(8,128)(2,1)S(1)}, bf16[16,144,256]{2,1,0:T(8,128)(2,1)}, f32[1,128]{1,0:T(1,128)}) custom-call(s32[1]{0:T(128)} %bitcast.me_ref, bf16[16,128,256]{2,1,0:T(8,128)(2,1)S(1)} %all-to-all-done.1.cold_ref, bf16[16,16,256]{2,1,0:T(8,128)(2,1)S(1)} %dynamic-slice_bitcast_fusion.hot_ref, ...), custom_call_target="tpu_custom_call" | custom-call | tf_op jit(solution)/shard_map/pallas_call | solution.py:223
  74.5 3.8 %all-to-all-start.3 = ((bf16[16,144,256]{2,1,0:T(8,128)(2,1)}), bf16[16,144,256]{2,1,0:T(8,128)(2,1)S(1)}, u32[]{:S(2)}, u32[]{:S(2)}) async-start(bf16[16,144,256]{2,1,0:T(8,128)(2,1)} %get-tuple-element.24), calls=%async_computation.3 | async-start | bytes 2359296 | tf_op jit(solution)/shard_map/all_to_all | solution.py:236
  78.3 2.6 %collective-permute-start.3 = (bf16[512,256]{1,0:T(8,128)(2,1)S(1)}, bf16[512,256]{1,0:T(8,128)(2,1)S(1)}, u32[]{:S(2)}, u32[]{:S(2)}) collective-permute-start(bf16[512,256]{1,0:T(8,128)(2,1)S(1)} %get-tuple-element.23), channel_id=1, source_target_pairs={{0,8},{8,0},{1,9},{9,1},{2,10},{10,2},{3,11},{11,3},{4,12},{12,4},... | collective-permute-start | bytes 786440 | tf_op jit(solution)/shard_map/ppermute | solution.py:30
  80.9 1.1 collective-permute-done.3
  82.0 0.9 fusion.1
  82.9 2.0 %collective-permute-start.4 = (bf16[128,256]{1,0:T(8,128)(2,1)S(1)}, bf16[128,256]{1,0:T(8,128)(2,1)S(1)}, u32[]{:S(2)}, u32[]{:S(2)}) collective-permute-start(bf16[128,256]{1,0:T(8,128)(2,1)S(1)} %get-tuple-element.36), channel_id=1, source_target_pairs={{0,32},{32,0},{1,33},{33,1},{2,34},{34,2},{3,35},{35,3},{4,36},{36... | collective-permute-start | bytes 196616 | tf_op jit(solution)/shard_map/ppermute | solution.py:30
  84.9 3.3 %collective-permute-done.4 = bf16[128,256]{1,0:T(8,128)(2,1)S(1)} collective-permute-done((bf16[128,256]{1,0:T(8,128)(2,1)S(1)}, bf16[128,256]{1,0:T(8,128)(2,1)S(1)}, u32[]{:S(2)}, u32[]{:S(2)}) %collective-permute-start.4) | collective-permute-done | bytes 65568 | tf_op jit(solution)/shard_map/ppermute | solution.py:30
  88.2 9.1 %all-to-all-done.3 = bf16[16,144,256]{2,1,0:T(8,128)(2,1)S(1)} async-done(((bf16[16,144,256]{2,1,0:T(8,128)(2,1)}), bf16[16,144,256]{2,1,0:T(8,128)(2,1)S(1)}, u32[]{:S(2)}, u32[]{:S(2)}) %all-to-all-start.3) | async-done | bytes 1179680 | tf_op jit(solution)/shard_map/all_to_all | solution.py:236
  97.5 16.9 %all_to_all.36 = bf16[4,48,256]{2,1,0:T(8,128)(2,1)S(1)} all-to-all(bf16[4,48,256]{2,1,0:T(8,128)(2,1)S(1)} %pad_maximum_fusion.1), channel_id=1, replica_groups=mesh['z8'=2,'z4'=2,'z2'=2,'z1'=2,'yl'=2,'c'=2,'x2'=2,'x1'=2,'yh'=2] {'z8..., dimensions={0} | all-to-all | bytes 196608 | tf_op jit(solution)/shard_map/all_to_all | solution.py:245
  114.5 6.9 %all_to_all.37 = bf16[4,16,256]{2,1,0:T(8,128)(2,1)S(1)} all-to-all(bf16[4,16,256]{2,1,0:T(8,128)(2,1)S(1)} %broadcast_in_dim.15), channel_id=1, replica_groups=mesh['z8'=2,'z4'=2,'z2'=2,'z1'=2,'yl'=2,'c'=2,'x2'=2,'x1'=2,'yh'=2] {'z2..., dimensions={0} | all-to-all | bytes 65536 | tf_op jit(solution)/shard_map/all_to_all | solution.py:26
  122.2 4.4 %all-to-all-start.6 = ((bf16[16,64,256]{2,1,0:T(8,128)(2,1)}), bf16[16,64,256]{2,1,0:T(8,128)(2,1)S(1)}, u32[]{:S(2)}, u32[]{:S(2)}) async-start(bf16[16,64,256]{2,1,0:T(8,128)(2,1)} %broadcast_in_dim.17), calls=%async_computation.6 | async-start | bytes 1048576 | tf_op jit(solution)/shard_map/all_to_all | solution.py:26
  126.6 2.3 %collective-permute-start.6 = (bf16[128,256]{1,0:T(8,128)(2,1)S(1)}, bf16[128,256]{1,0:T(8,128)(2,1)S(1)}, u32[]{:S(2)}, u32[]{:S(2)}) collective-permute-start(bf16[128,256]{1,0:T(8,128)(2,1)S(1)} %get-tuple-element.34), channel_id=1, source_target_pairs={{0,96},{32,64},{64,32},{96,0},{1,97},{33,65},{65,33},{97,1},{2,98}... | collective-permute-start | bytes 196616 | tf_op jit(solution)/shard_map/ppermute | solution.py:240
  128.9 3.2 %collective-permute-start.5 = (bf16[128,256]{1,0:T(8,128)(2,1)S(1)}, bf16[128,256]{1,0:T(8,128)(2,1)S(1)}, u32[]{:S(2)}, u32[]{:S(2)}) collective-permute-start(bf16[128,256]{1,0:T(8,128)(2,1)S(1)} %get-tuple-element.35), channel_id=1, source_target_pairs={{0,64},{64,0},{1,65},{65,1},{2,66},{66,2},{3,67},{67,3},{4,68},{68... | collective-permute-start | bytes 196616 | tf_op jit(solution)/shard_map/ppermute | solution.py:30
  132.1 1.3 collective-permute-done.6
  133.4 2.1 %collective-permute-done.5 = bf16[128,256]{1,0:T(8,128)(2,1)S(1)} collective-permute-done((bf16[128,256]{1,0:T(8,128)(2,1)S(1)}, bf16[128,256]{1,0:T(8,128)(2,1)S(1)}, u32[]{:S(2)}, u32[]{:S(2)}) %collective-permute-start.5) | collective-permute-done | bytes 65568 | tf_op jit(solution)/shard_map/ppermute | solution.py:30
  135.5 8.1 %collective-permute-start.7 = (bf16[1024,256]{1,0:T(8,128)(2,1)S(1)}, bf16[1024,256]{1,0:T(8,128)(2,1)S(1)}, u32[]{:S(2)}, u32[]{:S(2)}) collective-permute-start(bf16[1024,256]{1,0:T(8,128)(2,1)S(1)} %bitcast.14), channel_id=1, source_target_pairs={{0,8},{8,0},{1,9},{9,1},{2,10},{10,2},{3,11},{11,3},{4,12},{12,4},... | collective-permute-start | bytes 1572872 | tf_op jit(solution)/shard_map/ppermute | solution.py:30
  144.2 1.6 %fusion = bf16[128,256]{1,0:T(8,128)(2,1)} fusion(f32[512,256]{1,0:T(8,128)} %get-tuple-element.33, bf16[128,256]{1,0:T(8,128)(2,1)S(1)} %collective-permute-done.6, bf16[128,256]{1,0:T(8,128)(2,1)S(1)} %collective-permute-done.5, bf16[128,256]{1,0:T(8,128)(2,1)S(1)} %collective-permute-done.4), kind=kLoop, calls=%fused_computation.2 | loop fusion | flops 229376 | bytes 393216 | tf_op jit(solution)/shard_map/convert_element_type | solution.py:251
  145.8 1.0 shard_map.87
  (27 shorter events, 1.7 us)
Async XLA Ops:
  0.6 51.0 %copy-start = (bf16[2048,256]{1,0:T(8,128)(2,1)S(1)}, bf16[2048,256]{1,0:T(8,128)(2,1)}, u32[]{:S(2)}) copy-start(bf16[2048,256]{1,0:T(8,128)(2,1)} %param.6) | copy-start | bytes 3145732
  2.1 28.1 %all-to-all-start = ((bf16[4,32,256]{2,1,0:T(8,128)(2,1)}), bf16[4,32,256]{2,1,0:T(8,128)(2,1)S(1)}, u32[]{:S(2)}, u32[]{:S(2)}) async-start(bf16[4,32,256]{2,1,0:T(8,128)(2,1)} %broadcast_in_dim.12), calls=%async_computation | async-start | bytes 131072 | tf_op jit(solution)/shard_map/all_to_all | solution.py:26
  17.7 5.2 %collective-permute-start = (bf16[128,256]{1,0:T(8,128)(2,1)}, bf16[128,256]{1,0:T(8,128)(2,1)S(1)}, u32[]{:S(2)}, u32[]{:S(2)}) collective-permute-start(bf16[128,256]{1,0:T(8,128)(2,1)} %param.5), channel_id=1, source_target_pairs={{0,32},{32,0},{1,33},{33,1},{2,34},{34,2},{3,35},{35,3},{4,36},{36... | collective-permute-start | bytes 196616 | tf_op jit(solution)/shard_map/ppermute | solution.py:30
  31.3 6.9 %copy-start.3 = (bf16[128,256]{1,0:T(8,128)(2,1)S(1)}, bf16[128,256]{1,0:T(8,128)(2,1)}, u32[]{:S(2)}) copy-start(bf16[128,256]{1,0:T(8,128)(2,1)} %param.5) | copy-start | bytes 196612
  31.3 9.6 %copy-start.1 = (s32[65536]{0:T(1024)S(1)}, s32[65536]{0:T(1024)}, u32[]{:S(2)}) copy-start(s32[65536]{0:T(1024)} %param.9) | copy-start | bytes 786436
  31.3 9.6 %copy-start.2 = (s32[2048]{0:T(1024)S(1)}, s32[2048]{0:T(1024)}, u32[]{:S(2)}) copy-start(s32[2048]{0:T(1024)} %param.8) | copy-start | bytes 24580
  31.3 21.5 %all-to-all-start.1 = ((bf16[16,128,256]{2,1,0:T(8,128)(2,1)}), bf16[16,128,256]{2,1,0:T(8,128)(2,1)S(1)}, u32[]{:S(2)}, u32[]{:S(2)}) async-start(bf16[16,128,256]{2,1,0:T(8,128)(2,1)} %broadcast_in_dim.13), calls=%async_computation.1 | async-start | bytes 2097152 | tf_op jit(solution)/shard_map/all_to_all | solution.py:26
  38.2 8.7 %collective-permute-start.1 = (bf16[256,256]{1,0:T(8,128)(2,1)S(1)}, bf16[256,256]{1,0:T(8,128)(2,1)S(1)}, u32[]{:S(2)}, u32[]{:S(2)}) collective-permute-start(bf16[256,256]{1,0:T(8,128)(2,1)S(1)} %pad_maximum_fusion), channel_id=1, source_target_pairs={{0,64},{64,0},{1,65},{65,1},{2,66},{66,2},{3,67},{67,3},{4,68},{68... | collective-permute-start | bytes 393224 | tf_op jit(solution)/shard_map/ppermute | solution.py:30
  47.0 5.8 %collective-permute-start.2 = (bf16[512,256]{1,0:T(8,128)(2,1)S(1)}, bf16[512,256]{1,0:T(8,128)(2,1)S(1)}, u32[]{:S(2)}, u32[]{:S(2)}) collective-permute-start(bf16[512,256]{1,0:T(8,128)(2,1)S(1)} %constant_dynamic-update-slice_fusion.refs_0_), channel_id=1, source_target_pairs={{0,8},{8,0},{1,9},{9,1},{2,10},{10,2},{3,11},{11,3},{4,12},{12,4},... | collective-permute-start | bytes 786440 | tf_op jit(solution)/shard_map/ppermute | solution.py:30
  74.5 22.9 %all-to-all-start.3 = ((bf16[16,144,256]{2,1,0:T(8,128)(2,1)}), bf16[16,144,256]{2,1,0:T(8,128)(2,1)S(1)}, u32[]{:S(2)}, u32[]{:S(2)}) async-start(bf16[16,144,256]{2,1,0:T(8,128)(2,1)} %get-tuple-element.24), calls=%async_computation.3 | async-start | bytes 2359296 | tf_op jit(solution)/shard_map/all_to_all | solution.py:236
  78.3 3.7 %collective-permute-start.3 = (bf16[512,256]{1,0:T(8,128)(2,1)S(1)}, bf16[512,256]{1,0:T(8,128)(2,1)S(1)}, u32[]{:S(2)}, u32[]{:S(2)}) collective-permute-start(bf16[512,256]{1,0:T(8,128)(2,1)S(1)} %get-tuple-element.23), channel_id=1, source_target_pairs={{0,8},{8,0},{1,9},{9,1},{2,10},{10,2},{3,11},{11,3},{4,12},{12,4},... | collective-permute-start | bytes 786440 | tf_op jit(solution)/shard_map/ppermute | solution.py:30
  82.9 5.3 %collective-permute-start.4 = (bf16[128,256]{1,0:T(8,128)(2,1)S(1)}, bf16[128,256]{1,0:T(8,128)(2,1)S(1)}, u32[]{:S(2)}, u32[]{:S(2)}) collective-permute-start(bf16[128,256]{1,0:T(8,128)(2,1)S(1)} %get-tuple-element.36), channel_id=1, source_target_pairs={{0,32},{32,0},{1,33},{33,1},{2,34},{34,2},{3,35},{35,3},{4,36},{36... | collective-permute-start | bytes 196616 | tf_op jit(solution)/shard_map/ppermute | solution.py:30
  122.2 13.3 %all-to-all-start.6 = ((bf16[16,64,256]{2,1,0:T(8,128)(2,1)}), bf16[16,64,256]{2,1,0:T(8,128)(2,1)S(1)}, u32[]{:S(2)}, u32[]{:S(2)}) async-start(bf16[16,64,256]{2,1,0:T(8,128)(2,1)} %broadcast_in_dim.17), calls=%async_computation.6 | async-start | bytes 1048576 | tf_op jit(solution)/shard_map/all_to_all | solution.py:26
  126.6 6.8 %collective-permute-start.6 = (bf16[128,256]{1,0:T(8,128)(2,1)S(1)}, bf16[128,256]{1,0:T(8,128)(2,1)S(1)}, u32[]{:S(2)}, u32[]{:S(2)}) collective-permute-start(bf16[128,256]{1,0:T(8,128)(2,1)S(1)} %get-tuple-element.34), channel_id=1, source_target_pairs={{0,96},{32,64},{64,32},{96,0},{1,97},{33,65},{65,33},{97,1},{2,98}... | collective-permute-start | bytes 196616 | tf_op jit(solution)/shard_map/ppermute | solution.py:240
  128.9 6.6 %collective-permute-start.5 = (bf16[128,256]{1,0:T(8,128)(2,1)S(1)}, bf16[128,256]{1,0:T(8,128)(2,1)S(1)}, u32[]{:S(2)}, u32[]{:S(2)}) collective-permute-start(bf16[128,256]{1,0:T(8,128)(2,1)S(1)} %get-tuple-element.35), channel_id=1, source_target_pairs={{0,64},{64,0},{1,65},{65,1},{2,66},{66,2},{3,67},{67,3},{4,68},{68... | collective-permute-start | bytes 196616 | tf_op jit(solution)/shard_map/ppermute | solution.py:30
  135.5 10.3 %collective-permute-start.7 = (bf16[1024,256]{1,0:T(8,128)(2,1)S(1)}, bf16[1024,256]{1,0:T(8,128)(2,1)S(1)}, u32[]{:S(2)}, u32[]{:S(2)}) collective-permute-start(bf16[1024,256]{1,0:T(8,128)(2,1)S(1)} %bitcast.14), channel_id=1, source_target_pairs={{0,8},{8,0},{1,9},{9,1},{2,10},{10,2},{3,11},{11,3},{4,12},{12,4},... | collective-permute-start | bytes 1572872 | tf_op jit(solution)/shard_map/ppermute | solution.py:30

commit v9 on v7

--- a/solution.py
+++ b/solution.py
@@ -79,7 +79,7 @@
     block = row >> 5
     near = pick(block, NEAR)
     cold_col = near // near_chunk * width + (near % near_chunk) * (NF * shard)
-    cold_col += pick(block, FAR) * shard + (row & (shard - 1))
+    cold_col += (pick(block, FAR) ^ pick(me, FAR)) * shard + (row & (shard - 1))
     hot_near = (slot >> 6) & (NG - 1)
     hot_k = ((slot >> 10) << 2) | ((slot >> 4) & 3)
     hot_col = hot_near // near_chunk * width + near_chunk * NF * shard
@@ -144,6 +144,8 @@
     acc_ref[...] = jnp.zeros_like(acc_ref)
     n = NG // CHUNKS
     cold_rows = cold_ref.shape[1]
+    shard = cold_rows // NF
+    f = pick(me_ref[0], FAR)
 
     def step(g, carry):
         table = chunk_table(cold_ref, hot_ref, g)
@@ -152,7 +154,10 @@
         w = (jnp.exp(s - logs) - jnp.where(where, 1.0, 0.0)).astype(BF)
         item = jnp.dot(w, rows, preferred_element_type=F32).astype(BF)
         wide = item.shape[-1]
-        item_ref[pl.ds(g * n, n), :cold_rows] = item[: n * cold_rows].reshape(n, -1, wide)
+        cold = item[: n * cold_rows].reshape(n, NF, shard, wide)
+        for q in range(NF):
+            there = pl.ds(pl.multiple_of((q ^ f) * shard, shard), shard)
+            item_ref[pl.ds(g * n, n), there] = cold[:, q]
         item_ref[pl.ds(g * n, n), cold_rows:] = item[n * cold_rows :].reshape(n, -1, wide)
         acc_ref[...] += lax.dot_general(table, w, TN, preferred_element_type=F32)
         return carry
@@ -202,8 +207,9 @@
         compiler_params=params,
     )(at_me, hot_ids.reshape(-1, 128), targets.reshape(-1, 1, own))
 
-    far = spread(cold_table, FAR).reshape(NF * shard, width)
-    far, rows[1] = lax.optimization_barrier((far, rows[1]))
+    far = [cold_table, swap(cold_table, "z4"), swap(cold_table, "z8")]
+    far.append(lax.ppermute(cold_table, ("z8", "z4"), [(i, 3 - i) for i in range(4)]))
+    far, rows[1] = lax.optimization_barrier((jnp.concatenate(far, axis=0), rows[1]))
     cold = spread(far, NEAR)
     rows = jnp.concatenate(rows, axis=0)
     other, column = lax.optimization_barrier((swap(rows, "z2"), column))

time: 146 us -> 149 us (1.021)
  starting transfers between devices: 56.3 us -> 64.4 us
  waiting for transfers between devices: 22 us -> 15.3 us
  blocking collectives: 49.3 us -> 51.9 us
    ppermute x7 -> x9, starting transfers between devices: 27.8 us -> 49.4 us  [swap(): return lax.ppermute(x, axis, [(0, 1), (1, 0)])]
    all_to_all x2 -> x1, starting transfers between devices: 22.5 us -> 6.89 us  [spread(): return lax.all_to_all(jnp.broadcast_to(x[None], (n, *x.shape)), axes, 0, 0)]
    all_to_all x2 -> x1, waiting for transfers between devices: 7.29 us -> 0.01 us  [spread(): return lax.all_to_all(jnp.broadcast_to(x[None], (n, *x.shape)), axes, 0, 0)]
    ppermute x0 -> x1, waiting for transfers between devices: none -> 3.99 us  [body(): lax.ppermute(cold_table, ('z8', 'z4'), [(i, 3 - i) for i in range(4)])]
    ppermute x7 -> x9, waiting for transfers between devices: 10.9 us -> 7.53 us  [swap(): return lax.ppermute(x, axis, [(0, 1), (1, 0)])]
    all_to_all x1, blocking collectives: 17 us -> 19.8 us  [body(): lax.all_to_all(jnp.concatenate([cold_part, hot_part], axis=1), FAR, 0, 0)]
    ppermute x0 -> x1, starting transfers between devices: none -> 1.92 us  [body(): lax.ppermute(cold_table, ('z8', 'z4'), [(i, 3 - i) for i in range(4)])]
  transfers between devices with their start and end apart: 11 -> 13, of which waited for: 9 -> 8; matrix products, arithmetic and copies ran while one was open for 1% -> 1% of each run, Pallas kernels for 2% -> 2%
where the time goes in v9:
time: 149 us; the launch traced here: 148 us
  starting transfers between devices  64.4 us (43%)
  blocking collectives  51.9 us (35%)
  waiting for transfers between devices  15.3 us (10%)
  Pallas kernels  12.4 us (8%)
  local copies, waits for them, and re-layouts  1.82 us (1%)
  other arithmetic  1.67 us (1%)
    ppermute x9, starting transfers between devices, swap(): return lax.ppermute(x, axis, [(0, 1), (1, 0)])  49.4 us
    all_to_all x2, blocking collectives, spread(): return lax.all_to_all(jnp.broadcast_to(x[None], (n, *x.shape)), axes, 0, 0)  19.9 us
    all_to_all x1, blocking collectives, body(): lax.all_to_all(jnp.concatenate([cold_part, hot_part], axis=1), FAR, 0, 0)  19.8 us
    all_to_all x1, blocking collectives, body(): stats = lax.all_to_all(stats, COLS, 0, 0)  12.1 us
    ppermute x9, waiting for transfers between devices, swap(): return lax.ppermute(x, axis, [(0, 1), (1, 0)])  7.53 us
    all_to_all x1, starting transfers between devices, spread(): return lax.all_to_all(jnp.broadcast_to(x[None], (n, *x.shape)), axes, 0, 0)  6.89 us
    pallas_call x1, Pallas kernels, body(): pl.pallas_call(grads_kernel, out_shape=(jax.ShapeDtypeStruct((count // 2,...  5.56 us
    all_to_all x1, starting transfers between devices, body(): near = lax.all_to_all(item_part, NEAR, 0, 0)  4 us
  transfers between devices with their start and end apart: 13, of which 8 were waited for; matrix products, arithmetic and copies ran while one was open for 1% of the time, Pallas kernels for 2%

profile of v9, /device:TPU:1, one launch (start us, length us, event | category | flops | bytes accessed | tf_op | source)
XLA Modules:
  0.0 148.3 jit_solution(16492407198669200545)
XLA Ops:
  0.6 16.4 %collective-permute-start.1 = (bf16[32,256]{1,0:T(8,128)(2,1)}, bf16[32,256]{1,0:T(8,128)(2,1)S(1)}, u32[]{:S(2)}, u32[]{:S(2)}) collective-permute-start(bf16[32,256]{1,0:T(8,128)(2,1)} %param.7), channel_id=1, source_target_pairs={{0,256},{256,0},{1,257},{257,1},{2,258},{258,2},{3,259},{259,3},{4... | collective-permute-start | bytes 49160 | tf_op jit(solution)/shard_map/ppermute | solution.py:30
  17.1 4.0 %collective-permute-start = (bf16[32,256]{1,0:T(8,128)(2,1)}, bf16[32,256]{1,0:T(8,128)(2,1)S(1)}, u32[]{:S(2)}, u32[]{:S(2)}) collective-permute-start(bf16[32,256]{1,0:T(8,128)(2,1)} %param.7), channel_id=1, source_target_pairs={{0,128},{128,0},{1,129},{129,1},{2,130},{130,2},{3,131},{131,3},{4... | collective-permute-start | bytes 49160 | tf_op jit(solution)/shard_map/ppermute | solution.py:30
  21.1 1.9 %collective-permute-start.2 = (bf16[32,256]{1,0:T(8,128)(2,1)}, bf16[32,256]{1,0:T(8,128)(2,1)S(1)}, u32[]{:S(2)}, u32[]{:S(2)}) collective-permute-start(bf16[32,256]{1,0:T(8,128)(2,1)} %param.7), channel_id=1, source_target_pairs={{0,384},{128,256},{256,128},{384,0},{1,385},{129,257},{257,129},{3... | collective-permute-start | bytes 49160 | tf_op jit(solution)/shard_map/ppermute | solution.py:211
  23.0 2.6 %collective-permute-start.3 = (bf16[128,256]{1,0:T(8,128)(2,1)}, bf16[128,256]{1,0:T(8,128)(2,1)S(1)}, u32[]{:S(2)}, u32[]{:S(2)}) collective-permute-start(bf16[128,256]{1,0:T(8,128)(2,1)} %param.5), channel_id=1, source_target_pairs={{0,32},{32,0},{1,33},{33,1},{2,34},{34,2},{3,35},{35,3},{4,36},{36... | collective-permute-start | bytes 196616 | tf_op jit(solution)/shard_map/ppermute | solution.py:30
  25.7 4.0 %collective-permute-done.2 = bf16[32,256]{1,0:T(8,128)(2,1)S(1)} collective-permute-done((bf16[32,256]{1,0:T(8,128)(2,1)}, bf16[32,256]{1,0:T(8,128)(2,1)S(1)}, u32[]{:S(2)}, u32[]{:S(2)}) %collective-permute-start.2) | collective-permute-done | bytes 16416 | tf_op jit(solution)/shard_map/ppermute | solution.py:211
  29.7 0.7 pad_maximum_fusion.2
  30.4 1.1 broadcast_in_dim.10
  31.5 6.9 %all-to-all-start = ((bf16[16,128,256]{2,1,0:T(8,128)(2,1)}), bf16[16,128,256]{2,1,0:T(8,128)(2,1)S(1)}, u32[]{:S(2)}, u32[]{:S(2)}) async-start(bf16[16,128,256]{2,1,0:T(8,128)(2,1)} %broadcast_in_dim.10), calls=%async_computation | async-start | bytes 2097152 | tf_op jit(solution)/shard_map/all_to_all | solution.py:26
  38.4 3.1 %collective-permute-start.4 = (bf16[256,256]{1,0:T(8,128)(2,1)S(1)}, bf16[256,256]{1,0:T(8,128)(2,1)S(1)}, u32[]{:S(2)}, u32[]{:S(2)}) collective-permute-start(bf16[256,256]{1,0:T(8,128)(2,1)S(1)} %pad_maximum_fusion), channel_id=1, source_target_pairs={{0,64},{64,0},{1,65},{65,1},{2,66},{66,2},{3,67},{67,3},{4,68},{68... | collective-permute-start | bytes 393224 | tf_op jit(solution)/shard_map/ppermute | solution.py:30
  41.6 2.2 %shard_map.84.col_ref = s32[1,1024]{1,0:T(1,128)S(1)} custom-call(s32[1]{0:T(128)} %bitcast.me_ref, s32[16,128]{1,0:T(8,128)S(1)} %bitcast.16, s32[512,1,128]{2,1,0:T(1,128)S(1)} %bitcast.15), custom_call_target="tpu_custom_call" | custom-call | flops 12582912 | bytes 1048576 | tf_op jit(solution)/shard_map/pallas_call | solution.py:199
  43.8 2.9 %collective-permute-done.4 = bf16[256,256]{1,0:T(8,128)(2,1)S(1)} collective-permute-done((bf16[256,256]{1,0:T(8,128)(2,1)S(1)}, bf16[256,256]{1,0:T(8,128)(2,1)S(1)}, u32[]{:S(2)}, u32[]{:S(2)}) %collective-permute-start.4) | collective-permute-done | bytes 131104 | tf_op jit(solution)/shard_map/ppermute | solution.py:30
  46.7 5.4 %collective-permute-start.5 = (bf16[512,256]{1,0:T(8,128)(2,1)S(1)}, bf16[512,256]{1,0:T(8,128)(2,1)S(1)}, u32[]{:S(2)}, u32[]{:S(2)}) collective-permute-start(bf16[512,256]{1,0:T(8,128)(2,1)S(1)} %constant_dynamic-update-slice_fusion.refs_0_), channel_id=1, source_target_pairs={{0,8},{8,0},{1,9},{9,1},{2,10},{10,2},{3,11},{11,3},{4,12},{12,4},... | collective-permute-start | bytes 786440 | tf_op jit(solution)/shard_map/ppermute | solution.py:30
  52.2 1.1 collective-permute-done.5.refs_1_
  53.3 3.6 %shard_map.85 = f32[8,2,1024]{2,1,0:T(2,128)S(1)} custom-call(s32[1]{0:T(128)} %bitcast.me_ref, bf16[16,128,256]{2,1,0:T(8,128)(2,1)S(1)} %all-to-all-done.cold_ref, bf16[16,16,256]{2,1,0:T(8,128)(2,1)S(1)} %dynamic-slice_bitcast_fusion.hot_ref, s32[1,1024]{1,0:T(1,128)S(1)} %shard_map.84.col_ref, ...), custom_call_target="tpu_custom_call" | custom-call | tf_op jit(solution)/shard_map/pallas_call | solution.py:222
  56.9 12.1 %all_to_all.30.stats_ref = f32[8,2,1024]{2,1,0:T(2,128)S(1)} all-to-all(f32[8,2,1024]{2,1,0:T(2,128)S(1)} %shard_map.85), channel_id=1, replica_groups=mesh['z8'=2,'z4'=2,'z2'=2,'z1'=2,'yl'=2,'c'=2,'x2'=2,'x1'=2,'yh'=2] {'c'..., dimensions={0} | all-to-all | bytes 131072 | tf_op jit(solution)/shard_map/all_to_all | solution.py:228
  69.1 5.6 %shard_map.86 = (f32[512,256]{1,0:T(8,128)S(1)}, bf16[512,256]{1,0:T(8,128)(2,1)S(1)}, bf16[16,144,256]{2,1,0:T(8,128)(2,1)}, f32[1,128]{1,0:T(1,128)}) custom-call(s32[1]{0:T(128)} %bitcast.me_ref, bf16[16,128,256]{2,1,0:T(8,128)(2,1)S(1)} %all-to-all-done.cold_ref, bf16[16,16,256]{2,1,0:T(8,128)(2,1)S(1)} %dynamic-slice_bitcast_fusion.hot_ref, ...), custom_call_target="tpu_custom_call" | custom-call | tf_op jit(solution)/shard_map/pallas_call | solution.py:229
  74.6 4.0 %all-to-all-start.2 = ((bf16[16,144,256]{2,1,0:T(8,128)(2,1)}), bf16[16,144,256]{2,1,0:T(8,128)(2,1)S(1)}, u32[]{:S(2)}, u32[]{:S(2)}) async-start(bf16[16,144,256]{2,1,0:T(8,128)(2,1)} %get-tuple-element.22), calls=%async_computation.2 | async-start | bytes 2359296 | tf_op jit(solution)/shard_map/all_to_all | solution.py:242
  78.6 2.6 %collective-permute-start.6 = (bf16[512,256]{1,0:T(8,128)(2,1)S(1)}, bf16[512,256]{1,0:T(8,128)(2,1)S(1)}, u32[]{:S(2)}, u32[]{:S(2)}) collective-permute-start(bf16[512,256]{1,0:T(8,128)(2,1)S(1)} %get-tuple-element.21), channel_id=1, source_target_pairs={{0,8},{8,0},{1,9},{9,1},{2,10},{10,2},{3,11},{11,3},{4,12},{12,4},... | collective-permute-start | bytes 786440 | tf_op jit(solution)/shard_map/ppermute | solution.py:30
  81.2 1.1 collective-permute-done.6
  82.5 2.2 %collective-permute-start.9 = (bf16[128,256]{1,0:T(8,128)(2,1)S(1)}, bf16[128,256]{1,0:T(8,128)(2,1)S(1)}, u32[]{:S(2)}, u32[]{:S(2)}) collective-permute-start(bf16[128,256]{1,0:T(8,128)(2,1)S(1)} %get-tuple-element.30), channel_id=1, source_target_pairs={{0,96},{32,64},{64,32},{96,0},{1,97},{33,65},{65,33},{97,1},{2,98}... | collective-permute-start | bytes 196616 | tf_op jit(solution)/shard_map/ppermute | solution.py:246
  84.7 2.9 %collective-permute-start.8 = (bf16[128,256]{1,0:T(8,128)(2,1)S(1)}, bf16[128,256]{1,0:T(8,128)(2,1)S(1)}, u32[]{:S(2)}, u32[]{:S(2)}) collective-permute-start(bf16[128,256]{1,0:T(8,128)(2,1)S(1)} %get-tuple-element.31), channel_id=1, source_target_pairs={{0,64},{64,0},{1,65},{65,1},{2,66},{66,2},{3,67},{67,3},{4,68},{68... | collective-permute-start | bytes 196616 | tf_op jit(solution)/shard_map/ppermute | solution.py:30
  87.6 4.2 %collective-permute-start.7 = (bf16[128,256]{1,0:T(8,128)(2,1)S(1)}, bf16[128,256]{1,0:T(8,128)(2,1)S(1)}, u32[]{:S(2)}, u32[]{:S(2)}) collective-permute-start(bf16[128,256]{1,0:T(8,128)(2,1)S(1)} %get-tuple-element.32), channel_id=1, source_target_pairs={{0,32},{32,0},{1,33},{33,1},{2,34},{34,2},{3,35},{35,3},{4,36},{36... | collective-permute-start | bytes 196616 | tf_op jit(solution)/shard_map/ppermute | solution.py:30
  91.8 1.0 collective-permute-done.8
  92.8 1.1 collective-permute-done.7
  93.9 3.8 %all-to-all-done.2 = bf16[16,144,256]{2,1,0:T(8,128)(2,1)S(1)} async-done(((bf16[16,144,256]{2,1,0:T(8,128)(2,1)}), bf16[16,144,256]{2,1,0:T(8,128)(2,1)S(1)}, u32[]{:S(2)}, u32[]{:S(2)}) %all-to-all-start.2) | async-done | bytes 1179680 | tf_op jit(solution)/shard_map/all_to_all | solution.py:242
  97.9 19.8 %all_to_all.31 = bf16[4,48,256]{2,1,0:T(8,128)(2,1)S(1)} all-to-all(bf16[4,48,256]{2,1,0:T(8,128)(2,1)S(1)} %pad_maximum_fusion.1), channel_id=1, replica_groups=mesh['z8'=2,'z4'=2,'z2'=2,'z1'=2,'yl'=2,'c'=2,'x2'=2,'x1'=2,'yh'=2] {'z8..., dimensions={0} | all-to-all | bytes 196608 | tf_op jit(solution)/shard_map/all_to_all | solution.py:252
  117.8 6.9 %all_to_all.32 = bf16[4,16,256]{2,1,0:T(8,128)(2,1)S(1)} all-to-all(bf16[4,16,256]{2,1,0:T(8,128)(2,1)S(1)} %broadcast_in_dim.12), channel_id=1, replica_groups=mesh['z8'=2,'z4'=2,'z2'=2,'z1'=2,'yl'=2,'c'=2,'x2'=2,'x1'=2,'yh'=2] {'z2..., dimensions={0} | all-to-all | bytes 65536 | tf_op jit(solution)/shard_map/all_to_all | solution.py:26
  124.7 13.1 %all_to_all.33 = bf16[16,64,256]{2,1,0:T(8,128)(2,1)S(1)} all-to-all(bf16[16,64,256]{2,1,0:T(8,128)(2,1)S(1)} %broadcast_in_dim.14), channel_id=1, replica_groups=mesh['z8'=2,'z4'=2,'z2'=2,'z1'=2,'yl'=2,'c'=2,'x2'=2,'x1'=2,'yh'=2] {'yl..., dimensions={0} | all-to-all | bytes 1048576 | tf_op jit(solution)/shard_map/all_to_all | solution.py:26
  137.7 8.1 %collective-permute-start.10 = (bf16[1024,256]{1,0:T(8,128)(2,1)S(1)}, bf16[1024,256]{1,0:T(8,128)(2,1)S(1)}, u32[]{:S(2)}, u32[]{:S(2)}) collective-permute-start(bf16[1024,256]{1,0:T(8,128)(2,1)S(1)} %bitcast.13), channel_id=1, source_target_pairs={{0,8},{8,0},{1,9},{9,1},{2,10},{10,2},{3,11},{11,3},{4,12},{12,4},... | collective-permute-start | bytes 1572872 | tf_op jit(solution)/shard_map/ppermute | solution.py:30
  145.8 0.7 fusion
  146.5 0.6 slice.43
  147.4 1.0 shard_map.87
  (30 shorter events, 0.7 us)
Async XLA Ops:
  0.6 51.6 %copy-start = (bf16[2048,256]{1,0:T(8,128)(2,1)S(1)}, bf16[2048,256]{1,0:T(8,128)(2,1)}, u32[]{:S(2)}) copy-start(bf16[2048,256]{1,0:T(8,128)(2,1)} %param.6) | copy-start | bytes 3145732
  0.6 25.0 %collective-permute-start.1 = (bf16[32,256]{1,0:T(8,128)(2,1)}, bf16[32,256]{1,0:T(8,128)(2,1)S(1)}, u32[]{:S(2)}, u32[]{:S(2)}) collective-permute-start(bf16[32,256]{1,0:T(8,128)(2,1)} %param.7), channel_id=1, source_target_pairs={{0,256},{256,0},{1,257},{257,1},{2,258},{258,2},{3,259},{259,3},{4... | collective-permute-start | bytes 49160 | tf_op jit(solution)/shard_map/ppermute | solution.py:30
  17.1 8.6 %collective-permute-start = (bf16[32,256]{1,0:T(8,128)(2,1)}, bf16[32,256]{1,0:T(8,128)(2,1)S(1)}, u32[]{:S(2)}, u32[]{:S(2)}) collective-permute-start(bf16[32,256]{1,0:T(8,128)(2,1)} %param.7), channel_id=1, source_target_pairs={{0,128},{128,0},{1,129},{129,1},{2,130},{130,2},{3,131},{131,3},{4... | collective-permute-start | bytes 49160 | tf_op jit(solution)/shard_map/ppermute | solution.py:30
  21.1 8.6 %collective-permute-start.2 = (bf16[32,256]{1,0:T(8,128)(2,1)}, bf16[32,256]{1,0:T(8,128)(2,1)S(1)}, u32[]{:S(2)}, u32[]{:S(2)}) collective-permute-start(bf16[32,256]{1,0:T(8,128)(2,1)} %param.7), channel_id=1, source_target_pairs={{0,384},{128,256},{256,128},{384,0},{1,385},{129,257},{257,129},{3... | collective-permute-start | bytes 49160 | tf_op jit(solution)/shard_map/ppermute | solution.py:211
  23.0 7.4 %collective-permute-start.3 = (bf16[128,256]{1,0:T(8,128)(2,1)}, bf16[128,256]{1,0:T(8,128)(2,1)S(1)}, u32[]{:S(2)}, u32[]{:S(2)}) collective-permute-start(bf16[128,256]{1,0:T(8,128)(2,1)} %param.5), channel_id=1, source_target_pairs={{0,32},{32,0},{1,33},{33,1},{2,34},{34,2},{3,35},{35,3},{4,36},{36... | collective-permute-start | bytes 196616 | tf_op jit(solution)/shard_map/ppermute | solution.py:30
  31.5 6.9 %copy-start.3 = (bf16[128,256]{1,0:T(8,128)(2,1)S(1)}, bf16[128,256]{1,0:T(8,128)(2,1)}, u32[]{:S(2)}) copy-start(bf16[128,256]{1,0:T(8,128)(2,1)} %param.5) | copy-start | bytes 196612
  31.5 10.1 %copy-start.1 = (s32[65536]{0:T(1024)S(1)}, s32[65536]{0:T(1024)}, u32[]{:S(2)}) copy-start(s32[65536]{0:T(1024)} %param.9) | copy-start | bytes 786436
  31.5 10.1 %copy-start.2 = (s32[2048]{0:T(1024)S(1)}, s32[2048]{0:T(1024)}, u32[]{:S(2)}) copy-start(s32[2048]{0:T(1024)} %param.8) | copy-start | bytes 24580
  31.5 21.8 %all-to-all-start = ((bf16[16,128,256]{2,1,0:T(8,128)(2,1)}), bf16[16,128,256]{2,1,0:T(8,128)(2,1)S(1)}, u32[]{:S(2)}, u32[]{:S(2)}) async-start(bf16[16,128,256]{2,1,0:T(8,128)(2,1)} %broadcast_in_dim.10), calls=%async_computation | async-start | bytes 2097152 | tf_op jit(solution)/shard_map/all_to_all | solution.py:26
  38.4 8.3 %collective-permute-start.4 = (bf16[256,256]{1,0:T(8,128)(2,1)S(1)}, bf16[256,256]{1,0:T(8,128)(2,1)S(1)}, u32[]{:S(2)}, u32[]{:S(2)}) collective-permute-start(bf16[256,256]{1,0:T(8,128)(2,1)S(1)} %pad_maximum_fusion), channel_id=1, source_target_pairs={{0,64},{64,0},{1,65},{65,1},{2,66},{66,2},{3,67},{67,3},{4,68},{68... | collective-permute-start | bytes 393224 | tf_op jit(solution)/shard_map/ppermute | solution.py:30
  46.7 6.6 %collective-permute-start.5 = (bf16[512,256]{1,0:T(8,128)(2,1)S(1)}, bf16[512,256]{1,0:T(8,128)(2,1)S(1)}, u32[]{:S(2)}, u32[]{:S(2)}) collective-permute-start(bf16[512,256]{1,0:T(8,128)(2,1)S(1)} %constant_dynamic-update-slice_fusion.refs_0_), channel_id=1, source_target_pairs={{0,8},{8,0},{1,9},{9,1},{2,10},{10,2},{3,11},{11,3},{4,12},{12,4},... | collective-permute-start | bytes 786440 | tf_op jit(solution)/shard_map/ppermute | solution.py:30
  74.6 23.1 %all-to-all-start.2 = ((bf16[16,144,256]{2,1,0:T(8,128)(2,1)}), bf16[16,144,256]{2,1,0:T(8,128)(2,1)S(1)}, u32[]{:S(2)}, u32[]{:S(2)}) async-start(bf16[16,144,256]{2,1,0:T(8,128)(2,1)} %get-tuple-element.22), calls=%async_computation.2 | async-start | bytes 2359296 | tf_op jit(solution)/shard_map/all_to_all | solution.py:242
  78.6 3.7 %collective-permute-start.6 = (bf16[512,256]{1,0:T(8,128)(2,1)S(1)}, bf16[512,256]{1,0:T(8,128)(2,1)S(1)}, u32[]{:S(2)}, u32[]{:S(2)}) collective-permute-start(bf16[512,256]{1,0:T(8,128)(2,1)S(1)} %get-tuple-element.21), channel_id=1, source_target_pairs={{0,8},{8,0},{1,9},{9,1},{2,10},{10,2},{3,11},{11,3},{4,12},{12,4},... | collective-permute-start | bytes 786440 | tf_op jit(solution)/shard_map/ppermute | solution.py:30
  82.5 9.3 %collective-permute-start.9 = (bf16[128,256]{1,0:T(8,128)(2,1)S(1)}, bf16[128,256]{1,0:T(8,128)(2,1)S(1)}, u32[]{:S(2)}, u32[]{:S(2)}) collective-permute-start(bf16[128,256]{1,0:T(8,128)(2,1)S(1)} %get-tuple-element.30), channel_id=1, source_target_pairs={{0,96},{32,64},{64,32},{96,0},{1,97},{33,65},{65,33},{97,1},{2,98}... | collective-permute-start | bytes 196616 | tf_op jit(solution)/shard_map/ppermute | solution.py:246
  84.7 8.2 %collective-permute-start.8 = (bf16[128,256]{1,0:T(8,128)(2,1)S(1)}, bf16[128,256]{1,0:T(8,128)(2,1)S(1)}, u32[]{:S(2)}, u32[]{:S(2)}) collective-permute-start(bf16[128,256]{1,0:T(8,128)(2,1)S(1)} %get-tuple-element.31), channel_id=1, source_target_pairs={{0,64},{64,0},{1,65},{65,1},{2,66},{66,2},{3,67},{67,3},{4,68},{68... | collective-permute-start | bytes 196616 | tf_op jit(solution)/shard_map/ppermute | solution.py:30
  87.6 6.3 %collective-permute-start.7 = (bf16[128,256]{1,0:T(8,128)(2,1)S(1)}, bf16[128,256]{1,0:T(8,128)(2,1)S(1)}, u32[]{:S(2)}, u32[]{:S(2)}) collective-permute-start(bf16[128,256]{1,0:T(8,128)(2,1)S(1)} %get-tuple-element.32), channel_id=1, source_target_pairs={{0,32},{32,0},{1,33},{33,1},{2,34},{34,2},{3,35},{35,3},{4,36},{36... | collective-permute-start | bytes 196616 | tf_op jit(solution)/shard_map/ppermute | solution.py:30
  137.7 9.6 %collective-permute-start.10 = (bf16[1024,256]{1,0:T(8,128)(2,1)S(1)}, bf16[1024,256]{1,0:T(8,128)(2,1)S(1)}, u32[]{:S(2)}, u32[]{:S(2)}) collective-permute-start(bf16[1024,256]{1,0:T(8,128)(2,1)S(1)} %bitcast.13), channel_id=1, source_target_pairs={{0,8},{8,0},{1,9},{9,1},{2,10},{10,2},{3,11},{11,3},{4,12},{12,4},... | collective-permute-start | bytes 1572872 | tf_op jit(solution)/shard_map/ppermute | solution.py:30

commit v10 on v7

--- a/solution.py
+++ b/solution.py
@@ -11,7 +11,7 @@
 AXES = ("z8", "z4", "z2", "z1", "yl", "c", "x2", "x1", "yh")
 COLS = ("c", "z2", "z1")
 HALF = ("z2", "z1")
-NEAR = ("yl", "x2", "x1", "yh")
+NEAR = ("x2", "x1", "yh", "yl")
 FAR = ("z8", "z4")
 NC, NG, NF = 2 ** len(COLS), 2 ** len(NEAR), 2 ** len(FAR)
 BF = jnp.bfloat16
@@ -163,17 +163,17 @@
     send_ref[...] = acc_ref[:, half:].T.astype(BF)
 
 
-def place_kernel(me_ref, own_ref, other_ref, out_ref, sems):
-    core = bit(me_ref[0], "c")
-    half = own_ref.shape[0]
-    first = pltpu.make_async_copy(own_ref, out_ref.at[pl.ds(core * half, half)], sems.at[0])
-    second = pltpu.make_async_copy(
-        other_ref, out_ref.at[pl.ds((1 - core) * half, half)], sems.at[1]
-    )
-    first.start()
-    second.start()
-    first.wait()
-    second.wait()
+def place_kernel(first_ref, second_ref, out_ref, sems):
+    part = first_ref.shape[1]
+    copies = []
+    for core in range(2):
+        for i, ref in enumerate((first_ref, second_ref)):
+            there = out_ref.at[pl.ds((2 * core + i) * part, part)]
+            copies.append(pltpu.make_async_copy(ref.at[core], there, sems.at[2 * core + i]))
+    for copy in copies:
+        copy.start()
+    for copy in copies:
+        copy.wait()
 
 
 def body(queries, hot_table, cold_table, hot_ids, targets):
@@ -239,24 +239,26 @@
     others = [swap(sends[1], "z1"), swap(sends[2], "z2")]
     others.append(lax.ppermute(sends[3], ("z2", "z1"), [(i, 3 - i) for i in range(4)]))
     near, *others = lax.optimization_barrier((near, *others))
-    grad_queries = (keep[0] + sum(x.astype(F32) for x in others)).astype(BF)
     near = jnp.sum(near.astype(F32), axis=0).astype(BF)
     cold_part = near[: NF * shard].reshape(NF, shard, width)
     hot_part = jnp.broadcast_to(near[None, NF * shard :], (NF, hot_own, width))
     far = lax.all_to_all(jnp.concatenate([cold_part, hot_part], axis=1), FAR, 0, 0)
-    far = jnp.sum(far.astype(F32), axis=0).astype(BF)
-    grad_cold = far[:shard]
-    grad_hot = spread(far[shard:], HALF).reshape(-1, width)
+    grad_queries = (keep[0] + sum(x.astype(F32) for x in others)).astype(BF)
+    far, grad_queries = lax.optimization_barrier((far, grad_queries))
+    grad_cold = jnp.sum(far[:, :shard].astype(F32), axis=0).astype(BF)
+    grad_hot = jnp.sum(far[:, shard:].astype(F32), axis=0).astype(BF)
+    grad_hot = spread(grad_hot, HALF).reshape(-1, width)
+    grad_hot, grad_cold = lax.optimization_barrier((grad_hot, grad_cold))
     grad_hot = spread(grad_hot, NEAR)
-    grad_hot = grad_hot.reshape(hot // 2, width)
+    grad_hot = grad_hot.reshape(2, hot // 4, width)
     grad_hot = pl.pallas_call(
         place_kernel,
         out_shape=jax.ShapeDtypeStruct((hot, width), BF),
-        in_specs=[smem, vmem, vmem],
+        in_specs=[vmem, vmem],
         out_specs=pl.BlockSpec(memory_space=pl.ANY),
-        scratch_shapes=[pltpu.SemaphoreType.DMA((2,))],
-        compiler_params=params,
-    )(at_me, grad_hot, swap(grad_hot, "c"))
+        scratch_shapes=[pltpu.SemaphoreType.DMA((4,))],
+        compiler_params=params,
+    )(lax.all_gather(grad_hot[0], "c"), lax.all_gather(grad_hot[1], "c"))
     return grad_queries, grad_hot, grad_cold, loss[0]
 
 

time: 146 us -> 148 us (1.014)
  blocking collectives: 49.3 us -> 37.2 us
  waiting for transfers between devices: 22 us -> 33.8 us
  other arithmetic: 0.94 us -> 3.9 us
    all_to_all x1 -> x0, blocking collectives: 17 us -> none  [body(): lax.all_to_all(jnp.concatenate([cold_part, hot_part], axis=1), FAR, 0, 0)]
    all_to_all x0 -> x1, waiting for transfers between devices: none -> 10.3 us  [body(): lax.all_to_all(jnp.concatenate([cold_part, hot_part], axis=1), FAR, 0, 0)]
    all_gather x0 -> x2, blocking collectives: none -> 9.95 us  [the longest x1 7.78 us: body(): lax.all_gather(grad_hot[0], 'c')]
    ppermute x7 -> x6, starting transfers between devices: 27.8 us -> 19.5 us  [swap(): return lax.ppermute(x, axis, [(0, 1), (1, 0)])]
    all_to_all x0 -> x1, starting transfers between devices: none -> 4.44 us  [body(): lax.all_to_all(jnp.concatenate([cold_part, hot_part], axis=1), FAR, 0, 0)]
    all_to_all x2 -> x1, blocking collectives: 19.9 us -> 15.5 us  [spread(): return lax.all_to_all(jnp.broadcast_to(x[None], (n, *x.shape)), axes, 0, 0)]
    all_to_all x2 -> x3, waiting for transfers between devices: 7.29 us -> 11.5 us  [spread(): return lax.all_to_all(jnp.broadcast_to(x[None], (n, *x.shape)), axes, 0, 0)]
    all_to_all x2 -> x3, starting transfers between devices: 22.5 us -> 25.8 us  [spread(): return lax.all_to_all(jnp.broadcast_to(x[None], (n, *x.shape)), axes, 0, 0)]
  transfers between devices with their start and end apart: 11 -> 12, of which waited for: 9 -> 11; matrix products, arithmetic and copies ran while one was open for 1% -> 2% of each run, Pallas kernels for 2% -> 2%
where the time goes in v10:
time: 148 us; the launch traced here: 147 us
  starting transfers between devices  55.6 us (38%)
  blocking collectives  37.2 us (25%)
  waiting for transfers between devices  33.8 us (23%)
  Pallas kernels  12.4 us (8%)
  other arithmetic  3.9 us (3%)
  local copies, waits for them, and re-layouts  3.3 us (2%)
    all_to_all x3, starting transfers between devices, spread(): return lax.all_to_all(jnp.broadcast_to(x[None], (n, *x.shape)), axes, 0, 0)  25.8 us
    ppermute x6, starting transfers between devices, swap(): return lax.ppermute(x, axis, [(0, 1), (1, 0)])  19.5 us
    all_to_all x1, blocking collectives, spread(): return lax.all_to_all(jnp.broadcast_to(x[None], (n, *x.shape)), axes, 0, 0)  15.5 us
    all_to_all x1, blocking collectives, body(): stats = lax.all_to_all(stats, COLS, 0, 0)  11.8 us
    all_to_all x3, waiting for transfers between devices, spread(): return lax.all_to_all(jnp.broadcast_to(x[None], (n, *x.shape)), axes, 0, 0)  11.5 us
    ppermute x6, waiting for transfers between devices, swap(): return lax.ppermute(x, axis, [(0, 1), (1, 0)])  10.7 us
    all_to_all x1, waiting for transfers between devices, body(): lax.all_to_all(jnp.concatenate([cold_part, hot_part], axis=1), FAR, 0, 0)  10.3 us
    all_gather x1, blocking collectives, body(): lax.all_gather(grad_hot[0], 'c')  7.78 us
  transfers between devices with their start and end apart: 12, of which 11 were waited for; matrix products, arithmetic and copies ran while one was open for 2% of the time, Pallas kernels for 2%

profile of v10, /device:TPU:1, one launch (start us, length us, event | category | flops | bytes accessed | tf_op | source)
XLA Modules:
  0.0 147.0 jit_solution(17380632427182614521)
XLA Ops:
  0.6 1.4 broadcast_in_dim.10
  2.1 15.6 %all-to-all-start = ((bf16[4,32,256]{2,1,0:T(8,128)(2,1)}), bf16[4,32,256]{2,1,0:T(8,128)(2,1)S(1)}, u32[]{:S(2)}, u32[]{:S(2)}) async-start(bf16[4,32,256]{2,1,0:T(8,128)(2,1)} %broadcast_in_dim.10), calls=%async_computation | async-start | bytes 131072 | tf_op jit(solution)/shard_map/all_to_all | solution.py:26
  17.7 2.6 %collective-permute-start = (bf16[128,256]{1,0:T(8,128)(2,1)}, bf16[128,256]{1,0:T(8,128)(2,1)S(1)}, u32[]{:S(2)}, u32[]{:S(2)}) collective-permute-start(bf16[128,256]{1,0:T(8,128)(2,1)} %param.5), channel_id=1, source_target_pairs={{0,32},{32,0},{1,33},{33,1},{2,34},{34,2},{3,35},{35,3},{4,36},{36... | collective-permute-start | bytes 196616 | tf_op jit(solution)/shard_map/ppermute | solution.py:30
  20.4 2.6 %collective-permute-done = bf16[128,256]{1,0:T(8,128)(2,1)S(1)} collective-permute-done((bf16[128,256]{1,0:T(8,128)(2,1)}, bf16[128,256]{1,0:T(8,128)(2,1)S(1)}, u32[]{:S(2)}, u32[]{:S(2)}) %collective-permute-start) | collective-permute-done | bytes 65568 | tf_op jit(solution)/shard_map/ppermute | solution.py:30
  22.9 7.3 %all-to-all-done = bf16[4,32,256]{2,1,0:T(8,128)(2,1)S(1)} async-done(((bf16[4,32,256]{2,1,0:T(8,128)(2,1)}), bf16[4,32,256]{2,1,0:T(8,128)(2,1)S(1)}, u32[]{:S(2)}, u32[]{:S(2)}) %all-to-all-start) | async-done | bytes 65568 | tf_op jit(solution)/shard_map/all_to_all | solution.py:26
  30.2 1.1 broadcast_in_dim.11
  31.3 6.9 %all-to-all-start.1 = ((bf16[16,128,256]{2,1,0:T(8,128)(2,1)}), bf16[16,128,256]{2,1,0:T(8,128)(2,1)S(1)}, u32[]{:S(2)}, u32[]{:S(2)}) async-start(bf16[16,128,256]{2,1,0:T(8,128)(2,1)} %broadcast_in_dim.11), calls=%async_computation.1 | async-start | bytes 2097152 | tf_op jit(solution)/shard_map/all_to_all | solution.py:26
  38.2 2.7 %collective-permute-start.1 = (bf16[256,256]{1,0:T(8,128)(2,1)S(1)}, bf16[256,256]{1,0:T(8,128)(2,1)S(1)}, u32[]{:S(2)}, u32[]{:S(2)}) collective-permute-start(bf16[256,256]{1,0:T(8,128)(2,1)S(1)} %pad_maximum_fusion), channel_id=1, source_target_pairs={{0,64},{64,0},{1,65},{65,1},{2,66},{66,2},{3,67},{67,3},{4,68},{68... | collective-permute-start | bytes 393224 | tf_op jit(solution)/shard_map/ppermute | solution.py:30
  40.9 2.2 %shard_map.84.col_ref = s32[1,1024]{1,0:T(1,128)S(1)} custom-call(s32[1]{0:T(128)} %bitcast.me_ref, s32[16,128]{1,0:T(8,128)S(1)} %bitcast.16, s32[512,1,128]{2,1,0:T(1,128)S(1)} %bitcast.15), custom_call_target="tpu_custom_call" | custom-call | flops 12582912 | bytes 1048576 | tf_op jit(solution)/shard_map/pallas_call | solution.py:194
  43.2 3.8 %collective-permute-done.1 = bf16[256,256]{1,0:T(8,128)(2,1)S(1)} collective-permute-done((bf16[256,256]{1,0:T(8,128)(2,1)S(1)}, bf16[256,256]{1,0:T(8,128)(2,1)S(1)}, u32[]{:S(2)}, u32[]{:S(2)}) %collective-permute-start.1) | collective-permute-done | bytes 131104 | tf_op jit(solution)/shard_map/ppermute | solution.py:30
  47.0 4.7 %collective-permute-start.2 = (bf16[512,256]{1,0:T(8,128)(2,1)S(1)}, bf16[512,256]{1,0:T(8,128)(2,1)S(1)}, u32[]{:S(2)}, u32[]{:S(2)}) collective-permute-start(bf16[512,256]{1,0:T(8,128)(2,1)S(1)} %constant_dynamic-update-slice_fusion.refs_0_), channel_id=1, source_target_pairs={{0,8},{8,0},{1,9},{9,1},{2,10},{10,2},{3,11},{11,3},{4,12},{12,4},... | collective-permute-start | bytes 786440 | tf_op jit(solution)/shard_map/ppermute | solution.py:30
  51.7 1.1 collective-permute-done.2.refs_1_
  53.2 3.6 %shard_map.85 = f32[8,2,1024]{2,1,0:T(2,128)S(1)} custom-call(s32[1]{0:T(128)} %bitcast.me_ref, bf16[16,128,256]{2,1,0:T(8,128)(2,1)S(1)} %all-to-all-done.1.cold_ref, bf16[16,16,256]{2,1,0:T(8,128)(2,1)S(1)} %dynamic-slice_bitcast_fusion.hot_ref, s32[1,1024]{1,0:T(1,128)S(1)} %shard_map.84.col_ref, ...), custom_call_target="tpu_custom_call" | custom-call | tf_op jit(solution)/shard_map/pallas_call | solution.py:216
  56.8 11.8 %all_to_all.35.stats_ref = f32[8,2,1024]{2,1,0:T(2,128)S(1)} all-to-all(f32[8,2,1024]{2,1,0:T(2,128)S(1)} %shard_map.85), channel_id=1, replica_groups=mesh['z8'=2,'z4'=2,'z2'=2,'z1'=2,'yl'=2,'c'=2,'x2'=2,'x1'=2,'yh'=2] {'c'..., dimensions={0} | all-to-all | bytes 131072 | tf_op jit(solution)/shard_map/all_to_all | solution.py:222
  68.5 5.6 %shard_map.86 = (f32[512,256]{1,0:T(8,128)S(1)}, bf16[512,256]{1,0:T(8,128)(2,1)S(1)}, bf16[16,144,256]{2,1,0:T(8,128)(2,1)}, f32[1,128]{1,0:T(1,128)}) custom-call(s32[1]{0:T(128)} %bitcast.me_ref, bf16[16,128,256]{2,1,0:T(8,128)(2,1)S(1)} %all-to-all-done.1.cold_ref, bf16[16,16,256]{2,1,0:T(8,128)(2,1)S(1)} %dynamic-slice_bitcast_fusion.hot_ref, ...), custom_call_target="tpu_custom_call" | custom-call | tf_op jit(solution)/shard_map/pallas_call | solution.py:223
  74.1 3.7 %all-to-all-start.3 = ((bf16[16,144,256]{2,1,0:T(8,128)(2,1)}), bf16[16,144,256]{2,1,0:T(8,128)(2,1)S(1)}, u32[]{:S(2)}, u32[]{:S(2)}) async-start(bf16[16,144,256]{2,1,0:T(8,128)(2,1)} %get-tuple-element.24), calls=%async_computation.3 | async-start | bytes 2359296 | tf_op jit(solution)/shard_map/all_to_all | solution.py:236
  77.8 2.4 %collective-permute-start.3 = (bf16[512,256]{1,0:T(8,128)(2,1)S(1)}, bf16[512,256]{1,0:T(8,128)(2,1)S(1)}, u32[]{:S(2)}, u32[]{:S(2)}) collective-permute-start(bf16[512,256]{1,0:T(8,128)(2,1)S(1)} %get-tuple-element.26), channel_id=1, source_target_pairs={{0,8},{8,0},{1,9},{9,1},{2,10},{10,2},{3,11},{11,3},{4,12},{12,4},... | collective-permute-start | bytes 786440 | tf_op jit(solution)/shard_map/ppermute | solution.py:30
  80.2 1.1 collective-permute-done.3
  82.3 2.2 %collective-permute-start.6 = (bf16[128,256]{1,0:T(8,128)(2,1)S(1)}, bf16[128,256]{1,0:T(8,128)(2,1)S(1)}, u32[]{:S(2)}, u32[]{:S(2)}) collective-permute-start(bf16[128,256]{1,0:T(8,128)(2,1)S(1)} %get-tuple-element.40), channel_id=1, source_target_pairs={{0,96},{32,64},{64,32},{96,0},{1,97},{33,65},{65,33},{97,1},{2,98}... | collective-permute-start | bytes 196616 | tf_op jit(solution)/shard_map/ppermute | solution.py:240
  84.4 2.9 %collective-permute-start.5 = (bf16[128,256]{1,0:T(8,128)(2,1)S(1)}, bf16[128,256]{1,0:T(8,128)(2,1)S(1)}, u32[]{:S(2)}, u32[]{:S(2)}) collective-permute-start(bf16[128,256]{1,0:T(8,128)(2,1)S(1)} %get-tuple-element.41), channel_id=1, source_target_pairs={{0,64},{64,0},{1,65},{65,1},{2,66},{66,2},{3,67},{67,3},{4,68},{68... | collective-permute-start | bytes 196616 | tf_op jit(solution)/shard_map/ppermute | solution.py:30
  87.4 4.2 %collective-permute-start.4 = (bf16[128,256]{1,0:T(8,128)(2,1)S(1)}, bf16[128,256]{1,0:T(8,128)(2,1)S(1)}, u32[]{:S(2)}, u32[]{:S(2)}) collective-permute-start(bf16[128,256]{1,0:T(8,128)(2,1)S(1)} %get-tuple-element.42), channel_id=1, source_target_pairs={{0,32},{32,0},{1,33},{33,1},{2,34},{34,2},{3,35},{35,3},{4,36},{36... | collective-permute-start | bytes 196616 | tf_op jit(solution)/shard_map/ppermute | solution.py:30
  91.6 1.0 collective-permute-done.5
  92.6 1.1 collective-permute-done.4
  93.7 1.3 all-to-all-done.3
  95.8 4.4 %all-to-all-start.4 = ((bf16[4,48,256]{2,1,0:T(8,128)(2,1)}), bf16[4,48,256]{2,1,0:T(8,128)(2,1)S(1)}, u32[]{:S(2)}, u32[]{:S(2)}) async-start(bf16[4,48,256]{2,1,0:T(8,128)(2,1)} %pad_maximum_fusion.1), calls=%async_computation.4 | async-start | bytes 196608 | tf_op jit(solution)/shard_map/all_to_all | solution.py:245
  100.2 1.6 %fusion = bf16[128,256]{1,0:T(8,128)(2,1)} fusion(f32[512,256]{1,0:T(8,128)} %get-tuple-element.37, bf16[128,256]{1,0:T(8,128)(2,1)S(1)} %collective-permute-done.6, bf16[128,256]{1,0:T(8,128)(2,1)S(1)} %collective-permute-done.5, bf16[128,256]{1,0:T(8,128)(2,1)S(1)} %collective-permute-done.4), kind=kLoop, calls=%fused_computation.2 | loop fusion | flops 229376 | bytes 393216 | tf_op jit(solution)/shard_map/convert_element_type | solution.py:246
  101.8 10.3 %all-to-all-done.4 = bf16[4,48,256]{2,1,0:T(8,128)(2,1)S(1)} async-done(((bf16[4,48,256]{2,1,0:T(8,128)(2,1)}), bf16[4,48,256]{2,1,0:T(8,128)(2,1)S(1)}, u32[]{:S(2)}, u32[]{:S(2)}) %all-to-all-start.4) | async-done | bytes 98336 | tf_op jit(solution)/shard_map/all_to_all | solution.py:245
  112.8 3.3 %all-to-all-start.5 = ((bf16[4,16,256]{2,1,0:T(8,128)(2,1)}), bf16[4,16,256]{2,1,0:T(8,128)(2,1)S(1)}, u32[]{:S(2)}, u32[]{:S(2)}) async-start(bf16[4,16,256]{2,1,0:T(8,128)(2,1)} %broadcast_in_dim.13), calls=%async_computation.5 | async-start | bytes 65536 | tf_op jit(solution)/shard_map/all_to_all | solution.py:26
  116.6 3.9 %all-to-all-done.5 = bf16[4,16,256]{2,1,0:T(8,128)(2,1)S(1)} async-done(((bf16[4,16,256]{2,1,0:T(8,128)(2,1)}), bf16[4,16,256]{2,1,0:T(8,128)(2,1)S(1)}, u32[]{:S(2)}, u32[]{:S(2)}) %all-to-all-start.5) | async-done | bytes 32800 | tf_op jit(solution)/shard_map/all_to_all | solution.py:26
  120.5 15.5 %all_to_all.36 = bf16[16,64,256]{2,1,0:T(8,128)(2,1)S(1)} all-to-all(bf16[16,64,256]{2,1,0:T(8,128)(2,1)S(1)} %broadcast_in_dim.14), channel_id=1, replica_groups=mesh['z8'=2,'z4'=2,'z2'=2,'z1'=2,'yl'=2,'c'=2,'x2'=2,'x1'=2,'yh'=2] {'x2..., dimensions={0} | all-to-all | bytes 1048576 | tf_op jit(solution)/shard_map/all_to_all | solution.py:26
  136.1 7.8 %all_gather.6.first_ref = bf16[2,512,256]{2,1,0:T(8,128)(2,1)S(1)} all-gather(bf16[1,512,256]{2,1,0:T(8,128)(2,1)S(1)} %bitcast.18), channel_id=1, replica_groups=mesh['z8'=2,'z4'=2,'z2'=2,'z1'=2,'yl'=2,'c'=2,'x2'=2,'x1'=2,'yh'=2] {'c'}, dimensions={0}, use_global_device_ids=true | all-gather | bytes 786432 | tf_op jit(solution)/shard_map/all_gather | solution.py:261
  143.9 2.2 %all_gather.7.second_ref = bf16[2,512,256]{2,1,0:T(8,128)(2,1)S(1)} all-gather(bf16[1,512,256]{2,1,0:T(8,128)(2,1)S(1)} %bitcast.17), channel_id=1, replica_groups=mesh['z8'=2,'z4'=2,'z2'=2,'z1'=2,'yl'=2,'c'=2,'x2'=2,'x1'=2,'yh'=2] {'c'}, dimensions={0}, use_global_device_ids=true | all-gather | bytes 786432 | tf_op jit(solution)/shard_map/all_gather | solution.py:261
  (28 shorter events, 4.5 us)
Async XLA Ops:
  0.6 51.0 %copy-start = (bf16[2048,256]{1,0:T(8,128)(2,1)S(1)}, bf16[2048,256]{1,0:T(8,128)(2,1)}, u32[]{:S(2)}) copy-start(bf16[2048,256]{1,0:T(8,128)(2,1)} %param.6) | copy-start | bytes 3145732
  2.1 28.1 %all-to-all-start = ((bf16[4,32,256]{2,1,0:T(8,128)(2,1)}), bf16[4,32,256]{2,1,0:T(8,128)(2,1)S(1)}, u32[]{:S(2)}, u32[]{:S(2)}) async-start(bf16[4,32,256]{2,1,0:T(8,128)(2,1)} %broadcast_in_dim.10), calls=%async_computation | async-start | bytes 131072 | tf_op jit(solution)/shard_map/all_to_all | solution.py:26
  17.7 5.2 %collective-permute-start = (bf16[128,256]{1,0:T(8,128)(2,1)}, bf16[128,256]{1,0:T(8,128)(2,1)S(1)}, u32[]{:S(2)}, u32[]{:S(2)}) collective-permute-start(bf16[128,256]{1,0:T(8,128)(2,1)} %param.5), channel_id=1, source_target_pairs={{0,32},{32,0},{1,33},{33,1},{2,34},{34,2},{3,35},{35,3},{4,36},{36... | collective-permute-start | bytes 196616 | tf_op jit(solution)/shard_map/ppermute | solution.py:30
  31.3 6.9 %copy-start.3 = (bf16[128,256]{1,0:T(8,128)(2,1)S(1)}, bf16[128,256]{1,0:T(8,128)(2,1)}, u32[]{:S(2)}) copy-start(bf16[128,256]{1,0:T(8,128)(2,1)} %param.5) | copy-start | bytes 196612
  31.3 9.6 %copy-start.1 = (s32[65536]{0:T(1024)S(1)}, s32[65536]{0:T(1024)}, u32[]{:S(2)}) copy-start(s32[65536]{0:T(1024)} %param.9) | copy-start | bytes 786436
  31.3 9.6 %copy-start.2 = (s32[2048]{0:T(1024)S(1)}, s32[2048]{0:T(1024)}, u32[]{:S(2)}) copy-start(s32[2048]{0:T(1024)} %param.8) | copy-start | bytes 24580
  31.3 21.9 %all-to-all-start.1 = ((bf16[16,128,256]{2,1,0:T(8,128)(2,1)}), bf16[16,128,256]{2,1,0:T(8,128)(2,1)S(1)}, u32[]{:S(2)}, u32[]{:S(2)}) async-start(bf16[16,128,256]{2,1,0:T(8,128)(2,1)} %broadcast_in_dim.11), calls=%async_computation.1 | async-start | bytes 2097152 | tf_op jit(solution)/shard_map/all_to_all | solution.py:26
  38.2 8.7 %collective-permute-start.1 = (bf16[256,256]{1,0:T(8,128)(2,1)S(1)}, bf16[256,256]{1,0:T(8,128)(2,1)S(1)}, u32[]{:S(2)}, u32[]{:S(2)}) collective-permute-start(bf16[256,256]{1,0:T(8,128)(2,1)S(1)} %pad_maximum_fusion), channel_id=1, source_target_pairs={{0,64},{64,0},{1,65},{65,1},{2,66},{66,2},{3,67},{67,3},{4,68},{68... | collective-permute-start | bytes 393224 | tf_op jit(solution)/shard_map/ppermute | solution.py:30
  47.0 5.8 %collective-permute-start.2 = (bf16[512,256]{1,0:T(8,128)(2,1)S(1)}, bf16[512,256]{1,0:T(8,128)(2,1)S(1)}, u32[]{:S(2)}, u32[]{:S(2)}) collective-permute-start(bf16[512,256]{1,0:T(8,128)(2,1)S(1)} %constant_dynamic-update-slice_fusion.refs_0_), channel_id=1, source_target_pairs={{0,8},{8,0},{1,9},{9,1},{2,10},{10,2},{3,11},{11,3},{4,12},{12,4},... | collective-permute-start | bytes 786440 | tf_op jit(solution)/shard_map/ppermute | solution.py:30
  74.1 20.9 %all-to-all-start.3 = ((bf16[16,144,256]{2,1,0:T(8,128)(2,1)}), bf16[16,144,256]{2,1,0:T(8,128)(2,1)S(1)}, u32[]{:S(2)}, u32[]{:S(2)}) async-start(bf16[16,144,256]{2,1,0:T(8,128)(2,1)} %get-tuple-element.24), calls=%async_computation.3 | async-start | bytes 2359296 | tf_op jit(solution)/shard_map/all_to_all | solution.py:236
  77.8 3.6 %collective-permute-start.3 = (bf16[512,256]{1,0:T(8,128)(2,1)S(1)}, bf16[512,256]{1,0:T(8,128)(2,1)S(1)}, u32[]{:S(2)}, u32[]{:S(2)}) collective-permute-start(bf16[512,256]{1,0:T(8,128)(2,1)S(1)} %get-tuple-element.26), channel_id=1, source_target_pairs={{0,8},{8,0},{1,9},{9,1},{2,10},{10,2},{3,11},{11,3},{4,12},{12,4},... | collective-permute-start | bytes 786440 | tf_op jit(solution)/shard_map/ppermute | solution.py:30
  82.3 9.3 %collective-permute-start.6 = (bf16[128,256]{1,0:T(8,128)(2,1)S(1)}, bf16[128,256]{1,0:T(8,128)(2,1)S(1)}, u32[]{:S(2)}, u32[]{:S(2)}) collective-permute-start(bf16[128,256]{1,0:T(8,128)(2,1)S(1)} %get-tuple-element.40), channel_id=1, source_target_pairs={{0,96},{32,64},{64,32},{96,0},{1,97},{33,65},{65,33},{97,1},{2,98}... | collective-permute-start | bytes 196616 | tf_op jit(solution)/shard_map/ppermute | solution.py:240
  84.4 8.1 %collective-permute-start.5 = (bf16[128,256]{1,0:T(8,128)(2,1)S(1)}, bf16[128,256]{1,0:T(8,128)(2,1)S(1)}, u32[]{:S(2)}, u32[]{:S(2)}) collective-permute-start(bf16[128,256]{1,0:T(8,128)(2,1)S(1)} %get-tuple-element.41), channel_id=1, source_target_pairs={{0,64},{64,0},{1,65},{65,1},{2,66},{66,2},{3,67},{67,3},{4,68},{68... | collective-permute-start | bytes 196616 | tf_op jit(solution)/shard_map/ppermute | solution.py:30
  87.4 6.3 %collective-permute-start.4 = (bf16[128,256]{1,0:T(8,128)(2,1)S(1)}, bf16[128,256]{1,0:T(8,128)(2,1)S(1)}, u32[]{:S(2)}, u32[]{:S(2)}) collective-permute-start(bf16[128,256]{1,0:T(8,128)(2,1)S(1)} %get-tuple-element.42), channel_id=1, source_target_pairs={{0,32},{32,0},{1,33},{33,1},{2,34},{34,2},{3,35},{35,3},{4,36},{36... | collective-permute-start | bytes 196616 | tf_op jit(solution)/shard_map/ppermute | solution.py:30
  95.8 16.3 %all-to-all-start.4 = ((bf16[4,48,256]{2,1,0:T(8,128)(2,1)}), bf16[4,48,256]{2,1,0:T(8,128)(2,1)S(1)}, u32[]{:S(2)}, u32[]{:S(2)}) async-start(bf16[4,48,256]{2,1,0:T(8,128)(2,1)} %pad_maximum_fusion.1), calls=%async_computation.4 | async-start | bytes 196608 | tf_op jit(solution)/shard_map/all_to_all | solution.py:245
  112.8 7.7 %all-to-all-start.5 = ((bf16[4,16,256]{2,1,0:T(8,128)(2,1)}), bf16[4,16,256]{2,1,0:T(8,128)(2,1)S(1)}, u32[]{:S(2)}, u32[]{:S(2)}) async-start(bf16[4,16,256]{2,1,0:T(8,128)(2,1)} %broadcast_in_dim.13), calls=%async_computation.5 | async-start | bytes 65536 | tf_op jit(solution)/shard_map/all_to_all | solution.py:26

commit v11 on v7

--- a/solution.py
+++ b/solution.py
@@ -9,9 +9,9 @@
 from jax.sharding import PartitionSpec as P
 
 AXES = ("z8", "z4", "z2", "z1", "yl", "c", "x2", "x1", "yh")
-COLS = ("c", "z2", "z1")
+COLS = ("z2", "z1", "c")
 HALF = ("z2", "z1")
-NEAR = ("yl", "x2", "x1", "yh")
+NEAR = ("x2", "x1", "yh", "yl")
 FAR = ("z8", "z4")
 NC, NG, NF = 2 ** len(COLS), 2 ** len(NEAR), 2 ** len(FAR)
 BF = jnp.bfloat16
@@ -28,6 +28,11 @@
 
 def swap(x, axis):
     return lax.ppermute(x, axis, [(0, 1), (1, 0)])
+
+
+def around(by_z1, by_z2, by_both):
+    both = lax.ppermute(by_both, ("z2", "z1"), [(i, 3 - i) for i in range(4)])
+    return swap(by_z1, "z1"), swap(by_z2, "z2"), both
 
 
 def bit(index, axis):
@@ -81,7 +86,7 @@
     cold_col = near // near_chunk * width + (near % near_chunk) * (NF * shard)
     cold_col += pick(block, FAR) * shard + (row & (shard - 1))
     hot_near = (slot >> 6) & (NG - 1)
-    hot_k = ((slot >> 10) << 2) | ((slot >> 4) & 3)
+    hot_k = (((slot >> 4) & 3) << 1) | (slot >> 10)
     hot_col = hot_near // near_chunk * width + near_chunk * NF * shard
     hot_col += (hot_near % near_chunk) * hot_own + (slot & (hot_own - 1))
     column = jnp.where(is_hot, hot_col, cold_col)
@@ -127,7 +132,7 @@
 
 
 def grads_kernel(me_ref, cold_ref, hot_ref, col_ref, stats_ref, *refs):
-    *row_refs, keep_ref, send_ref, item_ref, loss_ref, acc_ref = refs
+    *row_refs, keep_ref, send_1, send_2, send_3, item_ref, loss_ref, acc_ref = refs
     rows = jnp.concatenate([r[...] for r in row_refs], axis=0)
     cols = col_ref[...]
     k = pick(me_ref[0], COLS)
@@ -158,9 +163,10 @@
         return carry
 
     lax.fori_loop(0, CHUNKS, step, 0, unroll=True)
-    half = acc_ref.shape[1] // 2
-    keep_ref[...] = acc_ref[:, :half].T
-    send_ref[...] = acc_ref[:, half:].T.astype(BF)
+    quarter = acc_ref.shape[1] // 4
+    keep_ref[...] = acc_ref[:, :quarter].T
+    for j, ref in enumerate((send_1, send_2, send_3)):
+        ref[...] = acc_ref[:, (j + 1) * quarter : (j + 2) * quarter].T.astype(BF)
 
 
 def place_kernel(me_ref, own_ref, other_ref, out_ref, sems):
@@ -189,7 +195,7 @@
     vmem = pl.BlockSpec(memory_space=pltpu.VMEM)
     smem = pl.BlockSpec(memory_space=pltpu.SMEM)
 
-    rows = [queries, swap(queries, "z1")]
+    pair = jnp.concatenate([queries, swap(queries, "c")], axis=0)
 
     column = pl.pallas_call(
         decode_kernel,
@@ -203,14 +209,12 @@
     )(at_me, hot_ids.reshape(-1, 128), targets.reshape(-1, 1, own))
 
     far = spread(cold_table, FAR).reshape(NF * shard, width)
-    far, rows[1] = lax.optimization_barrier((far, rows[1]))
+    far, pair = lax.optimization_barrier((far, pair))
     cold = spread(far, NEAR)
-    rows = jnp.concatenate(rows, axis=0)
-    other, column = lax.optimization_barrier((swap(rows, "z2"), column))
-    rows = jnp.concatenate([rows, other], axis=0)
-    rows = [rows, swap(rows, "c")]
+    rows = [pair, *around(pair, pair, pair)]
+    rows[3], column = lax.optimization_barrier((rows[3], column))
     mine = hot_table.reshape(2, NG, NC // 2, hot_own, width)
-    mine = lax.dynamic_slice(mine, (k >> 2, 0, k & 3, 0, 0), (1, NG, 1, hot_own, width))
+    mine = lax.dynamic_slice(mine, (k & 1, 0, k >> 1, 0, 0), (1, NG, 1, hot_own, width))
     mine = mine.reshape(NG, hot_own, width)
 
     stats = pl.pallas_call(
@@ -220,11 +224,11 @@
         compiler_params=params,
     )(at_me, cold, mine, column, *rows)
     stats = lax.all_to_all(stats, COLS, 0, 0)
-    keep, send, item_part, loss = pl.pallas_call(
+    keep, *sends, item_part, loss = pl.pallas_call(
         grads_kernel,
         out_shape=(
-            jax.ShapeDtypeStruct((count // 2, width), F32),
-            jax.ShapeDtypeStruct((count // 2, width), BF),
+            jax.ShapeDtypeStruct((count // 4, width), F32),
+            *[jax.ShapeDtypeStruct((count // 4, width), BF)] * 3,
             jax.ShapeDtypeStruct((NG, NF * shard + hot_own, width), BF),
             jax.ShapeDtypeStruct((1, own), F32),
         ),
@@ -234,12 +238,8 @@
     )(at_me, cold, mine, column, stats, *rows)
 
     near = lax.all_to_all(item_part, NEAR, 0, 0)
-    keep = (keep + swap(send, "c").astype(F32)).reshape(4, own, width)
-    sends = keep.astype(BF)
-    others = [swap(sends[1], "z1"), swap(sends[2], "z2")]
-    others.append(lax.ppermute(sends[3], ("z2", "z1"), [(i, 3 - i) for i in range(4)]))
-    near, *others = lax.optimization_barrier((near, *others))
-    grad_queries = (keep[0] + sum(x.astype(F32) for x in others)).astype(BF)
+    keep = keep + sum(x.astype(F32) for x in around(*sends))
+    near, keep, other = lax.optimization_barrier((near, keep[:own], keep[own:].astype(BF)))
     near = jnp.sum(near.astype(F32), axis=0).astype(BF)
     cold_part = near[: NF * shard].reshape(NF, shard, width)
     hot_part = jnp.broadcast_to(near[None, NF * shard :], (NF, hot_own, width))
@@ -248,7 +248,8 @@
     grad_cold = far[:shard]
     grad_hot = spread(far[shard:], HALF).reshape(-1, width)
     grad_hot = spread(grad_hot, NEAR)
-    grad_hot = grad_hot.reshape(hot // 2, width)
+    grad_hot, other = lax.optimization_barrier((grad_hot.reshape(hot // 2, width), other))
+    grad_queries = (keep + swap(other, "c").astype(F32)).astype(BF)
     grad_hot = pl.pallas_call(
         place_kernel,
         out_shape=jax.ShapeDtypeStruct((hot, width), BF),

time: 146 us -> 148 us (1.014)
  starting transfers between devices: 56.3 us -> 59.7 us
    ppermute x1 -> x2, starting transfers between devices: 2.18 us -> 8.06 us  [around(): both = lax.ppermute(by_both, ('z2', 'z1'), [(i, 3 - i) for i in range(4)])]
    ppermute x7, starting transfers between devices: 27.8 us -> 22.6 us  [swap(): return lax.ppermute(x, axis, [(0, 1), (1, 0)])]
    all_to_all x2, blocking collectives: 19.9 us -> 23.4 us  [spread(): return lax.all_to_all(jnp.broadcast_to(x[None], (n, *x.shape)), axes, 0, 0)]
    all_to_all x1, waiting for transfers between devices: 3.76 us -> 1.09 us  [body(): near = lax.all_to_all(item_part, NEAR, 0, 0)]
    all_to_all x1, starting transfers between devices: 3.81 us -> 6.47 us  [body(): near = lax.all_to_all(item_part, NEAR, 0, 0)]
    all_to_all x1, blocking collectives: 17 us -> 14.6 us  [body(): lax.all_to_all(jnp.concatenate([cold_part, hot_part], axis=1), FAR, 0, 0)]
    all_to_all x1, blocking collectives: 12.5 us -> 10.7 us  [body(): stats = lax.all_to_all(stats, COLS, 0, 0)]
  transfers between devices with their start and end apart: 11 -> 12, of which waited for: 9 -> 6; matrix products, arithmetic and copies ran while one was open for 1% -> 1% of each run, Pallas kernels for 2% -> 2%
where the time goes in v11:
time: 148 us; the launch traced here: 147 us
  starting transfers between devices  59.7 us (40%)
  blocking collectives  48.7 us (33%)
  waiting for transfers between devices  20.6 us (14%)
  Pallas kernels  12.4 us (8%)
  local copies, waits for them, and re-layouts  3.24 us (2%)
  other arithmetic  1.74 us (1%)
    all_to_all x2, blocking collectives, spread(): return lax.all_to_all(jnp.broadcast_to(x[None], (n, *x.shape)), axes, 0, 0)  23.4 us
    ppermute x7, starting transfers between devices, swap(): return lax.ppermute(x, axis, [(0, 1), (1, 0)])  22.6 us
    all_to_all x2, starting transfers between devices, spread(): return lax.all_to_all(jnp.broadcast_to(x[None], (n, *x.shape)), axes, 0, 0)  22.5 us
    all_to_all x1, blocking collectives, body(): lax.all_to_all(jnp.concatenate([cold_part, hot_part], axis=1), FAR, 0, 0)  14.6 us
    ppermute x7, waiting for transfers between devices, swap(): return lax.ppermute(x, axis, [(0, 1), (1, 0)])  11.8 us
    all_to_all x1, blocking collectives, body(): stats = lax.all_to_all(stats, COLS, 0, 0)  10.7 us
    ppermute x2, starting transfers between devices, around(): both = lax.ppermute(by_both, ('z2', 'z1'), [(i, 3 - i) for i in range(4)])  8.06 us
    all_to_all x2, waiting for transfers between devices, spread(): return lax.all_to_all(jnp.broadcast_to(x[None], (n, *x.shape)), axes, 0, 0)  7.7 us
  transfers between devices with their start and end apart: 12, of which 6 were waited for; matrix products, arithmetic and copies ran while one was open for 1% of the time, Pallas kernels for 2%

profile of v11, /device:TPU:1, one launch (start us, length us, event | category | flops | bytes accessed | tf_op | source)
XLA Modules:
  0.0 147.3 jit_solution(7920291399148192402)
XLA Ops:
  0.6 1.4 broadcast_in_dim.12
  2.1 15.6 %all-to-all-start = ((bf16[4,32,256]{2,1,0:T(8,128)(2,1)}), bf16[4,32,256]{2,1,0:T(8,128)(2,1)S(1)}, u32[]{:S(2)}, u32[]{:S(2)}) async-start(bf16[4,32,256]{2,1,0:T(8,128)(2,1)} %broadcast_in_dim.12), calls=%async_computation | async-start | bytes 131072 | tf_op jit(solution)/shard_map/all_to_all | solution.py:26
  17.7 2.9 %collective-permute-start = (bf16[128,256]{1,0:T(8,128)(2,1)}, bf16[128,256]{1,0:T(8,128)(2,1)S(1)}, u32[]{:S(2)}, u32[]{:S(2)}) collective-permute-start(bf16[128,256]{1,0:T(8,128)(2,1)} %param.5), channel_id=1, source_target_pairs={{0,8},{8,0},{1,9},{9,1},{2,10},{10,2},{3,11},{11,3},{4,12},{12,4},... | collective-permute-start | bytes 196616 | tf_op jit(solution)/shard_map/ppermute | solution.py:30
  20.6 1.1 collective-permute-done
  21.7 0.8 pad_maximum_fusion.refs_0_
  22.5 7.7 %all-to-all-done = bf16[4,32,256]{2,1,0:T(8,128)(2,1)S(1)} async-done(((bf16[4,32,256]{2,1,0:T(8,128)(2,1)}), bf16[4,32,256]{2,1,0:T(8,128)(2,1)S(1)}, u32[]{:S(2)}, u32[]{:S(2)}) %all-to-all-start) | async-done | bytes 65568 | tf_op jit(solution)/shard_map/all_to_all | solution.py:26
  30.2 1.1 broadcast_in_dim.13
  31.3 6.9 %all-to-all-start.1 = ((bf16[16,128,256]{2,1,0:T(8,128)(2,1)}), bf16[16,128,256]{2,1,0:T(8,128)(2,1)S(1)}, u32[]{:S(2)}, u32[]{:S(2)}) async-start(bf16[16,128,256]{2,1,0:T(8,128)(2,1)} %broadcast_in_dim.13), calls=%async_computation.1 | async-start | bytes 2097152 | tf_op jit(solution)/shard_map/all_to_all | solution.py:26
  38.2 3.6 %collective-permute-start.1 = (bf16[256,256]{1,0:T(8,128)(2,1)S(1)}, bf16[256,256]{1,0:T(8,128)(2,1)S(1)}, u32[]{:S(2)}, u32[]{:S(2)}) collective-permute-start(bf16[256,256]{1,0:T(8,128)(2,1)S(1)} %pad_maximum_fusion.refs_0_), channel_id=1, source_target_pairs={{0,96},{32,64},{64,32},{96,0},{1,97},{33,65},{65,33},{97,1},{2,98}... | collective-permute-start | bytes 393224 | tf_op jit(solution)/shard_map/ppermute | solution.py:34
  41.8 1.9 %collective-permute-start.3 = (bf16[256,256]{1,0:T(8,128)(2,1)S(1)}, bf16[256,256]{1,0:T(8,128)(2,1)S(1)}, u32[]{:S(2)}, u32[]{:S(2)}) collective-permute-start(bf16[256,256]{1,0:T(8,128)(2,1)S(1)} %pad_maximum_fusion.refs_0_), channel_id=1, source_target_pairs={{0,64},{64,0},{1,65},{65,1},{2,66},{66,2},{3,67},{67,3},{4,68},{68... | collective-permute-start | bytes 393224 | tf_op jit(solution)/shard_map/ppermute | solution.py:30
  43.7 3.8 %collective-permute-start.2 = (bf16[256,256]{1,0:T(8,128)(2,1)S(1)}, bf16[256,256]{1,0:T(8,128)(2,1)S(1)}, u32[]{:S(2)}, u32[]{:S(2)}) collective-permute-start(bf16[256,256]{1,0:T(8,128)(2,1)S(1)} %pad_maximum_fusion.refs_0_), channel_id=1, source_target_pairs={{0,32},{32,0},{1,33},{33,1},{2,34},{34,2},{3,35},{35,3},{4,36},{36... | collective-permute-start | bytes 393224 | tf_op jit(solution)/shard_map/ppermute | solution.py:30
  47.5 2.2 %shard_map.84.col_ref = s32[1,1024]{1,0:T(1,128)S(1)} custom-call(s32[1]{0:T(128)} %bitcast.me_ref, s32[16,128]{1,0:T(8,128)S(1)} %bitcast.17, s32[512,1,128]{2,1,0:T(1,128)S(1)} %bitcast.16), custom_call_target="tpu_custom_call" | custom-call | flops 12582912 | bytes 1048576 | tf_op jit(solution)/shard_map/pallas_call | solution.py:200
  49.8 3.8 %collective-permute-done.3.refs_2_ = bf16[256,256]{1,0:T(8,128)(2,1)S(1)} collective-permute-done((bf16[256,256]{1,0:T(8,128)(2,1)S(1)}, bf16[256,256]{1,0:T(8,128)(2,1)S(1)}, u32[]{:S(2)}, u32[]{:S(2)}) %collective-permute-start.3) | collective-permute-done | bytes 131104 | tf_op jit(solution)/shard_map/ppermute | solution.py:30
  53.6 3.6 %shard_map.85 = f32[8,2,1024]{2,1,0:T(2,128)S(1)} custom-call(s32[1]{0:T(128)} %bitcast.me_ref, bf16[16,128,256]{2,1,0:T(8,128)(2,1)S(1)} %all-to-all-done.1.cold_ref, bf16[16,16,256]{2,1,0:T(8,128)(2,1)S(1)} %dynamic-slice_bitcast_fusion.hot_ref, s32[1,1024]{1,0:T(1,128)S(1)} %shard_map.84.col_ref, bf16[256,256]{1,0:T(8,128)(2,1)S(1)} %pad_maximum_fusion.refs_0_, ...), custom_call_target="tpu_custom_call" | custom-call | tf_op jit(solution)/shard_map/pallas_call | solution.py:220
  57.3 10.7 %all_to_all.35.stats_ref = f32[8,2,1024]{2,1,0:T(2,128)S(1)} all-to-all(f32[8,2,1024]{2,1,0:T(2,128)S(1)} %shard_map.85), channel_id=1, replica_groups=mesh['z8'=2,'z4'=2,'z2'=2,'z1'=2,'yl'=2,'c'=2,'x2'=2,'x1'=2,'yh'=2] {'z2..., dimensions={0} | all-to-all | bytes 131072 | tf_op jit(solution)/shard_map/all_to_all | solution.py:226
  68.0 5.6 %shard_map.86 = (f32[256,256]{1,0:T(8,128)S(1)}, bf16[256,256]{1,0:T(8,128)(2,1)S(1)}, bf16[256,256]{1,0:T(8,128)(2,1)S(1)}, bf16[256,256]{1,0:T(8,128)(2,1)S(1)...) custom-call(s32[1]{0:T(128)} %bitcast.me_ref, bf16[16,128,256]{2,1,0:T(8,128)(2,1)S(1)} %all-to-all-done.1.cold_ref, ...), custom_call_target="tpu_custom_call" | custom-call | tf_op jit(solution)/shard_map/pallas_call | solution.py:227
  73.6 6.5 %all-to-all-start.3 = ((bf16[16,144,256]{2,1,0:T(8,128)(2,1)}), bf16[16,144,256]{2,1,0:T(8,128)(2,1)S(1)}, u32[]{:S(2)}, u32[]{:S(2)}) async-start(bf16[16,144,256]{2,1,0:T(8,128)(2,1)} %get-tuple-element.23), calls=%async_computation.3 | async-start | bytes 2359296 | tf_op jit(solution)/shard_map/all_to_all | solution.py:240
  80.0 2.4 %collective-permute-start.4 = (bf16[256,256]{1,0:T(8,128)(2,1)S(1)}, bf16[256,256]{1,0:T(8,128)(2,1)S(1)}, u32[]{:S(2)}, u32[]{:S(2)}) collective-permute-start(bf16[256,256]{1,0:T(8,128)(2,1)S(1)} %get-tuple-element.25), channel_id=1, source_target_pairs={{0,32},{32,0},{1,33},{33,1},{2,34},{34,2},{3,35},{35,3},{4,36},{36... | collective-permute-start | bytes 393224 | tf_op jit(solution)/shard_map/ppermute | solution.py:30
  82.5 2.3 %collective-permute-start.5 = (bf16[256,256]{1,0:T(8,128)(2,1)S(1)}, bf16[256,256]{1,0:T(8,128)(2,1)S(1)}, u32[]{:S(2)}, u32[]{:S(2)}) collective-permute-start(bf16[256,256]{1,0:T(8,128)(2,1)S(1)} %get-tuple-element.26), channel_id=1, source_target_pairs={{0,64},{64,0},{1,65},{65,1},{2,66},{66,2},{3,67},{67,3},{4,68},{68... | collective-permute-start | bytes 393224 | tf_op jit(solution)/shard_map/ppermute | solution.py:30
  84.8 4.5 %collective-permute-start.6 = (bf16[256,256]{1,0:T(8,128)(2,1)S(1)}, bf16[256,256]{1,0:T(8,128)(2,1)S(1)}, u32[]{:S(2)}, u32[]{:S(2)}) collective-permute-start(bf16[256,256]{1,0:T(8,128)(2,1)S(1)} %get-tuple-element.27), channel_id=1, source_target_pairs={{0,96},{32,64},{64,32},{96,0},{1,97},{33,65},{65,33},{97,1},{2,98}... | collective-permute-start | bytes 393224 | tf_op jit(solution)/shard_map/ppermute | solution.py:34
  89.3 6.3 %collective-permute-done.5 = bf16[256,256]{1,0:T(8,128)(2,1)S(1)} collective-permute-done((bf16[256,256]{1,0:T(8,128)(2,1)S(1)}, bf16[256,256]{1,0:T(8,128)(2,1)S(1)}, u32[]{:S(2)}, u32[]{:S(2)}) %collective-permute-start.5) | collective-permute-done | bytes 131104 | tf_op jit(solution)/shard_map/ppermute | solution.py:30
  95.7 1.1 all-to-all-done.3
  96.8 0.2 reduce_sum.24
  97.0 14.6 %all_to_all.36 = bf16[4,48,256]{2,1,0:T(8,128)(2,1)S(1)} all-to-all(bf16[4,48,256]{2,1,0:T(8,128)(2,1)S(1)} %pad_maximum_fusion.1), channel_id=1, replica_groups=mesh['z8'=2,'z4'=2,'z2'=2,'z1'=2,'yl'=2,'c'=2,'x2'=2,'x1'=2,'yh'=2] {'z8..., dimensions={0} | all-to-all | bytes 196608 | tf_op jit(solution)/shard_map/all_to_all | solution.py:246
  111.6 7.7 %all_to_all.37 = bf16[4,16,256]{2,1,0:T(8,128)(2,1)S(1)} all-to-all(bf16[4,16,256]{2,1,0:T(8,128)(2,1)S(1)} %broadcast_in_dim.15), channel_id=1, replica_groups=mesh['z8'=2,'z4'=2,'z2'=2,'z1'=2,'yl'=2,'c'=2,'x2'=2,'x1'=2,'yh'=2] {'z2..., dimensions={0} | all-to-all | bytes 65536 | tf_op jit(solution)/shard_map/all_to_all | solution.py:26
  119.4 15.7 %all_to_all.38 = bf16[16,64,256]{2,1,0:T(8,128)(2,1)S(1)} all-to-all(bf16[16,64,256]{2,1,0:T(8,128)(2,1)S(1)} %broadcast_in_dim.17), channel_id=1, replica_groups=mesh['z8'=2,'z4'=2,'z2'=2,'z1'=2,'yl'=2,'c'=2,'x2'=2,'x1'=2,'yh'=2] {'x2..., dimensions={0} | all-to-all | bytes 1048576 | tf_op jit(solution)/shard_map/all_to_all | solution.py:26
  135.1 7.4 %collective-permute-start.8 = (bf16[1024,256]{1,0:T(8,128)(2,1)S(1)}, bf16[1024,256]{1,0:T(8,128)(2,1)S(1)}, u32[]{:S(2)}, u32[]{:S(2)}) collective-permute-start(bf16[1024,256]{1,0:T(8,128)(2,1)S(1)} %bitcast.14), channel_id=1, source_target_pairs={{0,8},{8,0},{1,9},{9,1},{2,10},{10,2},{3,11},{11,3},{4,12},{12,4},... | collective-permute-start | bytes 1572872 | tf_op jit(solution)/shard_map/ppermute | solution.py:30
  142.5 1.9 %collective-permute-start.7 = (bf16[128,256]{1,0:T(8,128)(2,1)S(1)}, bf16[128,256]{1,0:T(8,128)(2,1)S(1)}, u32[]{:S(2)}, u32[]{:S(2)}) collective-permute-start(bf16[128,256]{1,0:T(8,128)(2,1)S(1)} %slice.32), channel_id=1, source_target_pairs={{0,8},{8,0},{1,9},{9,1},{2,10},{10,2},{3,11},{11,3},{4,12},{12,4},... | collective-permute-start | bytes 196616 | tf_op jit(solution)/shard_map/ppermute | solution.py:30
  144.4 0.6 slice.30
  145.0 0.6 collective-permute-done.7
  145.7 0.6 add_convert_fusion
  146.3 1.0 shard_map.87
  (27 shorter events, 0.2 us)
Async XLA Ops:
  0.6 49.1 %copy-start = (bf16[2048,256]{1,0:T(8,128)(2,1)S(1)}, bf16[2048,256]{1,0:T(8,128)(2,1)}, u32[]{:S(2)}) copy-start(bf16[2048,256]{1,0:T(8,128)(2,1)} %param.6) | copy-start | bytes 3145732
  2.1 28.1 %all-to-all-start = ((bf16[4,32,256]{2,1,0:T(8,128)(2,1)}), bf16[4,32,256]{2,1,0:T(8,128)(2,1)S(1)}, u32[]{:S(2)}, u32[]{:S(2)}) async-start(bf16[4,32,256]{2,1,0:T(8,128)(2,1)} %broadcast_in_dim.12), calls=%async_computation | async-start | bytes 131072 | tf_op jit(solution)/shard_map/all_to_all | solution.py:26
  17.7 4.0 %collective-permute-start = (bf16[128,256]{1,0:T(8,128)(2,1)}, bf16[128,256]{1,0:T(8,128)(2,1)S(1)}, u32[]{:S(2)}, u32[]{:S(2)}) collective-permute-start(bf16[128,256]{1,0:T(8,128)(2,1)} %param.5), channel_id=1, source_target_pairs={{0,8},{8,0},{1,9},{9,1},{2,10},{10,2},{3,11},{11,3},{4,12},{12,4},... | collective-permute-start | bytes 196616 | tf_op jit(solution)/shard_map/ppermute | solution.py:30
  31.3 16.2 %copy-start.1 = (s32[65536]{0:T(1024)S(1)}, s32[65536]{0:T(1024)}, u32[]{:S(2)}) copy-start(s32[65536]{0:T(1024)} %param.9) | copy-start | bytes 786436
  31.3 16.2 %copy-start.2 = (s32[2048]{0:T(1024)S(1)}, s32[2048]{0:T(1024)}, u32[]{:S(2)}) copy-start(s32[2048]{0:T(1024)} %param.8) | copy-start | bytes 24580
  31.3 22.3 %all-to-all-start.1 = ((bf16[16,128,256]{2,1,0:T(8,128)(2,1)}), bf16[16,128,256]{2,1,0:T(8,128)(2,1)S(1)}, u32[]{:S(2)}, u32[]{:S(2)}) async-start(bf16[16,128,256]{2,1,0:T(8,128)(2,1)} %broadcast_in_dim.13), calls=%async_computation.1 | async-start | bytes 2097152 | tf_op jit(solution)/shard_map/all_to_all | solution.py:26
  38.2 11.6 %collective-permute-start.1 = (bf16[256,256]{1,0:T(8,128)(2,1)S(1)}, bf16[256,256]{1,0:T(8,128)(2,1)S(1)}, u32[]{:S(2)}, u32[]{:S(2)}) collective-permute-start(bf16[256,256]{1,0:T(8,128)(2,1)S(1)} %pad_maximum_fusion.refs_0_), channel_id=1, source_target_pairs={{0,96},{32,64},{64,32},{96,0},{1,97},{33,65},{65,33},{97,1},{2,98}... | collective-permute-start | bytes 393224 | tf_op jit(solution)/shard_map/ppermute | solution.py:34
  41.8 11.9 %collective-permute-start.3 = (bf16[256,256]{1,0:T(8,128)(2,1)S(1)}, bf16[256,256]{1,0:T(8,128)(2,1)S(1)}, u32[]{:S(2)}, u32[]{:S(2)}) collective-permute-start(bf16[256,256]{1,0:T(8,128)(2,1)S(1)} %pad_maximum_fusion.refs_0_), channel_id=1, source_target_pairs={{0,64},{64,0},{1,65},{65,1},{2,66},{66,2},{3,67},{67,3},{4,68},{68... | collective-permute-start | bytes 393224 | tf_op jit(solution)/shard_map/ppermute | solution.py:30
  43.7 9.9 %collective-permute-start.2 = (bf16[256,256]{1,0:T(8,128)(2,1)S(1)}, bf16[256,256]{1,0:T(8,128)(2,1)S(1)}, u32[]{:S(2)}, u32[]{:S(2)}) collective-permute-start(bf16[256,256]{1,0:T(8,128)(2,1)S(1)} %pad_maximum_fusion.refs_0_), channel_id=1, source_target_pairs={{0,32},{32,0},{1,33},{33,1},{2,34},{34,2},{3,35},{35,3},{4,36},{36... | collective-permute-start | bytes 393224 | tf_op jit(solution)/shard_map/ppermute | solution.py:30
  73.6 23.2 %all-to-all-start.3 = ((bf16[16,144,256]{2,1,0:T(8,128)(2,1)}), bf16[16,144,256]{2,1,0:T(8,128)(2,1)S(1)}, u32[]{:S(2)}, u32[]{:S(2)}) async-start(bf16[16,144,256]{2,1,0:T(8,128)(2,1)} %get-tuple-element.23), calls=%async_computation.3 | async-start | bytes 2359296 | tf_op jit(solution)/shard_map/all_to_all | solution.py:240
  80.0 9.3 %collective-permute-start.4 = (bf16[256,256]{1,0:T(8,128)(2,1)S(1)}, bf16[256,256]{1,0:T(8,128)(2,1)S(1)}, u32[]{:S(2)}, u32[]{:S(2)}) collective-permute-start(bf16[256,256]{1,0:T(8,128)(2,1)S(1)} %get-tuple-element.25), channel_id=1, source_target_pairs={{0,32},{32,0},{1,33},{33,1},{2,34},{34,2},{3,35},{35,3},{4,36},{36... | collective-permute-start | bytes 393224 | tf_op jit(solution)/shard_map/ppermute | solution.py:30
  82.5 13.1 %collective-permute-start.5 = (bf16[256,256]{1,0:T(8,128)(2,1)S(1)}, bf16[256,256]{1,0:T(8,128)(2,1)S(1)}, u32[]{:S(2)}, u32[]{:S(2)}) collective-permute-start(bf16[256,256]{1,0:T(8,128)(2,1)S(1)} %get-tuple-element.26), channel_id=1, source_target_pairs={{0,64},{64,0},{1,65},{65,1},{2,66},{66,2},{3,67},{67,3},{4,68},{68... | collective-permute-start | bytes 393224 | tf_op jit(solution)/shard_map/ppermute | solution.py:30
  84.8 10.8 %collective-permute-start.6 = (bf16[256,256]{1,0:T(8,128)(2,1)S(1)}, bf16[256,256]{1,0:T(8,128)(2,1)S(1)}, u32[]{:S(2)}, u32[]{:S(2)}) collective-permute-start(bf16[256,256]{1,0:T(8,128)(2,1)S(1)} %get-tuple-element.27), channel_id=1, source_target_pairs={{0,96},{32,64},{64,32},{96,0},{1,97},{33,65},{65,33},{97,1},{2,98}... | collective-permute-start | bytes 393224 | tf_op jit(solution)/shard_map/ppermute | solution.py:34
  95.7 16.0 %copy-start.3 = (f32[256,256]{1,0:T(8,128)}, f32[256,256]{1,0:T(8,128)S(1)}, u32[]{:S(2)}) copy-start(f32[256,256]{1,0:T(8,128)S(1)} %add_add_fusion) | copy-start | bytes 786436
  111.6 34.0 %slice-start = ((f32[256,256]{1,0:T(8,128)}), f32[128,256]{1,0:T(8,128)S(1)}, s32[]{:S(2)}) async-start(f32[256,256]{1,0:T(8,128)} %copy-done.3), calls=%async_computation.7 | async-start | bytes 262144 | tf_op jit(solution)/shard_map/slice | solution.py:242
  135.1 11.2 %collective-permute-start.8 = (bf16[1024,256]{1,0:T(8,128)(2,1)S(1)}, bf16[1024,256]{1,0:T(8,128)(2,1)S(1)}, u32[]{:S(2)}, u32[]{:S(2)}) collective-permute-start(bf16[1024,256]{1,0:T(8,128)(2,1)S(1)} %bitcast.14), channel_id=1, source_target_pairs={{0,8},{8,0},{1,9},{9,1},{2,10},{10,2},{3,11},{11,3},{4,12},{12,4},... | collective-permute-start | bytes 1572872 | tf_op jit(solution)/shard_map/ppermute | solution.py:30
  142.5 3.1 %collective-permute-start.7 = (bf16[128,256]{1,0:T(8,128)(2,1)S(1)}, bf16[128,256]{1,0:T(8,128)(2,1)S(1)}, u32[]{:S(2)}, u32[]{:S(2)}) collective-permute-start(bf16[128,256]{1,0:T(8,128)(2,1)S(1)} %slice.32), channel_id=1, source_target_pairs={{0,8},{8,0},{1,9},{9,1},{2,10},{10,2},{3,11},{11,3},{4,12},{12,4},... | collective-permute-start | bytes 196616 | tf_op jit(solution)/shard_map/ppermute | solution.py:30

commit v12 on v11

--- a/solution.py
+++ b/solution.py
@@ -9,7 +9,7 @@
 from jax.sharding import PartitionSpec as P
 
 AXES = ("z8", "z4", "z2", "z1", "yl", "c", "x2", "x1", "yh")
-COLS = ("z2", "z1", "c")
+COLS = ("c", "z2", "z1")
 HALF = ("z2", "z1")
 NEAR = ("x2", "x1", "yh", "yl")
 FAR = ("z8", "z4")
@@ -86,7 +86,7 @@
     cold_col = near // near_chunk * width + (near % near_chunk) * (NF * shard)
     cold_col += pick(block, FAR) * shard + (row & (shard - 1))
     hot_near = (slot >> 6) & (NG - 1)
-    hot_k = (((slot >> 4) & 3) << 1) | (slot >> 10)
+    hot_k = ((slot >> 10) << 2) | ((slot >> 4) & 3)
     hot_col = hot_near // near_chunk * width + near_chunk * NF * shard
     hot_col += (hot_near % near_chunk) * hot_own + (slot & (hot_own - 1))
     column = jnp.where(is_hot, hot_col, cold_col)
@@ -163,10 +163,12 @@
         return carry
 
     lax.fori_loop(0, CHUNKS, step, 0, unroll=True)
-    quarter = acc_ref.shape[1] // 4
-    keep_ref[...] = acc_ref[:, :quarter].T
-    for j, ref in enumerate((send_1, send_2, send_3)):
-        ref[...] = acc_ref[:, (j + 1) * quarter : (j + 2) * quarter].T.astype(BF)
+    own = acc_ref.shape[1] // NC
+    for j, ref in enumerate((keep_ref, send_1, send_2, send_3)):
+        for core in range(2):
+            p = core * (NC // 2) + j
+            part = acc_ref[:, p * own : (p + 1) * own].T
+            ref[core * own : (core + 1) * own] = part.astype(ref.dtype)
 
 
 def place_kernel(me_ref, own_ref, other_ref, out_ref, sems):
@@ -195,7 +197,7 @@
     vmem = pl.BlockSpec(memory_space=pltpu.VMEM)
     smem = pl.BlockSpec(memory_space=pltpu.SMEM)
 
-    pair = jnp.concatenate([queries, swap(queries, "c")], axis=0)
+    rows = [queries, swap(queries, "z1")]
 
     column = pl.pallas_call(
         decode_kernel,
@@ -209,12 +211,14 @@
     )(at_me, hot_ids.reshape(-1, 128), targets.reshape(-1, 1, own))
 
     far = spread(cold_table, FAR).reshape(NF * shard, width)
-    far, pair = lax.optimization_barrier((far, pair))
+    far, rows[1] = lax.optimization_barrier((far, rows[1]))
     cold = spread(far, NEAR)
-    rows = [pair, *around(pair, pair, pair)]
-    rows[3], column = lax.optimization_barrier((rows[3], column))
+    rows = jnp.concatenate(rows, axis=0)
+    other, column = lax.optimization_barrier((swap(rows, "z2"), column))
+    rows = jnp.concatenate([rows, other], axis=0)
+    rows = [rows, swap(rows, "c")]
     mine = hot_table.reshape(2, NG, NC // 2, hot_own, width)
-    mine = lax.dynamic_slice(mine, (k & 1, 0, k >> 1, 0, 0), (1, NG, 1, hot_own, width))
+    mine = lax.dynamic_slice(mine, (k >> 2, 0, k & 3, 0, 0), (1, NG, 1, hot_own, width))
     mine = mine.reshape(NG, hot_own, width)
 
     stats = pl.pallas_call(
@@ -244,12 +248,13 @@
     cold_part = near[: NF * shard].reshape(NF, shard, width)
     hot_part = jnp.broadcast_to(near[None, NF * shard :], (NF, hot_own, width))
     far = lax.all_to_all(jnp.concatenate([cold_part, hot_part], axis=1), FAR, 0, 0)
+    far, other = lax.optimization_barrier((far, swap(other, "c")))
+    grad_queries = (keep + other.astype(F32)).astype(BF)
     far = jnp.sum(far.astype(F32), axis=0).astype(BF)
     grad_cold = far[:shard]
     grad_hot = spread(far[shard:], HALF).reshape(-1, width)
     grad_hot = spread(grad_hot, NEAR)
-    grad_hot, other = lax.optimization_barrier((grad_hot.reshape(hot // 2, width), other))
-    grad_queries = (keep + swap(other, "c").astype(F32)).astype(BF)
+    grad_hot = grad_hot.reshape(hot // 2, width)
     grad_hot = pl.pallas_call(
         place_kernel,
         out_shape=jax.ShapeDtypeStruct((hot, width), BF),

time: 148 us -> 147 us (level)
  blocking collectives: 48.7 us -> 34.9 us
  waiting for transfers between devices: 20.6 us -> 29.5 us
  starting transfers between devices: 59.7 us -> 63.2 us
    all_to_all x1 -> x0, blocking collectives: 14.6 us -> none  [body(): lax.all_to_all(jnp.concatenate([cold_part, hot_part], axis=1), FAR, 0, 0)]
    all_to_all x0 -> x1, waiting for transfers between devices: none -> 5.59 us  [body(): lax.all_to_all(jnp.concatenate([cold_part, hot_part], axis=1), FAR, 0, 0)]
    ppermute x7, starting transfers between devices: 22.6 us -> 27.4 us  [swap(): return lax.ppermute(x, axis, [(0, 1), (1, 0)])]
    all_to_all x0 -> x1, starting transfers between devices: none -> 4.51 us  [body(): lax.all_to_all(jnp.concatenate([cold_part, hot_part], axis=1), FAR, 0, 0)]
    ppermute x2 -> x1, starting transfers between devices: 8.06 us -> 5.09 us  [around(): both = lax.ppermute(by_both, ('z2', 'z1'), [(i, 3 - i) for i in range(4)])]
    all_to_all x1, starting transfers between devices: 6.47 us -> 3.7 us  [body(): near = lax.all_to_all(item_part, NEAR, 0, 0)]
    ppermute x7, waiting for transfers between devices: 11.8 us -> 14 us  [swap(): return lax.ppermute(x, axis, [(0, 1), (1, 0)])]
  transfers between devices with their start and end apart: 12 -> 12, of which waited for: 6 -> 10; matrix products, arithmetic and copies ran while one was open for 1% -> 1% of each run, Pallas kernels for 2% -> 2%
where the time goes in v12:
time: 147 us; the launch traced here: 146 us
  starting transfers between devices  63.2 us (43%)
  blocking collectives  34.9 us (24%)
  waiting for transfers between devices  29.5 us (20%)
  Pallas kernels  12.5 us (9%)
  local copies, waits for them, and re-layouts  3.26 us (2%)
  other arithmetic  1.55 us (1%)
    ppermute x7, starting transfers between devices, swap(): return lax.ppermute(x, axis, [(0, 1), (1, 0)])  27.4 us
    all_to_all x2, blocking collectives, spread(): return lax.all_to_all(jnp.broadcast_to(x[None], (n, *x.shape)), axes, 0, 0)  23.2 us
    all_to_all x2, starting transfers between devices, spread(): return lax.all_to_all(jnp.broadcast_to(x[None], (n, *x.shape)), axes, 0, 0)  22.5 us
    ppermute x7, waiting for transfers between devices, swap(): return lax.ppermute(x, axis, [(0, 1), (1, 0)])  14 us
    all_to_all x1, blocking collectives, body(): stats = lax.all_to_all(stats, COLS, 0, 0)  11.8 us
    all_to_all x2, waiting for transfers between devices, spread(): return lax.all_to_all(jnp.broadcast_to(x[None], (n, *x.shape)), axes, 0, 0)  7.63 us
    pallas_call x1, Pallas kernels, body(): pl.pallas_call(grads_kernel, out_shape=(jax.ShapeDtypeStruct((count // 4,...  5.66 us
    all_to_all x1, waiting for transfers between devices, body(): lax.all_to_all(jnp.concatenate([cold_part, hot_part], axis=1), FAR, 0, 0)  5.59 us
  transfers between devices with their start and end apart: 12, of which 10 were waited for; matrix products, arithmetic and copies ran while one was open for 1% of the time, Pallas kernels for 2%

profile of v12, /device:TPU:1, one launch (start us, length us, event | category | flops | bytes accessed | tf_op | source)
XLA Modules:
  0.0 145.9 jit_solution(15823962636098690216)
XLA Ops:
  0.6 1.4 broadcast_in_dim.12
  2.1 15.6 %all-to-all-start = ((bf16[4,32,256]{2,1,0:T(8,128)(2,1)}), bf16[4,32,256]{2,1,0:T(8,128)(2,1)S(1)}, u32[]{:S(2)}, u32[]{:S(2)}) async-start(bf16[4,32,256]{2,1,0:T(8,128)(2,1)} %broadcast_in_dim.12), calls=%async_computation | async-start | bytes 131072 | tf_op jit(solution)/shard_map/all_to_all | solution.py:26
  17.7 2.6 %collective-permute-start = (bf16[128,256]{1,0:T(8,128)(2,1)}, bf16[128,256]{1,0:T(8,128)(2,1)S(1)}, u32[]{:S(2)}, u32[]{:S(2)}) collective-permute-start(bf16[128,256]{1,0:T(8,128)(2,1)} %param.5), channel_id=1, source_target_pairs={{0,32},{32,0},{1,33},{33,1},{2,34},{34,2},{3,35},{35,3},{4,36},{36... | collective-permute-start | bytes 196616 | tf_op jit(solution)/shard_map/ppermute | solution.py:30
  20.4 2.6 %collective-permute-done = bf16[128,256]{1,0:T(8,128)(2,1)S(1)} collective-permute-done((bf16[128,256]{1,0:T(8,128)(2,1)}, bf16[128,256]{1,0:T(8,128)(2,1)S(1)}, u32[]{:S(2)}, u32[]{:S(2)}) %collective-permute-start) | collective-permute-done | bytes 65568 | tf_op jit(solution)/shard_map/ppermute | solution.py:30
  22.9 7.3 %all-to-all-done = bf16[4,32,256]{2,1,0:T(8,128)(2,1)S(1)} async-done(((bf16[4,32,256]{2,1,0:T(8,128)(2,1)}), bf16[4,32,256]{2,1,0:T(8,128)(2,1)S(1)}, u32[]{:S(2)}, u32[]{:S(2)}) %all-to-all-start) | async-done | bytes 65568 | tf_op jit(solution)/shard_map/all_to_all | solution.py:26
  30.2 1.1 broadcast_in_dim.13
  31.3 6.9 %all-to-all-start.1 = ((bf16[16,128,256]{2,1,0:T(8,128)(2,1)}), bf16[16,128,256]{2,1,0:T(8,128)(2,1)S(1)}, u32[]{:S(2)}, u32[]{:S(2)}) async-start(bf16[16,128,256]{2,1,0:T(8,128)(2,1)} %broadcast_in_dim.13), calls=%async_computation.1 | async-start | bytes 2097152 | tf_op jit(solution)/shard_map/all_to_all | solution.py:26
  38.2 2.7 %collective-permute-start.1 = (bf16[256,256]{1,0:T(8,128)(2,1)S(1)}, bf16[256,256]{1,0:T(8,128)(2,1)S(1)}, u32[]{:S(2)}, u32[]{:S(2)}) collective-permute-start(bf16[256,256]{1,0:T(8,128)(2,1)S(1)} %pad_maximum_fusion), channel_id=1, source_target_pairs={{0,64},{64,0},{1,65},{65,1},{2,66},{66,2},{3,67},{67,3},{4,68},{68... | collective-permute-start | bytes 393224 | tf_op jit(solution)/shard_map/ppermute | solution.py:30
  40.9 2.2 %shard_map.84.col_ref = s32[1,1024]{1,0:T(1,128)S(1)} custom-call(s32[1]{0:T(128)} %bitcast.me_ref, s32[16,128]{1,0:T(8,128)S(1)} %bitcast.17, s32[512,1,128]{2,1,0:T(1,128)S(1)} %bitcast.16), custom_call_target="tpu_custom_call" | custom-call | flops 12582912 | bytes 1048576 | tf_op jit(solution)/shard_map/pallas_call | solution.py:202
  43.2 3.8 %collective-permute-done.1 = bf16[256,256]{1,0:T(8,128)(2,1)S(1)} collective-permute-done((bf16[256,256]{1,0:T(8,128)(2,1)S(1)}, bf16[256,256]{1,0:T(8,128)(2,1)S(1)}, u32[]{:S(2)}, u32[]{:S(2)}) %collective-permute-start.1) | collective-permute-done | bytes 131104 | tf_op jit(solution)/shard_map/ppermute | solution.py:30
  47.0 4.7 %collective-permute-start.2 = (bf16[512,256]{1,0:T(8,128)(2,1)S(1)}, bf16[512,256]{1,0:T(8,128)(2,1)S(1)}, u32[]{:S(2)}, u32[]{:S(2)}) collective-permute-start(bf16[512,256]{1,0:T(8,128)(2,1)S(1)} %constant_dynamic-update-slice_fusion.refs_0_), channel_id=1, source_target_pairs={{0,8},{8,0},{1,9},{9,1},{2,10},{10,2},{3,11},{11,3},{4,12},{12,4},... | collective-permute-start | bytes 786440 | tf_op jit(solution)/shard_map/ppermute | solution.py:30
  51.7 1.1 collective-permute-done.2.refs_1_
  53.2 3.6 %shard_map.85 = f32[8,2,1024]{2,1,0:T(2,128)S(1)} custom-call(s32[1]{0:T(128)} %bitcast.me_ref, bf16[16,128,256]{2,1,0:T(8,128)(2,1)S(1)} %all-to-all-done.1.cold_ref, bf16[16,16,256]{2,1,0:T(8,128)(2,1)S(1)} %dynamic-slice_bitcast_fusion.hot_ref, s32[1,1024]{1,0:T(1,128)S(1)} %shard_map.84.col_ref, ...), custom_call_target="tpu_custom_call" | custom-call | tf_op jit(solution)/shard_map/pallas_call | solution.py:224
  56.8 11.8 %all_to_all.35.stats_ref = f32[8,2,1024]{2,1,0:T(2,128)S(1)} all-to-all(f32[8,2,1024]{2,1,0:T(2,128)S(1)} %shard_map.85), channel_id=1, replica_groups=mesh['z8'=2,'z4'=2,'z2'=2,'z1'=2,'yl'=2,'c'=2,'x2'=2,'x1'=2,'yh'=2] {'c'..., dimensions={0} | all-to-all | bytes 131072 | tf_op jit(solution)/shard_map/all_to_all | solution.py:230
  68.5 5.7 %shard_map.86 = (f32[256,256]{1,0:T(8,128)S(1)}, bf16[256,256]{1,0:T(8,128)(2,1)S(1)}, bf16[256,256]{1,0:T(8,128)(2,1)S(1)}, bf16[256,256]{1,0:T(8,128)(2,1)S(1)...) custom-call(s32[1]{0:T(128)} %bitcast.me_ref, bf16[16,128,256]{2,1,0:T(8,128)(2,1)S(1)} %all-to-all-done.1.cold_ref, ...), custom_call_target="tpu_custom_call" | custom-call | tf_op jit(solution)/shard_map/pallas_call | solution.py:231
  74.2 3.7 %all-to-all-start.3 = ((bf16[16,144,256]{2,1,0:T(8,128)(2,1)}), bf16[16,144,256]{2,1,0:T(8,128)(2,1)S(1)}, u32[]{:S(2)}, u32[]{:S(2)}) async-start(bf16[16,144,256]{2,1,0:T(8,128)(2,1)} %get-tuple-element.23), calls=%async_computation.3 | async-start | bytes 2359296 | tf_op jit(solution)/shard_map/all_to_all | solution.py:244
  77.9 2.0 %collective-permute-start.3 = (bf16[256,256]{1,0:T(8,128)(2,1)S(1)}, bf16[256,256]{1,0:T(8,128)(2,1)S(1)}, u32[]{:S(2)}, u32[]{:S(2)}) collective-permute-start(bf16[256,256]{1,0:T(8,128)(2,1)S(1)} %get-tuple-element.25), channel_id=1, source_target_pairs={{0,32},{32,0},{1,33},{33,1},{2,34},{34,2},{3,35},{35,3},{4,36},{36... | collective-permute-start | bytes 393224 | tf_op jit(solution)/shard_map/ppermute | solution.py:30
  79.9 2.2 %collective-permute-start.4 = (bf16[256,256]{1,0:T(8,128)(2,1)S(1)}, bf16[256,256]{1,0:T(8,128)(2,1)S(1)}, u32[]{:S(2)}, u32[]{:S(2)}) collective-permute-start(bf16[256,256]{1,0:T(8,128)(2,1)S(1)} %get-tuple-element.26), channel_id=1, source_target_pairs={{0,64},{64,0},{1,65},{65,1},{2,66},{66,2},{3,67},{67,3},{4,68},{68... | collective-permute-start | bytes 393224 | tf_op jit(solution)/shard_map/ppermute | solution.py:30
  82.1 5.1 %collective-permute-start.5 = (bf16[256,256]{1,0:T(8,128)(2,1)S(1)}, bf16[256,256]{1,0:T(8,128)(2,1)S(1)}, u32[]{:S(2)}, u32[]{:S(2)}) collective-permute-start(bf16[256,256]{1,0:T(8,128)(2,1)S(1)} %get-tuple-element.27), channel_id=1, source_target_pairs={{0,96},{32,64},{64,32},{96,0},{1,97},{33,65},{65,33},{97,1},{2,98}... | collective-permute-start | bytes 393224 | tf_op jit(solution)/shard_map/ppermute | solution.py:34
  87.2 5.5 %collective-permute-done.4 = bf16[256,256]{1,0:T(8,128)(2,1)S(1)} collective-permute-done((bf16[256,256]{1,0:T(8,128)(2,1)S(1)}, bf16[256,256]{1,0:T(8,128)(2,1)S(1)}, u32[]{:S(2)}, u32[]{:S(2)}) %collective-permute-start.4) | collective-permute-done | bytes 131104 | tf_op jit(solution)/shard_map/ppermute | solution.py:30
  92.7 2.3 %all-to-all-done.3 = bf16[16,144,256]{2,1,0:T(8,128)(2,1)S(1)} async-done(((bf16[16,144,256]{2,1,0:T(8,128)(2,1)}), bf16[16,144,256]{2,1,0:T(8,128)(2,1)S(1)}, u32[]{:S(2)}, u32[]{:S(2)}) %all-to-all-start.3) | async-done | bytes 1179680 | tf_op jit(solution)/shard_map/all_to_all | solution.py:244
  95.2 0.7 pad_maximum_fusion.1
  95.9 4.5 %all-to-all-start.4 = ((bf16[4,48,256]{2,1,0:T(8,128)(2,1)}), bf16[4,48,256]{2,1,0:T(8,128)(2,1)S(1)}, u32[]{:S(2)}, u32[]{:S(2)}) async-start(bf16[4,48,256]{2,1,0:T(8,128)(2,1)} %pad_maximum_fusion.1), calls=%async_computation.4 | async-start | bytes 196608 | tf_op jit(solution)/shard_map/all_to_all | solution.py:250
  100.4 5.4 %collective-permute-start.6 = (bf16[128,256]{1,0:T(8,128)(2,1)S(1)}, bf16[128,256]{1,0:T(8,128)(2,1)S(1)}, u32[]{:S(2)}, u32[]{:S(2)}) collective-permute-start(bf16[128,256]{1,0:T(8,128)(2,1)S(1)} %slice.32), channel_id=1, source_target_pairs={{0,8},{8,0},{1,9},{9,1},{2,10},{10,2},{3,11},{11,3},{4,12},{12,4},... | collective-permute-start | bytes 196616 | tf_op jit(solution)/shard_map/ppermute | solution.py:30
  105.8 0.9 collective-permute-done.6
  106.7 5.6 %all-to-all-done.4 = bf16[4,48,256]{2,1,0:T(8,128)(2,1)S(1)} async-done(((bf16[4,48,256]{2,1,0:T(8,128)(2,1)}), bf16[4,48,256]{2,1,0:T(8,128)(2,1)S(1)}, u32[]{:S(2)}, u32[]{:S(2)}) %all-to-all-start.4) | async-done | bytes 98336 | tf_op jit(solution)/shard_map/all_to_all | solution.py:250
  112.3 7.1 %all_to_all.36 = bf16[4,16,256]{2,1,0:T(8,128)(2,1)S(1)} all-to-all(bf16[4,16,256]{2,1,0:T(8,128)(2,1)S(1)} %broadcast_in_dim.15), channel_id=1, replica_groups=mesh['z8'=2,'z4'=2,'z2'=2,'z1'=2,'yl'=2,'c'=2,'x2'=2,'x1'=2,'yh'=2] {'z2..., dimensions={0} | all-to-all | bytes 65536 | tf_op jit(solution)/shard_map/all_to_all | solution.py:26
  119.5 16.1 %all_to_all.37 = bf16[16,64,256]{2,1,0:T(8,128)(2,1)S(1)} all-to-all(bf16[16,64,256]{2,1,0:T(8,128)(2,1)S(1)} %broadcast_in_dim.17), channel_id=1, replica_groups=mesh['z8'=2,'z4'=2,'z2'=2,'z1'=2,'yl'=2,'c'=2,'x2'=2,'x1'=2,'yh'=2] {'x2..., dimensions={0} | all-to-all | bytes 1048576 | tf_op jit(solution)/shard_map/all_to_all | solution.py:26
  135.6 7.8 %collective-permute-start.7 = (bf16[1024,256]{1,0:T(8,128)(2,1)S(1)}, bf16[1024,256]{1,0:T(8,128)(2,1)S(1)}, u32[]{:S(2)}, u32[]{:S(2)}) collective-permute-start(bf16[1024,256]{1,0:T(8,128)(2,1)S(1)} %bitcast.14), channel_id=1, source_target_pairs={{0,8},{8,0},{1,9},{9,1},{2,10},{10,2},{3,11},{11,3},{4,12},{12,4},... | collective-permute-start | bytes 1572872 | tf_op jit(solution)/shard_map/ppermute | solution.py:30
  143.4 0.6 slice.30
  144.0 0.6 add_convert_fusion
  144.9 1.0 shard_map.87
  (31 shorter events, 1.0 us)
Async XLA Ops:
  0.6 51.0 %copy-start = (bf16[2048,256]{1,0:T(8,128)(2,1)S(1)}, bf16[2048,256]{1,0:T(8,128)(2,1)}, u32[]{:S(2)}) copy-start(bf16[2048,256]{1,0:T(8,128)(2,1)} %param.6) | copy-start | bytes 3145732
  2.1 28.1 %all-to-all-start = ((bf16[4,32,256]{2,1,0:T(8,128)(2,1)}), bf16[4,32,256]{2,1,0:T(8,128)(2,1)S(1)}, u32[]{:S(2)}, u32[]{:S(2)}) async-start(bf16[4,32,256]{2,1,0:T(8,128)(2,1)} %broadcast_in_dim.12), calls=%async_computation | async-start | bytes 131072 | tf_op jit(solution)/shard_map/all_to_all | solution.py:26
  17.7 5.2 %collective-permute-start = (bf16[128,256]{1,0:T(8,128)(2,1)}, bf16[128,256]{1,0:T(8,128)(2,1)S(1)}, u32[]{:S(2)}, u32[]{:S(2)}) collective-permute-start(bf16[128,256]{1,0:T(8,128)(2,1)} %param.5), channel_id=1, source_target_pairs={{0,32},{32,0},{1,33},{33,1},{2,34},{34,2},{3,35},{35,3},{4,36},{36... | collective-permute-start | bytes 196616 | tf_op jit(solution)/shard_map/ppermute | solution.py:30
  31.3 6.9 %copy-start.4 = (bf16[128,256]{1,0:T(8,128)(2,1)S(1)}, bf16[128,256]{1,0:T(8,128)(2,1)}, u32[]{:S(2)}) copy-start(bf16[128,256]{1,0:T(8,128)(2,1)} %param.5) | copy-start | bytes 196612
  31.3 9.6 %copy-start.1 = (s32[65536]{0:T(1024)S(1)}, s32[65536]{0:T(1024)}, u32[]{:S(2)}) copy-start(s32[65536]{0:T(1024)} %param.9) | copy-start | bytes 786436
  31.3 9.6 %copy-start.2 = (s32[2048]{0:T(1024)S(1)}, s32[2048]{0:T(1024)}, u32[]{:S(2)}) copy-start(s32[2048]{0:T(1024)} %param.8) | copy-start | bytes 24580
  31.3 21.9 %all-to-all-start.1 = ((bf16[16,128,256]{2,1,0:T(8,128)(2,1)}), bf16[16,128,256]{2,1,0:T(8,128)(2,1)S(1)}, u32[]{:S(2)}, u32[]{:S(2)}) async-start(bf16[16,128,256]{2,1,0:T(8,128)(2,1)} %broadcast_in_dim.13), calls=%async_computation.1 | async-start | bytes 2097152 | tf_op jit(solution)/shard_map/all_to_all | solution.py:26
  38.2 8.7 %collective-permute-start.1 = (bf16[256,256]{1,0:T(8,128)(2,1)S(1)}, bf16[256,256]{1,0:T(8,128)(2,1)S(1)}, u32[]{:S(2)}, u32[]{:S(2)}) collective-permute-start(bf16[256,256]{1,0:T(8,128)(2,1)S(1)} %pad_maximum_fusion), channel_id=1, source_target_pairs={{0,64},{64,0},{1,65},{65,1},{2,66},{66,2},{3,67},{67,3},{4,68},{68... | collective-permute-start | bytes 393224 | tf_op jit(solution)/shard_map/ppermute | solution.py:30
  47.0 5.8 %collective-permute-start.2 = (bf16[512,256]{1,0:T(8,128)(2,1)S(1)}, bf16[512,256]{1,0:T(8,128)(2,1)S(1)}, u32[]{:S(2)}, u32[]{:S(2)}) collective-permute-start(bf16[512,256]{1,0:T(8,128)(2,1)S(1)} %constant_dynamic-update-slice_fusion.refs_0_), channel_id=1, source_target_pairs={{0,8},{8,0},{1,9},{9,1},{2,10},{10,2},{3,11},{11,3},{4,12},{12,4},... | collective-permute-start | bytes 786440 | tf_op jit(solution)/shard_map/ppermute | solution.py:30
  74.2 20.8 %all-to-all-start.3 = ((bf16[16,144,256]{2,1,0:T(8,128)(2,1)}), bf16[16,144,256]{2,1,0:T(8,128)(2,1)S(1)}, u32[]{:S(2)}, u32[]{:S(2)}) async-start(bf16[16,144,256]{2,1,0:T(8,128)(2,1)} %get-tuple-element.23), calls=%async_computation.3 | async-start | bytes 2359296 | tf_op jit(solution)/shard_map/all_to_all | solution.py:244
  77.9 9.3 %collective-permute-start.3 = (bf16[256,256]{1,0:T(8,128)(2,1)S(1)}, bf16[256,256]{1,0:T(8,128)(2,1)S(1)}, u32[]{:S(2)}, u32[]{:S(2)}) collective-permute-start(bf16[256,256]{1,0:T(8,128)(2,1)S(1)} %get-tuple-element.25), channel_id=1, source_target_pairs={{0,32},{32,0},{1,33},{33,1},{2,34},{34,2},{3,35},{35,3},{4,36},{36... | collective-permute-start | bytes 393224 | tf_op jit(solution)/shard_map/ppermute | solution.py:30
  79.9 12.7 %collective-permute-start.4 = (bf16[256,256]{1,0:T(8,128)(2,1)S(1)}, bf16[256,256]{1,0:T(8,128)(2,1)S(1)}, u32[]{:S(2)}, u32[]{:S(2)}) collective-permute-start(bf16[256,256]{1,0:T(8,128)(2,1)S(1)} %get-tuple-element.26), channel_id=1, source_target_pairs={{0,64},{64,0},{1,65},{65,1},{2,66},{66,2},{3,67},{67,3},{4,68},{68... | collective-permute-start | bytes 393224 | tf_op jit(solution)/shard_map/ppermute | solution.py:30
  82.1 10.6 %collective-permute-start.5 = (bf16[256,256]{1,0:T(8,128)(2,1)S(1)}, bf16[256,256]{1,0:T(8,128)(2,1)S(1)}, u32[]{:S(2)}, u32[]{:S(2)}) collective-permute-start(bf16[256,256]{1,0:T(8,128)(2,1)S(1)} %get-tuple-element.27), channel_id=1, source_target_pairs={{0,96},{32,64},{64,32},{96,0},{1,97},{33,65},{65,33},{97,1},{2,98}... | collective-permute-start | bytes 393224 | tf_op jit(solution)/shard_map/ppermute | solution.py:34
  92.7 19.6 %copy-start.3 = (f32[256,256]{1,0:T(8,128)}, f32[256,256]{1,0:T(8,128)S(1)}, u32[]{:S(2)}) copy-start(f32[256,256]{1,0:T(8,128)S(1)} %add_add_fusion) | copy-start | bytes 786436
  95.9 16.4 %all-to-all-start.4 = ((bf16[4,48,256]{2,1,0:T(8,128)(2,1)}), bf16[4,48,256]{2,1,0:T(8,128)(2,1)S(1)}, u32[]{:S(2)}, u32[]{:S(2)}) async-start(bf16[4,48,256]{2,1,0:T(8,128)(2,1)} %pad_maximum_fusion.1), calls=%async_computation.4 | async-start | bytes 196608 | tf_op jit(solution)/shard_map/all_to_all | solution.py:250
  100.4 6.3 %collective-permute-start.6 = (bf16[128,256]{1,0:T(8,128)(2,1)S(1)}, bf16[128,256]{1,0:T(8,128)(2,1)S(1)}, u32[]{:S(2)}, u32[]{:S(2)}) collective-permute-start(bf16[128,256]{1,0:T(8,128)(2,1)S(1)} %slice.32), channel_id=1, source_target_pairs={{0,8},{8,0},{1,9},{9,1},{2,10},{10,2},{3,11},{11,3},{4,12},{12,4},... | collective-permute-start | bytes 196616 | tf_op jit(solution)/shard_map/ppermute | solution.py:30
  112.3 31.7 %slice-start = ((f32[256,256]{1,0:T(8,128)}), f32[128,256]{1,0:T(8,128)S(1)}, s32[]{:S(2)}) async-start(f32[256,256]{1,0:T(8,128)} %copy-done.3), calls=%async_computation.7 | async-start | bytes 262144 | tf_op jit(solution)/shard_map/slice | solution.py:246
  135.6 9.3 %collective-permute-start.7 = (bf16[1024,256]{1,0:T(8,128)(2,1)S(1)}, bf16[1024,256]{1,0:T(8,128)(2,1)S(1)}, u32[]{:S(2)}, u32[]{:S(2)}) collective-permute-start(bf16[1024,256]{1,0:T(8,128)(2,1)S(1)} %bitcast.14), channel_id=1, source_target_pairs={{0,8},{8,0},{1,9},{9,1},{2,10},{10,2},{3,11},{11,3},{4,12},{12,4},... | collective-permute-start | bytes 1572872 | tf_op jit(solution)/shard_map/ppermute | solution.py:30

commit v13 on v12

--- a/solution.py
+++ b/solution.py
@@ -171,15 +171,16 @@
             ref[core * own : (core + 1) * own] = part.astype(ref.dtype)
 
 
-def place_kernel(me_ref, own_ref, other_ref, out_ref, sems):
+def place_kernel(me_ref, own_ref, other_ref, keep_ref, out_ref, query_ref, sems):
     core = bit(me_ref[0], "c")
     half = own_ref.shape[0]
     first = pltpu.make_async_copy(own_ref, out_ref.at[pl.ds(core * half, half)], sems.at[0])
     second = pltpu.make_async_copy(
-        other_ref, out_ref.at[pl.ds((1 - core) * half, half)], sems.at[1]
+        other_ref.at[pl.ds(0, half)], out_ref.at[pl.ds((1 - core) * half, half)], sems.at[1]
     )
     first.start()
     second.start()
+    query_ref[...] = (keep_ref[...] + other_ref[half:].astype(F32)).astype(query_ref.dtype)
     first.wait()
     second.wait()
 
@@ -248,21 +249,23 @@
     cold_part = near[: NF * shard].reshape(NF, shard, width)
     hot_part = jnp.broadcast_to(near[None, NF * shard :], (NF, hot_own, width))
     far = lax.all_to_all(jnp.concatenate([cold_part, hot_part], axis=1), FAR, 0, 0)
-    far, other = lax.optimization_barrier((far, swap(other, "c")))
-    grad_queries = (keep + other.astype(F32)).astype(BF)
     far = jnp.sum(far.astype(F32), axis=0).astype(BF)
     grad_cold = far[:shard]
     grad_hot = spread(far[shard:], HALF).reshape(-1, width)
     grad_hot = spread(grad_hot, NEAR)
     grad_hot = grad_hot.reshape(hot // 2, width)
-    grad_hot = pl.pallas_call(
+    swapped = swap(jnp.concatenate([grad_hot, other], axis=0), "c")
+    grad_hot, grad_queries = pl.pallas_call(
         place_kernel,
-        out_shape=jax.ShapeDtypeStruct((hot, width), BF),
-        in_specs=[smem, vmem, vmem],
-        out_specs=pl.BlockSpec(memory_space=pl.ANY),
+        out_shape=(
+            jax.ShapeDtypeStruct((hot, width), BF),
+            jax.ShapeDtypeStruct((own, width), BF),
+        ),
+        in_specs=[smem, vmem, vmem, vmem],
+        out_specs=(pl.BlockSpec(memory_space=pl.ANY), vmem),
         scratch_shapes=[pltpu.SemaphoreType.DMA((2,))],
         compiler_params=params,
-    )(at_me, grad_hot, swap(grad_hot, "c"))
+    )(at_me, grad_hot, swapped, keep)
     return grad_queries, grad_hot, grad_cold, loss[0]
 
 

time: 147 us -> 146 us (level)
  blocking collectives: 34.9 us -> 50.9 us
  starting transfers between devices: 63.2 us -> 53.4 us
  waiting for transfers between devices: 29.5 us -> 23.8 us
    all_to_all x0 -> x1, blocking collectives: none -> 16.1 us  [body(): lax.all_to_all(jnp.concatenate([cold_part, hot_part], axis=1), FAR, 0, 0)]
    all_to_all x1 -> x0, waiting for transfers between devices: 5.59 us -> none  [body(): lax.all_to_all(jnp.concatenate([cold_part, hot_part], axis=1), FAR, 0, 0)]
    ppermute x7 -> x6, starting transfers between devices: 27.4 us -> 22 us  [swap(): return lax.ppermute(x, axis, [(0, 1), (1, 0)])]
    all_to_all x1 -> x0, starting transfers between devices: 4.51 us -> none  [body(): lax.all_to_all(jnp.concatenate([cold_part, hot_part], axis=1), FAR, 0, 0)]
    ppermute x7 -> x6, waiting for transfers between devices: 14 us -> 13.9 us  [swap(): return lax.ppermute(x, axis, [(0, 1), (1, 0)])]
  transfers between devices with their start and end apart: 12 -> 10, of which waited for: 10 -> 8; matrix products, arithmetic and copies ran while one was open for 1% -> 1% of each run, Pallas kernels for 2% -> 2%
where the time goes in v13:
time: 146 us
  starting transfers between devices  53.4 us (37%)
  blocking collectives  50.9 us (35%)
  waiting for transfers between devices  23.8 us (16%)
  Pallas kernels  13.1 us (9%)
  local copies, waits for them, and re-layouts  3.26 us (2%)
    all_to_all x2, blocking collectives, spread(): return lax.all_to_all(jnp.broadcast_to(x[None], (n, *x.shape)), axes, 0, 0)  23 us
    all_to_all x2, starting transfers between devices, spread(): return lax.all_to_all(jnp.broadcast_to(x[None], (n, *x.shape)), axes, 0, 0)  22.5 us
    ppermute x6, starting transfers between devices, swap(): return lax.ppermute(x, axis, [(0, 1), (1, 0)])  22 us
    all_to_all x1, blocking collectives, body(): lax.all_to_all(jnp.concatenate([cold_part, hot_part], axis=1), FAR, 0, 0)  16.1 us
    ppermute x6, waiting for transfers between devices, swap(): return lax.ppermute(x, axis, [(0, 1), (1, 0)])  13.9 us
    all_to_all x1, blocking collectives, body(): stats = lax.all_to_all(stats, COLS, 0, 0)  11.8 us
    all_to_all x2, waiting for transfers between devices, spread(): return lax.all_to_all(jnp.broadcast_to(x[None], (n, *x.shape)), axes, 0, 0)  7.63 us
    pallas_call x1, Pallas kernels, body(): pl.pallas_call(grads_kernel, out_shape=(jax.ShapeDtypeStruct((count // 4,...  5.63 us
  transfers between devices with their start and end apart: 10, of which 8 were waited for; matrix products, arithmetic and copies ran while one was open for 1% of the time, Pallas kernels for 2%

profile of v13, /device:TPU:1, one launch (start us, length us, event | category | flops | bytes accessed | tf_op | source)
XLA Modules:
  0.0 145.6 jit_solution(985749025048017069)
XLA Ops:
  0.6 0.0 copy-start
  0.6 1.4 broadcast_in_dim.12
  2.1 15.6 %all-to-all-start = ((bf16[4,32,256]{2,1,0:T(8,128)(2,1)}), bf16[4,32,256]{2,1,0:T(8,128)(2,1)S(1)}, u32[]{:S(2)}, u32[]{:S(2)}) async-start(bf16[4,32,256]{2,1,0:T(8,128)(2,1)} %broadcast_in_dim.12), calls=%async_computation | async-start | bytes 131072 | tf_op jit(solution)/shard_map/all_to_all | solution.py:26
  17.7 2.6 %collective-permute-start = (bf16[128,256]{1,0:T(8,128)(2,1)}, bf16[128,256]{1,0:T(8,128)(2,1)S(1)}, u32[]{:S(2)}, u32[]{:S(2)}) collective-permute-start(bf16[128,256]{1,0:T(8,128)(2,1)} %param.5), channel_id=1, source_target_pairs={{0,32},{32,0},{1,33},{33,1},{2,34},{34,2},{3,35},{35,3},{4,36},{36... | collective-permute-start | bytes 196616 | tf_op jit(solution)/shard_map/ppermute | solution.py:30
  20.4 2.6 %collective-permute-done = bf16[128,256]{1,0:T(8,128)(2,1)S(1)} collective-permute-done((bf16[128,256]{1,0:T(8,128)(2,1)}, bf16[128,256]{1,0:T(8,128)(2,1)S(1)}, u32[]{:S(2)}, u32[]{:S(2)}) %collective-permute-start) | collective-permute-done | bytes 65568 | tf_op jit(solution)/shard_map/ppermute | solution.py:30
  22.9 7.3 %all-to-all-done = bf16[4,32,256]{2,1,0:T(8,128)(2,1)S(1)} async-done(((bf16[4,32,256]{2,1,0:T(8,128)(2,1)}), bf16[4,32,256]{2,1,0:T(8,128)(2,1)S(1)}, u32[]{:S(2)}, u32[]{:S(2)}) %all-to-all-start) | async-done | bytes 65568 | tf_op jit(solution)/shard_map/all_to_all | solution.py:26
  30.2 1.1 broadcast_in_dim.13
  31.3 6.9 %all-to-all-start.1 = ((bf16[16,128,256]{2,1,0:T(8,128)(2,1)}), bf16[16,128,256]{2,1,0:T(8,128)(2,1)S(1)}, u32[]{:S(2)}, u32[]{:S(2)}) async-start(bf16[16,128,256]{2,1,0:T(8,128)(2,1)} %broadcast_in_dim.13), calls=%async_computation.1 | async-start | bytes 2097152 | tf_op jit(solution)/shard_map/all_to_all | solution.py:26
  38.2 2.7 %collective-permute-start.1 = (bf16[256,256]{1,0:T(8,128)(2,1)S(1)}, bf16[256,256]{1,0:T(8,128)(2,1)S(1)}, u32[]{:S(2)}, u32[]{:S(2)}) collective-permute-start(bf16[256,256]{1,0:T(8,128)(2,1)S(1)} %pad_maximum_fusion.1), channel_id=1, source_target_pairs={{0,64},{64,0},{1,65},{65,1},{2,66},{66,2},{3,67},{67,3},{4,68},{68... | collective-permute-start | bytes 393224 | tf_op jit(solution)/shard_map/ppermute | solution.py:30
  40.9 2.2 %shard_map.84.col_ref = s32[1,1024]{1,0:T(1,128)S(1)} custom-call(s32[1]{0:T(128)} %bitcast.me_ref, s32[16,128]{1,0:T(8,128)S(1)} %bitcast.17, s32[512,1,128]{2,1,0:T(1,128)S(1)} %bitcast.16), custom_call_target="tpu_custom_call" | custom-call | flops 12582912 | bytes 1048576 | tf_op jit(solution)/shard_map/pallas_call | solution.py:203
  43.2 3.8 %collective-permute-done.1 = bf16[256,256]{1,0:T(8,128)(2,1)S(1)} collective-permute-done((bf16[256,256]{1,0:T(8,128)(2,1)S(1)}, bf16[256,256]{1,0:T(8,128)(2,1)S(1)}, u32[]{:S(2)}, u32[]{:S(2)}) %collective-permute-start.1) | collective-permute-done | bytes 131104 | tf_op jit(solution)/shard_map/ppermute | solution.py:30
  47.0 4.7 %collective-permute-start.2 = (bf16[512,256]{1,0:T(8,128)(2,1)S(1)}, bf16[512,256]{1,0:T(8,128)(2,1)S(1)}, u32[]{:S(2)}, u32[]{:S(2)}) collective-permute-start(bf16[512,256]{1,0:T(8,128)(2,1)S(1)} %constant_dynamic-update-slice_fusion.refs_0_), channel_id=1, source_target_pairs={{0,8},{8,0},{1,9},{9,1},{2,10},{10,2},{3,11},{11,3},{4,12},{12,4},... | collective-permute-start | bytes 786440 | tf_op jit(solution)/shard_map/ppermute | solution.py:30
  51.7 1.1 collective-permute-done.2.refs_1_
  52.8 0.3 all-to-all-done.1.cold_ref
  53.2 3.6 %shard_map.85 = f32[8,2,1024]{2,1,0:T(2,128)S(1)} custom-call(s32[1]{0:T(128)} %bitcast.me_ref, bf16[16,128,256]{2,1,0:T(8,128)(2,1)S(1)} %all-to-all-done.1.cold_ref, bf16[16,16,256]{2,1,0:T(8,128)(2,1)S(1)} %dynamic-slice_bitcast_fusion.hot_ref, s32[1,1024]{1,0:T(1,128)S(1)} %shard_map.84.col_ref, ...), custom_call_target="tpu_custom_call" | custom-call | tf_op jit(solution)/shard_map/pallas_call | solution.py:225
  56.8 11.8 %all_to_all.35.stats_ref = f32[8,2,1024]{2,1,0:T(2,128)S(1)} all-to-all(f32[8,2,1024]{2,1,0:T(2,128)S(1)} %shard_map.85), channel_id=1, replica_groups=mesh['z8'=2,'z4'=2,'z2'=2,'z1'=2,'yl'=2,'c'=2,'x2'=2,'x1'=2,'yh'=2] {'c'..., dimensions={0} | all-to-all | bytes 131072 | tf_op jit(solution)/shard_map/all_to_all | solution.py:231
  68.5 5.6 %shard_map.86 = (f32[256,256]{1,0:T(8,128)S(1)}, bf16[256,256]{1,0:T(8,128)(2,1)S(1)}, bf16[256,256]{1,0:T(8,128)(2,1)S(1)}, bf16[256,256]{1,0:T(8,128)(2,1)S(1)...) custom-call(s32[1]{0:T(128)} %bitcast.me_ref, bf16[16,128,256]{2,1,0:T(8,128)(2,1)S(1)} %all-to-all-done.1.cold_ref, ...), custom_call_target="tpu_custom_call" | custom-call | tf_op jit(solution)/shard_map/pallas_call | solution.py:232
  74.2 3.7 %all-to-all-start.3 = ((bf16[16,144,256]{2,1,0:T(8,128)(2,1)}), bf16[16,144,256]{2,1,0:T(8,128)(2,1)S(1)}, u32[]{:S(2)}, u32[]{:S(2)}) async-start(bf16[16,144,256]{2,1,0:T(8,128)(2,1)} %get-tuple-element.23), calls=%async_computation.3 | async-start | bytes 2359296 | tf_op jit(solution)/shard_map/all_to_all | solution.py:245
  77.9 2.0 %collective-permute-start.3 = (bf16[256,256]{1,0:T(8,128)(2,1)S(1)}, bf16[256,256]{1,0:T(8,128)(2,1)S(1)}, u32[]{:S(2)}, u32[]{:S(2)}) collective-permute-start(bf16[256,256]{1,0:T(8,128)(2,1)S(1)} %get-tuple-element.25), channel_id=1, source_target_pairs={{0,32},{32,0},{1,33},{33,1},{2,34},{34,2},{3,35},{35,3},{4,36},{36... | collective-permute-start | bytes 393224 | tf_op jit(solution)/shard_map/ppermute | solution.py:30
  79.9 2.2 %collective-permute-start.4 = (bf16[256,256]{1,0:T(8,128)(2,1)S(1)}, bf16[256,256]{1,0:T(8,128)(2,1)S(1)}, u32[]{:S(2)}, u32[]{:S(2)}) collective-permute-start(bf16[256,256]{1,0:T(8,128)(2,1)S(1)} %get-tuple-element.26), channel_id=1, source_target_pairs={{0,64},{64,0},{1,65},{65,1},{2,66},{66,2},{3,67},{67,3},{4,68},{68... | collective-permute-start | bytes 393224 | tf_op jit(solution)/shard_map/ppermute | solution.py:30
  82.0 5.1 %collective-permute-start.5 = (bf16[256,256]{1,0:T(8,128)(2,1)S(1)}, bf16[256,256]{1,0:T(8,128)(2,1)S(1)}, u32[]{:S(2)}, u32[]{:S(2)}) collective-permute-start(bf16[256,256]{1,0:T(8,128)(2,1)S(1)} %get-tuple-element.27), channel_id=1, source_target_pairs={{0,96},{32,64},{64,32},{96,0},{1,97},{33,65},{65,33},{97,1},{2,98}... | collective-permute-start | bytes 393224 | tf_op jit(solution)/shard_map/ppermute | solution.py:34
  87.2 5.4 %collective-permute-done.4 = bf16[256,256]{1,0:T(8,128)(2,1)S(1)} collective-permute-done((bf16[256,256]{1,0:T(8,128)(2,1)S(1)}, bf16[256,256]{1,0:T(8,128)(2,1)S(1)}, u32[]{:S(2)}, u32[]{:S(2)}) %collective-permute-start.4) | collective-permute-done | bytes 131104 | tf_op jit(solution)/shard_map/ppermute | solution.py:30
  92.6 0.1 add_add_fusion
  92.7 2.3 %all-to-all-done.3 = bf16[16,144,256]{2,1,0:T(8,128)(2,1)S(1)} async-done(((bf16[16,144,256]{2,1,0:T(8,128)(2,1)}), bf16[16,144,256]{2,1,0:T(8,128)(2,1)S(1)}, u32[]{:S(2)}, u32[]{:S(2)}) %all-to-all-start.3) | async-done | bytes 1179680 | tf_op jit(solution)/shard_map/all_to_all | solution.py:245
  95.0 0.2 reduce_sum.24
  95.2 16.1 %all_to_all.36 = bf16[4,48,256]{2,1,0:T(8,128)(2,1)S(1)} all-to-all(bf16[4,48,256]{2,1,0:T(8,128)(2,1)S(1)} %pad_maximum_fusion.2), channel_id=1, replica_groups=mesh['z8'=2,'z4'=2,'z2'=2,'z1'=2,'yl'=2,'c'=2,'x2'=2,'x1'=2,'yh'=2] {'z8..., dimensions={0} | all-to-all | bytes 196608 | tf_op jit(solution)/shard_map/all_to_all | solution.py:251
  111.4 7.0 %all_to_all.37 = bf16[4,16,256]{2,1,0:T(8,128)(2,1)S(1)} all-to-all(bf16[4,16,256]{2,1,0:T(8,128)(2,1)S(1)} %broadcast_in_dim.15), channel_id=1, replica_groups=mesh['z8'=2,'z4'=2,'z2'=2,'z1'=2,'yl'=2,'c'=2,'x2'=2,'x1'=2,'yh'=2] {'z2..., dimensions={0} | all-to-all | bytes 65536 | tf_op jit(solution)/shard_map/all_to_all | solution.py:26
  118.5 16.0 %all_to_all.38 = bf16[16,64,256]{2,1,0:T(8,128)(2,1)S(1)} all-to-all(bf16[16,64,256]{2,1,0:T(8,128)(2,1)S(1)} %broadcast_in_dim.17), channel_id=1, replica_groups=mesh['z8'=2,'z4'=2,'z2'=2,'z1'=2,'yl'=2,'c'=2,'x2'=2,'x1'=2,'yh'=2] {'x2..., dimensions={0} | all-to-all | bytes 1048576 | tf_op jit(solution)/shard_map/all_to_all | solution.py:26
  134.5 7.9 %collective-permute-start.6 = (bf16[1152,256]{1,0:T(8,128)(2,1)S(1)}, bf16[1152,256]{1,0:T(8,128)(2,1)S(1)}, u32[]{:S(2)}, u32[]{:S(2)}) collective-permute-start(bf16[1152,256]{1,0:T(8,128)(2,1)S(1)} %pad_maximum_fusion), channel_id=1, source_target_pairs={{0,8},{8,0},{1,9},{9,1},{2,10},{10,2},{3,11},{11,3},{4,12},{12,4},... | collective-permute-start | bytes 1769480 | tf_op jit(solution)/shard_map/ppermute | solution.py:30
  142.4 0.6 slice.30
  143.0 1.0 collective-permute-done.6.other_ref
  144.0 1.6 %shard_map.87 = (bf16[2048,256]{1,0:T(8,128)(2,1)}, bf16[128,256]{1,0:T(8,128)(2,1)}) custom-call(s32[1]{0:T(128)} %bitcast.me_ref, bf16[1024,256]{1,0:T(8,128)(2,1)S(1)} %bitcast.15, bf16[1152,256]{1,0:T(8,128)(2,1)S(1)} %collective-permute-done.6.other_ref, f32[128,256]{1,0:T(8,128)S(1)} %slice.25.keep_ref), custom_call_target="tpu_custom_call" | custom-call | tf_op jit(solution)/shard_map/pallas_call | solution.py:258
  (25 shorter events, 0.2 us)
Async XLA Ops:
  0.6 51.0 %copy-start = (bf16[2048,256]{1,0:T(8,128)(2,1)S(1)}, bf16[2048,256]{1,0:T(8,128)(2,1)}, u32[]{:S(2)}) copy-start(bf16[2048,256]{1,0:T(8,128)(2,1)} %param.6) | copy-start | bytes 3145732
  2.1 28.1 %all-to-all-start = ((bf16[4,32,256]{2,1,0:T(8,128)(2,1)}), bf16[4,32,256]{2,1,0:T(8,128)(2,1)S(1)}, u32[]{:S(2)}, u32[]{:S(2)}) async-start(bf16[4,32,256]{2,1,0:T(8,128)(2,1)} %broadcast_in_dim.12), calls=%async_computation | async-start | bytes 131072 | tf_op jit(solution)/shard_map/all_to_all | solution.py:26
  17.7 5.2 %collective-permute-start = (bf16[128,256]{1,0:T(8,128)(2,1)}, bf16[128,256]{1,0:T(8,128)(2,1)S(1)}, u32[]{:S(2)}, u32[]{:S(2)}) collective-permute-start(bf16[128,256]{1,0:T(8,128)(2,1)} %param.5), channel_id=1, source_target_pairs={{0,32},{32,0},{1,33},{33,1},{2,34},{34,2},{3,35},{35,3},{4,36},{36... | collective-permute-start | bytes 196616 | tf_op jit(solution)/shard_map/ppermute | solution.py:30
  31.3 6.9 %copy-start.3 = (bf16[128,256]{1,0:T(8,128)(2,1)S(1)}, bf16[128,256]{1,0:T(8,128)(2,1)}, u32[]{:S(2)}) copy-start(bf16[128,256]{1,0:T(8,128)(2,1)} %param.5) | copy-start | bytes 196612
  31.3 9.6 %copy-start.1 = (s32[65536]{0:T(1024)S(1)}, s32[65536]{0:T(1024)}, u32[]{:S(2)}) copy-start(s32[65536]{0:T(1024)} %param.9) | copy-start | bytes 786436
  31.3 9.6 %copy-start.2 = (s32[2048]{0:T(1024)S(1)}, s32[2048]{0:T(1024)}, u32[]{:S(2)}) copy-start(s32[2048]{0:T(1024)} %param.8) | copy-start | bytes 24580
  31.3 21.9 %all-to-all-start.1 = ((bf16[16,128,256]{2,1,0:T(8,128)(2,1)}), bf16[16,128,256]{2,1,0:T(8,128)(2,1)S(1)}, u32[]{:S(2)}, u32[]{:S(2)}) async-start(bf16[16,128,256]{2,1,0:T(8,128)(2,1)} %broadcast_in_dim.13), calls=%async_computation.1 | async-start | bytes 2097152 | tf_op jit(solution)/shard_map/all_to_all | solution.py:26
  38.2 8.7 %collective-permute-start.1 = (bf16[256,256]{1,0:T(8,128)(2,1)S(1)}, bf16[256,256]{1,0:T(8,128)(2,1)S(1)}, u32[]{:S(2)}, u32[]{:S(2)}) collective-permute-start(bf16[256,256]{1,0:T(8,128)(2,1)S(1)} %pad_maximum_fusion.1), channel_id=1, source_target_pairs={{0,64},{64,0},{1,65},{65,1},{2,66},{66,2},{3,67},{67,3},{4,68},{68... | collective-permute-start | bytes 393224 | tf_op jit(solution)/shard_map/ppermute | solution.py:30
  47.0 5.8 %collective-permute-start.2 = (bf16[512,256]{1,0:T(8,128)(2,1)S(1)}, bf16[512,256]{1,0:T(8,128)(2,1)S(1)}, u32[]{:S(2)}, u32[]{:S(2)}) collective-permute-start(bf16[512,256]{1,0:T(8,128)(2,1)S(1)} %constant_dynamic-update-slice_fusion.refs_0_), channel_id=1, source_target_pairs={{0,8},{8,0},{1,9},{9,1},{2,10},{10,2},{3,11},{11,3},{4,12},{12,4},... | collective-permute-start | bytes 786440 | tf_op jit(solution)/shard_map/ppermute | solution.py:30
  74.2 20.9 %all-to-all-start.3 = ((bf16[16,144,256]{2,1,0:T(8,128)(2,1)}), bf16[16,144,256]{2,1,0:T(8,128)(2,1)S(1)}, u32[]{:S(2)}, u32[]{:S(2)}) async-start(bf16[16,144,256]{2,1,0:T(8,128)(2,1)} %get-tuple-element.23), calls=%async_computation.3 | async-start | bytes 2359296 | tf_op jit(solution)/shard_map/all_to_all | solution.py:245
  77.9 9.3 %collective-permute-start.3 = (bf16[256,256]{1,0:T(8,128)(2,1)S(1)}, bf16[256,256]{1,0:T(8,128)(2,1)S(1)}, u32[]{:S(2)}, u32[]{:S(2)}) collective-permute-start(bf16[256,256]{1,0:T(8,128)(2,1)S(1)} %get-tuple-element.25), channel_id=1, source_target_pairs={{0,32},{32,0},{1,33},{33,1},{2,34},{34,2},{3,35},{35,3},{4,36},{36... | collective-permute-start | bytes 393224 | tf_op jit(solution)/shard_map/ppermute | solution.py:30
  79.9 12.7 %collective-permute-start.4 = (bf16[256,256]{1,0:T(8,128)(2,1)S(1)}, bf16[256,256]{1,0:T(8,128)(2,1)S(1)}, u32[]{:S(2)}, u32[]{:S(2)}) collective-permute-start(bf16[256,256]{1,0:T(8,128)(2,1)S(1)} %get-tuple-element.26), channel_id=1, source_target_pairs={{0,64},{64,0},{1,65},{65,1},{2,66},{66,2},{3,67},{67,3},{4,68},{68... | collective-permute-start | bytes 393224 | tf_op jit(solution)/shard_map/ppermute | solution.py:30
  82.0 10.6 %collective-permute-start.5 = (bf16[256,256]{1,0:T(8,128)(2,1)S(1)}, bf16[256,256]{1,0:T(8,128)(2,1)S(1)}, u32[]{:S(2)}, u32[]{:S(2)}) collective-permute-start(bf16[256,256]{1,0:T(8,128)(2,1)S(1)} %get-tuple-element.27), channel_id=1, source_target_pairs={{0,96},{32,64},{64,32},{96,0},{1,97},{33,65},{65,33},{97,1},{2,98}... | collective-permute-start | bytes 393224 | tf_op jit(solution)/shard_map/ppermute | solution.py:34
  134.5 9.5 %collective-permute-start.6 = (bf16[1152,256]{1,0:T(8,128)(2,1)S(1)}, bf16[1152,256]{1,0:T(8,128)(2,1)S(1)}, u32[]{:S(2)}, u32[]{:S(2)}) collective-permute-start(bf16[1152,256]{1,0:T(8,128)(2,1)S(1)} %pad_maximum_fusion), channel_id=1, source_target_pairs={{0,8},{8,0},{1,9},{9,1},{2,10},{10,2},{3,11},{11,3},{4,12},{12,4},... | collective-permute-start | bytes 1769480 | tf_op jit(solution)/shard_map/ppermute | solution.py:30

commit v14 on v13

--- a/solution.py
+++ b/solution.py
@@ -132,7 +132,7 @@
 
 
 def grads_kernel(me_ref, cold_ref, hot_ref, col_ref, stats_ref, *refs):
-    *row_refs, keep_ref, send_1, send_2, send_3, item_ref, loss_ref, acc_ref = refs
+    *row_refs, keep_ref, send_1, send_2, send_3, out_ref, loss_ref, acc_ref, item_ref, sems = refs
     rows = jnp.concatenate([r[...] for r in row_refs], axis=0)
     cols = col_ref[...]
     k = pick(me_ref[0], COLS)
@@ -150,6 +150,10 @@
     n = NG // CHUNKS
     cold_rows = cold_ref.shape[1]
 
+    def copy_out(g):
+        there = pl.ds(g * n, n)
+        return pltpu.make_async_copy(item_ref.at[there], out_ref.at[there], sems.at[g])
+
     def step(g, carry):
         table = chunk_table(cold_ref, hot_ref, g)
         s = lax.dot_general(table, rows, NT, preferred_element_type=F32)
@@ -159,6 +163,7 @@
         wide = item.shape[-1]
         item_ref[pl.ds(g * n, n), :cold_rows] = item[: n * cold_rows].reshape(n, -1, wide)
         item_ref[pl.ds(g * n, n), cold_rows:] = item[n * cold_rows :].reshape(n, -1, wide)
+        copy_out(g).start()
         acc_ref[...] += lax.dot_general(table, w, TN, preferred_element_type=F32)
         return carry
 
@@ -169,9 +174,11 @@
             p = core * (NC // 2) + j
             part = acc_ref[:, p * own : (p + 1) * own].T
             ref[core * own : (core + 1) * own] = part.astype(ref.dtype)
-
-
-def place_kernel(me_ref, own_ref, other_ref, keep_ref, out_ref, query_ref, sems):
+    for g in range(CHUNKS):
+        copy_out(g).wait()
+
+
+def place_kernel(me_ref, own_ref, other_ref, keep_ref, out_ref, query_ref, sum_ref, sems):
     core = bit(me_ref[0], "c")
     half = own_ref.shape[0]
     first = pltpu.make_async_copy(own_ref, out_ref.at[pl.ds(core * half, half)], sems.at[0])
@@ -180,9 +187,12 @@
     )
     first.start()
     second.start()
-    query_ref[...] = (keep_ref[...] + other_ref[half:].astype(F32)).astype(query_ref.dtype)
+    sum_ref[...] = (keep_ref[...] + other_ref[half:].astype(F32)).astype(sum_ref.dtype)
+    third = pltpu.make_async_copy(sum_ref, query_ref, sems.at[2])
+    third.start()
     first.wait()
     second.wait()
+    third.wait()
 
 
 def body(queries, hot_table, cold_table, hot_ids, targets):
@@ -238,7 +248,12 @@
             jax.ShapeDtypeStruct((1, own), F32),
         ),
         in_specs=[smem] + [vmem] * (4 + len(rows)),
-        scratch_shapes=[pltpu.VMEM((width, count), F32)],
+        out_specs=(vmem, vmem, vmem, vmem, pl.BlockSpec(memory_space=pl.ANY), vmem),
+        scratch_shapes=[
+            pltpu.VMEM((width, count), F32),
+            pltpu.VMEM((NG, NF * shard + hot_own, width), BF),
+            pltpu.SemaphoreType.DMA((CHUNKS,)),
+        ],
         compiler_params=params,
     )(at_me, cold, mine, column, stats, *rows)
 
@@ -262,8 +277,8 @@
             jax.ShapeDtypeStruct((own, width), BF),
         ),
         in_specs=[smem, vmem, vmem, vmem],
-        out_specs=(pl.BlockSpec(memory_space=pl.ANY), vmem),
-        scratch_shapes=[pltpu.SemaphoreType.DMA((2,))],
+        out_specs=(pl.BlockSpec(memory_space=pl.ANY),) * 2,
+        scratch_shapes=[pltpu.VMEM((own, width), BF), pltpu.SemaphoreType.DMA((3,))],
         compiler_params=params,
     )(at_me, grad_hot, swapped, keep)
     return grad_queries, grad_hot, grad_cold, loss[0]

time: 146 us -> 146 us (level)
  no operation moved by 1% of the time
where the time goes in v14:
time: 146 us; the launch traced here: 145 us
  starting transfers between devices  53.3 us (37%)
  blocking collectives  51 us (35%)
  waiting for transfers between devices  23.8 us (16%)
  Pallas kernels  12.4 us (8%)
  local copies, waits for them, and re-layouts  3.26 us (2%)
    all_to_all x2, blocking collectives, spread(): return lax.all_to_all(jnp.broadcast_to(x[None], (n, *x.shape)), axes, 0, 0)  23.1 us
    all_to_all x2, starting transfers between devices, spread(): return lax.all_to_all(jnp.broadcast_to(x[None], (n, *x.shape)), axes, 0, 0)  22.5 us
    ppermute x6, starting transfers between devices, swap(): return lax.ppermute(x, axis, [(0, 1), (1, 0)])  22 us
    all_to_all x1, blocking collectives, body(): lax.all_to_all(jnp.concatenate([cold_part, hot_part], axis=1), FAR, 0, 0)  16.1 us
    ppermute x6, waiting for transfers between devices, swap(): return lax.ppermute(x, axis, [(0, 1), (1, 0)])  13.9 us
    all_to_all x1, blocking collectives, body(): stats = lax.all_to_all(stats, COLS, 0, 0)  11.8 us
    all_to_all x2, waiting for transfers between devices, spread(): return lax.all_to_all(jnp.broadcast_to(x[None], (n, *x.shape)), axes, 0, 0)  7.63 us
    pallas_call x1, Pallas kernels, body(): pl.pallas_call(grads_kernel, out_shape=(jax.ShapeDtypeStruct((count // 4,...  5.59 us
  transfers between devices with their start and end apart: 10, of which 8 were waited for; matrix products, arithmetic and copies ran while one was open for 1% of the time, Pallas kernels for 2%

profile of v14, /device:TPU:1, one launch (start us, length us, event | category | flops | bytes accessed | tf_op | source)
XLA Modules:
  0.0 145.0 jit_solution(8924756480372089261)
XLA Ops:
  0.6 0.0 copy-start
  0.6 1.4 broadcast_in_dim.12
  2.1 15.6 %all-to-all-start = ((bf16[4,32,256]{2,1,0:T(8,128)(2,1)}), bf16[4,32,256]{2,1,0:T(8,128)(2,1)S(1)}, u32[]{:S(2)}, u32[]{:S(2)}) async-start(bf16[4,32,256]{2,1,0:T(8,128)(2,1)} %broadcast_in_dim.12), calls=%async_computation | async-start | bytes 131072 | tf_op jit(solution)/shard_map/all_to_all | solution.py:26
  17.7 2.6 %collective-permute-start = (bf16[128,256]{1,0:T(8,128)(2,1)}, bf16[128,256]{1,0:T(8,128)(2,1)S(1)}, u32[]{:S(2)}, u32[]{:S(2)}) collective-permute-start(bf16[128,256]{1,0:T(8,128)(2,1)} %param.5), channel_id=1, source_target_pairs={{0,32},{32,0},{1,33},{33,1},{2,34},{34,2},{3,35},{35,3},{4,36},{36... | collective-permute-start | bytes 196616 | tf_op jit(solution)/shard_map/ppermute | solution.py:30
  20.4 2.6 %collective-permute-done = bf16[128,256]{1,0:T(8,128)(2,1)S(1)} collective-permute-done((bf16[128,256]{1,0:T(8,128)(2,1)}, bf16[128,256]{1,0:T(8,128)(2,1)S(1)}, u32[]{:S(2)}, u32[]{:S(2)}) %collective-permute-start) | collective-permute-done | bytes 65568 | tf_op jit(solution)/shard_map/ppermute | solution.py:30
  22.9 7.3 %all-to-all-done = bf16[4,32,256]{2,1,0:T(8,128)(2,1)S(1)} async-done(((bf16[4,32,256]{2,1,0:T(8,128)(2,1)}), bf16[4,32,256]{2,1,0:T(8,128)(2,1)S(1)}, u32[]{:S(2)}, u32[]{:S(2)}) %all-to-all-start) | async-done | bytes 65568 | tf_op jit(solution)/shard_map/all_to_all | solution.py:26
  30.2 1.1 broadcast_in_dim.13
  31.3 6.9 %all-to-all-start.1 = ((bf16[16,128,256]{2,1,0:T(8,128)(2,1)}), bf16[16,128,256]{2,1,0:T(8,128)(2,1)S(1)}, u32[]{:S(2)}, u32[]{:S(2)}) async-start(bf16[16,128,256]{2,1,0:T(8,128)(2,1)} %broadcast_in_dim.13), calls=%async_computation.1 | async-start | bytes 2097152 | tf_op jit(solution)/shard_map/all_to_all | solution.py:26
  38.2 2.7 %collective-permute-start.1 = (bf16[256,256]{1,0:T(8,128)(2,1)S(1)}, bf16[256,256]{1,0:T(8,128)(2,1)S(1)}, u32[]{:S(2)}, u32[]{:S(2)}) collective-permute-start(bf16[256,256]{1,0:T(8,128)(2,1)S(1)} %pad_maximum_fusion.1), channel_id=1, source_target_pairs={{0,64},{64,0},{1,65},{65,1},{2,66},{66,2},{3,67},{67,3},{4,68},{68... | collective-permute-start | bytes 393224 | tf_op jit(solution)/shard_map/ppermute | solution.py:30
  40.9 2.2 %shard_map.84.col_ref = s32[1,1024]{1,0:T(1,128)S(1)} custom-call(s32[1]{0:T(128)} %bitcast.me_ref, s32[16,128]{1,0:T(8,128)S(1)} %bitcast.17, s32[512,1,128]{2,1,0:T(1,128)S(1)} %bitcast.16), custom_call_target="tpu_custom_call" | custom-call | flops 12582912 | bytes 1048576 | tf_op jit(solution)/shard_map/pallas_call | solution.py:213
  43.2 3.8 %collective-permute-done.1 = bf16[256,256]{1,0:T(8,128)(2,1)S(1)} collective-permute-done((bf16[256,256]{1,0:T(8,128)(2,1)S(1)}, bf16[256,256]{1,0:T(8,128)(2,1)S(1)}, u32[]{:S(2)}, u32[]{:S(2)}) %collective-permute-start.1) | collective-permute-done | bytes 131104 | tf_op jit(solution)/shard_map/ppermute | solution.py:30
  47.0 4.7 %collective-permute-start.2 = (bf16[512,256]{1,0:T(8,128)(2,1)S(1)}, bf16[512,256]{1,0:T(8,128)(2,1)S(1)}, u32[]{:S(2)}, u32[]{:S(2)}) collective-permute-start(bf16[512,256]{1,0:T(8,128)(2,1)S(1)} %constant_dynamic-update-slice_fusion.refs_0_), channel_id=1, source_target_pairs={{0,8},{8,0},{1,9},{9,1},{2,10},{10,2},{3,11},{11,3},{4,12},{12,4},... | collective-permute-start | bytes 786440 | tf_op jit(solution)/shard_map/ppermute | solution.py:30
  51.7 1.1 collective-permute-done.2.refs_1_
  52.8 0.3 all-to-all-done.1.cold_ref
  53.2 3.6 %shard_map.85 = f32[8,2,1024]{2,1,0:T(2,128)S(1)} custom-call(s32[1]{0:T(128)} %bitcast.me_ref, bf16[16,128,256]{2,1,0:T(8,128)(2,1)S(1)} %all-to-all-done.1.cold_ref, bf16[16,16,256]{2,1,0:T(8,128)(2,1)S(1)} %dynamic-slice_bitcast_fusion.hot_ref, s32[1,1024]{1,0:T(1,128)S(1)} %shard_map.84.col_ref, ...), custom_call_target="tpu_custom_call" | custom-call | tf_op jit(solution)/shard_map/pallas_call | solution.py:235
  56.8 11.8 %all_to_all.35.stats_ref = f32[8,2,1024]{2,1,0:T(2,128)S(1)} all-to-all(f32[8,2,1024]{2,1,0:T(2,128)S(1)} %shard_map.85), channel_id=1, replica_groups=mesh['z8'=2,'z4'=2,'z2'=2,'z1'=2,'yl'=2,'c'=2,'x2'=2,'x1'=2,'yh'=2] {'c'..., dimensions={0} | all-to-all | bytes 131072 | tf_op jit(solution)/shard_map/all_to_all | solution.py:241
  68.5 5.6 %shard_map.86 = (f32[256,256]{1,0:T(8,128)S(1)}, bf16[256,256]{1,0:T(8,128)(2,1)S(1)}, bf16[256,256]{1,0:T(8,128)(2,1)S(1)}, bf16[256,256]{1,0:T(8,128)(2,1)S(1)...) custom-call(s32[1]{0:T(128)} %bitcast.me_ref, bf16[16,128,256]{2,1,0:T(8,128)(2,1)S(1)} %all-to-all-done.1.cold_ref, ...), custom_call_target="tpu_custom_call" | custom-call | tf_op jit(solution)/shard_map/pallas_call | solution.py:242
  74.1 3.7 %all-to-all-start.3 = ((bf16[16,144,256]{2,1,0:T(8,128)(2,1)}), bf16[16,144,256]{2,1,0:T(8,128)(2,1)S(1)}, u32[]{:S(2)}, u32[]{:S(2)}) async-start(bf16[16,144,256]{2,1,0:T(8,128)(2,1)} %get-tuple-element.23), calls=%async_computation.3 | async-start | bytes 2359296 | tf_op jit(solution)/shard_map/all_to_all | solution.py:260
  77.8 2.0 %collective-permute-start.3 = (bf16[256,256]{1,0:T(8,128)(2,1)S(1)}, bf16[256,256]{1,0:T(8,128)(2,1)S(1)}, u32[]{:S(2)}, u32[]{:S(2)}) collective-permute-start(bf16[256,256]{1,0:T(8,128)(2,1)S(1)} %get-tuple-element.25), channel_id=1, source_target_pairs={{0,32},{32,0},{1,33},{33,1},{2,34},{34,2},{3,35},{35,3},{4,36},{36... | collective-permute-start | bytes 393224 | tf_op jit(solution)/shard_map/ppermute | solution.py:30
  79.9 2.2 %collective-permute-start.4 = (bf16[256,256]{1,0:T(8,128)(2,1)S(1)}, bf16[256,256]{1,0:T(8,128)(2,1)S(1)}, u32[]{:S(2)}, u32[]{:S(2)}) collective-permute-start(bf16[256,256]{1,0:T(8,128)(2,1)S(1)} %get-tuple-element.26), channel_id=1, source_target_pairs={{0,64},{64,0},{1,65},{65,1},{2,66},{66,2},{3,67},{67,3},{4,68},{68... | collective-permute-start | bytes 393224 | tf_op jit(solution)/shard_map/ppermute | solution.py:30
  82.0 5.1 %collective-permute-start.5 = (bf16[256,256]{1,0:T(8,128)(2,1)S(1)}, bf16[256,256]{1,0:T(8,128)(2,1)S(1)}, u32[]{:S(2)}, u32[]{:S(2)}) collective-permute-start(bf16[256,256]{1,0:T(8,128)(2,1)S(1)} %get-tuple-element.27), channel_id=1, source_target_pairs={{0,96},{32,64},{64,32},{96,0},{1,97},{33,65},{65,33},{97,1},{2,98}... | collective-permute-start | bytes 393224 | tf_op jit(solution)/shard_map/ppermute | solution.py:34
  87.1 5.4 %collective-permute-done.4 = bf16[256,256]{1,0:T(8,128)(2,1)S(1)} collective-permute-done((bf16[256,256]{1,0:T(8,128)(2,1)S(1)}, bf16[256,256]{1,0:T(8,128)(2,1)S(1)}, u32[]{:S(2)}, u32[]{:S(2)}) %collective-permute-start.4) | collective-permute-done | bytes 131104 | tf_op jit(solution)/shard_map/ppermute | solution.py:30
  92.6 0.1 add_add_fusion
  92.7 2.3 %all-to-all-done.3 = bf16[16,144,256]{2,1,0:T(8,128)(2,1)S(1)} async-done(((bf16[16,144,256]{2,1,0:T(8,128)(2,1)}), bf16[16,144,256]{2,1,0:T(8,128)(2,1)S(1)}, u32[]{:S(2)}, u32[]{:S(2)}) %all-to-all-start.3) | async-done | bytes 1179680 | tf_op jit(solution)/shard_map/all_to_all | solution.py:260
  95.0 0.2 reduce_sum.24
  95.2 16.1 %all_to_all.36 = bf16[4,48,256]{2,1,0:T(8,128)(2,1)S(1)} all-to-all(bf16[4,48,256]{2,1,0:T(8,128)(2,1)S(1)} %pad_maximum_fusion.2), channel_id=1, replica_groups=mesh['z8'=2,'z4'=2,'z2'=2,'z1'=2,'yl'=2,'c'=2,'x2'=2,'x1'=2,'yh'=2] {'z8..., dimensions={0} | all-to-all | bytes 196608 | tf_op jit(solution)/shard_map/all_to_all | solution.py:266
  111.4 7.0 %all_to_all.37 = bf16[4,16,256]{2,1,0:T(8,128)(2,1)S(1)} all-to-all(bf16[4,16,256]{2,1,0:T(8,128)(2,1)S(1)} %broadcast_in_dim.15), channel_id=1, replica_groups=mesh['z8'=2,'z4'=2,'z2'=2,'z1'=2,'yl'=2,'c'=2,'x2'=2,'x1'=2,'yh'=2] {'z2..., dimensions={0} | all-to-all | bytes 65536 | tf_op jit(solution)/shard_map/all_to_all | solution.py:26
  118.4 16.1 %all_to_all.38 = bf16[16,64,256]{2,1,0:T(8,128)(2,1)S(1)} all-to-all(bf16[16,64,256]{2,1,0:T(8,128)(2,1)S(1)} %broadcast_in_dim.17), channel_id=1, replica_groups=mesh['z8'=2,'z4'=2,'z2'=2,'z1'=2,'yl'=2,'c'=2,'x2'=2,'x1'=2,'yh'=2] {'x2..., dimensions={0} | all-to-all | bytes 1048576 | tf_op jit(solution)/shard_map/all_to_all | solution.py:26
  134.6 7.8 %collective-permute-start.6 = (bf16[1152,256]{1,0:T(8,128)(2,1)S(1)}, bf16[1152,256]{1,0:T(8,128)(2,1)S(1)}, u32[]{:S(2)}, u32[]{:S(2)}) collective-permute-start(bf16[1152,256]{1,0:T(8,128)(2,1)S(1)} %pad_maximum_fusion), channel_id=1, source_target_pairs={{0,8},{8,0},{1,9},{9,1},{2,10},{10,2},{3,11},{11,3},{4,12},{12,4},... | collective-permute-start | bytes 1769480 | tf_op jit(solution)/shard_map/ppermute | solution.py:30
  142.4 0.6 slice.30
  143.0 1.0 collective-permute-done.6.other_ref
  144.0 1.0 shard_map.87
  (25 shorter events, 0.2 us)
Async XLA Ops:
  0.6 51.0 %copy-start = (bf16[2048,256]{1,0:T(8,128)(2,1)S(1)}, bf16[2048,256]{1,0:T(8,128)(2,1)}, u32[]{:S(2)}) copy-start(bf16[2048,256]{1,0:T(8,128)(2,1)} %param.6) | copy-start | bytes 3145732
  2.1 28.1 %all-to-all-start = ((bf16[4,32,256]{2,1,0:T(8,128)(2,1)}), bf16[4,32,256]{2,1,0:T(8,128)(2,1)S(1)}, u32[]{:S(2)}, u32[]{:S(2)}) async-start(bf16[4,32,256]{2,1,0:T(8,128)(2,1)} %broadcast_in_dim.12), calls=%async_computation | async-start | bytes 131072 | tf_op jit(solution)/shard_map/all_to_all | solution.py:26
  17.7 5.2 %collective-permute-start = (bf16[128,256]{1,0:T(8,128)(2,1)}, bf16[128,256]{1,0:T(8,128)(2,1)S(1)}, u32[]{:S(2)}, u32[]{:S(2)}) collective-permute-start(bf16[128,256]{1,0:T(8,128)(2,1)} %param.5), channel_id=1, source_target_pairs={{0,32},{32,0},{1,33},{33,1},{2,34},{34,2},{3,35},{35,3},{4,36},{36... | collective-permute-start | bytes 196616 | tf_op jit(solution)/shard_map/ppermute | solution.py:30
  31.3 6.9 %copy-start.3 = (bf16[128,256]{1,0:T(8,128)(2,1)S(1)}, bf16[128,256]{1,0:T(8,128)(2,1)}, u32[]{:S(2)}) copy-start(bf16[128,256]{1,0:T(8,128)(2,1)} %param.5) | copy-start | bytes 196612
  31.3 9.6 %copy-start.1 = (s32[65536]{0:T(1024)S(1)}, s32[65536]{0:T(1024)}, u32[]{:S(2)}) copy-start(s32[65536]{0:T(1024)} %param.9) | copy-start | bytes 786436
  31.3 9.6 %copy-start.2 = (s32[2048]{0:T(1024)S(1)}, s32[2048]{0:T(1024)}, u32[]{:S(2)}) copy-start(s32[2048]{0:T(1024)} %param.8) | copy-start | bytes 24580
  31.3 21.9 %all-to-all-start.1 = ((bf16[16,128,256]{2,1,0:T(8,128)(2,1)}), bf16[16,128,256]{2,1,0:T(8,128)(2,1)S(1)}, u32[]{:S(2)}, u32[]{:S(2)}) async-start(bf16[16,128,256]{2,1,0:T(8,128)(2,1)} %broadcast_in_dim.13), calls=%async_computation.1 | async-start | bytes 2097152 | tf_op jit(solution)/shard_map/all_to_all | solution.py:26
  38.2 8.7 %collective-permute-start.1 = (bf16[256,256]{1,0:T(8,128)(2,1)S(1)}, bf16[256,256]{1,0:T(8,128)(2,1)S(1)}, u32[]{:S(2)}, u32[]{:S(2)}) collective-permute-start(bf16[256,256]{1,0:T(8,128)(2,1)S(1)} %pad_maximum_fusion.1), channel_id=1, source_target_pairs={{0,64},{64,0},{1,65},{65,1},{2,66},{66,2},{3,67},{67,3},{4,68},{68... | collective-permute-start | bytes 393224 | tf_op jit(solution)/shard_map/ppermute | solution.py:30
  47.0 5.8 %collective-permute-start.2 = (bf16[512,256]{1,0:T(8,128)(2,1)S(1)}, bf16[512,256]{1,0:T(8,128)(2,1)S(1)}, u32[]{:S(2)}, u32[]{:S(2)}) collective-permute-start(bf16[512,256]{1,0:T(8,128)(2,1)S(1)} %constant_dynamic-update-slice_fusion.refs_0_), channel_id=1, source_target_pairs={{0,8},{8,0},{1,9},{9,1},{2,10},{10,2},{3,11},{11,3},{4,12},{12,4},... | collective-permute-start | bytes 786440 | tf_op jit(solution)/shard_map/ppermute | solution.py:30
  74.1 20.9 %all-to-all-start.3 = ((bf16[16,144,256]{2,1,0:T(8,128)(2,1)}), bf16[16,144,256]{2,1,0:T(8,128)(2,1)S(1)}, u32[]{:S(2)}, u32[]{:S(2)}) async-start(bf16[16,144,256]{2,1,0:T(8,128)(2,1)} %get-tuple-element.23), calls=%async_computation.3 | async-start | bytes 2359296 | tf_op jit(solution)/shard_map/all_to_all | solution.py:260
  77.8 9.3 %collective-permute-start.3 = (bf16[256,256]{1,0:T(8,128)(2,1)S(1)}, bf16[256,256]{1,0:T(8,128)(2,1)S(1)}, u32[]{:S(2)}, u32[]{:S(2)}) collective-permute-start(bf16[256,256]{1,0:T(8,128)(2,1)S(1)} %get-tuple-element.25), channel_id=1, source_target_pairs={{0,32},{32,0},{1,33},{33,1},{2,34},{34,2},{3,35},{35,3},{4,36},{36... | collective-permute-start | bytes 393224 | tf_op jit(solution)/shard_map/ppermute | solution.py:30
  79.9 12.7 %collective-permute-start.4 = (bf16[256,256]{1,0:T(8,128)(2,1)S(1)}, bf16[256,256]{1,0:T(8,128)(2,1)S(1)}, u32[]{:S(2)}, u32[]{:S(2)}) collective-permute-start(bf16[256,256]{1,0:T(8,128)(2,1)S(1)} %get-tuple-element.26), channel_id=1, source_target_pairs={{0,64},{64,0},{1,65},{65,1},{2,66},{66,2},{3,67},{67,3},{4,68},{68... | collective-permute-start | bytes 393224 | tf_op jit(solution)/shard_map/ppermute | solution.py:30
  82.0 10.6 %collective-permute-start.5 = (bf16[256,256]{1,0:T(8,128)(2,1)S(1)}, bf16[256,256]{1,0:T(8,128)(2,1)S(1)}, u32[]{:S(2)}, u32[]{:S(2)}) collective-permute-start(bf16[256,256]{1,0:T(8,128)(2,1)S(1)} %get-tuple-element.27), channel_id=1, source_target_pairs={{0,96},{32,64},{64,32},{96,0},{1,97},{33,65},{65,33},{97,1},{2,98}... | collective-permute-start | bytes 393224 | tf_op jit(solution)/shard_map/ppermute | solution.py:34
  134.6 9.5 %collective-permute-start.6 = (bf16[1152,256]{1,0:T(8,128)(2,1)S(1)}, bf16[1152,256]{1,0:T(8,128)(2,1)S(1)}, u32[]{:S(2)}, u32[]{:S(2)}) collective-permute-start(bf16[1152,256]{1,0:T(8,128)(2,1)S(1)} %pad_maximum_fusion), channel_id=1, source_target_pairs={{0,8},{8,0},{1,9},{9,1},{2,10},{10,2},{3,11},{11,3},{4,12},{12,4},... | collective-permute-start | bytes 1769480 | tf_op jit(solution)/shard_map/ppermute | solution.py:30

commit v15 on v14

--- a/solution.py
+++ b/solution.py
@@ -225,9 +225,9 @@
     far, rows[1] = lax.optimization_barrier((far, rows[1]))
     cold = spread(far, NEAR)
     rows = jnp.concatenate(rows, axis=0)
-    other, column = lax.optimization_barrier((swap(rows, "z2"), column))
-    rows = jnp.concatenate([rows, other], axis=0)
-    rows = [rows, swap(rows, "c")]
+    across = swap(rows, "c")
+    other, column, across = lax.optimization_barrier((swap(rows, "z2"), column, across))
+    rows = [rows, other, across, swap(other, "c")]
     mine = hot_table.reshape(2, NG, NC // 2, hot_own, width)
     mine = lax.dynamic_slice(mine, (k >> 2, 0, k & 3, 0, 0), (1, NG, 1, hot_own, width))
     mine = mine.reshape(NG, hot_own, width)

time: 146 us -> 150 us (1.027)
  starting transfers between devices: 53.3 us -> 60.3 us
  blocking collectives: 51 us -> 48 us
    ppermute x6 -> x7, starting transfers between devices: 22 us -> 25.8 us  [swap(): return lax.ppermute(x, axis, [(0, 1), (1, 0)])]
    all_to_all x1, starting transfers between devices: 3.71 us -> 6.94 us  [body(): near = lax.all_to_all(item_part, NEAR, 0, 0)]
    all_to_all x1, blocking collectives: 11.8 us -> 8.97 us  [body(): stats = lax.all_to_all(stats, COLS, 0, 0)]
    ppermute x6 -> x7, waiting for transfers between devices: 13.9 us -> 14.3 us  [swap(): return lax.ppermute(x, axis, [(0, 1), (1, 0)])]
  transfers between devices with their start and end apart: 10 -> 11, of which waited for: 8 -> 7; matrix products, arithmetic and copies ran while one was open for 1% -> 0% of each run, Pallas kernels for 2% -> 1%
where the time goes in v15:
time: 150 us; the launch traced here: 149 us
  starting transfers between devices  60.3 us (40%)
  blocking collectives  48 us (32%)
  waiting for transfers between devices  23.8 us (16%)
  Pallas kernels  12.4 us (8%)
  local copies, waits for them, and re-layouts  3.25 us (2%)
    ppermute x7, starting transfers between devices, swap(): return lax.ppermute(x, axis, [(0, 1), (1, 0)])  25.8 us
    all_to_all x2, starting transfers between devices, spread(): return lax.all_to_all(jnp.broadcast_to(x[None], (n, *x.shape)), axes, 0, 0)  22.5 us
    all_to_all x2, blocking collectives, spread(): return lax.all_to_all(jnp.broadcast_to(x[None], (n, *x.shape)), axes, 0, 0)  22.4 us
    all_to_all x1, blocking collectives, body(): lax.all_to_all(jnp.concatenate([cold_part, hot_part], axis=1), FAR, 0, 0)  16.6 us
    ppermute x7, waiting for transfers between devices, swap(): return lax.ppermute(x, axis, [(0, 1), (1, 0)])  14.3 us
    all_to_all x1, blocking collectives, body(): stats = lax.all_to_all(stats, COLS, 0, 0)  8.97 us
    all_to_all x2, waiting for transfers between devices, spread(): return lax.all_to_all(jnp.broadcast_to(x[None], (n, *x.shape)), axes, 0, 0)  7.29 us
    all_to_all x1, starting transfers between devices, body(): near = lax.all_to_all(item_part, NEAR, 0, 0)  6.94 us
  transfers between devices with their start and end apart: 11, of which 7 were waited for; matrix products, arithmetic and copies ran while one was open for 0% of the time, Pallas kernels for 1%

profile of v15, /device:TPU:1, one launch (start us, length us, event | category | flops | bytes accessed | tf_op | source)
XLA Modules:
  0.0 149.1 jit_solution(16445022622929103889)
XLA Ops:
  0.6 0.0 copy-start
  0.6 1.4 broadcast_in_dim.12
  2.1 15.6 %all-to-all-start = ((bf16[4,32,256]{2,1,0:T(8,128)(2,1)}), bf16[4,32,256]{2,1,0:T(8,128)(2,1)S(1)}, u32[]{:S(2)}, u32[]{:S(2)}) async-start(bf16[4,32,256]{2,1,0:T(8,128)(2,1)} %broadcast_in_dim.12), calls=%async_computation | async-start | bytes 131072 | tf_op jit(solution)/shard_map/all_to_all | solution.py:26
  17.7 2.6 %collective-permute-start = (bf16[128,256]{1,0:T(8,128)(2,1)}, bf16[128,256]{1,0:T(8,128)(2,1)S(1)}, u32[]{:S(2)}, u32[]{:S(2)}) collective-permute-start(bf16[128,256]{1,0:T(8,128)(2,1)} %param.5), channel_id=1, source_target_pairs={{0,32},{32,0},{1,33},{33,1},{2,34},{34,2},{3,35},{35,3},{4,36},{36... | collective-permute-start | bytes 196616 | tf_op jit(solution)/shard_map/ppermute | solution.py:30
  20.4 2.6 %collective-permute-done = bf16[128,256]{1,0:T(8,128)(2,1)S(1)} collective-permute-done((bf16[128,256]{1,0:T(8,128)(2,1)}, bf16[128,256]{1,0:T(8,128)(2,1)S(1)}, u32[]{:S(2)}, u32[]{:S(2)}) %collective-permute-start) | collective-permute-done | bytes 65568 | tf_op jit(solution)/shard_map/ppermute | solution.py:30
  22.9 7.3 %all-to-all-done = bf16[4,32,256]{2,1,0:T(8,128)(2,1)S(1)} async-done(((bf16[4,32,256]{2,1,0:T(8,128)(2,1)}), bf16[4,32,256]{2,1,0:T(8,128)(2,1)S(1)}, u32[]{:S(2)}, u32[]{:S(2)}) %all-to-all-start) | async-done | bytes 65568 | tf_op jit(solution)/shard_map/all_to_all | solution.py:26
  30.2 1.1 broadcast_in_dim.13
  31.3 6.9 %all-to-all-start.1 = ((bf16[16,128,256]{2,1,0:T(8,128)(2,1)}), bf16[16,128,256]{2,1,0:T(8,128)(2,1)S(1)}, u32[]{:S(2)}, u32[]{:S(2)}) async-start(bf16[16,128,256]{2,1,0:T(8,128)(2,1)} %broadcast_in_dim.13), calls=%async_computation.1 | async-start | bytes 2097152 | tf_op jit(solution)/shard_map/all_to_all | solution.py:26
  38.2 3.8 %collective-permute-start.2 = (bf16[256,256]{1,0:T(8,128)(2,1)S(1)}, bf16[256,256]{1,0:T(8,128)(2,1)S(1)}, u32[]{:S(2)}, u32[]{:S(2)}) collective-permute-start(bf16[256,256]{1,0:T(8,128)(2,1)S(1)} %constant_dynamic-update-slice_fusion.refs_0_), channel_id=1, source_target_pairs={{0,8},{8,0},{1,9},{9,1},{2,10},{10,2},{3,11},{11,3},{4,12},{12,4},... | collective-permute-start | bytes 393224 | tf_op jit(solution)/shard_map/ppermute | solution.py:30
  42.0 4.0 %collective-permute-start.1 = (bf16[256,256]{1,0:T(8,128)(2,1)S(1)}, bf16[256,256]{1,0:T(8,128)(2,1)S(1)}, u32[]{:S(2)}, u32[]{:S(2)}) collective-permute-start(bf16[256,256]{1,0:T(8,128)(2,1)S(1)} %constant_dynamic-update-slice_fusion.refs_0_), channel_id=1, source_target_pairs={{0,64},{64,0},{1,65},{65,1},{2,66},{66,2},{3,67},{67,3},{4,68},{68... | collective-permute-start | bytes 393224 | tf_op jit(solution)/shard_map/ppermute | solution.py:30
  46.1 2.2 %shard_map.84.col_ref = s32[1,1024]{1,0:T(1,128)S(1)} custom-call(s32[1]{0:T(128)} %bitcast.me_ref, s32[16,128]{1,0:T(8,128)S(1)} %bitcast.17, s32[512,1,128]{2,1,0:T(1,128)S(1)} %bitcast.16), custom_call_target="tpu_custom_call" | custom-call | flops 12582912 | bytes 1048576 | tf_op jit(solution)/shard_map/pallas_call | solution.py:213
  48.4 4.4 %collective-permute-done.1.refs_1_ = bf16[256,256]{1,0:T(8,128)(2,1)S(1)} collective-permute-done((bf16[256,256]{1,0:T(8,128)(2,1)S(1)}, bf16[256,256]{1,0:T(8,128)(2,1)S(1)}, u32[]{:S(2)}, u32[]{:S(2)}) %collective-permute-start.1) | collective-permute-done | bytes 131104 | tf_op jit(solution)/shard_map/ppermute | solution.py:30
  52.7 2.7 %collective-permute-start.3 = (bf16[256,256]{1,0:T(8,128)(2,1)S(1)}, bf16[256,256]{1,0:T(8,128)(2,1)S(1)}, u32[]{:S(2)}, u32[]{:S(2)}) collective-permute-start(bf16[256,256]{1,0:T(8,128)(2,1)S(1)} %collective-permute-done.1.refs_1_), channel_id=1, source_target_pairs={{0,8},{8,0},{1,9},{9,1},{2,10},{10,2},{3,11},{11,3},{4,12},{12,4},... | collective-permute-start | bytes 393224 | tf_op jit(solution)/shard_map/ppermute | solution.py:30
  55.5 0.9 collective-permute-done.3.refs_3_
  56.4 3.6 %shard_map.85 = f32[8,2,1024]{2,1,0:T(2,128)S(1)} custom-call(s32[1]{0:T(128)} %bitcast.me_ref, bf16[16,128,256]{2,1,0:T(8,128)(2,1)S(1)} %all-to-all-done.1.cold_ref, bf16[16,16,256]{2,1,0:T(8,128)(2,1)S(1)} %dynamic-slice_bitcast_fusion.hot_ref, s32[1,1024]{1,0:T(1,128)S(1)} %shard_map.84.col_ref, ...), custom_call_target="tpu_custom_call" | custom-call | tf_op jit(solution)/shard_map/pallas_call | solution.py:235
  60.0 9.0 %all_to_all.35.stats_ref = f32[8,2,1024]{2,1,0:T(2,128)S(1)} all-to-all(f32[8,2,1024]{2,1,0:T(2,128)S(1)} %shard_map.85), channel_id=1, replica_groups=mesh['z8'=2,'z4'=2,'z2'=2,'z1'=2,'yl'=2,'c'=2,'x2'=2,'x1'=2,'yh'=2] {'c'..., dimensions={0} | all-to-all | bytes 131072 | tf_op jit(solution)/shard_map/all_to_all | solution.py:241
  69.0 5.6 %shard_map.86 = (f32[256,256]{1,0:T(8,128)S(1)}, bf16[256,256]{1,0:T(8,128)(2,1)S(1)}, bf16[256,256]{1,0:T(8,128)(2,1)S(1)}, bf16[256,256]{1,0:T(8,128)(2,1)S(1)...) custom-call(s32[1]{0:T(128)} %bitcast.me_ref, bf16[16,128,256]{2,1,0:T(8,128)(2,1)S(1)} %all-to-all-done.1.cold_ref, ...), custom_call_target="tpu_custom_call" | custom-call | tf_op jit(solution)/shard_map/pallas_call | solution.py:242
  74.6 6.9 %all-to-all-start.3 = ((bf16[16,144,256]{2,1,0:T(8,128)(2,1)}), bf16[16,144,256]{2,1,0:T(8,128)(2,1)S(1)}, u32[]{:S(2)}, u32[]{:S(2)}) async-start(bf16[16,144,256]{2,1,0:T(8,128)(2,1)} %get-tuple-element.25), calls=%async_computation.3 | async-start | bytes 2359296 | tf_op jit(solution)/shard_map/all_to_all | solution.py:260
  81.5 2.0 %collective-permute-start.4 = (bf16[256,256]{1,0:T(8,128)(2,1)S(1)}, bf16[256,256]{1,0:T(8,128)(2,1)S(1)}, u32[]{:S(2)}, u32[]{:S(2)}) collective-permute-start(bf16[256,256]{1,0:T(8,128)(2,1)S(1)} %get-tuple-element.27), channel_id=1, source_target_pairs={{0,32},{32,0},{1,33},{33,1},{2,34},{34,2},{3,35},{35,3},{4,36},{36... | collective-permute-start | bytes 393224 | tf_op jit(solution)/shard_map/ppermute | solution.py:30
  83.6 2.2 %collective-permute-start.5 = (bf16[256,256]{1,0:T(8,128)(2,1)S(1)}, bf16[256,256]{1,0:T(8,128)(2,1)S(1)}, u32[]{:S(2)}, u32[]{:S(2)}) collective-permute-start(bf16[256,256]{1,0:T(8,128)(2,1)S(1)} %get-tuple-element.28), channel_id=1, source_target_pairs={{0,64},{64,0},{1,65},{65,1},{2,66},{66,2},{3,67},{67,3},{4,68},{68... | collective-permute-start | bytes 393224 | tf_op jit(solution)/shard_map/ppermute | solution.py:30
  85.7 5.1 %collective-permute-start.6 = (bf16[256,256]{1,0:T(8,128)(2,1)S(1)}, bf16[256,256]{1,0:T(8,128)(2,1)S(1)}, u32[]{:S(2)}, u32[]{:S(2)}) collective-permute-start(bf16[256,256]{1,0:T(8,128)(2,1)S(1)} %get-tuple-element.29), channel_id=1, source_target_pairs={{0,96},{32,64},{64,32},{96,0},{1,97},{33,65},{65,33},{97,1},{2,98}... | collective-permute-start | bytes 393224 | tf_op jit(solution)/shard_map/ppermute | solution.py:34
  90.8 5.4 %collective-permute-done.5 = bf16[256,256]{1,0:T(8,128)(2,1)S(1)} collective-permute-done((bf16[256,256]{1,0:T(8,128)(2,1)S(1)}, bf16[256,256]{1,0:T(8,128)(2,1)S(1)}, u32[]{:S(2)}, u32[]{:S(2)}) %collective-permute-start.5) | collective-permute-done | bytes 131104 | tf_op jit(solution)/shard_map/ppermute | solution.py:30
  96.3 0.1 add_add_fusion
  96.4 2.2 %all-to-all-done.3 = bf16[16,144,256]{2,1,0:T(8,128)(2,1)S(1)} async-done(((bf16[16,144,256]{2,1,0:T(8,128)(2,1)}), bf16[16,144,256]{2,1,0:T(8,128)(2,1)S(1)}, u32[]{:S(2)}, u32[]{:S(2)}) %all-to-all-start.3) | async-done | bytes 1179680 | tf_op jit(solution)/shard_map/all_to_all | solution.py:260
  98.6 0.2 reduce_sum.24
  98.8 16.6 %all_to_all.36 = bf16[4,48,256]{2,1,0:T(8,128)(2,1)S(1)} all-to-all(bf16[4,48,256]{2,1,0:T(8,128)(2,1)S(1)} %pad_maximum_fusion.1), channel_id=1, replica_groups=mesh['z8'=2,'z4'=2,'z2'=2,'z1'=2,'yl'=2,'c'=2,'x2'=2,'x1'=2,'yh'=2] {'z8..., dimensions={0} | all-to-all | bytes 196608 | tf_op jit(solution)/shard_map/all_to_all | solution.py:266
  115.5 7.0 %all_to_all.37 = bf16[4,16,256]{2,1,0:T(8,128)(2,1)S(1)} all-to-all(bf16[4,16,256]{2,1,0:T(8,128)(2,1)S(1)} %broadcast_in_dim.15), channel_id=1, replica_groups=mesh['z8'=2,'z4'=2,'z2'=2,'z1'=2,'yl'=2,'c'=2,'x2'=2,'x1'=2,'yh'=2] {'z2..., dimensions={0} | all-to-all | bytes 65536 | tf_op jit(solution)/shard_map/all_to_all | solution.py:26
  122.5 15.4 %all_to_all.38 = bf16[16,64,256]{2,1,0:T(8,128)(2,1)S(1)} all-to-all(bf16[16,64,256]{2,1,0:T(8,128)(2,1)S(1)} %broadcast_in_dim.17), channel_id=1, replica_groups=mesh['z8'=2,'z4'=2,'z2'=2,'z1'=2,'yl'=2,'c'=2,'x2'=2,'x1'=2,'yh'=2] {'x2..., dimensions={0} | all-to-all | bytes 1048576 | tf_op jit(solution)/shard_map/all_to_all | solution.py:26
  138.0 8.5 %collective-permute-start.7 = (bf16[1152,256]{1,0:T(8,128)(2,1)S(1)}, bf16[1152,256]{1,0:T(8,128)(2,1)S(1)}, u32[]{:S(2)}, u32[]{:S(2)}) collective-permute-start(bf16[1152,256]{1,0:T(8,128)(2,1)S(1)} %pad_maximum_fusion), channel_id=1, source_target_pairs={{0,8},{8,0},{1,9},{9,1},{2,10},{10,2},{3,11},{11,3},{4,12},{12,4},... | collective-permute-start | bytes 1769480 | tf_op jit(solution)/shard_map/ppermute | solution.py:30
  146.5 0.6 slice.30
  147.1 1.0 collective-permute-done.7.other_ref
  148.1 1.0 shard_map.87
  (25 shorter events, 0.2 us)
Async XLA Ops:
  0.6 54.8 %copy-start = (bf16[2048,256]{1,0:T(8,128)(2,1)S(1)}, bf16[2048,256]{1,0:T(8,128)(2,1)}, u32[]{:S(2)}) copy-start(bf16[2048,256]{1,0:T(8,128)(2,1)} %param.6) | copy-start | bytes 3145732
  2.1 28.1 %all-to-all-start = ((bf16[4,32,256]{2,1,0:T(8,128)(2,1)}), bf16[4,32,256]{2,1,0:T(8,128)(2,1)S(1)}, u32[]{:S(2)}, u32[]{:S(2)}) async-start(bf16[4,32,256]{2,1,0:T(8,128)(2,1)} %broadcast_in_dim.12), calls=%async_computation | async-start | bytes 131072 | tf_op jit(solution)/shard_map/all_to_all | solution.py:26
  17.7 5.2 %collective-permute-start = (bf16[128,256]{1,0:T(8,128)(2,1)}, bf16[128,256]{1,0:T(8,128)(2,1)S(1)}, u32[]{:S(2)}, u32[]{:S(2)}) collective-permute-start(bf16[128,256]{1,0:T(8,128)(2,1)} %param.5), channel_id=1, source_target_pairs={{0,32},{32,0},{1,33},{33,1},{2,34},{34,2},{3,35},{35,3},{4,36},{36... | collective-permute-start | bytes 196616 | tf_op jit(solution)/shard_map/ppermute | solution.py:30
  31.3 6.9 %copy-start.3 = (bf16[128,256]{1,0:T(8,128)(2,1)S(1)}, bf16[128,256]{1,0:T(8,128)(2,1)}, u32[]{:S(2)}) copy-start(bf16[128,256]{1,0:T(8,128)(2,1)} %param.5) | copy-start | bytes 196612
  31.3 14.8 %copy-start.1 = (s32[65536]{0:T(1024)S(1)}, s32[65536]{0:T(1024)}, u32[]{:S(2)}) copy-start(s32[65536]{0:T(1024)} %param.9) | copy-start | bytes 786436
  31.3 14.8 %copy-start.2 = (s32[2048]{0:T(1024)S(1)}, s32[2048]{0:T(1024)}, u32[]{:S(2)}) copy-start(s32[2048]{0:T(1024)} %param.8) | copy-start | bytes 24580
  31.3 25.1 %all-to-all-start.1 = ((bf16[16,128,256]{2,1,0:T(8,128)(2,1)}), bf16[16,128,256]{2,1,0:T(8,128)(2,1)S(1)}, u32[]{:S(2)}, u32[]{:S(2)}) async-start(bf16[16,128,256]{2,1,0:T(8,128)(2,1)} %broadcast_in_dim.13), calls=%async_computation.1 | async-start | bytes 2097152 | tf_op jit(solution)/shard_map/all_to_all | solution.py:26
  38.2 10.1 %collective-permute-start.2 = (bf16[256,256]{1,0:T(8,128)(2,1)S(1)}, bf16[256,256]{1,0:T(8,128)(2,1)S(1)}, u32[]{:S(2)}, u32[]{:S(2)}) collective-permute-start(bf16[256,256]{1,0:T(8,128)(2,1)S(1)} %constant_dynamic-update-slice_fusion.refs_0_), channel_id=1, source_target_pairs={{0,8},{8,0},{1,9},{9,1},{2,10},{10,2},{3,11},{11,3},{4,12},{12,4},... | collective-permute-start | bytes 393224 | tf_op jit(solution)/shard_map/ppermute | solution.py:30
  42.0 10.7 %collective-permute-start.1 = (bf16[256,256]{1,0:T(8,128)(2,1)S(1)}, bf16[256,256]{1,0:T(8,128)(2,1)S(1)}, u32[]{:S(2)}, u32[]{:S(2)}) collective-permute-start(bf16[256,256]{1,0:T(8,128)(2,1)S(1)} %constant_dynamic-update-slice_fusion.refs_0_), channel_id=1, source_target_pairs={{0,64},{64,0},{1,65},{65,1},{2,66},{66,2},{3,67},{67,3},{4,68},{68... | collective-permute-start | bytes 393224 | tf_op jit(solution)/shard_map/ppermute | solution.py:30
  52.7 3.7 %collective-permute-start.3 = (bf16[256,256]{1,0:T(8,128)(2,1)S(1)}, bf16[256,256]{1,0:T(8,128)(2,1)S(1)}, u32[]{:S(2)}, u32[]{:S(2)}) collective-permute-start(bf16[256,256]{1,0:T(8,128)(2,1)S(1)} %collective-permute-done.1.refs_1_), channel_id=1, source_target_pairs={{0,8},{8,0},{1,9},{9,1},{2,10},{10,2},{3,11},{11,3},{4,12},{12,4},... | collective-permute-start | bytes 393224 | tf_op jit(solution)/shard_map/ppermute | solution.py:30
  74.6 24.0 %all-to-all-start.3 = ((bf16[16,144,256]{2,1,0:T(8,128)(2,1)}), bf16[16,144,256]{2,1,0:T(8,128)(2,1)S(1)}, u32[]{:S(2)}, u32[]{:S(2)}) async-start(bf16[16,144,256]{2,1,0:T(8,128)(2,1)} %get-tuple-element.25), calls=%async_computation.3 | async-start | bytes 2359296 | tf_op jit(solution)/shard_map/all_to_all | solution.py:260
  81.5 9.3 %collective-permute-start.4 = (bf16[256,256]{1,0:T(8,128)(2,1)S(1)}, bf16[256,256]{1,0:T(8,128)(2,1)S(1)}, u32[]{:S(2)}, u32[]{:S(2)}) collective-permute-start(bf16[256,256]{1,0:T(8,128)(2,1)S(1)} %get-tuple-element.27), channel_id=1, source_target_pairs={{0,32},{32,0},{1,33},{33,1},{2,34},{34,2},{3,35},{35,3},{4,36},{36... | collective-permute-start | bytes 393224 | tf_op jit(solution)/shard_map/ppermute | solution.py:30
  83.6 12.7 %collective-permute-start.5 = (bf16[256,256]{1,0:T(8,128)(2,1)S(1)}, bf16[256,256]{1,0:T(8,128)(2,1)S(1)}, u32[]{:S(2)}, u32[]{:S(2)}) collective-permute-start(bf16[256,256]{1,0:T(8,128)(2,1)S(1)} %get-tuple-element.28), channel_id=1, source_target_pairs={{0,64},{64,0},{1,65},{65,1},{2,66},{66,2},{3,67},{67,3},{4,68},{68... | collective-permute-start | bytes 393224 | tf_op jit(solution)/shard_map/ppermute | solution.py:30
  85.7 10.5 %collective-permute-start.6 = (bf16[256,256]{1,0:T(8,128)(2,1)S(1)}, bf16[256,256]{1,0:T(8,128)(2,1)S(1)}, u32[]{:S(2)}, u32[]{:S(2)}) collective-permute-start(bf16[256,256]{1,0:T(8,128)(2,1)S(1)} %get-tuple-element.29), channel_id=1, source_target_pairs={{0,96},{32,64},{64,32},{96,0},{1,97},{33,65},{65,33},{97,1},{2,98}... | collective-permute-start | bytes 393224 | tf_op jit(solution)/shard_map/ppermute | solution.py:34
  138.0 10.1 %collective-permute-start.7 = (bf16[1152,256]{1,0:T(8,128)(2,1)S(1)}, bf16[1152,256]{1,0:T(8,128)(2,1)S(1)}, u32[]{:S(2)}, u32[]{:S(2)}) collective-permute-start(bf16[1152,256]{1,0:T(8,128)(2,1)S(1)} %pad_maximum_fusion), channel_id=1, source_target_pairs={{0,8},{8,0},{1,9},{9,1},{2,10},{10,2},{3,11},{11,3},{4,12},{12,4},... | collective-permute-start | bytes 1769480 | tf_op jit(solution)/shard_map/ppermute | solution.py:30
